TPU v7x, 32 devices: a whole 2x2x4 slice. The times are simulated.
32 devices in a mesh: expert: 4 (over z), context: 4 (over y, core), dp: 2 (over x).
Axes of the slice: x: 2, y: 2, z: 4, core: 2. Of those that a mesh axis runs over, the one named last changes fastest.
Arguments:
- hidden_in: bfloat16 [8, 1024, 2048], P(('expert', 'dp'), 'context'), may hold values from -6 to 6
- out_grad: bfloat16 [8, 1024, 2048], P(('expert', 'dp'), 'context'), may hold values from -6 to 6
- routes: int32 [8, 1024, 8], P(('expert', 'dp'), 'context'), may hold values from 0 to 15, all different within a row; in each aligned block of 256 rows (0 to 255, 256 to 511, ..., all dimensions but the last counted through in order) at most 144 rows name the same one
- attn_gain: bfloat16 [2048], P(('expert', 'context')), may hold values from 0.25 to 1.75
- w_query: bfloat16 [2048, 2048], P(('expert', 'context')), may hold values from -0.125 to 0.125
- w_key: bfloat16 [2048, 2048], P(('expert', 'context')), may hold values from -0.125 to 0.125
- w_value: bfloat16 [2048, 2048], P(('expert', 'context')), may hold values from -0.125 to 0.125
- q_gain: bfloat16 [2048], P(('expert', 'context')), may hold values from 0.25 to 1.75
- k_gain: bfloat16 [2048], P(('expert', 'context')), may hold values from 0.25 to 1.75
- w_out: bfloat16 [2048, 2048], P(('expert', 'context')), may hold values from -2.5 to 2.5
- ffn_gain: bfloat16 [2048], P(('expert', 'context')), may hold values from 0.25 to 1.75
- w_router: bfloat16 [2048, 16], P(('expert', 'context')), may hold values from -0.0625 to 0.0625
- w_gate: bfloat16 [16, 2048, 1024], P('expert'), may hold values from -0.125 to 0.125
- w_up: bfloat16 [16, 2048, 1024], P('expert'), may hold values from -0.125 to 0.125
- w_down: bfloat16 [16, 1024, 2048], P('expert'), may hold values from -0.75 to 0.75
Outputs:
- hidden_out: bfloat16 [8, 1024, 2048], P(('expert', 'dp'), 'context')
- input_grad: bfloat16 [8, 1024, 2048], P(('expert', 'dp'), 'context')
- attn_gain_grad: float32 [2048], P(('expert', 'context'))
- w_query_grad: float32 [2048, 2048], P(('expert', 'context'))
- w_key_grad: float32 [2048, 2048], P(('expert', 'context'))
- w_value_grad: float32 [2048, 2048], P(('expert', 'context'))
- q_gain_grad: float32 [2048], P(('expert', 'context'))
- k_gain_grad: float32 [2048], P(('expert', 'context'))
- w_out_grad: float32 [2048, 2048], P(('expert', 'context'))
- ffn_gain_grad: float32 [2048], P(('expert', 'context'))
- w_router_grad: float32 [2048, 16], P(('expert', 'context'))
- w_gate_grad: float32 [16, 2048, 1024], P('expert')
- w_up_grad: float32 [16, 2048, 1024], P('expert')
- w_down_grad: float32 [16, 1024, 2048], P('expert')
Inputs may be any that keep to these rules, and one draw needn't show every extreme that they name: `routes`: each token names 8 different experts. At most 144 tokens of one device name the same expert, a bound that some block reaches of one device.
All inputs are finite; a program needn't handle non-finite values.
Results may differ from a plain program's by a relative error of at most 0.02.
Values may be sent and summed in bfloat16 or wider, within the bound.
No kernel may reach another device: no remote copies, remote signals or barrier semaphores. Data moves between devices by JAX's collectives and lax.ppermute only.
A program may use at most 512 MiB of HBM per device.

v0:
```python
import functools

import jax
import jax.numpy as jnp
from jax import lax
from jax.sharding import PartitionSpec as P

HEADS = 16
HDIM = 128

epsilon = 1e-06
rope_base = 10000.0
F32 = jnp.float32
BF16 = jnp.bfloat16


def dot(left, right, contract):
    return lax.dot_general(
        left, right, (((contract[0],), (contract[1],)), ((), ())), preferred_element_type=F32
    )


def rms_factor(values):
    return lax.rsqrt(jnp.mean(values * values, axis=-1, keepdims=True) + epsilon)


def norm_back(grad_out, values, factor, gain_vector):
    scaled = grad_out * gain_vector
    grad_in = factor * scaled - values * factor**3 * jnp.mean(
        scaled * values, axis=-1, keepdims=True
    )
    gain_grad = jnp.sum(grad_out * values * factor, axis=0)
    return (grad_in, gain_grad)


def rotate(values, cosine, sine_part):
    first_half = values[..., : HDIM // 2]
    second_half = values[..., HDIM // 2 :]
    return jnp.concatenate(
        [
            first_half * cosine - second_half * sine_part,
            second_half * cosine + first_half * sine_part,
        ],
        axis=-1,
    )


def gather(values, axis):
    return lax.all_gather(values, axis, axis=0, tiled=True)


def scatter_sum(values, axis):
    return lax.psum_scatter(values, axis, scatter_dimension=0, tiled=True)


def head_rows(weight, context, mine):
    rows, width = weight.shape
    per = HEADS // context
    split = weight.reshape(rows, per, context, HDIM)
    return split.transpose(2, 0, 1, 3).reshape(context, rows, per * HDIM)


def body(
    hidden_in,
    out_grad,
    routes,
    attn_gain,
    w_query,
    w_key,
    w_value,
    q_gain,
    k_gain,
    w_out,
    ffn_gain,
    w_router,
    w_gate,
    w_up,
    w_down,
):
    groups = lax.axis_size("expert")
    context = lax.axis_size("context")
    my_group = lax.axis_index("expert")
    my_context = lax.axis_index("context")
    tokens = hidden_in.shape[1]
    width = hidden_in.shape[2]
    rows = w_query.shape[0]
    local_experts = w_gate.shape[0]
    experts_all = w_router.shape[1]
    length = tokens * context
    per = HEADS // context
    local = per * HDIM
    score_scale = HDIM ** (-0.5)

    hidden_all = gather(hidden_in[0], "context")
    small = jnp.concatenate(
        [
            attn_gain[:, None],
            q_gain[:, None],
            k_gain[:, None],
            ffn_gain[:, None],
            w_router,
        ],
        axis=1,
    )
    small_all = gather(small, ("expert", "context"))
    columns = jnp.concatenate(
        [head_rows(w, context, my_context) for w in (w_query, w_key, w_value)], axis=2
    )
    columns = lax.all_to_all(columns, "context", split_axis=0, concat_axis=0, tiled=True)
    qkv_w = gather(columns.reshape(context * rows, 3 * local), "expert")
    whole_heads = rows == HDIM
    if whole_heads:
        out_w = gather(w_out, "expert")
    else:
        out_w = gather(w_out, ("expert", "context")).reshape(per, context, HDIM, width)
        out_w = lax.dynamic_index_in_dim(out_w, my_context, 1, keepdims=False)
        out_w = out_w.reshape(local, width)
    upstream_all = gather(out_grad[0], "expert")
    routes_all = gather(routes[0], "expert")

    gain_attn = small_all[:, 0].astype(F32)
    gain_ffn = small_all[:, 3].astype(F32)
    router_w = small_all[:, 4:]

    def mine(vector):
        table = vector.reshape(per, context, HDIM)
        return lax.dynamic_index_in_dim(table, my_context, 1, keepdims=False).astype(F32)

    gain_query, gain_key = mine(small_all[:, 1]), mine(small_all[:, 2])

    source_all = hidden_all.astype(F32)
    factor_all = rms_factor(source_all)
    normed = (source_all * factor_all * gain_attn).astype(BF16)
    source = hidden_in[0].astype(F32)
    factor_one = rms_factor(source)
    qkv = dot(normed, qkv_w, (1, 0))
    query_raw = qkv[:, :local]
    key_raw = qkv[:, local : 2 * local]
    value_low = qkv[:, 2 * local :].astype(BF16).reshape(length, per, HDIM)
    squares = jnp.stack(
        [jnp.sum(query_raw * query_raw, axis=-1), jnp.sum(key_raw * key_raw, axis=-1)], axis=0
    )
    squares = lax.psum(squares, "context")
    factors = lax.rsqrt(squares / width + epsilon)
    factor_query, factor_key = factors[0][:, None, None], factors[1][:, None, None]
    query_raw = query_raw.reshape(length, per, HDIM)
    key_raw = key_raw.reshape(length, per, HDIM)
    positions = jnp.arange(length, dtype=jnp.int32).astype(F32)
    frequency = rope_base ** (-jnp.arange(HDIM // 2, dtype=F32) * 2.0 / HDIM)
    angles = positions[:, None] * frequency[None, :]
    cosine = jnp.cos(angles)[:, None, :]
    sine_part = jnp.sin(angles)[:, None, :]
    query_low = rotate(query_raw * factor_query * gain_query, cosine, sine_part).astype(BF16)
    key_low = rotate(key_raw * factor_key * gain_key, cosine, sine_part).astype(BF16)
    scores = (
        jnp.einsum("qhd,khd->hqk", query_low, key_low, preferred_element_type=F32) * score_scale
    )
    score_max = jnp.max(scores, axis=-1, keepdims=True)
    denominator = jnp.sum(jnp.exp(scores - score_max), axis=-1, keepdims=True)
    logsum = score_max + jnp.log(denominator)
    probs = jnp.exp(scores - logsum)
    mixed_low = (
        jnp.einsum("hqk,khd->qhd", probs.astype(BF16), value_low, preferred_element_type=F32)
        .reshape(length, local)
        .astype(BF16)
    )
    mixed_out = scatter_sum(dot(mixed_low, out_w, (1, 0)).astype(BF16), "context")
    residual = source + mixed_out.astype(F32)
    factor_two = rms_factor(residual)
    normed_two = (residual * factor_two * gain_ffn).astype(BF16)

    rows_all = gather(normed_two, "expert")
    logits = dot(rows_all, router_w, (1, 0))
    ids = jnp.arange(experts_all, dtype=jnp.int32)
    chosen = jnp.any(routes_all[:, :, None] == ids, axis=1)
    top = jnp.max(jnp.where(chosen, logits, -jnp.inf), axis=-1, keepdims=True)
    raised = jnp.where(chosen, jnp.exp(jnp.where(chosen, logits - top, 0.0)), 0.0)
    weights_all = raised / jnp.sum(raised, axis=-1, keepdims=True)
    weights_here = lax.dynamic_slice_in_dim(
        weights_all, my_group * local_experts, local_experts, axis=1
    )
    out_part = 0.0
    row_part = 0.0
    gate_grads, grads = [], []
    for e in range(local_experts):
        weight = weights_here[:, e : e + 1]
        gate_pre = dot(rows_all, w_gate[e], (1, 0))
        up_pre = dot(rows_all, w_up[e], (1, 0))
        sigmoid = jax.nn.sigmoid(gate_pre)
        activated = gate_pre * sigmoid
        hidden = activated * up_pre
        hidden_low = (weight * hidden).astype(BF16)
        out_part = out_part + dot(hidden_low, w_down[e], (1, 0))
        hidden_grad = dot(upstream_all, w_down[e], (1, 1))
        gate_grads.append(jnp.sum(hidden * hidden_grad, axis=-1))
        hidden_grad = hidden_grad * weight
        gate_pre_grad = (hidden_grad * up_pre * sigmoid * (1.0 + gate_pre * (1.0 - sigmoid))).astype(
            BF16
        )
        up_pre_grad = (hidden_grad * activated).astype(BF16)
        row_part = (
            row_part + dot(gate_pre_grad, w_gate[e], (1, 1)) + dot(up_pre_grad, w_up[e], (1, 1))
        )
        local_grads = (
            dot(rows_all, gate_pre_grad, (0, 0)).astype(BF16),
            dot(rows_all, up_pre_grad, (0, 0)).astype(BF16),
            dot(hidden_low, upstream_all, (0, 0)).astype(BF16),
        )
        grads.append(lax.psum(local_grads, ("context", "dp")))
    expert_grads = [jnp.stack([g[i].astype(F32) for g in grads]) for i in range(3)]

    row_back = scatter_sum(row_part.astype(BF16), "expert").astype(F32)
    gate_grad = jnp.stack(gate_grads, axis=1).reshape(groups, tokens, local_experts)
    gate_grad = lax.all_to_all(gate_grad, "expert", split_axis=0, concat_axis=0, tiled=True)
    gate_grad = gate_grad.transpose(1, 0, 2).reshape(tokens, experts_all)
    produced_sum = scatter_sum(out_part.astype(BF16), "expert").astype(F32)
    hidden_out = (residual + produced_sum).astype(BF16)[None]

    upstream = out_grad[0].astype(F32)
    weights_own = lax.dynamic_slice_in_dim(weights_all, my_group * tokens, tokens, axis=0)
    weighted = jnp.sum(weights_own * gate_grad, axis=-1, keepdims=True)
    logit_grad = (weights_own * (gate_grad - weighted)).astype(BF16)
    router_grad = dot(normed_two, logit_grad, (0, 0))
    normed_two_grad = dot(logit_grad, router_w, (1, 1)) + row_back
    residual_part, ffn_gain_grad = norm_back(normed_two_grad, residual, factor_two, gain_ffn)
    residual_grad = upstream + residual_part

    attn_grad = gather(residual_grad.astype(BF16), "context")
    out_w_grad = dot(mixed_low, attn_grad, (0, 0))
    mixed_grad = dot(attn_grad, out_w, (1, 1)).astype(BF16).reshape(length, per, HDIM)
    scores = (
        jnp.einsum("qhd,khd->hqk", query_low, key_low, preferred_element_type=F32) * score_scale
    )
    probs = jnp.exp(scores - logsum)
    prob_grad = jnp.einsum("qhd,khd->hqk", mixed_grad, value_low, preferred_element_type=F32)
    row_shift = jnp.sum(probs * prob_grad, axis=-1, keepdims=True)
    score_grad = (probs * (prob_grad - row_shift)).astype(BF16)
    query_rot = (
        jnp.einsum("hqk,khd->qhd", score_grad, key_low, preferred_element_type=F32) * score_scale
    )
    key_rot = (
        jnp.einsum("hqk,qhd->khd", score_grad, query_low, preferred_element_type=F32) * score_scale
    )
    value_grad = jnp.einsum(
        "hqk,qhd->khd", probs.astype(BF16), mixed_grad, preferred_element_type=F32
    )
    query_back = rotate(query_rot, cosine, -sine_part)
    key_back = rotate(key_rot, cosine, -sine_part)
    sums = jnp.stack(
        [
            jnp.sum(query_back * gain_query * query_raw, axis=(1, 2)),
            jnp.sum(key_back * gain_key * key_raw, axis=(1, 2)),
        ],
        axis=0,
    )
    sums = lax.psum(sums, "context") / width
    query_grad = (
        factor_query * query_back * gain_query
        - query_raw * factor_query**3 * sums[0][:, None, None]
    )
    key_grad = (
        factor_key * key_back * gain_key - key_raw * factor_key**3 * sums[1][:, None, None]
    )
    q_gain_grad = jnp.sum(query_back * query_raw * factor_query, axis=0)
    k_gain_grad = jnp.sum(key_back * key_raw * factor_key, axis=0)
    qkv_grad = jnp.concatenate(
        [g.reshape(length, local).astype(BF16) for g in (query_grad, key_grad, value_grad)], axis=1
    )
    normed_grad = scatter_sum(dot(qkv_grad, qkv_w, (1, 1)).astype(BF16), "context").astype(F32)
    source_part, attn_gain_grad = norm_back(normed_grad, source, factor_one, gain_attn)
    input_grad = (residual_grad + source_part).astype(BF16)[None]

    qkv_w_grad = dot(normed, qkv_grad, (0, 0)).astype(BF16)
    qkv_w_grad = lax.psum(scatter_sum(qkv_w_grad, "expert"), "dp")
    qkv_w_grad = lax.all_to_all(
        qkv_w_grad.reshape(context, rows, 3 * local),
        "context",
        split_axis=0,
        concat_axis=0,
        tiled=True,
    ).astype(F32)
    qkv_w_grad = qkv_w_grad.reshape(context, rows, 3, per, HDIM).transpose(2, 1, 3, 0, 4)
    qkv_w_grad = qkv_w_grad.reshape(3, rows, width)
    if whole_heads:
        out_w_grad = lax.psum(scatter_sum(out_w_grad.astype(BF16), "expert"), "dp").astype(F32)
        head_gains = jnp.stack([q_gain_grad, k_gain_grad], axis=1)
        head_gains = lax.psum(scatter_sum(head_gains, "expert"), "dp")[0]
        q_gain_grad, k_gain_grad = head_gains[0], head_gains[1]
    else:
        spread = jnp.zeros((per, context, HDIM, width), BF16)
        spread = lax.dynamic_update_slice_in_dim(
            spread, out_w_grad.astype(BF16).reshape(per, 1, HDIM, width), my_context, 1
        )
        spread = scatter_sum(spread.reshape(width, width), ("expert", "context"))
        out_w_grad = lax.psum(spread, "dp").astype(F32)
        head_gains = jnp.stack([q_gain_grad, k_gain_grad], axis=2)
        spread = jnp.zeros((per, context, HDIM, 2), F32)
        spread = lax.dynamic_update_slice_in_dim(spread, head_gains[:, None], my_context, 1)
        spread = scatter_sum(spread.reshape(width, 2), ("expert", "context"))
        head_gains = lax.psum(spread, "dp")
        q_gain_grad, k_gain_grad = head_gains[:, 0], head_gains[:, 1]
    small_grad = jnp.concatenate(
        [router_grad, attn_gain_grad[:, None], ffn_gain_grad[:, None]], axis=1
    )
    small_grad = lax.psum(scatter_sum(small_grad, ("expert", "context")), "dp")
    return (
        hidden_out,
        input_grad,
        small_grad[:, experts_all],
        qkv_w_grad[0],
        qkv_w_grad[1],
        qkv_w_grad[2],
        q_gain_grad,
        k_gain_grad,
        out_w_grad,
        small_grad[:, experts_all + 1],
        small_grad[:, :experts_all],
        expert_grads[0],
        expert_grads[1],
        expert_grads[2],
    )


def solution(mesh):
    tokens = P(("expert", "dp"), "context", None)
    vector = P(("expert", "context"))
    matrix = P(("expert", "context"), None)
    expert = P("expert", None, None)
    in_specs = (
        tokens,
        tokens,
        tokens,
        vector,
        matrix,
        matrix,
        matrix,
        vector,
        vector,
        matrix,
        vector,
        matrix,
        expert,
        expert,
        expert,
    )
    out_specs = (
        tokens,
        tokens,
        vector,
        matrix,
        matrix,
        matrix,
        vector,
        vector,
        matrix,
        vector,
        matrix,
        expert,
        expert,
        expert,
    )
    return jax.shard_map(body, mesh=mesh, in_specs=in_specs, out_specs=out_specs, check_vma=False)
```

profile of v0, /device:TPU:0, one launch (start us, length us, event | category | flops | bytes accessed | tf_op | source)
XLA Modules:
  0.0 1859.6 jit_solution(17370269111792130607)
XLA Ops:
  11.2 37.3 %all_to_all.15 = bf16[4,128,1536]{1,2,0:T(8,128)(2,1)S(1)} all-to-all(bf16[4,128,1536]{1,2,0:T(8,128)(2,1)S(1)} %pad_maximum_fusion.1), channel_id=1, replica_groups=mesh['expert'=4,'context'=4,'dp'=2] {'context'}, dimensions={0} | all-to-all | bytes 3145728 | tf_op jit(solution)/shard_map/all_to_all | solution.py:109
  51.2 20.6 %all_gather.25 = bf16[2048,20]{0,1:T(8,128)(2,1)S(1)} all-gather(bf16[128,20]{0,1:T(8,128)(2,1)S(1)} %concatenate.31), channel_id=1, replica_groups=mesh['expert'=4,'context'=4,'dp'=2] {'expert','context'}, dimensions={0}, use_global_device_ids=true | all-gather | bytes 87040 | tf_op jit(solution)/shard_map/all_gather | solution.py:49
  79.4 98.4 %all-gather.10.cloned.1.call-done = bf16[2048,1536]{1,0:T(8,128)(2,1)} async-done(((bf16[512,1536]{1,0:T(8,128)(2,1)}), bf16[2048,1536]{1,0:T(8,128)(2,1)}) %all-gather.10.cloned.1.call-update) | async-done | bytes 6291472 | tf_op jit(solution)/shard_map/all_gather | solution.py:49
  177.8 10.1 fusion.130
  191.3 7.5 psum.126
  202.4 7.4 multiply_reduce_fusion.1
  209.8 8.6 exponential_reduce_fusion
  219.1 9.5 convolution_convert_fusion.6
  236.7 40.9 %reduce-scatter.8.cloned.1.call-done = bf16[256,2048]{1,0:T(8,128)(2,1)} async-done(((bf16[1024,2048]{1,0:T(8,128)(2,1)}), bf16[256,2048]{1,0:T(8,128)(2,1)}) %reduce-scatter.8.cloned.1.call-update) | async-done | bytes 1048592 | tf_op jit(solution)/shard_map/reduce_scatter | solution.py:53
  282.5 13.4 all-gather.1
  295.9 64.1 %all-gather.20.cloned.1.call-done = bf16[1,1024,2048]{2,1,0:T(8,128)(2,1)} async-done(((bf16[1,256,2048]{2,1,0:T(8,128)(2,1)}), bf16[1,1024,2048]{2,1,0:T(8,128)(2,1)}) %all-gather.20.cloned.1.call-update) | async-done | bytes 4194320 | tf_op jit(solution)/shard_map/all_gather | solution.py:49
  360.0 10.1 fusion.12
  370.2 8.7 fusion.14
  391.1 50.3 %all-gather.14.cloned.1.call-done = bf16[1024,2048]{1,0:T(8,128)(2,1)} async-done(((bf16[256,2048]{1,0:T(8,128)(2,1)}), bf16[1024,2048]{1,0:T(8,128)(2,1)}) %all-gather.14.cloned.1.call-update) | async-done | bytes 4194320 | tf_op jit(solution)/shard_map/all_gather | solution.py:49
  445.1 6.7 fusion.25
  451.8 10.9 multiply_convert_fusion.2
  462.7 7.2 fusion.23
  470.0 9.1 fusion.27
  479.0 8.3 fusion.36
  487.3 11.7 multiply_convert_fusion.4
  499.0 10.6 fusion.34
  509.6 9.1 fusion.38
  518.6 8.4 fusion.47
  527.0 12.0 multiply_convert_fusion.6
  539.0 10.5 fusion.45
  549.5 9.1 fusion.49
  558.5 8.3 fusion.58
  566.9 11.7 multiply_convert_fusion.8
  578.6 10.5 fusion.56
  589.1 21.7 %add_convert_fusion = bf16[1024,2048]{1,0:T(8,128)(2,1)} fusion(f32[1024,2048]{1,0:T(8,128)S(1)} %fusion.23, f32[1024,2048]{1,0:T(8,128)} %fusion.27, f32[1024,2048]{1,0:T(8,128)} %fusion.34, f32[1024,2048]{1,0:T(8,128)} %fusion.38, f32[1024,2048]{1,0:T(8,128)} %fusion.45, f32[1024,2048]{1,0:T(8,128)} %fusion.49, f32[1024,2048]{1,0:T(8,128)} %fusion.56, ...), kind=kOutput, calls=%fused_computation.14 | convolution fusion | flops 4311744512 | bytes 69206016 | tf_op jit(solution)/shard_map/dot_general | solution.py:18
  615.4 7.1 all-to-all-done.1
  622.5 64.0 %reduce-scatter.12.cloned.1.call-done = bf16[256,2048]{1,0:T(8,128)(2,1)} async-done(((bf16[1024,2048]{1,0:T(8,128)(2,1)}), bf16[256,2048]{1,0:T(8,128)(2,1)}) %reduce-scatter.12.cloned.1.call-update) | async-done | bytes 1048592 | tf_op jit(solution)/shard_map/reduce_scatter | solution.py:53
  693.4 34.4 %all-gather.16.cloned.1.call-done = bf16[1024,2048]{1,0:T(8,128)(2,1)} async-done(((bf16[256,2048]{1,0:T(8,128)(2,1)}), bf16[1024,2048]{1,0:T(8,128)(2,1)}) %all-gather.16.cloned.1.call-update) | async-done | bytes 4194320 | tf_op jit(solution)/shard_map/all_gather | solution.py:49
  733.2 10.2 convolution_convert_fusion.4
  743.4 10.2 multiply_reduce_fusion
  753.6 10.4 multiply_convert_fusion
  764.1 7.1 multiply_bitcast_fusion.1
  780.9 6.8 fusion.124
  800.9 11.1 convolution_convert_fusion.1
  813.5 9.4 fusion.21
  822.9 9.5 fusion.32
  832.4 9.2 fusion.43
  841.6 14.0 add_convert_fusion.1
  856.2 9.7 convert_bitcast_fusion.8
  865.9 6.3 convert_bitcast_fusion.9
  872.2 6.4 convert_bitcast_fusion.10
  878.6 6.3 convert_bitcast_fusion.11
  884.9 6.3 convert_bitcast_fusion.4
  891.3 6.5 convert_bitcast_fusion.5
  897.8 6.4 convert_bitcast_fusion.6
  904.1 6.4 convert_bitcast_fusion.7
  922.8 6.4 convert_bitcast_fusion.2
  932.2 9.3 convert_bitcast_fusion.3
  948.7 11.3 convolution_convert_fusion
  961.2 12.0 all-reduce
  978.6 16.3 reduce-scatter.16.cloned.1.call-done
  994.9 8.7 all-reduce.1
  1005.3 588.0 %all-reduce.7.cloned.1.call-done = (bf16[1,2048,1024]{2,1,0:T(8,128)(2,1)}, bf16[1,2048,1024]{2,1,0:T(8,128)(2,1)}, bf16[1,2048,1024]{2,1,0:T(8,128)(2,1)}, bf16...) async-done(((bf16[1,2048,1024]{2,1,0:T(8,128)(2,1)}, ...) | async-done | bytes 50331664 | tf_op jit(solution)/shard_map/psum | solution.py:209
  1593.3 18.4 maximum_convert_fusion
  1611.7 27.8 %reduce-scatter.20.cloned.1.call-done = bf16[128,2048]{1,0:T(8,128)(2,1)} async-done(((bf16[512,2048]{1,0:T(8,128)(2,1)}), bf16[128,2048]{1,0:T(8,128)(2,1)}) %reduce-scatter.20.cloned.1.call-update) | async-done | bytes 524304 | tf_op jit(solution)/shard_map/reduce_scatter | solution.py:53
  1639.5 113.0 %reduce-scatter.18.cloned.1.call-done = bf16[512,1536]{1,0:T(8,128)(2,1)} async-done(((bf16[2048,1536]{1,0:T(8,128)(2,1)}), bf16[512,1536]{1,0:T(8,128)(2,1)}) %reduce-scatter.18.cloned.1.call-update) | async-done | bytes 1572880 | tf_op jit(solution)/shard_map/reduce_scatter | solution.py:53
  1752.5 18.3 maximum_convert_fusion.1
  1770.8 47.6 %all-reduce.9.cloned.1.call-done = (bf16[4,128,1536]{2,1,0:T(8,128)(2,1)}, bf16[128,2048]{1,0:T(8,128)(2,1)}) async-done(((bf16[4,128,1536]{2,1,0:T(8,128)(2,1)}, bf16[128,2048]{1,0:T(8,128)(2,1)}), (bf16[4,128,1536]{2,1,0:T(8,128)(2,1)}, bf16[128,2048]{1,0:T(8,128)(2,1)})) %all-reduce.9.cloned.1.call-update) | async-done | bytes 2097168 | tf_op jit(solution)/shard_map/psum | solution.py:274
  1822.8 18.4 maximum_convert_fusion.2
  (327 shorter events, 138.1 us)
Async XLA Ops:
  7.2 68.9 %all-gather.18.cloned.1.call-start = ((), (), s32[]{:S(2)}) async-start(), calls=%async_computation.21 | async-start | bytes 5242880 | tf_op jit(solution)/shard_map/all_gather | solution.py:49
  7.9 169.9 %all-gather.10.cloned.1.call-start = ((), (), s32[]{:S(2)}) async-start(), calls=%async_computation.10 | async-start | bytes 7864320 | tf_op jit(solution)/shard_map/all_gather | solution.py:49
  11.2 39.8 %copy-start.66 = (bf16[128,16]{0,1:T(8,128)(2,1)S(1)}, bf16[128,16]{0,1:T(8,128)(2,1)}, u32[]{:S(2)}) copy-start(bf16[128,16]{0,1:T(8,128)(2,1)} %param.26) | copy-start | bytes 12292
  11.2 39.8 %copy-start.71 = (bf16[128]{0:T(256)(128)(2,1)S(1)}, bf16[128]{0:T(256)(128)(2,1)}, u32[]{:S(2)}) copy-start(bf16[128]{0:T(256)(128)(2,1)} %param.18) | copy-start | bytes 772
  11.2 39.8 %copy-start.72 = (bf16[128]{0:T(256)(128)(2,1)S(1)}, bf16[128]{0:T(256)(128)(2,1)}, u32[]{:S(2)}) copy-start(bf16[128]{0:T(256)(128)(2,1)} %param.22) | copy-start | bytes 772
  11.2 39.8 %copy-start.73 = (bf16[128]{0:T(256)(128)(2,1)S(1)}, bf16[128]{0:T(256)(128)(2,1)}, u32[]{:S(2)}) copy-start(bf16[128]{0:T(256)(128)(2,1)} %param.23) | copy-start | bytes 772
  11.2 39.8 %copy-start.74 = (bf16[128]{0:T(256)(128)(2,1)S(1)}, bf16[128]{0:T(256)(128)(2,1)}, u32[]{:S(2)}) copy-start(bf16[128]{0:T(256)(128)(2,1)} %param.25) | copy-start | bytes 772
  50.1 178.4 %all-gather.12.cloned.1.call-start = ((), (), s32[]{:S(2)}) async-start(), calls=%async_computation.11 | async-start | bytes 2621440 | tf_op jit(solution)/shard_map/all_gather | solution.py:49
  50.9 226.7 %reduce-scatter.8.cloned.1.call-start = ((), (), s32[]{:S(2)}) async-start(), calls=%async_computation.12 | async-start | bytes 5242880 | tf_op jit(solution)/shard_map/reduce_scatter | solution.py:53
  71.8 369.6 %copy-start.37 = (bf16[2048,20]{0,1:T(8,128)(2,1)}, bf16[2048,20]{0,1:T(8,128)(2,1)S(1)}, u32[]{:S(2)}) copy-start(bf16[2048,20]{0,1:T(8,128)(2,1)S(1)} %all_gather.25) | copy-start | bytes 245764
  71.9 105.9 %copy-start.48 = (f32[2048,1]{0,1:T(1,128)}, f32[2048,1]{0,1:T(1,128)S(1)}, u32[]{:S(2)}) copy-start(f32[2048,1]{0,1:T(1,128)S(1)} %get-tuple-element.85) | copy-start | bytes 24580
  71.9 207.9 %copy-start.41 = (f32[2048,1]{0,1:T(1,128)}, f32[2048,1]{0,1:T(1,128)S(1)}, u32[]{:S(2)}) copy-start(f32[2048,1]{0,1:T(1,128)S(1)} %get-tuple-element.84) | copy-start | bytes 24580
  76.1 124.8 %copy-start.22 = (f32[1024,64]{1,0:T(8,128)}, f32[1024,64]{1,0:T(8,128)S(1)}, u32[]{:S(2)}) copy-start(f32[1024,64]{1,0:T(8,128)S(1)} %get-tuple-element.98) | copy-start | bytes 786436
  79.3 108.6 %copy-start.67 = (f32[1024]{0:T(1024)}, f32[1024]{0:T(1024)S(1)}, u32[]{:S(2)}) copy-start(f32[1024]{0:T(1024)S(1)} %add_rsqrt_fusion.1) | copy-start | bytes 12292
  235.6 41.9 %copy-start.1 = (bf16[1,256,2048]{2,1,0:T(8,128)(2,1)S(1)}, bf16[1,256,2048]{2,1,0:T(8,128)(2,1)}, u32[]{:S(2)}) copy-start(bf16[1,256,2048]{2,1,0:T(8,128)(2,1)} %param.15) | copy-start | bytes 3145732
  235.6 46.8 %copy-start.62 = (s32[1,256,8]{1,2,0:T(8,128)S(1)}, s32[1,256,8]{1,2,0:T(8,128)}, u32[]{:S(2)}) copy-start(s32[1,256,8]{1,2,0:T(8,128)} %param.17) | copy-start | bytes 24580
  235.6 124.4 %all-gather.20.cloned.1.call-start = ((), (), s32[]{:S(2)}) async-start(), calls=%async_computation.22 | async-start | bytes 5242880 | tf_op jit(solution)/shard_map/all_gather | solution.py:49
  236.2 205.2 %all-gather.14.cloned.1.call-start = ((), (), s32[]{:S(2)}) async-start(), calls=%async_computation.13 | async-start | bytes 5242880 | tf_op jit(solution)/shard_map/all_gather | solution.py:49
  279.8 90.3 %copy-start.54 = (f32[256]{0:T(256)}, f32[256]{0:T(256)S(1)}, u32[]{:S(2)}) copy-start(f32[256]{0:T(256)S(1)} %get-tuple-element.108) | copy-start | bytes 3076
  282.4 404.2 %reduce-scatter.12.cloned.1.call-start = ((), (), s32[]{:S(2)}) async-start(), calls=%async_computation.15 | async-start | bytes 5242880 | tf_op jit(solution)/shard_map/reduce_scatter | solution.py:53
  360.0 10.2 copy-start.75
  360.0 18.8 %slice-start.4 = ((s8[16777216]{0:T(1024)(128)(4,1)}), s8[4194304]{0:T(1024)(128)(4,1)S(1)}, s32[]{:S(2)}) async-start(s8[16777216]{0:T(1024)(128)(4,1)} %bitcast.414), calls=%async_computation.29 | async-start | bytes 8388608
  360.0 18.8 %slice-start.5 = ((s8[16777216]{0:T(1024)(128)(4,1)}), s8[4194304]{0:T(1024)(128)(4,1)S(1)}, s32[]{:S(2)}) async-start(s8[16777216]{0:T(1024)(128)(4,1)} %bitcast.414), calls=%async_computation.30 | async-start | bytes 8388608
  499.0 10.6 copy-start.88
  499.0 10.6 copy-start.90
  539.0 10.5 copy-start.92
  539.0 10.5 copy-start.94
  578.6 10.5 copy-start.96
  578.6 10.5 copy-start.20
  610.8 11.7 copy-start.40
  610.8 75.8 %copy-start.2 = (bf16[1,256,2048]{2,1,0:T(8,128)(2,1)S(1)}, bf16[1,256,2048]{2,1,0:T(8,128)(2,1)}, u32[]{:S(2)}) copy-start(bf16[1,256,2048]{2,1,0:T(8,128)(2,1)} %param.15) | copy-start | bytes 3145732
  610.8 75.8 %copy-start.9 = (bf16[256,2048]{1,0:T(8,128)(2,1)S(1)}, bf16[256,2048]{1,0:T(8,128)(2,1)}, u32[]{:S(2)}) copy-start(bf16[256,2048]{1,0:T(8,128)(2,1)} %reduce-scatter.8.cloned.1.call-done) | copy-start | bytes 3145732
  610.8 75.8 %copy-start.38 = (bf16[2048,20]{0,1:T(8,128)(2,1)S(1)}, bf16[2048,20]{0,1:T(8,128)(2,1)}, u32[]{:S(2)}) copy-start(bf16[2048,20]{0,1:T(8,128)(2,1)} %copy-done.37) | copy-start | bytes 245764
  610.8 75.8 %copy-start.42 = (f32[2048,1]{0,1:T(1,128)S(1)}, f32[2048,1]{0,1:T(1,128)}, u32[]{:S(2)}) copy-start(f32[2048,1]{0,1:T(1,128)} %copy-done.41) | copy-start | bytes 24580
  610.8 75.8 %copy-start.55 = (f32[256]{0:T(256)S(1)}, f32[256]{0:T(256)}, u32[]{:S(2)}) copy-start(f32[256]{0:T(256)} %copy-done.54) | copy-start | bytes 3076
  610.9 80.0 %copy-start.11 = (bf16[1,256,2048]{2,1,0:T(8,128)(2,1)S(1)}, bf16[1,256,2048]{2,1,0:T(8,128)(2,1)}, u32[]{:S(2)}) copy-start(bf16[1,256,2048]{2,1,0:T(8,128)(2,1)} %param.16) | copy-start | bytes 3145732
  610.9 80.0 %copy-start.58 = (f32[256]{0:T(256)S(1)}, f32[256]{0:T(256)}, u32[]{:S(2)}) copy-start(f32[256]{0:T(256)} %get-tuple-element.107) | copy-start | bytes 3076
  612.1 10.4 all-to-all-start.1
  615.3 112.5 %all-gather.16.cloned.1.call-start = ((), (), s32[]{:S(2)}) async-start(), calls=%async_computation.16 | async-start | bytes 5242880 | tf_op jit(solution)/shard_map/all_gather | solution.py:49
  622.5 70.1 %copy-start.50 = (bf16[256,16]{0,1:T(8,128)(2,1)}, bf16[256,16]{0,1:T(8,128)(2,1)S(1)}, u32[]{:S(2)}) copy-start(bf16[256,16]{0,1:T(8,128)(2,1)S(1)} %multiply_convert_fusion.14) | copy-start | bytes 24580
  692.7 236.8 %reduce-scatter.14.cloned.1.call-start = ((), (), s32[]{:S(2)}) async-start(), calls=%async_computation.17 | async-start | bytes 5242880 | tf_op jit(solution)/shard_map/reduce_scatter | solution.py:53
  727.8 15.6 slice-start
  727.8 15.6 slice-start.1
  733.2 10.2 slice-start.2
  733.2 10.2 slice-start.3
  743.4 10.2 copy-start.34
  753.6 10.5 copy-start.15
  780.9 12.9 copy-start.57
  812.0 161.9 %reduce-scatter.10.cloned.1.call-start = ((), (), s32[]{:S(2)}) async-start(), calls=%async_computation.14 | async-start | bytes 5242880 | tf_op jit(solution)/shard_map/reduce_scatter | solution.py:53
  855.7 139.2 %reduce-scatter.16.cloned.1.call-start = ((), (), s32[]{:S(2)}) async-start(), calls=%async_computation.18 | async-start | bytes 208896 | tf_op jit(solution)/shard_map/reduce_scatter | solution.py:53
  856.2 9.7 copy-start.19
  856.2 9.7 copy-start.91
  932.1 661.2 %all-reduce.7.cloned.1.call-start = ((), (), s32[]{:S(2)}) async-start(), calls=%async_computation.23 | async-start | bytes 100663296 | tf_op jit(solution)/shard_map/psum | solution.py:209
  941.6 697.9 %reduce-scatter.20.cloned.1.call-start = ((), (), s32[]{:S(2)}) async-start(), calls=%async_computation.20 | async-start | bytes 2621440 | tf_op jit(solution)/shard_map/reduce_scatter | solution.py:53
  948.6 803.8 %reduce-scatter.18.cloned.1.call-start = ((), (), s32[]{:S(2)}) async-start(), calls=%async_computation.19 | async-start | bytes 7864320 | tf_op jit(solution)/shard_map/reduce_scatter | solution.py:53
  960.0 13.9 copy-start.10
  960.0 13.9 copy-start.12
  960.0 13.9 copy-start.43
  960.0 13.9 copy-start.56
  960.0 13.9 copy-start.59
  960.0 13.9 copy-start.61
  960.1 858.3 %all-reduce.9.cloned.1.call-start = ((), (), s32[]{:S(2)}) async-start(), calls=%async_computation.24 | async-start | bytes 4194304 | tf_op jit(solution)/shard_map/psum | solution.py:274
  1818.4 24.5 %all-to-all-start.2 = ((bf16[4,128,1536]{2,1,0:T(8,128)(2,1)}), bf16[4,128,1536]{2,1,0:T(8,128)(2,1)}, u32[]{:S(2)}, u32[]{:S(2)}) async-start(bf16[4,128,1536]{2,1,0:T(8,128)(2,1)} %get-tuple-element.43), calls=%async_computation.8 | async-start | bytes 3145728 | tf_op jit(solution)/shard_map/all_to_all | solution.py:275
  1822.7 18.4 copy-start.35
  (59 other events, 319.6 us)
Sparse Core Ops, SparseCore 0:
  9.6 50.1 all-gather.17
  61.9 115.8 all-gather.9
  179.4 44.1 all-gather.11
  235.7 41.7 reduce-scatter.7
  279.0 80.9 all-gather.19
  362.1 79.3 all-gather.13
  611.0 75.5 reduce-scatter.11
  692.8 34.9 all-gather.15
  812.1 45.5 reduce-scatter.13
  859.9 76.7 reduce-scatter.9
  940.8 54.0 reduce-scatter.15
  1001.6 591.6 all-reduce.6
  1595.6 43.8 reduce-scatter.19
  1642.3 110.0 reduce-scatter.17
  1754.7 63.6 all-reduce.8
where the time goes:
time: 1870 us; the launch traced here: 1860 us
  waiting for transfers between devices  1150 us (61%)
  matrix products  426 us (23%)
  other arithmetic  120 us (6%)
  blocking collectives  106 us (6%)
  local copies, waits for them, and re-layouts  28.9 us (2%)
    psum x1, waiting for transfers between devices, body(): grads.append(lax.psum(local_grads, ('context', 'dp')))  588 us
    dot_general x45, matrix products, dot(): lax.dot_general(left, right, (((contract[0],), (contract[1],)), ((), ()))...  377 us
    reduce_scatter x7, waiting for transfers between devices, scatter_sum(): return lax.psum_scatter(values, axis, scatter_dimension=0, tiled=True)  262 us
    all_gather x6, waiting for transfers between devices, gather(): return lax.all_gather(values, axis, axis=0, tiled=True)  247 us
    another operation x3, other arithmetic, body(): jnp.stack([g[i].astype(F32) for g in grads])  55 us
    psum x1, waiting for transfers between devices, body(): qkv_w_grad = lax.psum(scatter_sum(qkv_w_grad, 'expert'), 'dp')  47.6 us
  transfers between devices with their start and end apart: 17, of which 13 were waited for; matrix products, arithmetic and copies ran while one was open for 16% of the time, Pallas kernels for 0%

commit v1 on v0

v1 whole, which is shorter than its diff:
```python
import functools

import jax
import jax.numpy as jnp
from jax import lax
from jax.experimental import pallas as pl
from jax.experimental.pallas import tpu as pltpu
from jax.sharding import PartitionSpec as P

HEADS = 16
HDIM = 128
CHUNK = 256
ROWS = 1024
PIECES = 4

epsilon = 1e-06
rope_base = 10000.0
F32 = jnp.float32
BF16 = jnp.bfloat16
MIB = 1024 * 1024


def dot(left, right, contract):
    return lax.dot_general(
        left, right, (((contract[0],), (contract[1],)), ((), ())), preferred_element_type=F32
    )


def add_low(left, right):
    return (left.astype(F32) + right.astype(F32)).astype(BF16)


def total_low(terms):
    return functools.reduce(lambda a, b: a + b, [t.astype(F32) for t in terms]).astype(BF16)


FIRST = (("dp", 1), ("context", 2))
SECOND = (("context", 2), ("dp", 1))


class Order:
    def __init__(self):
        self.last = None

    def tie(self, values):
        if self.last is None:
            return values
        return lax.optimization_barrier((values, self.last))[0]

    def did(self, result):
        self.last = result

    def run(self, step, first, *rest):
        result = step(self.tie(first), *rest)
        self.did(result)
        return result


def rms_factor(values):
    return lax.rsqrt(jnp.mean(values * values, axis=-1, keepdims=True) + epsilon)


def norm_back(grad_out, values, factor, gain_vector):
    scaled = grad_out * gain_vector
    grad_in = factor * scaled - values * factor**3 * jnp.mean(
        scaled * values, axis=-1, keepdims=True
    )
    gain_grad = jnp.sum(grad_out * values * factor, axis=0)
    return (grad_in, gain_grad)


def rotate(values, cosine, sine_part):
    first_half = values[..., : HDIM // 2]
    second_half = values[..., HDIM // 2 :]
    return jnp.concatenate(
        [
            first_half * cosine - second_half * sine_part,
            second_half * cosine + first_half * sine_part,
        ],
        axis=-1,
    )


def swap(values, axis, bit):
    return lax.ppermute(values, axis, [(i, i ^ bit) for i in range(lax.axis_size(axis))])


def shift(values, by):
    n = lax.axis_size("expert")
    return lax.ppermute(values, "expert", [(i, (i + by) % n) for i in range(n)])


def context_gather(own):
    far = swap(own, "context", 2)
    near = swap(own, "context", 1)
    return [own, near, far, swap(far, "context", 1)]


def context_sum(blocks):
    got = swap(jnp.stack([blocks[1], blocks[3]]), "context", 1)
    far = swap(add_low(blocks[2], got[1]), "context", 2)
    return blocks[0].astype(F32) + got[0].astype(F32) + far.astype(F32)


def context_total(terms):
    got = swap(terms, "context", 1)
    terms = terms + jnp.stack([got[:, s ^ 1] for s in range(4)], axis=1)
    got = swap(terms, "context", 2)
    return terms + jnp.stack([got[:, s ^ 2] for s in range(4)], axis=1)


def ring_gather(own):
    held = [own]
    for _ in range(lax.axis_size("expert") - 1):
        held.append(shift(held[-1], 1))
    return held


def ring_sum(blocks, combine):
    n = len(blocks)
    total = blocks[1 % n]
    for s in range(2, n + 1):
        total = combine(blocks[s % n], shift(total, 1))
    return total


def take(blocks, index):
    return jnp.stack([lax.dynamic_index_in_dim(blocks, i, 0, keepdims=False) for i in index])


def rows_kernel(
    first,
    at_ref,
    x_ref,
    u_ref,
    mask_ref,
    router_ref,
    wg_ref,
    wu_ref,
    wd_ref,
    out_ref,
    row_ref,
    gate_ref,
    weights_ref,
    turned_ref,
    both_ref,
    hidden_ref,
    out_acc,
    row_acc,
    lanes,
    both_w,
):
    e, step = pl.program_id(0), pl.program_id(1)
    start = jnp.logical_and(e == 0, step == 0)
    rows, width = x_ref.shape
    chunk = wg_ref.shape[1]
    lane = lax.broadcasted_iota(jnp.int32, (rows, 128), 1)

    @pl.when(start)
    def _():
        out_acc[...] = jnp.zeros_like(out_acc)
        row_acc[...] = jnp.zeros_like(row_acc)
        gate_ref[...] = jnp.zeros_like(gate_ref)
        turned_ref[...] = x_ref[...].T
        logits = dot(x_ref[...], router_ref[...], (1, 0))
        chosen = mask_ref[...] > 0.5
        top = jnp.max(jnp.where(chosen, logits, -1e30), axis=-1, keepdims=True)
        raised = jnp.where(chosen, jnp.exp(jnp.where(chosen, logits - top, 0.0)), 0.0)
        weights_ref[...] = raised / jnp.sum(raised, axis=-1, keepdims=True)

    @pl.when(step == 0)
    def _():
        lanes[...] = jnp.zeros_like(lanes)

    both_w[:, :chunk] = wg_ref[...]
    both_w[:, chunk:] = wu_ref[...]
    weight = jnp.sum(
        jnp.where(lane == at_ref[0] + first + e, weights_ref[...], 0.0), axis=-1, keepdims=True
    )
    pre = dot(x_ref[...], both_w[...], (1, 0))
    gate_pre, up_pre = pre[:, :chunk], pre[:, chunk:]
    hidden_grad = dot(u_ref[...], wd_ref[...], (1, 1))
    sigmoid = 1.0 / (1.0 + jnp.exp(-gate_pre))
    activated = gate_pre * sigmoid
    hidden = activated * up_pre
    part = hidden * hidden_grad
    total = part[:, :128]
    for j in range(1, chunk // 128):
        total = total + part[:, j * 128 : (j + 1) * 128]
    lanes[...] += total
    hidden_low = (weight * hidden).astype(BF16)
    hidden_grad = weight * hidden_grad
    gate_low = (hidden_grad * up_pre * (sigmoid + activated * (1.0 - sigmoid))).astype(BF16)
    up_low = (hidden_grad * activated).astype(BF16)
    hidden_ref[...] = hidden_low
    both_ref[:, :chunk] = gate_low
    both_ref[:, chunk:] = up_low
    out_acc[...] += dot(hidden_low, wd_ref[...], (1, 0))
    row_acc[...] += dot(both_ref[...], both_w[...], (1, 1))

    @pl.when(step == pl.num_programs(1) - 1)
    def _():
        sums = jnp.sum(lanes[...], axis=-1, keepdims=True)
        gate_ref[...] += jnp.where(lane == first + e, sums, 0.0)
        out_ref[...] = out_acc[...].astype(BF16)
        row_ref[...] = row_acc[...].astype(BF16)


def run_rows(at, first, count, x, u, mask, router, w_gate, w_up, w_down):
    rows, width = x.shape
    ff = w_gate.shape[2]
    steps = ff // CHUNK

    def whole(shape):
        return pl.BlockSpec(
            shape, lambda e, s, a: (0,) * len(shape), pipeline_mode=pl.Buffered(1)
        )

    return pl.pallas_call(
        functools.partial(rows_kernel, first),
        grid_spec=pltpu.PrefetchScalarGridSpec(
            num_scalar_prefetch=1,
            grid=(count, steps),
            in_specs=[
                whole((rows, width)),
                whole((rows, width)),
                whole((rows, 128)),
                whole((width, 128)),
                pl.BlockSpec((None, width, CHUNK), lambda e, s, a: (first + e, 0, s)),
                pl.BlockSpec((None, width, CHUNK), lambda e, s, a: (first + e, 0, s)),
                pl.BlockSpec((None, CHUNK, width), lambda e, s, a: (first + e, s, 0)),
            ],
            out_specs=[
                whole((rows, width)),
                whole((rows, width)),
                whole((rows, 128)),
                whole((rows, 128)),
                whole((width, rows)),
                pl.BlockSpec((None, None, rows, 2 * CHUNK), lambda e, s, a: (e, s, 0, 0)),
                pl.BlockSpec((None, None, rows, CHUNK), lambda e, s, a: (e, s, 0, 0)),
            ],
            scratch_shapes=[
                pltpu.VMEM((rows, width), F32),
                pltpu.VMEM((rows, width), F32),
                pltpu.VMEM((rows, 128), F32),
                pltpu.VMEM((width, 2 * CHUNK), BF16),
            ],
        ),
        out_shape=[
            jax.ShapeDtypeStruct((rows, width), BF16),
            jax.ShapeDtypeStruct((rows, width), BF16),
            jax.ShapeDtypeStruct((rows, 128), F32),
            jax.ShapeDtypeStruct((rows, 128), F32),
            jax.ShapeDtypeStruct((width, rows), BF16),
            jax.ShapeDtypeStruct((count, steps, rows, 2 * CHUNK), BF16),
            jax.ShapeDtypeStruct((count, steps, rows, CHUNK), BF16),
        ],
        compiler_params=pltpu.CompilerParams(vmem_limit_bytes=56 * MIB),
        cost_estimate=pl.CostEstimate(
            flops=12 * rows * width * ff * count,
            bytes_accessed=6 * width * ff * count,
            transcendentals=rows * ff * count,
        ),
        name="rows",
    )(at, x, u, mask, router, w_gate, w_up, w_down)


def grads_kernel(sizes, bits_ref, *refs):
    n = len(sizes)
    turned, ups, boths, hiddens = (refs[i * n : (i + 1) * n] for i in range(4))
    send_ref, keep_ref, x_all, u_all, both, hidden = refs[4 * n :]
    step, steps = pl.program_id(0), pl.num_programs(0)
    width = x_all.shape[0]
    chunk = hidden.shape[1]

    spans, at = [], 0
    for size in sizes:
        spans.append(slice(at, at + size))
        at += size

    @pl.when(step == 0)
    def _():
        for span, t, u in zip(spans, turned, ups):
            x_all[:, span] = t[...]
            u_all[span, :] = u[...]

    for span, b, h in zip(spans, boths, hiddens):
        both[span, :] = b[...]
        hidden[span, :] = h[...]
    hidden_turned = hidden[...].T
    piece_rows = width // PIECES

    def store(ref):
        mask = jnp.where(step % 2 == 0, bits_ref[1], bits_ref[2])
        for p in range(PIECES):
            place = p ^ mask
            r = slice(p * piece_rows, (p + 1) * piece_rows)
            got = dot(x_all[r, :], both[...], (1, 0)).astype(BF16)
            ref[place, 0] = got[:, :chunk]
            ref[place, 1] = got[:, chunk:]
            down = dot(hidden_turned, u_all[:, r], (1, 0)).astype(BF16)
            for j in range(piece_rows // chunk):
                ref[place, 2, j * chunk : (j + 1) * chunk, :] = down[:, j * chunk : (j + 1) * chunk]

    @pl.when(step < steps // 2)
    def _():
        store(send_ref.at[0])

    @pl.when(step >= steps // 2)
    def _():
        store(keep_ref.at[0])


def run_grads(bits, segments):
    turned, ups, boths, hiddens, places = zip(*segments)
    width = turned[0].shape[0]
    sizes = tuple(u.shape[0] for u in ups)
    total = sum(sizes)
    steps = boths[0].shape[1]
    half = steps // 2
    piece_rows = width // PIECES

    def chunk_at(s, b):
        return ((1 - s // half) ^ b[0]) * half + s % half

    def whole(shape):
        return pl.BlockSpec(shape, lambda s, b: (0, 0), pipeline_mode=pl.Buffered(1))

    def chunked(size, columns, place):
        return pl.BlockSpec(
            (None, None, size, columns), lambda s, b: (place, chunk_at(s, b), 0, 0)
        )

    grads = (1, PIECES, 3, piece_rows, CHUNK)
    grads_out = jax.ShapeDtypeStruct((half,) + grads[1:], BF16)
    return pl.pallas_call(
        functools.partial(grads_kernel, sizes),
        grid_spec=pltpu.PrefetchScalarGridSpec(
            num_scalar_prefetch=1,
            grid=(steps,),
            in_specs=[whole((width, size)) for size in sizes]
            + [whole((size, width)) for size in sizes]
            + [chunked(size, 2 * CHUNK, p) for size, p in zip(sizes, places)]
            + [chunked(size, CHUNK, p) for size, p in zip(sizes, places)],
            out_specs=[
                pl.BlockSpec(grads, lambda s, b: (jnp.minimum(s, half - 1), 0, 0, 0, 0)),
                pl.BlockSpec(grads, lambda s, b: (jnp.maximum(s - half, 0), 0, 0, 0, 0)),
            ],
            scratch_shapes=[
                pltpu.VMEM((width, total), BF16),
                pltpu.VMEM((total, width), BF16),
                pltpu.VMEM((total, 2 * CHUNK), BF16),
                pltpu.VMEM((total, CHUNK), BF16),
            ],
        ),
        out_shape=[grads_out, grads_out],
        compiler_params=pltpu.CompilerParams(vmem_limit_bytes=56 * MIB),
        cost_estimate=pl.CostEstimate(
            flops=6 * total * width * steps * CHUNK,
            bytes_accessed=6 * width * steps * CHUNK + 8 * total * width,
            transcendentals=0,
        ),
        name="grads",
    )(bits, *turned, *ups, *boths, *hiddens)


class Summed:
    def __init__(self, order, send, keep):
        self.order, self.keep = order, keep
        self.ahead = ["halves", "quarters", "finals", "spread", "cross"]
        self.got = swap(send, "context", 1)

    def reach(self, name):
        while name in self.ahead:
            getattr(self, self.ahead.pop(0))()

    def halves(self):
        self.kept, self.coming = [], []
        for path in range(2):
            kept, got = self.keep[path], self.got[path]
            away = self.order.run(add_low, kept[2:], got[2:])
            self.coming.append(swap(away, *FIRST[path]))
        for path in range(2):
            self.kept.append(self.order.run(add_low, self.keep[path, :2], self.got[path, :2]))

    def quarters(self):
        kept, self.kept, coming, self.coming = self.kept, [], self.coming, []
        for path in range(2):
            away = self.order.run(add_low, kept[path][1], coming[path][1])
            self.coming.append(swap(away, *SECOND[path]))
        for path in range(2):
            self.kept.append(self.order.run(add_low, kept[path][0], coming[path][0]))

    def finals(self):
        self.own = []
        for path in range(2):
            final = self.order.run(add_low, self.kept[path], self.coming[path])
            self.own.append([final, swap(final, *SECOND[path]), swap(final, *FIRST[path])])

    def spread(self):
        for path in range(2):
            beside = self.order.tie(self.own[path][1])
            self.own[path].append(swap(beside, *FIRST[path]))
        self.other = [[swap(p, "context", 1) for p in path[:2]] for path in self.own]

    def cross(self):
        for path in range(2):
            ready = [self.order.tie(p) for p in self.own[path][2:]]
            self.other[path] += [swap(p, "context", 1) for p in ready]

    def place(self, bits, e, outs, shapes):
        pieces = [p for half in (self.own, self.other) for path in half for p in path]
        outs = place_grads(self.order.tie(bits), e, pieces, outs, shapes)
        self.order.did(outs[2])
        return outs


def place_kernel(e, first, bits_ref, *refs):
    ins = refs[:16]
    outs = refs[16:19] if first else refs[19:22]
    low, wide, in_sem, out_sem = refs[-4:]
    rows = low.shape[2]

    def fetch(i):
        return pltpu.make_async_copy(ins[i], low.at[i % 2], in_sem.at[i % 2])

    def drain(i):
        core, path, place = i // 8, i // 4 % 2, i % 4
        chunk = (core ^ bits_ref[0]) * 2 + path
        piece = place ^ bits_ref[1 + path]
        columns = pl.ds(pl.multiple_of(chunk * CHUNK, CHUNK), CHUNK)
        copies = []
        for k in range(2):
            copies.append(
                pltpu.make_async_copy(
                    wide.at[i % 2, k],
                    outs[k].at[e, pl.ds(pl.multiple_of(piece * rows, rows), rows), columns],
                    out_sem.at[i % 2, k],
                )
            )
        for j in range(rows // CHUNK):
            across = pl.ds(pl.multiple_of(piece * rows + j * CHUNK, CHUNK), CHUNK)
            copies.append(
                pltpu.make_async_copy(
                    wide.at[i % 2, 2, pl.ds(j * CHUNK, CHUNK)],
                    outs[2].at[e, columns, across],
                    out_sem.at[i % 2, 2 + j],
                )
            )
        return copies

    fetch(0).start()
    for i in range(16):
        if i + 1 < 16:
            fetch(i + 1).start()
        fetch(i).wait()
        if i >= 2:
            for copy in drain(i - 2):
                copy.wait()
        for k in range(3):

            @pl.loop(0, rows // 64)
            def _(t):
                r = pl.ds(pl.multiple_of(t * 64, 64), 64)
                wide[i % 2, k, r, :] = low[i % 2, k, r, :].astype(F32)

        for copy in drain(i):
            copy.start()
    for i in (14, 15):
        for copy in drain(i):
            copy.wait()


def place_grads(bits, e, pieces, outs, shapes):
    first = outs is None
    rows = pieces[0].shape[1]
    anywhere = pl.BlockSpec(memory_space=pl.ANY)
    operands = list(pieces) + ([] if first else list(outs))
    return pl.pallas_call(
        functools.partial(place_kernel, e, first),
        grid_spec=pltpu.PrefetchScalarGridSpec(
            num_scalar_prefetch=1,
            grid=(1,),
            in_specs=[anywhere] * len(operands),
            out_specs=[anywhere] * 3,
            scratch_shapes=[
                pltpu.VMEM((2, 3, rows, CHUNK), BF16),
                pltpu.VMEM((2, 3, rows, CHUNK), F32),
                pltpu.SemaphoreType.DMA((2,)),
                pltpu.SemaphoreType.DMA((2, 2 + rows // CHUNK)),
            ],
        ),
        out_shape=[jax.ShapeDtypeStruct(s, F32) for s in shapes],
        input_output_aliases={} if first else {17: 0, 18: 1, 19: 2},
        compiler_params=pltpu.CompilerParams(vmem_limit_bytes=16 * MIB),
        cost_estimate=pl.CostEstimate(
            flops=0, bytes_accessed=16 * 9 * rows * CHUNK * 2, transcendentals=0
        ),
        name="place",
    )(bits, *operands)


def body(
    hidden_in,
    out_grad,
    routes,
    attn_gain,
    w_query,
    w_key,
    w_value,
    q_gain,
    k_gain,
    w_out,
    ffn_gain,
    w_router,
    w_gate,
    w_up,
    w_down,
):
    groups = lax.axis_size("expert")
    context = lax.axis_size("context")
    my_group = lax.axis_index("expert")
    my_context = lax.axis_index("context")
    my_dp = lax.axis_index("dp")
    tokens = hidden_in.shape[1]
    width = hidden_in.shape[2]
    rows = w_query.shape[0]
    local_experts = w_gate.shape[0]
    experts_all = w_router.shape[1]
    length = tokens * context
    per = HEADS // context
    local = per * HDIM
    score_scale = HDIM ** (-0.5)
    core, side = my_context % 2, my_context // 2
    bits = jnp.stack([core, my_dp * 2 + side, side * 2 + my_dp]).astype(jnp.int32)
    ring = [(my_group - s) % groups for s in range(groups)]
    members = [my_context ^ s for s in range(context)]

    def half_columns(weight):
        split = weight.reshape(rows, 2, per // 2, context, HDIM)
        split = lax.dynamic_index_in_dim(split, my_dp, 1, keepdims=False)
        return split.transpose(2, 0, 1, 3).reshape(context, rows, local // 2)

    columns = jnp.concatenate([half_columns(w) for w in (w_query, w_key, w_value)], axis=2)
    pieces = [lax.dynamic_index_in_dim(columns, m, 0, keepdims=False) for m in members]
    pieces = [pieces[0]] + [swap(pieces[s], "context", s) for s in range(1, context)]
    half_w = take(jnp.stack(pieces), members).reshape(context * rows, 3 * local // 2)
    hidden_all = lax.optimization_barrier((hidden_in[0], half_w))[0]
    hidden_all = jnp.concatenate(context_gather(hidden_all), axis=0)
    small = jnp.concatenate(
        [attn_gain[None], q_gain[None], k_gain[None], ffn_gain[None], w_router.T], axis=0
    )
    small = take(jnp.stack(context_gather(small)), members)
    small = take(jnp.stack(ring_gather(small)), ring)
    small_all = small.transpose(2, 0, 1, 3).reshape(4 + experts_all, width)
    routes_ring = ring_gather(routes[0])
    halves = ring_gather(half_w)
    others = [swap(h, "dp", 1) for h in halves]
    qkv_w = jnp.concatenate(
        [jnp.concatenate(halves, axis=0), jnp.concatenate(others, axis=0)], axis=1
    )
    heads = [my_dp * 2, my_dp * 2 + 1, (1 - my_dp) * 2, (1 - my_dp) * 2 + 1]
    whole_heads = rows == HDIM
    if whole_heads:
        held = lax.optimization_barrier((w_out, halves[-1]))[0]
        held = lax.all_gather(held, "expert", axis=0)
        out_w = take(held, heads).reshape(local, width)
    else:
        out_w = lax.all_gather(w_out, ("expert", "context"), axis=0, tiled=True)
        out_w = out_w.reshape(per, context, HDIM, width)
        out_w = lax.dynamic_index_in_dim(out_w, my_context, 1, keepdims=False)
        out_w = take(out_w, heads).reshape(local, width)
    upstream_all = lax.optimization_barrier((out_grad[0], halves[-1]))[0]
    upstream_all = lax.all_gather(upstream_all, "expert", axis=0)

    gain_attn = small_all[0].astype(F32)
    gain_ffn = small_all[3].astype(F32)
    router_w = small_all[4:]
    router_wide = jnp.pad(router_w.T, ((0, 0), (0, 128 - experts_all)))

    def mine(vector):
        table = vector.reshape(per, context, HDIM)
        table = lax.dynamic_index_in_dim(table, my_context, 1, keepdims=False)
        return take(table, heads).astype(F32)

    gain_query, gain_key = mine(small_all[1]), mine(small_all[2])
    block = width // groups

    def to_ring(values):
        parts = [lax.dynamic_slice_in_dim(values, m * block, block, axis=1) for m in ring]
        return jnp.concatenate(parts, axis=1)

    source_all = hidden_all.astype(F32)
    factor_all = rms_factor(source_all)
    normed = to_ring((source_all * factor_all * gain_attn).astype(BF16))
    source = hidden_in[0].astype(F32)
    factor_one = rms_factor(source)
    qkv = dot(normed, qkv_w, (1, 0)).reshape(length, 2, 3, local // 2)
    query_raw = qkv[:, :, 0].reshape(length, per, HDIM)
    key_raw = qkv[:, :, 1].reshape(length, per, HDIM)
    value_low = qkv[:, :, 2].astype(BF16).reshape(length, per, HDIM)

    def slots(query, key):
        return jnp.stack([jnp.sum(v, axis=(1, 2)).reshape(context, tokens) for v in (query, key)])

    def per_row(values):
        return values.reshape(length)[:, None, None]

    squares = context_total(slots(query_raw * query_raw, key_raw * key_raw))
    factors = lax.rsqrt(squares / width + epsilon)
    factor_query, factor_key = per_row(factors[0]), per_row(factors[1])
    starts = jnp.stack([m * tokens for m in members])
    positions = (starts[:, None] + jnp.arange(tokens, dtype=jnp.int32)).reshape(length).astype(F32)
    frequency = rope_base ** (-jnp.arange(HDIM // 2, dtype=F32) * 2.0 / HDIM)
    angles = positions[:, None] * frequency[None, :]
    cosine = jnp.cos(angles)[:, None, :]
    sine_part = jnp.sin(angles)[:, None, :]
    query_low = rotate(query_raw * factor_query * gain_query, cosine, sine_part).astype(BF16)
    key_low = rotate(key_raw * factor_key * gain_key, cosine, sine_part).astype(BF16)
    scores = (
        jnp.einsum("qhd,khd->hqk", query_low, key_low, preferred_element_type=F32) * score_scale
    )
    score_max = jnp.max(scores, axis=-1, keepdims=True)
    denominator = jnp.sum(jnp.exp(scores - score_max), axis=-1, keepdims=True)
    logsum = score_max + jnp.log(denominator)
    probs = jnp.exp(scores - logsum)
    mixed_low = (
        jnp.einsum("hqk,khd->qhd", probs.astype(BF16), value_low, preferred_element_type=F32)
        .reshape(length, local)
        .astype(BF16)
    )
    mixed_out = dot(mixed_low, out_w, (1, 0)).astype(BF16).reshape(context, tokens, width)
    residual = source + context_sum([mixed_out[s] for s in range(context)])
    factor_two = rms_factor(residual)
    normed_two = (residual * factor_two * gain_ffn).astype(BF16)

    ids = jnp.arange(128, dtype=jnp.int32)
    masks = [jnp.any(r[:, :, None] == ids, axis=1).astype(F32) for r in routes_ring]
    at = jnp.reshape(my_group * local_experts, (1,)).astype(jnp.int32)
    order = Order()

    def upstream_of(slot):
        return lax.dynamic_index_in_dim(upstream_all, ring[slot], 0, keepdims=False)

    def rows_of(first, count, x, u, mask):
        result = run_rows(order.tie(at), first, count, x, u, mask, router_wide, w_gate, w_up, w_down)
        order.did(result[0])
        return result

    near = [[(0, local_experts)], [(0, local_experts)]]
    if local_experts == 4:
        near = [[(0, 2), (2, 2)]] * 2
    blocks = [normed_two, shift(normed_two, 1)]
    segments = [([0], []), ([1], [])]
    ups = [out_grad[0], upstream_of(1)]
    for slot in range(2):
        for i, (first, count) in enumerate(near[slot]):
            result = rows_of(first, count, blocks[slot], ups[slot], masks[slot])
            segments[slot][1].append((first, count, result))
            if slot == 0 or i == 0:
                if len(blocks) < groups:
                    held = order.tie(blocks[-1])
                    order.did(held)
                    blocks.append(shift(held, 1))
    while len(blocks) < groups:
        blocks.append(shift(blocks[-1], 1))
    far = []
    for slot in range(2, groups, 2):
        pair = [slot, slot + 1]
        x, u, mask = (
            jnp.concatenate(v, axis=0)
            for v in (
                [blocks[s] for s in pair],
                [upstream_of(s) for s in pair],
                [masks[s] for s in pair],
            )
        )
        far.append((x, u, mask))
        segments.append((pair, []))
        ups.append(u)

    def segment_of(segment, e):
        for first, count, result in segments[segment][1]:
            if first <= e < first + count:
                return (result[4], ups[segment], result[5], result[6], e - first)

    summed = []

    def advance(events):
        for e, name in events:
            if e < len(summed):
                summed[e].reach(name)

    during = {
        1: ([(0, "halves")], []),
        2: ([(0, "quarters"), (1, "halves")], [(0, "finals")]),
        3: ([(2, "halves")], [(1, "quarters")]),
    }
    for e in range(local_experts):
        for i, (x, u, mask) in enumerate(far):
            segments[2 + i][1].append((e, 1, rows_of(e, 1, x, u, mask)))
        advance(during.get(e, ([], []))[0])
        bunches = [[0, 1, 2]] + [[s, s + 1] for s in range(3, len(segments), 2)]
        results = []
        for bunch in bunches:
            got = run_grads(order.tie(bits), [segment_of(s, e) for s in bunch if s < len(segments)])
            order.did(got[0])
            results.append(got)
        send, keep = (
            total_low([r[i] for r in results]) if len(results) > 1 else results[0][i]
            for i in range(2)
        )
        summed.append(Summed(order, send, keep))
        advance(during.get(e, ([], []))[1])

    def total_of(slot, index):
        for pair, calls in segments:
            if slot in pair:
                at_row = pair.index(slot) * tokens
                parts = [result[index][at_row : at_row + tokens] for _, _, result in calls]
                return total_low(parts)

    def hop(index, total, slot):
        term = total_of(slot % groups, index)
        return order.run(add_low, term, shift(total, 1))

    gate_grad = [
        functools.reduce(
            lambda a, b: a + b,
            [result[2][pair.index(s) * tokens : (pair.index(s) + 1) * tokens] for _, _, result in calls],
        )
        for pair, calls in segments
        for s in pair
    ]
    gate_grad = [g[:, :local_experts].T for g in gate_grad]
    gate_grad = jnp.stack([gate_grad[0]] + [shift(gate_grad[s], -s) for s in range(1, groups)])
    gate_grad = take(gate_grad, [(g - my_group) % groups for g in range(groups)])
    gate_grad = gate_grad.reshape(experts_all, tokens).T

    row_total = total_of(1, 1)
    events = [
        [(3, "halves")],
        [(2, "quarters")],
        [(1, "finals")],
    ]
    for slot in range(2, groups + 1):
        row_total = hop(1, row_total, slot)
        advance(events[slot - 2] if slot - 2 < len(events) else [])
    row_back = row_total.astype(F32)

    upstream = out_grad[0].astype(F32)
    weights_own = segments[0][1][0][2][3][:, :experts_all]
    weighted = jnp.sum(weights_own * gate_grad, axis=-1, keepdims=True)
    logit_grad = (weights_own * (gate_grad - weighted)).astype(BF16)
    router_grad = dot(logit_grad, normed_two, (0, 0))
    normed_two_grad = dot(logit_grad, router_w, (1, 0)) + row_back
    residual_part, ffn_gain_grad = norm_back(normed_two_grad, residual, factor_two, gain_ffn)
    residual_grad = upstream + residual_part

    attn_grad = order.tie(residual_grad.astype(BF16))
    order.did(attn_grad)
    attn_grad = context_gather(attn_grad)
    advance([(3, "quarters"), (0, "spread")])
    out_total = hop(0, total_of(1, 0), 2)
    advance([(2, "finals")])
    attn_grad = order.tie(jnp.concatenate(attn_grad, axis=0))
    order.did(attn_grad)
    out_w_grad = dot(mixed_low, attn_grad, (0, 0)).astype(BF16).reshape(per, HDIM, width)
    mixed_grad = dot(attn_grad, out_w, (1, 1)).astype(BF16).reshape(length, per, HDIM)
    order.did(mixed_grad)
    for slot in range(3, groups + 1):
        out_total = hop(0, out_total, slot)
    hidden_out = (residual + out_total.astype(F32)).astype(BF16)[None]
    scores = (
        jnp.einsum("qhd,khd->hqk", query_low, key_low, preferred_element_type=F32) * score_scale
    )
    probs = jnp.exp(scores - logsum)
    prob_grad = jnp.einsum("qhd,khd->hqk", mixed_grad, value_low, preferred_element_type=F32)
    row_shift = jnp.sum(probs * prob_grad, axis=-1, keepdims=True)
    score_grad = (probs * (prob_grad - row_shift)).astype(BF16)
    query_rot = (
        jnp.einsum("hqk,khd->qhd", score_grad, key_low, preferred_element_type=F32) * score_scale
    )
    key_rot = (
        jnp.einsum("hqk,qhd->khd", score_grad, query_low, preferred_element_type=F32) * score_scale
    )
    value_grad = jnp.einsum(
        "hqk,qhd->khd", probs.astype(BF16), mixed_grad, preferred_element_type=F32
    )
    order.did(value_grad)
    advance([(3, "finals"), (0, "cross"), (1, "spread")])
    query_rot = order.tie(query_rot)
    query_back = rotate(query_rot, cosine, -sine_part)
    key_back = rotate(key_rot, cosine, -sine_part)
    sums = context_total(slots(query_back * gain_query * query_raw, key_back * gain_key * key_raw))
    sums = sums / width
    query_grad = (
        factor_query * query_back * gain_query - query_raw * factor_query**3 * per_row(sums[0])
    )
    key_grad = factor_key * key_back * gain_key - key_raw * factor_key**3 * per_row(sums[1])
    q_gain_grad = jnp.sum(query_back * query_raw * factor_query, axis=0)
    k_gain_grad = jnp.sum(key_back * key_raw * factor_key, axis=0)
    qkv_grad = jnp.stack(
        [
            g.astype(BF16).reshape(length, 2, local // 2)
            for g in (query_grad, key_grad, value_grad)
        ],
        axis=2,
    ).reshape(length, 3 * local)
    normed_grad = dot(qkv_grad, qkv_w, (1, 1)).astype(BF16).reshape(context, tokens, width)
    order.did(normed_grad)
    advance([(2, "spread"), (1, "cross"), (3, "spread")])
    normed_grad = context_sum([normed_grad[s] for s in range(context)])
    parts = [
        lax.dynamic_slice_in_dim(normed_grad, (my_group - m) % groups * block, block, axis=1)
        for m in range(groups)
    ]
    normed_grad = jnp.concatenate(parts, axis=1)
    source_part, attn_gain_grad = norm_back(normed_grad, source, factor_one, gain_attn)
    input_grad = (residual_grad + source_part).astype(BF16)[None]

    qkv_w_grad = dot(normed, qkv_grad, (0, 0)).astype(BF16)
    mine_w = ring_sum(list(qkv_w_grad.reshape(groups, context * rows, 3 * local)), add_low)
    flipped = mine_w.reshape(context, rows, 2, 3 * local // 2)
    got = swap(flipped, "dp", 1)
    mine_w = jnp.stack(
        [add_low(flipped[:, :, 0], got[:, :, 1]), add_low(flipped[:, :, 1], got[:, :, 0])], axis=1
    )
    pieces = [lax.dynamic_index_in_dim(mine_w, m, 0, keepdims=False) for m in members]
    pieces = [pieces[0]] + [swap(pieces[s], "context", s) for s in range(1, context)]
    dense = take(jnp.stack(pieces), members)
    dense = jnp.where(my_dp == 0, dense, dense[:, ::-1]).astype(F32)
    dense = dense.reshape(context, 2, rows, 3, per // 2, HDIM).transpose(3, 2, 1, 4, 0, 5)
    dense = dense.reshape(3, rows, width)
    if whole_heads:
        ordered = take(out_w_grad, [(m // 2 ^ my_dp) * 2 + m % 2 for m in ring])
        mine_out = ring_sum(list(ordered), add_low)
        out_w_grad = mine_out.astype(F32) + swap(mine_out, "dp", 1).astype(F32)
    else:
        spread = jnp.zeros((per, context, HDIM, width), BF16)
        for h in range(per):
            spread = lax.dynamic_update_slice(
                spread, out_w_grad[h][None, None], (heads[h], my_context, 0, 0)
            )
        spread = lax.psum_scatter(
            spread.reshape(width, width), ("expert", "context"), scatter_dimension=0, tiled=True
        )
        out_w_grad = lax.psum(spread, "dp").astype(F32)
    gains = jnp.zeros((2, per, context, HDIM), F32)
    for h in range(per):
        pair = jnp.stack([q_gain_grad[h], k_gain_grad[h]])[:, None, None]
        gains = lax.dynamic_update_slice(gains, pair, (0, heads[h], my_context, 0))
    small_grad = jnp.concatenate(
        [attn_gain_grad[None], ffn_gain_grad[None], gains.reshape(2, width), router_grad], axis=0
    )
    small_grad = small_grad.reshape(4 + experts_all, groups, context, rows).transpose(1, 2, 0, 3)
    small_grad = ring_sum(list(take(small_grad, ring)), lambda a, b: a + b)
    small_grad = take(small_grad, members)
    got = swap(jnp.stack([small_grad[1], small_grad[3]]), "context", 1)
    small_grad = small_grad[0] + got[0] + swap(small_grad[2] + got[1], "context", 2)
    small_grad = small_grad + swap(small_grad, "dp", 1)
    advance([(2, "cross"), (3, "cross")])
    expert_grads = None
    shapes = (w_gate.shape, w_up.shape, w_down.shape)
    for e in range(local_experts):
        summed[e].reach("cross")
        expert_grads = summed[e].place(bits, e, expert_grads, shapes)
    return (
        hidden_out,
        input_grad,
        small_grad[0],
        dense[0],
        dense[1],
        dense[2],
        small_grad[2],
        small_grad[3],
        out_w_grad,
        small_grad[1],
        small_grad[4:].T,
        expert_grads[0],
        expert_grads[1],
        expert_grads[2],
    )


def solution(mesh):
    tokens = P(("expert", "dp"), "context", None)
    vector = P(("expert", "context"))
    matrix = P(("expert", "context"), None)
    expert = P("expert", None, None)
    in_specs = (
        tokens,
        tokens,
        tokens,
        vector,
        matrix,
        matrix,
        matrix,
        vector,
        vector,
        matrix,
        vector,
        matrix,
        expert,
        expert,
        expert,
    )
    out_specs = (
        tokens,
        tokens,
        vector,
        matrix,
        matrix,
        matrix,
        vector,
        vector,
        matrix,
        vector,
        matrix,
        expert,
        expert,
        expert,
    )
    return jax.shard_map(body, mesh=mesh, in_specs=in_specs, out_specs=out_specs, check_vma=False)
```

time: 1870 us -> 1410 us (0.75)
  waiting for transfers between devices: 1150 us -> 588 us
  Pallas kernels: 0 us -> 335 us
  matrix products: 426 us -> 95.7 us
  blocking collectives: 106 us -> 0 us
  starting transfers between devices: 9.03 us -> 87.5 us
  local copies, waits for them, and re-layouts: 28.9 us -> 95.3 us
  other arithmetic: 120 us -> 183 us
    psum x2 -> x0, waiting for transfers between devices: 636 us -> none  [the longest x1 588 us: body(): grads.append(lax.psum(local_grads, ('context', 'dp')))]
    ppermute x0 -> x138, waiting for transfers between devices: none -> 585 us  [the longest x108 356 us: swap(): lax.ppermute(values, axis, [(i, i ^ bit) for i in range(lax.axis_size(axi...]
    pallas_call x0 -> x16, Pallas kernels: none -> 335 us  [the longest x8 184 us: run_rows(): pl.pallas_call(functools.partial(rows_kernel, first), grid_spec=pltpu.Pre...]
    dot_general x45 -> x8, matrix products: 377 us -> 51.6 us  [dot(): lax.dot_general(left, right, (((contract[0],), (contract[1],)), ((), ()))...]
    reduce_scatter x7 -> x0, waiting for transfers between devices: 262 us -> none  [scatter_sum(): return lax.psum_scatter(values, axis, scatter_dimension=0, tiled=True)]
    all_gather x6 -> x2, waiting for transfers between devices: 247 us -> 2.65 us  [the longest x1 2.63 us: body(): upstream_all = lax.all_gather(upstream_all, 'expert', axis=0)]
    convert_element_type x6 -> x69, other arithmetic: 10.2 us -> 100 us  [the longest x53 74.1 us: add_low(): return (left.astype(F32) + right.astype(F32)).astype(BF16)]
    ppermute x0 -> x138, starting transfers between devices: none -> 86.9 us  [the longest x108 72.7 us: swap(): lax.ppermute(values, axis, [(i, i ^ bit) for i in range(lax.axis_size(axi...]
  transfers between devices with their start and end apart: 17 -> 140, of which waited for: 13 -> 54; matrix products, arithmetic and copies ran while one was open for 16% -> 22% of each run, Pallas kernels for 0% -> 17%
where the time goes in v1:
time: 1410 us; the launch traced here: 1400 us
  waiting for transfers between devices  588 us (42%)
  Pallas kernels  335 us (24%)
  other arithmetic  183 us (13%)
  matrix products  95.7 us (7%)
  local copies, waits for them, and re-layouts  95.3 us (7%)
  starting transfers between devices  87.5 us (6%)
  between operations  17.9 us (1%)
    ppermute x108, waiting for transfers between devices, swap(): lax.ppermute(values, axis, [(i, i ^ bit) for i in range(lax.axis_size(axi...  356 us
    ppermute x30, waiting for transfers between devices, shift(): return lax.ppermute(values, 'expert', [(i, (i + by) % n) for i in range(n)])  229 us
    pallas_call x8, Pallas kernels, run_rows(): pl.pallas_call(functools.partial(rows_kernel, first), grid_spec=pltpu.Pre...  184 us
    pallas_call x4, Pallas kernels, run_grads(): pl.pallas_call(functools.partial(grads_kernel, sizes), grid_spec=pltpu.Pr...  94.4 us
    convert_element_type x53, other arithmetic, add_low(): return (left.astype(F32) + right.astype(F32)).astype(BF16)  74.1 us
    ppermute x108, starting transfers between devices, swap(): lax.ppermute(values, axis, [(i, i ^ bit) for i in range(lax.axis_size(axi...  72.7 us
    pallas_call x4, Pallas kernels, place_grads(): pl.pallas_call(functools.partial(place_kernel, e, first), grid_spec=pltpu...  56.6 us
    dot_general x8, matrix products, dot(): lax.dot_general(left, right, (((contract[0],), (contract[1],)), ((), ()))...  51.6 us
  transfers between devices with their start and end apart: 140, of which 54 were waited for; matrix products, arithmetic and copies ran while one was open for 22% of the time, Pallas kernels for 17%

profile of v1, /device:TPU:0, one launch (start us, length us, event | category | flops | bytes accessed | tf_op | source)
XLA Modules:
  0.0 1402.0 jit_solution(7904265956473600159)
XLA Ops:
  27.8 23.2 %collective-permute-done.7 = bf16[20,128]{1,0:T(8,128)(2,1)S(1)} collective-permute-done((bf16[20,128]{1,0:T(8,128)(2,1)S(1)}, bf16[20,128]{1,0:T(8,128)(2,1)S(1)}, u32[]{:S(2)}, u32[]{:S(2)}) %collective-permute-start.7) | collective-permute-done | bytes 5152 | tf_op jit(solution)/shard_map/ppermute | solution.py:85
  54.6 18.9 %collective-permute-done.9 = bf16[4,20,128]{2,1,0:T(8,128)(2,1)S(1)} collective-permute-done((bf16[4,20,128]{2,1,0:T(8,128)(2,1)S(1)}, bf16[4,20,128]{2,1,0:T(8,128)(2,1)S(1)}, u32[]{:S(2)}, u32[]{:S(2)}) %collective-permute-start.9) | collective-permute-done | bytes 20512 | tf_op jit(solution)/shard_map/ppermute | solution.py:90
  74.0 5.1 collective-permute-done.10
  85.2 14.6 %collective-permute-done.13 = bf16[512,768]{1,0:T(8,128)(2,1)} collective-permute-done((bf16[512,768]{1,0:T(8,128)(2,1)}, bf16[512,768]{1,0:T(8,128)(2,1)}, u32[]{:S(2)}, u32[]{:S(2)}) %collective-permute-start.13) | collective-permute-done | bytes 786464 | tf_op jit(solution)/shard_map/ppermute | solution.py:90
  106.1 13.1 collective-permute-done.14
  125.4 12.7 collective-permute-done.16
  138.1 16.9 %collective-permute-done.17 = bf16[512,768]{1,0:T(8,128)(2,1)} collective-permute-done((bf16[512,768]{1,0:T(8,128)(2,1)}, bf16[512,768]{1,0:T(8,128)(2,1)}, u32[]{:S(2)}, u32[]{:S(2)}) %collective-permute-start.17) | collective-permute-done | bytes 786464 | tf_op jit(solution)/shard_map/ppermute | solution.py:85
  154.9 13.7 collective-permute-done.18
  168.6 13.1 fusion.63
  181.7 5.0 multiply_reduce_fusion.9
  202.0 7.6 multiply_reduce_fusion.1
  209.6 8.6 exponential_reduce_fusion
  218.8 9.0 convolution_convert_fusion.4
  246.0 5.0 collective-permute-done.27
  251.8 5.2 collective-permute-done.28
  276.1 22.4 %rows.8 = (bf16[256,2048]{1,0:T(8,128)(2,1)}, bf16[256,2048]{1,0:T(8,128)(2,1)}, f32[256,128]{1,0:T(8,128)}, f32[256,128]{1,0:T(8,128)}, bf16[2048,256]{1,0:T(8,...) custom-call(s32[1]{0:T(128)} %bitcast.55.at_ref, bf16[256,2048]{1,0:T(8,128)(2,1)} %copy-done.57, ...), custom_call_target="tpu_custom_call" | custom-call | flops 12884901888 | bytes 25165824 | tf_op jit(solution)/shard_map/rows/pallas_call | solution.py:219
  298.6 22.7 %rows.9 = (bf16[256,2048]{1,0:T(8,128)(2,1)}, bf16[256,2048]{1,0:T(8,128)(2,1)}, f32[256,128]{1,0:T(8,128)}, f32[256,128]{1,0:T(8,128)}, bf16[2048,256]{1,0:T(8,...) custom-call(s32[1]{0:T(128)} %bitcast.55.at_ref, bf16[256,2048]{1,0:T(8,128)(2,1)} %copy-done.57, ...), custom_call_target="tpu_custom_call" | custom-call | flops 12884901888 | bytes 25165824 | tf_op jit(solution)/shard_map/rows/pallas_call | solution.py:219
  325.7 22.4 %rows.10 = (bf16[256,2048]{1,0:T(8,128)(2,1)}, bf16[256,2048]{1,0:T(8,128)(2,1)}, f32[256,128]{1,0:T(8,128)}, f32[256,128]{1,0:T(8,128)}, bf16[2048,256]{1,0:T(8...) custom-call(s32[1]{0:T(128)} %bitcast.55.at_ref, bf16[256,2048]{1,0:T(8,128)(2,1)} %copy-done.87, ...), custom_call_target="tpu_custom_call" | custom-call | flops 12884901888 | bytes 25165824 | tf_op jit(solution)/shard_map/rows/pallas_call | solution.py:219
  348.0 22.4 %rows.11 = (bf16[256,2048]{1,0:T(8,128)(2,1)}, bf16[256,2048]{1,0:T(8,128)(2,1)}, f32[256,128]{1,0:T(8,128)}, f32[256,128]{1,0:T(8,128)}, bf16[2048,256]{1,0:T(8...) custom-call(s32[1]{0:T(128)} %bitcast.55.at_ref, bf16[256,2048]{1,0:T(8,128)(2,1)} %copy-done.87, ...), custom_call_target="tpu_custom_call" | custom-call | flops 12884901888 | bytes 25165824 | tf_op jit(solution)/shard_map/rows/pallas_call | solution.py:219
  371.9 23.4 %rows.12 = (bf16[512,2048]{1,0:T(8,128)(2,1)}, bf16[512,2048]{1,0:T(8,128)(2,1)}, f32[512,128]{1,0:T(8,128)}, f32[512,128]{1,0:T(8,128)}, bf16[2048,512]{1,0:T(8...) custom-call(s32[1]{0:T(128)} %bitcast.55.at_ref, bf16[512,2048]{1,0:T(8,128)(2,1)} %copy-done.52, ...), custom_call_target="tpu_custom_call" | custom-call | flops 12884901888 | bytes 12582912 | tf_op jit(solution)/shard_map/rows/pallas_call | solution.py:219
  395.3 23.4 %grads.4 = (bf16[2,4,3,512,256]{4,3,2,1,0:T(8,128)(2,1)}, bf16[2,4,3,512,256]{4,3,2,1,0:T(8,128)(2,1)}) custom-call(s32[3]{0:T(128)} %pad_add_fusion.1.bits_ref, bf16[2048,256]{1,0:T(8,128)(2,1)} %get-tuple-element.191.refs_0_, bf16[2048,256]{1,0:T(8,128)(2,1)} %get-tuple-element.192.refs_1_, bf16[2048,512]{1,0:T(8,128)(2,1)} %get-tuple-element.193.refs_2_, ...), custom_call_target="tpu_custom_call" | custom-call | flops 12884901888 | bytes 29360128 | tf_op jit(solution)/shard_map/grads/pallas_call | solution.py:336
  422.3 23.5 %rows.13 = (bf16[512,2048]{1,0:T(8,128)(2,1)}, bf16[512,2048]{1,0:T(8,128)(2,1)}, f32[512,128]{1,0:T(8,128)}, f32[512,128]{1,0:T(8,128)}, bf16[2048,512]{1,0:T(8...) custom-call(s32[1]{0:T(128)} %bitcast.55.at_ref, bf16[512,2048]{1,0:T(8,128)(2,1)} %copy-done.52, ...), custom_call_target="tpu_custom_call" | custom-call | flops 12884901888 | bytes 12582912 | tf_op jit(solution)/shard_map/rows/pallas_call | solution.py:219
  453.0 23.2 %grads.5 = (bf16[2,4,3,512,256]{4,3,2,1,0:T(8,128)(2,1)}, bf16[2,4,3,512,256]{4,3,2,1,0:T(8,128)(2,1)}) custom-call(s32[3]{0:T(128)} %pad_add_fusion.1.bits_ref, bf16[2048,256]{1,0:T(8,128)(2,1)} %get-tuple-element.191.refs_0_, bf16[2048,256]{1,0:T(8,128)(2,1)} %get-tuple-element.192.refs_1_, bf16[2048,512]{1,0:T(8,128)(2,1)} %get-tuple-element.209.refs_2_, ...), custom_call_target="tpu_custom_call" | custom-call | flops 12884901888 | bytes 29360128 | tf_op jit(solution)/shard_map/grads/pallas_call | solution.py:336
  479.7 23.6 %rows.14 = (bf16[512,2048]{1,0:T(8,128)(2,1)}, bf16[512,2048]{1,0:T(8,128)(2,1)}, f32[512,128]{1,0:T(8,128)}, f32[512,128]{1,0:T(8,128)}, bf16[2048,512]{1,0:T(8...) custom-call(s32[1]{0:T(128)} %bitcast.55.at_ref, bf16[512,2048]{1,0:T(8,128)(2,1)} %copy-done.52, ...), custom_call_target="tpu_custom_call" | custom-call | flops 12884901888 | bytes 12582912 | tf_op jit(solution)/shard_map/rows/pallas_call | solution.py:219
  506.6 6.5 collective-permute-done.30
  530.1 23.9 %grads.6 = (bf16[2,4,3,512,256]{4,3,2,1,0:T(8,128)(2,1)}, bf16[2,4,3,512,256]{4,3,2,1,0:T(8,128)(2,1)}) custom-call(s32[3]{0:T(128)} %pad_add_fusion.1.bits_ref, bf16[2048,256]{1,0:T(8,128)(2,1)} %get-tuple-element.225.refs_0_, bf16[2048,256]{1,0:T(8,128)(2,1)} %get-tuple-element.226.refs_1_, bf16[2048,512]{1,0:T(8,128)(2,1)} %get-tuple-element.227.refs_2_, ...), custom_call_target="tpu_custom_call" | custom-call | flops 12884901888 | bytes 29360128 | tf_op jit(solution)/shard_map/grads/pallas_call | solution.py:336
  578.8 11.6 collective-permute-done.33
  598.3 23.5 %rows.15 = (bf16[512,2048]{1,0:T(8,128)(2,1)}, bf16[512,2048]{1,0:T(8,128)(2,1)}, f32[512,128]{1,0:T(8,128)}, f32[512,128]{1,0:T(8,128)}, bf16[2048,512]{1,0:T(8...) custom-call(s32[1]{0:T(128)} %bitcast.55.at_ref, bf16[512,2048]{1,0:T(8,128)(2,1)} %copy-done.52, ...), custom_call_target="tpu_custom_call" | custom-call | flops 12884901888 | bytes 12582912 | tf_op jit(solution)/shard_map/rows/pallas_call | solution.py:219
  633.8 23.9 %grads.7 = (bf16[2,4,3,512,256]{4,3,2,1,0:T(8,128)(2,1)}, bf16[2,4,3,512,256]{4,3,2,1,0:T(8,128)(2,1)}) custom-call(s32[3]{0:T(128)} %pad_add_fusion.1.bits_ref, bf16[2048,256]{1,0:T(8,128)(2,1)} %get-tuple-element.225.refs_0_, bf16[2048,256]{1,0:T(8,128)(2,1)} %get-tuple-element.226.refs_1_, bf16[2048,512]{1,0:T(8,128)(2,1)} %get-tuple-element.260.refs_2_, ...), custom_call_target="tpu_custom_call" | custom-call | flops 12884901888 | bytes 29360128 | tf_op jit(solution)/shard_map/grads/pallas_call | solution.py:336
  662.2 4.8 add_convert_fusion.16
  688.9 32.6 %collective-permute-done.41 = bf16[256,2048]{1,0:T(8,128)(2,1)S(1)} collective-permute-done((bf16[256,2048]{1,0:T(8,128)(2,1)}, bf16[256,2048]{1,0:T(8,128)(2,1)S(1)}, u32[]{:S(2)}, u32[]{:S(2)}) %collective-permute-start.41) | collective-permute-done | bytes 1048608 | tf_op jit(solution)/shard_map/ppermute | solution.py:90
  734.6 13.3 collective-permute-done.43
  751.4 11.9 collective-permute-done.45
  764.8 21.3 %collective-permute-done.46 = bf16[256,2048]{1,0:T(8,128)(2,1)S(1)} collective-permute-done((bf16[256,2048]{1,0:T(8,128)(2,1)S(1)}, bf16[256,2048]{1,0:T(8,128)(2,1)S(1)}, u32[]{:S(2)}, u32[]{:S(2)}) %collective-permute-start.46) | collective-permute-done | bytes 1048608 | tf_op jit(solution)/shard_map/ppermute | solution.py:90
  793.7 29.7 %collective-permute-done.52 = bf16[2,3,512,256]{3,2,1,0:T(8,128)(2,1)S(1)} collective-permute-done((bf16[2,3,512,256]{3,2,1,0:T(8,128)(2,1)S(1)}, bf16[2,3,512,256]{3,2,1,0:T(8,128)(2,1)S(1)}, u32[]{:S(2)}, u32[]{:S(2)}) %collective-permute-start.52) | collective-permute-done | bytes 1572896 | tf_op jit(solution)/shard_map/ppermute | solution.py:85
  830.3 28.8 %collective-permute-done.55 = bf16[3,512,256]{2,1,0:T(8,128)(2,1)S(1)} collective-permute-done((bf16[3,512,256]{2,1,0:T(8,128)(2,1)S(1)}, bf16[3,512,256]{2,1,0:T(8,128)(2,1)S(1)}, u32[]{:S(2)}, u32[]{:S(2)}) %collective-permute-start.55) | collective-permute-done | bytes 786464 | tf_op jit(solution)/shard_map/ppermute | solution.py:85
  870.8 11.5 multiply_reduce_fusion
  882.3 12.0 multiply_convert_fusion
  894.4 10.2 convolution_bitcast_fusion
  914.0 14.9 %collective-permute-done.60 = bf16[3,512,256]{2,1,0:T(8,128)(2,1)S(1)} collective-permute-done((bf16[3,512,256]{2,1,0:T(8,128)(2,1)S(1)}, bf16[3,512,256]{2,1,0:T(8,128)(2,1)S(1)}, u32[]{:S(2)}, u32[]{:S(2)}) %collective-permute-start.60) | collective-permute-done | bytes 786464 | tf_op jit(solution)/shard_map/ppermute | solution.py:85
  945.7 4.6 multiply_reduce_fusion.3
  950.4 6.2 convolution_convert_fusion.2
  963.4 33.2 %collective-permute-done.87.refs_7_ = bf16[3,512,256]{2,1,0:T(8,128)(2,1)S(1)} collective-permute-done((bf16[3,512,256]{2,1,0:T(8,128)(2,1)}, bf16[3,512,256]{2,1,0:T(8,128)(2,1)S(1)}, u32[]{:S(2)}, u32[]{:S(2)}) %collective-permute-start.87) | collective-permute-done | bytes 786464 | tf_op jit(solution)/shard_map/ppermute | solution.py:85
  1005.5 11.6 collective-permute-done.97.refs_2_
  1029.0 6.4 collective-permute-done.110.refs_1_
  1037.8 15.3 %collective-permute-done.113.refs_5_ = bf16[3,512,256]{2,1,0:T(8,128)(2,1)} collective-permute-done((bf16[3,512,256]{2,1,0:T(8,128)(2,1)}, bf16[3,512,256]{2,1,0:T(8,128)(2,1)}, u32[]{:S(2)}, u32[]{:S(2)}) %collective-permute-start.113) | collective-permute-done | bytes 786464 | tf_op jit(solution)/shard_map/ppermute | solution.py:85
  1053.1 15.0 %convolution_convert_fusion.1 = bf16[1024,2048]{1,0:T(8,128)(2,1)} fusion(bf16[1024,1536]{0,1:T(8,128)(2,1)} %bitcast.560, bf16[512,768]{1,0:T(8,128)(2,1)} %collective-permute-done.18, bf16[512,768]{1,0:T(8,128)(2,1)} %collective-permute-done.17, bf16[512,768]{1,0:T(8,128)(2,1)} %collective-permute-done.16, bf16[512,768]{1,0:T(8,128)(2,1)} %collective-permute-done.15, ...), kind=kOutput, calls=%fused_computation.22 | convolution fusion | flops 6494879744 | bytes 13631488 | tf_op jit(solution)/shard_map/dot_general | solution.py:24
  1073.4 11.9 collective-permute-done.78
  1087.0 11.2 convolution_convert_fusion
  1109.9 11.9 collective-permute-done.124.refs_1_
  1125.0 24.6 %collective-permute-done.79 = bf16[128,2048]{1,0:T(8,128)(2,1)S(1)} collective-permute-done((bf16[128,2048]{1,0:T(8,128)(2,1)S(1)}, bf16[128,2048]{1,0:T(8,128)(2,1)S(1)}, u32[]{:S(2)}, u32[]{:S(2)}) %collective-permute-start.79) | collective-permute-done | bytes 524320 | tf_op jit(solution)/shard_map/ppermute | solution.py:90
  1154.4 21.3 %collective-permute-done.64 = bf16[256,2048]{1,0:T(8,128)(2,1)S(1)} collective-permute-done((bf16[256,2048]{1,0:T(8,128)(2,1)S(1)}, bf16[256,2048]{1,0:T(8,128)(2,1)S(1)}, u32[]{:S(2)}, u32[]{:S(2)}) %collective-permute-start.64) | collective-permute-done | bytes 1048608 | tf_op jit(solution)/shard_map/ppermute | solution.py:85
  1180.0 11.0 collective-permute-done.115.refs_7_
  1191.5 14.9 %place.4 = (f32[4,2048,1024]{2,1,0:T(8,128)}, f32[4,2048,1024]{2,1,0:T(8,128)}, f32[4,1024,2048]{2,1,0:T(8,128)}) custom-call(s32[3]{0:T(128)S(1)} %copy-done.48, bf16[3,512,256]{2,1,0:T(8,128)(2,1)} %add_convert_fusion.29.refs_0_, bf16[3,512,256]{2,1,0:T(8,128)(2,1)} %collective-permute-done.82.refs_1_, ...), custom_call_target="tpu_custom_call" | custom-call | bytes 37748736 | tf_op jit(solution)/shard_map/place/pallas_call | solution.py:479
  1206.5 39.0 %collective-permute-done.65 = f32[4,20,128]{2,1,0:T(8,128)S(1)} collective-permute-done((f32[4,20,128]{2,1,0:T(8,128)S(1)}, f32[4,20,128]{2,1,0:T(8,128)S(1)}, u32[]{:S(2)}, u32[]{:S(2)}) %collective-permute-start.65) | collective-permute-done | bytes 40992 | tf_op jit(solution)/shard_map/ppermute | solution.py:90
  1249.2 4.9 collective-permute-done.66
  1254.2 11.5 collective-permute-done.126.refs_3_
  1269.8 12.6 place.5
  1283.1 9.0 collective-permute-done.67
  1293.0 13.3 place.6
  1326.5 15.8 %place.7 = (f32[4,2048,1024]{2,1,0:T(8,128)}, f32[4,2048,1024]{2,1,0:T(8,128)}, f32[4,1024,2048]{2,1,0:T(8,128)}) custom-call(s32[3]{0:T(128)S(1)} %copy-done.48, bf16[3,512,256]{2,1,0:T(8,128)(2,1)S(1)} %add_convert_fusion.23.refs_0_, bf16[3,512,256]{2,1,0:T(8,128)(2,1)S(1)} %copy-done.20, ...), custom_call_target="tpu_custom_call", output_to_operand_aliasing={{0}: (17, {}), {1}: (18, {}), {2}: (19, {})} | custom-call | bytes 37748736 | tf_op jit(solution)/shard_map/place/pallas_call | solution.py:479
  1349.1 10.5 collective-permute-done.70
  1363.2 8.3 collective-permute-done.77
  1371.6 7.8 collective-permute-done.76
  (867 shorter events, 393.5 us)
Async XLA Ops:
  7.2 220.6 %all-gather.5.cloned.1.call-start = ((), (), s32[]{:S(2)}) async-start(), calls=%async_computation | async-start | bytes 2621440 | tf_op jit(solution)/shard_map/all_gather | solution.py:566
  25.1 48.4 %collective-permute-start.4 = (bf16[256,2048]{1,0:T(8,128)(2,1)S(1)}, bf16[256,2048]{1,0:T(8,128)(2,1)S(1)}, u32[]{:S(2)}, u32[]{:S(2)}) collective-permute-start(bf16[256,2048]{1,0:T(8,128)(2,1)S(1)} %bitcast.533), channel_id=1, source_target_pairs={{0,4},{2,6},{4,0},{6,2},{1,5},{3,7},{5,1},{7,3},{8,12},{10,14},{12... | collective-permute-start | bytes 3145736 | tf_op jit(solution)/shard_map/ppermute | solution.py:85
  73.5 28.9 %collective-permute-start.3 = (bf16[256,2048]{1,0:T(8,128)(2,1)S(1)}, bf16[256,2048]{1,0:T(8,128)(2,1)}, u32[]{:S(2)}, u32[]{:S(2)}) collective-permute-start(bf16[256,2048]{1,0:T(8,128)(2,1)S(1)} %bitcast.534), channel_id=1, source_target_pairs={{0,2},{2,0},{4,6},{6,4},{1,3},{3,1},{5,7},{7,5},{8,10},{10,8},{12,... | collective-permute-start | bytes 3145736 | tf_op jit(solution)/shard_map/ppermute | solution.py:85
  73.5 30.4 %collective-permute-start.5 = (bf16[256,2048]{1,0:T(8,128)(2,1)S(1)}, bf16[256,2048]{1,0:T(8,128)(2,1)}, u32[]{:S(2)}, u32[]{:S(2)}) collective-permute-start(bf16[256,2048]{1,0:T(8,128)(2,1)S(1)} %collective-permute-done.4), channel_id=1, source_target_pairs={{0,2},{2,0},{4,6},{6,4},{1,3},{3,1},{5,7},{7,5},{8,10},{10,8},{12,... | collective-permute-start | bytes 3145736 | tf_op jit(solution)/shard_map/ppermute | solution.py:85
  101.9 36.2 %collective-permute-start.16 = (bf16[512,768]{1,0:T(8,128)(2,1)}, bf16[512,768]{1,0:T(8,128)(2,1)}, u32[]{:S(2)}, u32[]{:S(2)}) collective-permute-start(bf16[512,768]{1,0:T(8,128)(2,1)} %collective-permute-done.12), channel_id=1, source_target_pairs={{0,1},{1,0},{2,3},{3,2},{4,5},{5,4},{6,7},{7,6},{8,9},{9,8},{10,11... | collective-permute-start | bytes 2359304 | tf_op jit(solution)/shard_map/ppermute | solution.py:85
  102.4 52.5 %collective-permute-start.17 = (bf16[512,768]{1,0:T(8,128)(2,1)}, bf16[512,768]{1,0:T(8,128)(2,1)}, u32[]{:S(2)}, u32[]{:S(2)}) collective-permute-start(bf16[512,768]{1,0:T(8,128)(2,1)} %collective-permute-done.13), channel_id=1, source_target_pairs={{0,1},{1,0},{2,3},{3,2},{4,5},{5,4},{6,7},{7,6},{8,9},{9,8},{10,11... | collective-permute-start | bytes 2359304 | tf_op jit(solution)/shard_map/ppermute | solution.py:85
  119.2 49.4 %collective-permute-start.18 = (bf16[512,768]{1,0:T(8,128)(2,1)}, bf16[512,768]{1,0:T(8,128)(2,1)}, u32[]{:S(2)}, u32[]{:S(2)}) collective-permute-start(bf16[512,768]{1,0:T(8,128)(2,1)} %collective-permute-done.14), channel_id=1, source_target_pairs={{0,1},{1,0},{2,3},{3,2},{4,5},{5,4},{6,7},{7,6},{8,9},{9,8},{10,11... | collective-permute-start | bytes 2359304 | tf_op jit(solution)/shard_map/ppermute | solution.py:85
  124.8 146.4 %all-gather.7.cloned.1.call-start = ((), (), s32[]{:S(2)}) async-start(), calls=%async_computation.1 | async-start | bytes 5242880 | tf_op jit(solution)/shard_map/all_gather | solution.py:574
  268.5 30.0 %collective-permute-start.23 = (bf16[256,2048]{1,0:T(8,128)(2,1)S(1)}, bf16[256,2048]{1,0:T(8,128)(2,1)S(1)}, u32[]{:S(2)}, u32[]{:S(2)}) collective-permute-start(bf16[256,2048]{1,0:T(8,128)(2,1)S(1)} %multiply_convert_fusion.1.x_ref), channel_id=1, source_target_pairs={{0,8},{8,16},{16,24},{24,0},{1,9},{9,17},{17,25},{25,1},{2,10},{10... | collective-permute-start | bytes 3145736 | tf_op jit(solution)/shard_map/ppermute | solution.py:90
  325.3 45.3 %collective-permute-start.26 = (bf16[256,2048]{1,0:T(8,128)(2,1)S(1)}, bf16[256,2048]{1,0:T(8,128)(2,1)S(1)}, u32[]{:S(2)}, u32[]{:S(2)}) collective-permute-start(bf16[256,2048]{1,0:T(8,128)(2,1)S(1)} %collective-permute-done.24), channel_id=1, source_target_pairs={{0,8},{8,16},{16,24},{24,0},{1,9},{9,17},{17,25},{25,1},{2,10},{10... | collective-permute-start | bytes 3145736 | tf_op jit(solution)/shard_map/ppermute | solution.py:90
  476.2 42.9 %collective-permute-start.32 = (bf16[2,4,3,512,256]{4,3,2,1,0:T(8,128)(2,1)}, bf16[2,4,3,512,256]{4,3,2,1,0:T(8,128)(2,1)}, u32[]{:S(2)}, u32[]{:S(2)}) collective-permute-start(bf16[2,4,3,512,256]{4,3,2,1,0:T(8,128)(2,1)} %get-tuple-element.212), channel_id=1, source_target_pairs={{0,2},{2,0},{4,6},{6,4},{1,3},{3,1},{5,7},{7,5},{8,10},{10,8},{12,... | collective-permute-start | bytes 18874376 | tf_op jit(solution)/shard_map/ppermute | solution.py:85
  476.7 36.4 %collective-permute-start.30 = (bf16[2,3,512,256]{3,2,1,0:T(8,128)(2,1)S(1)}, bf16[2,3,512,256]{3,2,1,0:T(8,128)(2,1)S(1)}, u32[]{:S(2)}, u32[]{:S(2)}) collective-permute-start(bf16[2,3,512,256]{3,2,1,0:T(8,128)(2,1)S(1)} %fusion.19), channel_id=1, source_target_pairs={{0,1},{1,0},{2,3},{3,2},{4,5},{5,4},{6,7},{7,6},{8,9},{9,8},{10,11... | collective-permute-start | bytes 4718600 | tf_op jit(solution)/shard_map/ppermute | solution.py:85
  478.2 36.2 %collective-permute-start.31 = (bf16[2,3,512,256]{3,2,1,0:T(8,128)(2,1)S(1)}, bf16[2,3,512,256]{3,2,1,0:T(8,128)(2,1)}, u32[]{:S(2)}, u32[]{:S(2)}) collective-permute-start(bf16[2,3,512,256]{3,2,1,0:T(8,128)(2,1)S(1)} %fusion.18), channel_id=1, source_target_pairs={{0,4},{2,6},{4,0},{6,2},{1,5},{3,7},{5,1},{7,3},{8,12},{10,14},{12... | collective-permute-start | bytes 4718600 | tf_op jit(solution)/shard_map/ppermute | solution.py:85
  554.0 67.9 %collective-permute-start.38 = (bf16[2,4,3,512,256]{4,3,2,1,0:T(8,128)(2,1)}, bf16[2,4,3,512,256]{4,3,2,1,0:T(8,128)(2,1)}, u32[]{:S(2)}, u32[]{:S(2)}) collective-permute-start(bf16[2,4,3,512,256]{4,3,2,1,0:T(8,128)(2,1)} %get-tuple-element.234), channel_id=1, source_target_pairs={{0,2},{2,0},{4,6},{6,4},{1,3},{3,1},{5,7},{7,5},{8,10},{10,8},{12,... | collective-permute-start | bytes 18874376 | tf_op jit(solution)/shard_map/ppermute | solution.py:85
  577.5 103.8 %collective-permute-start.39 = (bf16[2,3,512,256]{3,2,1,0:T(8,128)(2,1)}, bf16[2,3,512,256]{3,2,1,0:T(8,128)(2,1)}, u32[]{:S(2)}, u32[]{:S(2)}) collective-permute-start(bf16[2,3,512,256]{3,2,1,0:T(8,128)(2,1)} %fusion.15), channel_id=1, source_target_pairs={{0,1},{1,0},{2,3},{3,2},{4,5},{5,4},{6,7},{7,6},{8,9},{9,8},{10,11... | collective-permute-start | bytes 4718600 | tf_op jit(solution)/shard_map/ppermute | solution.py:85
  578.2 105.2 %collective-permute-start.40 = (bf16[2,3,512,256]{3,2,1,0:T(8,128)(2,1)}, bf16[2,3,512,256]{3,2,1,0:T(8,128)(2,1)}, u32[]{:S(2)}, u32[]{:S(2)}) collective-permute-start(bf16[2,3,512,256]{3,2,1,0:T(8,128)(2,1)} %fusion.14), channel_id=1, source_target_pairs={{0,4},{2,6},{4,0},{6,2},{1,5},{3,7},{5,1},{7,3},{8,12},{10,14},{12... | collective-permute-start | bytes 4718600 | tf_op jit(solution)/shard_map/ppermute | solution.py:85
  657.7 66.9 %collective-permute-start.42 = (bf16[2,4,3,512,256]{4,3,2,1,0:T(8,128)(2,1)}, bf16[2,4,3,512,256]{4,3,2,1,0:T(8,128)(2,1)}, u32[]{:S(2)}, u32[]{:S(2)}) collective-permute-start(bf16[2,4,3,512,256]{4,3,2,1,0:T(8,128)(2,1)} %get-tuple-element.264), channel_id=1, source_target_pairs={{0,2},{2,0},{4,6},{6,4},{1,3},{3,1},{5,7},{7,5},{8,10},{10,8},{12,... | collective-permute-start | bytes 18874376 | tf_op jit(solution)/shard_map/ppermute | solution.py:85
  672.1 156.9 %collective-permute-start.54 = (bf16[256,2048]{1,0:T(8,128)(2,1)}, bf16[256,2048]{1,0:T(8,128)(2,1)}, u32[]{:S(2)}, u32[]{:S(2)}) collective-permute-start(bf16[256,2048]{1,0:T(8,128)(2,1)} %add_convert_fusion.7), channel_id=1, source_target_pairs={{0,8},{8,16},{16,24},{24,0},{1,9},{9,17},{17,25},{25,1},{2,10},{10... | collective-permute-start | bytes 3145736 | tf_op jit(solution)/shard_map/ppermute | solution.py:90
  675.2 46.3 %collective-permute-start.41 = (bf16[256,2048]{1,0:T(8,128)(2,1)}, bf16[256,2048]{1,0:T(8,128)(2,1)S(1)}, u32[]{:S(2)}, u32[]{:S(2)}) collective-permute-start(bf16[256,2048]{1,0:T(8,128)(2,1)} %add_convert_fusion.12), channel_id=1, source_target_pairs={{0,8},{8,16},{16,24},{24,0},{1,9},{9,17},{17,25},{25,1},{2,10},{10... | collective-permute-start | bytes 3145736 | tf_op jit(solution)/shard_map/ppermute | solution.py:90
  681.3 181.9 %collective-permute-start.82 = (bf16[3,512,256]{2,1,0:T(8,128)(2,1)}, bf16[3,512,256]{2,1,0:T(8,128)(2,1)}, u32[]{:S(2)}, u32[]{:S(2)}) collective-permute-start(bf16[3,512,256]{2,1,0:T(8,128)(2,1)} %add_convert_fusion.29.refs_0_), channel_id=1, source_target_pairs={{0,4},{2,6},{4,0},{6,2},{1,5},{3,7},{5,1},{7,3},{8,12},{10,14},{12... | collective-permute-start | bytes 2359304 | tf_op jit(solution)/shard_map/ppermute | solution.py:85
  683.4 66.2 %collective-permute-start.44 = (bf16[2,3,512,256]{3,2,1,0:T(8,128)(2,1)S(1)}, bf16[2,3,512,256]{3,2,1,0:T(8,128)(2,1)S(1)}, u32[]{:S(2)}, u32[]{:S(2)}) collective-permute-start(bf16[2,3,512,256]{3,2,1,0:T(8,128)(2,1)S(1)} %copy-done.121), channel_id=1, source_target_pairs={{0,1},{1,0},{2,3},{3,2},{4,5},{5,4},{6,7},{7,6},{8,9},{9,8},{10,11... | collective-permute-start | bytes 4718600 | tf_op jit(solution)/shard_map/ppermute | solution.py:85
  725.9 37.3 %collective-permute-start.45 = (bf16[2,3,512,256]{3,2,1,0:T(8,128)(2,1)S(1)}, bf16[2,3,512,256]{3,2,1,0:T(8,128)(2,1)S(1)}, u32[]{:S(2)}, u32[]{:S(2)}) collective-permute-start(bf16[2,3,512,256]{3,2,1,0:T(8,128)(2,1)S(1)} %copy-done.120), channel_id=1, source_target_pairs={{0,4},{2,6},{4,0},{6,2},{1,5},{3,7},{5,1},{7,3},{8,12},{10,14},{12... | collective-permute-start | bytes 4718600 | tf_op jit(solution)/shard_map/ppermute | solution.py:85
  747.9 42.5 %collective-permute-start.48 = (bf16[3,512,256]{2,1,0:T(8,128)(2,1)S(1)}, bf16[3,512,256]{2,1,0:T(8,128)(2,1)S(1)}, u32[]{:S(2)}, u32[]{:S(2)}) collective-permute-start(bf16[3,512,256]{2,1,0:T(8,128)(2,1)S(1)} %fusion.43), channel_id=1, source_target_pairs={{0,1},{1,0},{2,3},{3,2},{4,5},{5,4},{6,7},{7,6},{8,9},{9,8},{10,11... | collective-permute-start | bytes 2359304 | tf_op jit(solution)/shard_map/ppermute | solution.py:85
  749.6 38.8 %collective-permute-start.47 = (bf16[3,512,256]{2,1,0:T(8,128)(2,1)S(1)}, bf16[3,512,256]{2,1,0:T(8,128)(2,1)S(1)}, u32[]{:S(2)}, u32[]{:S(2)}) collective-permute-start(bf16[3,512,256]{2,1,0:T(8,128)(2,1)S(1)} %fusion.44), channel_id=1, source_target_pairs={{0,4},{2,6},{4,0},{6,2},{1,5},{3,7},{5,1},{7,3},{8,12},{10,14},{12... | collective-permute-start | bytes 2359304 | tf_op jit(solution)/shard_map/ppermute | solution.py:85
  786.1 37.3 %collective-permute-start.52 = (bf16[2,3,512,256]{3,2,1,0:T(8,128)(2,1)S(1)}, bf16[2,3,512,256]{3,2,1,0:T(8,128)(2,1)S(1)}, u32[]{:S(2)}, u32[]{:S(2)}) collective-permute-start(bf16[2,3,512,256]{3,2,1,0:T(8,128)(2,1)S(1)} %fusion.7), channel_id=1, source_target_pairs={{0,1},{1,0},{2,3},{3,2},{4,5},{5,4},{6,7},{7,6},{8,9},{9,8},{10,11... | collective-permute-start | bytes 4718600 | tf_op jit(solution)/shard_map/ppermute | solution.py:85
  788.4 37.8 %collective-permute-start.53 = (bf16[2,3,512,256]{3,2,1,0:T(8,128)(2,1)S(1)}, bf16[2,3,512,256]{3,2,1,0:T(8,128)(2,1)S(1)}, u32[]{:S(2)}, u32[]{:S(2)}) collective-permute-start(bf16[2,3,512,256]{3,2,1,0:T(8,128)(2,1)S(1)} %fusion.6), channel_id=1, source_target_pairs={{0,4},{2,6},{4,0},{6,2},{1,5},{3,7},{5,1},{7,3},{8,12},{10,14},{12... | collective-permute-start | bytes 4718600 | tf_op jit(solution)/shard_map/ppermute | solution.py:85
  790.4 73.5 %collective-permute-start.85 = (bf16[3,512,256]{2,1,0:T(8,128)(2,1)}, bf16[3,512,256]{2,1,0:T(8,128)(2,1)S(1)}, u32[]{:S(2)}, u32[]{:S(2)}) collective-permute-start(bf16[3,512,256]{2,1,0:T(8,128)(2,1)} %add_convert_fusion.28.refs_4_), channel_id=1, source_target_pairs={{0,1},{1,0},{2,3},{3,2},{4,5},{5,4},{6,7},{7,6},{8,9},{9,8},{10,11... | collective-permute-start | bytes 2359304 | tf_op jit(solution)/shard_map/ppermute | solution.py:85
  823.4 35.6 %collective-permute-start.50 = (bf16[256,2048]{1,0:T(8,128)(2,1)S(1)}, bf16[256,2048]{1,0:T(8,128)(2,1)S(1)}, u32[]{:S(2)}, u32[]{:S(2)}) collective-permute-start(bf16[256,2048]{1,0:T(8,128)(2,1)S(1)} %get-tuple-element.284), channel_id=1, source_target_pairs={{0,4},{2,6},{4,0},{6,2},{1,5},{3,7},{5,1},{7,3},{8,12},{10,14},{12... | collective-permute-start | bytes 3145736 | tf_op jit(solution)/shard_map/ppermute | solution.py:85
  826.2 32.8 %collective-permute-start.55 = (bf16[3,512,256]{2,1,0:T(8,128)(2,1)S(1)}, bf16[3,512,256]{2,1,0:T(8,128)(2,1)S(1)}, u32[]{:S(2)}, u32[]{:S(2)}) collective-permute-start(bf16[3,512,256]{2,1,0:T(8,128)(2,1)S(1)} %fusion.40), channel_id=1, source_target_pairs={{0,4},{2,6},{4,0},{6,2},{1,5},{3,7},{5,1},{7,3},{8,12},{10,14},{12... | collective-permute-start | bytes 2359304 | tf_op jit(solution)/shard_map/ppermute | solution.py:85
  829.0 36.7 %collective-permute-start.56 = (bf16[3,512,256]{2,1,0:T(8,128)(2,1)S(1)}, bf16[3,512,256]{2,1,0:T(8,128)(2,1)S(1)}, u32[]{:S(2)}, u32[]{:S(2)}) collective-permute-start(bf16[3,512,256]{2,1,0:T(8,128)(2,1)S(1)} %fusion.39), channel_id=1, source_target_pairs={{0,1},{1,0},{2,3},{3,2},{4,5},{5,4},{6,7},{7,6},{8,9},{9,8},{10,11... | collective-permute-start | bytes 2359304 | tf_op jit(solution)/shard_map/ppermute | solution.py:85
  863.2 96.4 %collective-permute-start.83 = (bf16[3,512,256]{2,1,0:T(8,128)(2,1)}, bf16[3,512,256]{2,1,0:T(8,128)(2,1)}, u32[]{:S(2)}, u32[]{:S(2)}) collective-permute-start(bf16[3,512,256]{2,1,0:T(8,128)(2,1)} %add_convert_fusion.29.refs_0_), channel_id=1, source_target_pairs={{0,1},{1,0},{2,3},{3,2},{4,5},{5,4},{6,7},{7,6},{8,9},{9,8},{10,11... | collective-permute-start | bytes 2359304 | tf_op jit(solution)/shard_map/ppermute | solution.py:85
  863.9 96.5 %collective-permute-start.86 = (bf16[3,512,256]{2,1,0:T(8,128)(2,1)}, bf16[3,512,256]{2,1,0:T(8,128)(2,1)}, u32[]{:S(2)}, u32[]{:S(2)}) collective-permute-start(bf16[3,512,256]{2,1,0:T(8,128)(2,1)} %add_convert_fusion.28.refs_4_), channel_id=1, source_target_pairs={{0,4},{2,6},{4,0},{6,2},{1,5},{3,7},{5,1},{7,3},{8,12},{10,14},{12... | collective-permute-start | bytes 2359304 | tf_op jit(solution)/shard_map/ppermute | solution.py:85
  865.7 131.8 %collective-permute-start.88 = (bf16[3,512,256]{2,1,0:T(8,128)(2,1)}, bf16[3,512,256]{2,1,0:T(8,128)(2,1)}, u32[]{:S(2)}, u32[]{:S(2)}) collective-permute-start(bf16[3,512,256]{2,1,0:T(8,128)(2,1)} %add_convert_fusion.29.refs_0_), channel_id=1, source_target_pairs={{0,2},{2,0},{4,6},{6,4},{1,3},{3,1},{5,7},{7,5},{8,10},{10,8},{12,... | collective-permute-start | bytes 2359304 | tf_op jit(solution)/shard_map/ppermute | solution.py:85
  866.8 89.9 %collective-permute-start.57 = (bf16[256,2048]{1,0:T(8,128)(2,1)}, bf16[256,2048]{1,0:T(8,128)(2,1)}, u32[]{:S(2)}, u32[]{:S(2)}) collective-permute-start(bf16[256,2048]{1,0:T(8,128)(2,1)} %add_convert_fusion.6), channel_id=1, source_target_pairs={{0,8},{8,16},{16,24},{24,0},{1,9},{9,17},{17,25},{25,1},{2,10},{10... | collective-permute-start | bytes 3145736 | tf_op jit(solution)/shard_map/ppermute | solution.py:90
  866.8 41.2 %collective-permute-start.59 = (bf16[3,512,256]{2,1,0:T(8,128)(2,1)}, bf16[3,512,256]{2,1,0:T(8,128)(2,1)S(1)}, u32[]{:S(2)}, u32[]{:S(2)}) collective-permute-start(bf16[3,512,256]{2,1,0:T(8,128)(2,1)} %fusion.36), channel_id=1, source_target_pairs={{0,4},{2,6},{4,0},{6,2},{1,5},{3,7},{5,1},{7,3},{8,12},{10,14},{12... | collective-permute-start | bytes 2359304 | tf_op jit(solution)/shard_map/ppermute | solution.py:85
  928.9 33.6 %collective-permute-start.84 = (bf16[3,512,256]{2,1,0:T(8,128)(2,1)}, bf16[3,512,256]{2,1,0:T(8,128)(2,1)}, u32[]{:S(2)}, u32[]{:S(2)}) collective-permute-start(bf16[3,512,256]{2,1,0:T(8,128)(2,1)} %collective-permute-done.82.refs_1_), channel_id=1, source_target_pairs={{0,1},{1,0},{2,3},{3,2},{4,5},{5,4},{6,7},{7,6},{8,9},{9,8},{10,11... | collective-permute-start | bytes 2359304 | tf_op jit(solution)/shard_map/ppermute | solution.py:85
  959.7 37.0 %collective-permute-start.96 = (bf16[3,512,256]{2,1,0:T(8,128)(2,1)S(1)}, bf16[3,512,256]{2,1,0:T(8,128)(2,1)S(1)}, u32[]{:S(2)}, u32[]{:S(2)}) collective-permute-start(bf16[3,512,256]{2,1,0:T(8,128)(2,1)S(1)} %add_convert_fusion.27.refs_0_), channel_id=1, source_target_pairs={{0,4},{2,6},{4,0},{6,2},{1,5},{3,7},{5,1},{7,3},{8,12},{10,14},{12... | collective-permute-start | bytes 2359304 | tf_op jit(solution)/shard_map/ppermute | solution.py:85
  960.5 36.6 %collective-permute-start.99 = (bf16[3,512,256]{2,1,0:T(8,128)(2,1)S(1)}, bf16[3,512,256]{2,1,0:T(8,128)(2,1)S(1)}, u32[]{:S(2)}, u32[]{:S(2)}) collective-permute-start(bf16[3,512,256]{2,1,0:T(8,128)(2,1)S(1)} %add_convert_fusion.26.refs_4_), channel_id=1, source_target_pairs={{0,1},{1,0},{2,3},{3,2},{4,5},{5,4},{6,7},{7,6},{8,9},{9,8},{10,11... | collective-permute-start | bytes 2359304 | tf_op jit(solution)/shard_map/ppermute | solution.py:85
  961.2 35.4 %collective-permute-start.87 = (bf16[3,512,256]{2,1,0:T(8,128)(2,1)}, bf16[3,512,256]{2,1,0:T(8,128)(2,1)S(1)}, u32[]{:S(2)}, u32[]{:S(2)}) collective-permute-start(bf16[3,512,256]{2,1,0:T(8,128)(2,1)} %copy-done.29), channel_id=1, source_target_pairs={{0,4},{2,6},{4,0},{6,2},{1,5},{3,7},{5,1},{7,3},{8,12},{10,14},{12... | collective-permute-start | bytes 2359304 | tf_op jit(solution)/shard_map/ppermute | solution.py:85
  962.6 35.6 %collective-permute-start.62 = (f32[2,4,256]{2,1,0:T(4,128)S(1)}, f32[2,4,256]{2,1,0:T(4,128)S(1)}, u32[]{:S(2)}, u32[]{:S(2)}) collective-permute-start(f32[2,4,256]{2,1,0:T(4,128)S(1)} %maximum_add_fusion.2), channel_id=1, source_target_pairs={{0,4},{2,6},{4,0},{6,2},{1,5},{3,7},{5,1},{7,3},{8,12},{10,14},{12... | collective-permute-start | bytes 24584 | tf_op jit(solution)/shard_map/ppermute | solution.py:85
  1004.2 31.3 %collective-permute-start.110 = (bf16[3,512,256]{2,1,0:T(8,128)(2,1)}, bf16[3,512,256]{2,1,0:T(8,128)(2,1)S(1)}, u32[]{:S(2)}, u32[]{:S(2)}) collective-permute-start(bf16[3,512,256]{2,1,0:T(8,128)(2,1)} %add_convert_fusion.25.refs_0_), channel_id=1, source_target_pairs={{0,4},{2,6},{4,0},{6,2},{1,5},{3,7},{5,1},{7,3},{8,12},{10,14},{12... | collective-permute-start | bytes 2359304 | tf_op jit(solution)/shard_map/ppermute | solution.py:85
  1018.6 34.5 %collective-permute-start.113 = (bf16[3,512,256]{2,1,0:T(8,128)(2,1)}, bf16[3,512,256]{2,1,0:T(8,128)(2,1)}, u32[]{:S(2)}, u32[]{:S(2)}) collective-permute-start(bf16[3,512,256]{2,1,0:T(8,128)(2,1)} %add_convert_fusion.24.refs_4_), channel_id=1, source_target_pairs={{0,1},{1,0},{2,3},{3,2},{4,5},{5,4},{6,7},{7,6},{8,9},{9,8},{10,11... | collective-permute-start | bytes 2359304 | tf_op jit(solution)/shard_map/ppermute | solution.py:85
  1027.3 40.7 %collective-permute-start.114 = (bf16[3,512,256]{2,1,0:T(8,128)(2,1)S(1)}, bf16[3,512,256]{2,1,0:T(8,128)(2,1)}, u32[]{:S(2)}, u32[]{:S(2)}) collective-permute-start(bf16[3,512,256]{2,1,0:T(8,128)(2,1)S(1)} %copy-done.1), channel_id=1, source_target_pairs={{0,4},{2,6},{4,0},{6,2},{1,5},{3,7},{5,1},{7,3},{8,12},{10,14},{12... | collective-permute-start | bytes 2359304 | tf_op jit(solution)/shard_map/ppermute | solution.py:85
  1029.0 39.6 %collective-permute-start.116 = (bf16[3,512,256]{2,1,0:T(8,128)(2,1)S(1)}, bf16[3,512,256]{2,1,0:T(8,128)(2,1)}, u32[]{:S(2)}, u32[]{:S(2)}) collective-permute-start(bf16[3,512,256]{2,1,0:T(8,128)(2,1)S(1)} %copy-done), channel_id=1, source_target_pairs={{0,2},{2,0},{4,6},{6,4},{1,3},{3,1},{5,7},{7,5},{8,10},{10,8},{12,... | collective-permute-start | bytes 2359304 | tf_op jit(solution)/shard_map/ppermute | solution.py:85
  1035.5 33.2 %collective-permute-start.120 = (bf16[3,512,256]{2,1,0:T(8,128)(2,1)S(1)}, bf16[3,512,256]{2,1,0:T(8,128)(2,1)}, u32[]{:S(2)}, u32[]{:S(2)}) collective-permute-start(bf16[3,512,256]{2,1,0:T(8,128)(2,1)S(1)} %copy-done.1), channel_id=1, source_target_pairs={{0,2},{2,0},{4,6},{6,4},{1,3},{3,1},{5,7},{7,5},{8,10},{10,8},{12,... | collective-permute-start | bytes 2359304 | tf_op jit(solution)/shard_map/ppermute | solution.py:85
  1037.8 31.3 %collective-permute-start.103 = (bf16[3,512,256]{2,1,0:T(8,128)(2,1)S(1)}, bf16[3,512,256]{2,1,0:T(8,128)(2,1)}, u32[]{:S(2)}, u32[]{:S(2)}) collective-permute-start(bf16[3,512,256]{2,1,0:T(8,128)(2,1)S(1)} %collective-permute-done.96.refs_1_), channel_id=1, source_target_pairs={{0,2},{2,0},{4,6},{6,4},{1,3},{3,1},{5,7},{7,5},{8,10},{10,8},{12,... | collective-permute-start | bytes 2359304 | tf_op jit(solution)/shard_map/ppermute | solution.py:85
  1099.9 51.9 %collective-permute-start.71 = (bf16[512,1536]{1,0:T(8,128)(2,1)S(1)}, bf16[512,1536]{1,0:T(8,128)(2,1)S(1)}, u32[]{:S(2)}, u32[]{:S(2)}) collective-permute-start(bf16[512,1536]{1,0:T(8,128)(2,1)S(1)} %unstack.23), channel_id=1, source_target_pairs={{0,8},{8,16},{16,24},{24,0},{1,9},{9,17},{17,25},{25,1},{2,10},{10... | collective-permute-start | bytes 4718600 | tf_op jit(solution)/shard_map/ppermute | solution.py:90
  1106.6 45.1 %collective-permute-start.127 = (bf16[3,512,256]{2,1,0:T(8,128)(2,1)S(1)}, bf16[3,512,256]{2,1,0:T(8,128)(2,1)}, u32[]{:S(2)}, u32[]{:S(2)}) collective-permute-start(bf16[3,512,256]{2,1,0:T(8,128)(2,1)S(1)} %add_convert_fusion.22.refs_4_), channel_id=1, source_target_pairs={{0,1},{1,0},{2,3},{3,2},{4,5},{5,4},{6,7},{7,6},{8,9},{9,8},{10,11... | collective-permute-start | bytes 2359304 | tf_op jit(solution)/shard_map/ppermute | solution.py:85
  1107.9 41.6 %collective-permute-start.79 = (bf16[128,2048]{1,0:T(8,128)(2,1)S(1)}, bf16[128,2048]{1,0:T(8,128)(2,1)S(1)}, u32[]{:S(2)}, u32[]{:S(2)}) collective-permute-start(bf16[128,2048]{1,0:T(8,128)(2,1)S(1)} %fusion.53), channel_id=1, source_target_pairs={{0,8},{8,16},{16,24},{24,0},{1,9},{9,17},{17,25},{25,1},{2,10},{10... | collective-permute-start | bytes 1572872 | tf_op jit(solution)/shard_map/ppermute | solution.py:90
  1121.8 31.7 %collective-permute-start.128 = (bf16[3,512,256]{2,1,0:T(8,128)(2,1)S(1)}, bf16[3,512,256]{2,1,0:T(8,128)(2,1)}, u32[]{:S(2)}, u32[]{:S(2)}) collective-permute-start(bf16[3,512,256]{2,1,0:T(8,128)(2,1)S(1)} %add_convert_fusion.22.refs_4_), channel_id=1, source_target_pairs={{0,4},{2,6},{4,0},{6,2},{1,5},{3,7},{5,1},{7,3},{8,12},{10,14},{12... | collective-permute-start | bytes 2359304 | tf_op jit(solution)/shard_map/ppermute | solution.py:85
  1124.9 29.4 %collective-permute-start.104 = (bf16[3,512,256]{2,1,0:T(8,128)(2,1)S(1)}, bf16[3,512,256]{2,1,0:T(8,128)(2,1)S(1)}, u32[]{:S(2)}, u32[]{:S(2)}) collective-permute-start(bf16[3,512,256]{2,1,0:T(8,128)(2,1)S(1)} %collective-permute-done.97.refs_2_), channel_id=1, source_target_pairs={{0,2},{2,0},{4,6},{6,4},{1,3},{3,1},{5,7},{7,5},{8,10},{10,8},{12,... | collective-permute-start | bytes 2359304 | tf_op jit(solution)/shard_map/ppermute | solution.py:85
  1153.6 37.4 %collective-permute-start.115 = (bf16[3,512,256]{2,1,0:T(8,128)(2,1)}, bf16[3,512,256]{2,1,0:T(8,128)(2,1)S(1)}, u32[]{:S(2)}, u32[]{:S(2)}) collective-permute-start(bf16[3,512,256]{2,1,0:T(8,128)(2,1)} %collective-permute-done.113.refs_5_), channel_id=1, source_target_pairs={{0,4},{2,6},{4,0},{6,2},{1,5},{3,7},{5,1},{7,3},{8,12},{10,14},{12... | collective-permute-start | bytes 2359304 | tf_op jit(solution)/shard_map/ppermute | solution.py:85
  1154.4 36.6 %collective-permute-start.118 = (bf16[3,512,256]{2,1,0:T(8,128)(2,1)S(1)}, bf16[3,512,256]{2,1,0:T(8,128)(2,1)S(1)}, u32[]{:S(2)}, u32[]{:S(2)}) collective-permute-start(bf16[3,512,256]{2,1,0:T(8,128)(2,1)S(1)} %collective-permute-done.111.refs_2_), channel_id=1, source_target_pairs={{0,2},{2,0},{4,6},{6,4},{1,3},{3,1},{5,7},{7,5},{8,10},{10,8},{12,... | collective-permute-start | bytes 2359304 | tf_op jit(solution)/shard_map/ppermute | solution.py:85
  1175.7 72.6 %collective-permute-start.72 = (bf16[512,1536]{1,0:T(8,128)(2,1)S(1)}, bf16[512,1536]{1,0:T(8,128)(2,1)S(1)}, u32[]{:S(2)}, u32[]{:S(2)}) collective-permute-start(bf16[512,1536]{1,0:T(8,128)(2,1)S(1)} %add_convert_fusion.2), channel_id=1, source_target_pairs={{0,8},{8,16},{16,24},{24,0},{1,9},{9,17},{17,25},{25,1},{2,10},{10... | collective-permute-start | bytes 4718600 | tf_op jit(solution)/shard_map/ppermute | solution.py:90
  1178.2 67.4 %collective-permute-start.58 = (bf16[256,2048]{1,0:T(8,128)(2,1)S(1)}, bf16[256,2048]{1,0:T(8,128)(2,1)}, u32[]{:S(2)}, u32[]{:S(2)}) collective-permute-start(bf16[256,2048]{1,0:T(8,128)(2,1)S(1)} %copy-done.127), channel_id=1, source_target_pairs={{0,8},{8,16},{16,24},{24,0},{1,9},{9,17},{17,25},{25,1},{2,10},{10... | collective-permute-start | bytes 3145736 | tf_op jit(solution)/shard_map/ppermute | solution.py:90
  1178.3 28.2 %collective-permute-start.122 = (bf16[3,512,256]{2,1,0:T(8,128)(2,1)}, bf16[3,512,256]{2,1,0:T(8,128)(2,1)S(1)}, u32[]{:S(2)}, u32[]{:S(2)}) collective-permute-start(bf16[3,512,256]{2,1,0:T(8,128)(2,1)} %collective-permute-done.114.refs_6_), channel_id=1, source_target_pairs={{0,2},{2,0},{4,6},{6,4},{1,3},{3,1},{5,7},{7,5},{8,10},{10,8},{12,... | collective-permute-start | bytes 2359304 | tf_op jit(solution)/shard_map/ppermute | solution.py:85
  1191.0 56.0 %collective-permute-start.80 = (bf16[128,2048]{1,0:T(8,128)(2,1)}, bf16[128,2048]{1,0:T(8,128)(2,1)S(1)}, u32[]{:S(2)}, u32[]{:S(2)}) collective-permute-start(bf16[128,2048]{1,0:T(8,128)(2,1)} %fusion.54), channel_id=1, source_target_pairs={{0,8},{8,16},{16,24},{24,0},{1,9},{9,17},{17,25},{25,1},{2,10},{10... | collective-permute-start | bytes 1572872 | tf_op jit(solution)/shard_map/ppermute | solution.py:90
  1191.0 54.6 %collective-permute-start.65 = (f32[4,20,128]{2,1,0:T(8,128)S(1)}, f32[4,20,128]{2,1,0:T(8,128)S(1)}, u32[]{:S(2)}, u32[]{:S(2)}) collective-permute-start(f32[4,20,128]{2,1,0:T(8,128)S(1)} %dynamic-slice_bitcast_fusion.7), channel_id=1, source_target_pairs={{0,8},{8,16},{16,24},{24,0},{1,9},{9,17},{17,25},{25,1},{2,10},{10... | collective-permute-start | bytes 122888 | tf_op jit(solution)/shard_map/ppermute | solution.py:90
  1206.4 42.2 %collective-permute-start.105 = (bf16[3,512,256]{2,1,0:T(8,128)(2,1)S(1)}, bf16[3,512,256]{2,1,0:T(8,128)(2,1)S(1)}, u32[]{:S(2)}, u32[]{:S(2)}) collective-permute-start(bf16[3,512,256]{2,1,0:T(8,128)(2,1)S(1)} %collective-permute-done.98.refs_3_), channel_id=1, source_target_pairs={{0,2},{2,0},{4,6},{6,4},{1,3},{3,1},{5,7},{7,5},{8,10},{10,8},{12,... | collective-permute-start | bytes 2359304 | tf_op jit(solution)/shard_map/ppermute | solution.py:85
  1248.6 33.9 %collective-permute-start.119 = (bf16[3,512,256]{2,1,0:T(8,128)(2,1)S(1)}, bf16[3,512,256]{2,1,0:T(8,128)(2,1)S(1)}, u32[]{:S(2)}, u32[]{:S(2)}) collective-permute-start(bf16[3,512,256]{2,1,0:T(8,128)(2,1)S(1)} %collective-permute-done.112.refs_3_), channel_id=1, source_target_pairs={{0,2},{2,0},{4,6},{6,4},{1,3},{3,1},{5,7},{7,5},{8,10},{10,8},{12,... | collective-permute-start | bytes 2359304 | tf_op jit(solution)/shard_map/ppermute | solution.py:85
  1248.7 33.9 %collective-permute-start.123 = (bf16[3,512,256]{2,1,0:T(8,128)(2,1)S(1)}, bf16[3,512,256]{2,1,0:T(8,128)(2,1)S(1)}, u32[]{:S(2)}, u32[]{:S(2)}) collective-permute-start(bf16[3,512,256]{2,1,0:T(8,128)(2,1)S(1)} %collective-permute-done.115.refs_7_), channel_id=1, source_target_pairs={{0,2},{2,0},{4,6},{6,4},{1,3},{3,1},{5,7},{7,5},{8,10},{10,8},{12,... | collective-permute-start | bytes 2359304 | tf_op jit(solution)/shard_map/ppermute | solution.py:85
  1254.1 56.5 %collective-permute-start.73 = (bf16[512,1536]{1,0:T(8,128)(2,1)S(1)}, bf16[512,1536]{1,0:T(8,128)(2,1)S(1)}, u32[]{:S(2)}, u32[]{:S(2)}) collective-permute-start(bf16[512,1536]{1,0:T(8,128)(2,1)S(1)} %add_convert_fusion.1), channel_id=1, source_target_pairs={{0,8},{8,16},{16,24},{24,0},{1,9},{9,17},{17,25},{25,1},{2,10},{10... | collective-permute-start | bytes 4718600 | tf_op jit(solution)/shard_map/ppermute | solution.py:90
  1265.7 40.6 %collective-permute-start.130 = (bf16[3,512,256]{2,1,0:T(8,128)(2,1)S(1)}, bf16[3,512,256]{2,1,0:T(8,128)(2,1)S(1)}, u32[]{:S(2)}, u32[]{:S(2)}) collective-permute-start(bf16[3,512,256]{2,1,0:T(8,128)(2,1)S(1)} %add_convert_fusion.23.refs_0_), channel_id=1, source_target_pairs={{0,2},{2,0},{4,6},{6,4},{1,3},{3,1},{5,7},{7,5},{8,10},{10,8},{12,... | collective-permute-start | bytes 2359304 | tf_op jit(solution)/shard_map/ppermute | solution.py:85
  1323.3 36.3 %collective-permute-start.74 = (bf16[4,128,2,768]{3,1,0,2:T(8,128)(2,1)S(1)}, bf16[4,128,2,768]{3,1,0,2:T(8,128)(2,1)S(1)}, u32[]{:S(2)}, u32[]{:S(2)}) collective-permute-start(bf16[4,128,2,768]{3,1,0,2:T(8,128)(2,1)S(1)} %copy.224), channel_id=1, source_target_pairs={{0,1},{1,0},{2,3},{3,2},{4,5},{5,4},{6,7},{7,6},{8,9},{9,8},{10,11... | collective-permute-start | bytes 4718600 | tf_op jit(solution)/shard_map/ppermute | solution.py:85
  (260 other events, 4575.4 us)
Sparse Core Ops, SparseCore 0:
  124.9 43.2 all-gather.4
  189.8 81.4 all-gather.6

commit v2 on v1

--- a/solution.py
+++ b/solution.py
@@ -1,4 +1,5 @@
 import functools
+import math
 
 import jax
 import jax.numpy as jnp
@@ -69,16 +70,149 @@
     return (grad_in, gain_grad)
 
 
-def rotate(values, cosine, sine_part):
-    first_half = values[..., : HDIM // 2]
-    second_half = values[..., HDIM // 2 :]
-    return jnp.concatenate(
-        [
-            first_half * cosine - second_half * sine_part,
-            second_half * cosine + first_half * sine_part,
+def half_turn(values):
+    return pltpu.roll(values, HDIM // 2, 1)
+
+
+def attend_kernel(
+    q_ref, k_ref, v_ref, fq_ref, fk_ref, gq_ref, gk_ref, cos_ref, sin_ref,
+    ql_ref, kl_ref, vl_ref, mixed_ref, logsum_ref,
+):
+    length = q_ref.shape[0]
+    block = min(256, length)
+    cosine, sine = cos_ref[...], sin_ref[...]
+    query = q_ref[...] * fq_ref[...] * gq_ref[0]
+    key = k_ref[...] * fk_ref[...] * gk_ref[0]
+    ql_ref[...] = (query * cosine + half_turn(query) * sine).astype(BF16)
+    kl_ref[...] = (key * cosine + half_turn(key) * sine).astype(BF16)
+    value = v_ref[...].astype(BF16)
+    vl_ref[...] = value
+    turned = value.T
+    for b in range(length // block):
+        r = slice(b * block, (b + 1) * block)
+        scores = dot(kl_ref[...], ql_ref[r, :], (1, 1)) * HDIM ** (-0.5)
+        top = jnp.max(scores, axis=0, keepdims=True)
+        raised = jnp.exp(scores - top)
+        total = jnp.sum(raised, axis=0, keepdims=True)
+        mixed = dot(turned, raised.astype(BF16), (1, 0)) / total
+        mixed_ref[r, :] = mixed.T.astype(BF16)
+        logsum_ref[0, :, r] = top + jnp.log(total)
+
+
+def attend_back_kernel(
+    ql_ref, kl_ref, vl_ref, grad_ref, logsum_ref, q_ref, k_ref, fq_ref, fk_ref, gq_ref, gk_ref,
+    cos_ref, sin_ref, qb_ref, kb_ref, vg_ref, qs_ref, ks_ref, qg_ref, kg_ref, k_acc, v_acc, q_acc,
+):
+    length = ql_ref.shape[0]
+    block = min(256, length)
+    scale = HDIM ** (-0.5)
+
+    @pl.when(pl.program_id(0) == 0)
+    def _():
+        qs_ref[...] = jnp.zeros_like(qs_ref)
+        ks_ref[...] = jnp.zeros_like(ks_ref)
+
+    for b in range(length // block):
+        r = slice(b * block, (b + 1) * block)
+        query, grad = ql_ref[r, :], grad_ref[r, :]
+        scores = dot(kl_ref[...], query, (1, 1)) * scale
+        probs = jnp.exp(scores - logsum_ref[0, :, r])
+        prob_grad = dot(vl_ref[...], grad, (1, 1))
+        moved = jnp.sum(probs * prob_grad, axis=0, keepdims=True)
+        score_grad = (probs * (prob_grad - moved)).astype(BF16)
+        value_part = dot(probs.astype(BF16), grad, (1, 0))
+        key_part = dot(score_grad, query, (1, 0))
+        if b == 0:
+            v_acc[...] = value_part
+            k_acc[...] = key_part
+        else:
+            v_acc[...] += value_part
+            k_acc[...] += key_part
+        q_acc[r, :] = dot(score_grad, kl_ref[...], (0, 0))
+    vg_ref[...] = v_acc[...].astype(BF16)
+    cosine, sine = cos_ref[...], sin_ref[...]
+    for acc, back_ref, raw_ref, f_ref, g_ref, sum_ref, gain_ref in (
+        (q_acc, qb_ref, q_ref, fq_ref, gq_ref, qs_ref, qg_ref),
+        (k_acc, kb_ref, k_ref, fk_ref, gk_ref, ks_ref, kg_ref),
+    ):
+        turned = acc[...] * scale
+        back = turned * cosine - half_turn(turned) * sine
+        product = back * raw_ref[...]
+        back_ref[...] = back
+        sum_ref[...] += product * g_ref[0]
+        gain_ref[0] = jnp.sum(product * f_ref[...], axis=0, keepdims=True)
+
+
+def head_specs(length):
+    return {
+        "head": pl.BlockSpec((length, HDIM), lambda h: (0, h)),
+        "whole": pl.BlockSpec((length, HDIM), lambda h: (0, 0)),
+        "column": pl.BlockSpec((length, 1), lambda h: (0, 0)),
+        "gain": pl.BlockSpec((1, 1, HDIM), lambda h: (h, 0, 0)),
+        "row": pl.BlockSpec((1, 1, length), lambda h: (h, 0, 0)),
+    }
+
+
+def attend(qkv, fq, fk, gq, gk, cosine, sine):
+    length, heads = qkv.shape[0], gq.shape[0]
+    spec = head_specs(length)
+
+    def part(i):
+        return pl.BlockSpec((length, HDIM), lambda h: (0, i * heads + h))
+
+    low = jax.ShapeDtypeStruct((length, heads * HDIM), BF16)
+    return pl.pallas_call(
+        attend_kernel,
+        grid=(heads,),
+        in_specs=[part(0), part(1), part(2)]
+        + [spec[n] for n in ("column", "column", "gain", "gain", "whole", "whole")],
+        out_specs=[spec["head"]] * 4 + [spec["row"]],
+        out_shape=[low] * 4 + [jax.ShapeDtypeStruct((heads, 1, length), F32)],
+        compiler_params=pltpu.CompilerParams(vmem_limit_bytes=40 * MIB),
+        cost_estimate=pl.CostEstimate(
+            flops=10 * heads * length * length * HDIM,
+            bytes_accessed=20 * length * heads * HDIM,
+            transcendentals=heads * length * length,
+        ),
+        name="attend",
+    )(qkv, qkv, qkv, fq, fk, gq, gk, cosine, sine)
+
+
+def attend_back(ql, kl, vl, grad, logsum, qkv, fq, fk, gq, gk, cosine, sine):
+    length, heads = qkv.shape[0], gq.shape[0]
+    spec = head_specs(length)
+
+    def part(i):
+        return pl.BlockSpec((length, HDIM), lambda h: (0, i * heads + h))
+
+    def shape(kind, *dims):
+        return jax.ShapeDtypeStruct(dims, kind)
+
+    return pl.pallas_call(
+        attend_back_kernel,
+        grid=(heads,),
+        in_specs=[spec["head"]] * 4
+        + [spec["row"], part(0), part(1)]
+        + [spec[n] for n in ("column", "column", "gain", "gain", "whole", "whole")],
+        out_specs=[spec["head"]] * 3 + [spec["whole"]] * 2 + [spec["gain"]] * 2,
+        out_shape=[
+            shape(F32, length, heads * HDIM),
+            shape(F32, length, heads * HDIM),
+            shape(BF16, length, heads * HDIM),
+            shape(F32, length, HDIM),
+            shape(F32, length, HDIM),
+            shape(F32, heads, 1, HDIM),
+            shape(F32, heads, 1, HDIM),
         ],
-        axis=-1,
-    )
+        scratch_shapes=[pltpu.VMEM((length, HDIM), F32)] * 3,
+        compiler_params=pltpu.CompilerParams(vmem_limit_bytes=48 * MIB),
+        cost_estimate=pl.CostEstimate(
+            flops=20 * heads * length * length * HDIM,
+            bytes_accessed=30 * length * heads * HDIM,
+            transcendentals=heads * length * length,
+        ),
+        name="attend_back",
+    )(ql, kl, vl, grad, logsum, qkv, qkv, fq, fk, gq, gk, cosine, sine)
 
 
 def swap(values, axis, bit):
@@ -364,94 +498,117 @@
     )(bits, *turned, *ups, *boths, *hiddens)
 
 
+def add_kernel(picks, joined, *refs):
+    outs = [refs[-1].at[i] for i in range(len(picks))] if joined else refs[-len(picks) :]
+
+    def at(ref, index):
+        return ref[index] if index is not None else ref[...]
+
+    for out, terms in zip(outs, picks):
+        left, right = (at(refs[i], index) for i, index in terms)
+        out[...] = (left.astype(F32) + right.astype(F32)).astype(BF16)
+
+
+def add_pieces(picks, shapes, ins, last, joined=False):
+
+    parts = 4
+
+    def cut(shape):
+        block = shape[:-2] + (shape[-2] // parts, shape[-1])
+        return pl.BlockSpec(block, lambda i: (0,) * (len(shape) - 2) + (i, 0))
+
+    moved = sum(i.size for i in ins) + sum(math.prod(s) for s in shapes)
+    return pl.pallas_call(
+        functools.partial(add_kernel, picks, joined),
+        grid=(parts,),
+        in_specs=[cut(i.shape) for i in ins] + [pl.BlockSpec(memory_space=pl.ANY)],
+        out_specs=[cut(s) for s in shapes],
+        out_shape=[jax.ShapeDtypeStruct(s, BF16) for s in shapes],
+        compiler_params=pltpu.CompilerParams(vmem_limit_bytes=32 * MIB),
+        cost_estimate=pl.CostEstimate(flops=moved, bytes_accessed=2 * moved, transcendentals=0),
+        name="add_pieces",
+    )(*ins, last)
+
+
 class Summed:
     def __init__(self, order, send, keep):
         self.order, self.keep = order, keep
-        self.ahead = ["halves", "quarters", "finals", "spread", "cross"]
+        self.ahead = ["halves", "quarters", "finals"]
         self.got = swap(send, "context", 1)
 
     def reach(self, name):
         while name in self.ahead:
             getattr(self, self.ahead.pop(0))()
 
+    def add(self, picks, shapes, ins, joined=False):
+        outs = add_pieces(picks, shapes, ins, self.order.last, joined)
+        self.order.did(outs[0])
+        return outs
+
     def halves(self):
-        self.kept, self.coming = [], []
-        for path in range(2):
-            kept, got = self.keep[path], self.got[path]
-            away = self.order.run(add_low, kept[2:], got[2:])
-            self.coming.append(swap(away, *FIRST[path]))
-        for path in range(2):
-            self.kept.append(self.order.run(add_low, self.keep[path, :2], self.got[path, :2]))
+        shape = (2,) + self.keep.shape[2:]
+        picks = [
+            [(0, (path, slice(at, at + 2))), (1, (path, slice(at, at + 2)))]
+            for at in (2, 0)
+            for path in range(2)
+        ]
+        outs = self.add(picks, [shape] * 4, [self.keep, self.got])
+        self.coming = [swap(outs[path], *FIRST[path]) for path in range(2)]
+        self.kept = outs[2:]
 
     def quarters(self):
-        kept, self.kept, coming, self.coming = self.kept, [], self.coming, []
-        for path in range(2):
-            away = self.order.run(add_low, kept[path][1], coming[path][1])
-            self.coming.append(swap(away, *SECOND[path]))
-        for path in range(2):
-            self.kept.append(self.order.run(add_low, kept[path][0], coming[path][0]))
+        shape = self.keep.shape[2:]
+        picks = [[(path, at), (2 + path, at)] for at in (1, 0) for path in range(2)]
+        outs = self.add(picks, [shape] * 4, [*self.kept, *self.coming])
+        self.coming = [swap(outs[path], *SECOND[path]) for path in range(2)]
+        self.kept = outs[2:]
 
     def finals(self):
-        self.own = []
-        for path in range(2):
-            final = self.order.run(add_low, self.kept[path], self.coming[path])
-            self.own.append([final, swap(final, *SECOND[path]), swap(final, *FIRST[path])])
-
-    def spread(self):
-        for path in range(2):
-            beside = self.order.tie(self.own[path][1])
-            self.own[path].append(swap(beside, *FIRST[path]))
-        self.other = [[swap(p, "context", 1) for p in path[:2]] for path in self.own]
-
-    def cross(self):
-        for path in range(2):
-            ready = [self.order.tie(p) for p in self.own[path][2:]]
-            self.other[path] += [swap(p, "context", 1) for p in ready]
-
-    def place(self, bits, e, outs, shapes):
-        pieces = [p for half in (self.own, self.other) for path in half for p in path]
-        outs = place_grads(self.order.tie(bits), e, pieces, outs, shapes)
-        self.order.did(outs[2])
-        return outs
-
-
-def place_kernel(e, first, bits_ref, *refs):
-    ins = refs[:16]
-    outs = refs[16:19] if first else refs[19:22]
-    low, wide, in_sem, out_sem = refs[-4:]
+        shape = self.keep.shape[2:]
+        picks = [[(path, None), (2 + path, None)] for path in range(2)]
+        own = self.add(picks, [(2,) + shape], [*self.kept, *self.coming], True)[0]
+        self.all = lax.all_gather(own, ("context", "dp"), axis=0)
+
+
+def place_kernel(e, first, last_ref, *refs):
+    source = refs[0]
+    outs = refs[1:4] if first else refs[4:7]
+    token_ref, low, wide, in_sem, out_sem = refs[-5:]
     rows = low.shape[2]
+    count = 2 * source.shape[0]
+    token_ref[...] = jnp.zeros_like(token_ref)
 
     def fetch(i):
-        return pltpu.make_async_copy(ins[i], low.at[i % 2], in_sem.at[i % 2])
+        return pltpu.make_async_copy(source.at[i // 2, i % 2], low.at[i % 2], in_sem.at[i % 2])
 
     def drain(i):
-        core, path, place = i // 8, i // 4 % 2, i % 4
-        chunk = (core ^ bits_ref[0]) * 2 + path
-        piece = place ^ bits_ref[1 + path]
-        columns = pl.ds(pl.multiple_of(chunk * CHUNK, CHUNK), CHUNK)
+        path, member = i % 2, i // 2
+        side, core, dp = member // 4, member // 2 % 2, member % 2
+        chunk = core * 2 + path
+        piece = (dp * 2 + side, side * 2 + dp)[path]
+        columns = pl.ds(chunk * CHUNK, CHUNK)
         copies = []
         for k in range(2):
             copies.append(
                 pltpu.make_async_copy(
                     wide.at[i % 2, k],
-                    outs[k].at[e, pl.ds(pl.multiple_of(piece * rows, rows), rows), columns],
+                    outs[k].at[e, pl.ds(piece * rows, rows), columns],
                     out_sem.at[i % 2, k],
                 )
             )
         for j in range(rows // CHUNK):
-            across = pl.ds(pl.multiple_of(piece * rows + j * CHUNK, CHUNK), CHUNK)
             copies.append(
                 pltpu.make_async_copy(
                     wide.at[i % 2, 2, pl.ds(j * CHUNK, CHUNK)],
-                    outs[2].at[e, columns, across],
+                    outs[2].at[e, columns, pl.ds(piece * rows + j * CHUNK, CHUNK)],
                     out_sem.at[i % 2, 2 + j],
                 )
             )
         return copies
 
     fetch(0).start()
-    for i in range(16):
-        if i + 1 < 16:
+    for i in range(count):
+        if i + 1 < count:
             fetch(i + 1).start()
         fetch(i).wait()
         if i >= 2:
@@ -466,38 +623,34 @@
 
         for copy in drain(i):
             copy.start()
-    for i in (14, 15):
+    for i in (count - 2, count - 1):
         for copy in drain(i):
             copy.wait()
 
 
-def place_grads(bits, e, pieces, outs, shapes):
+def place_grads(e, gathered, last, outs, shapes):
     first = outs is None
-    rows = pieces[0].shape[1]
+    rows = gathered.shape[3]
     anywhere = pl.BlockSpec(memory_space=pl.ANY)
-    operands = list(pieces) + ([] if first else list(outs))
+    operands = [last, gathered] + ([] if first else list(outs[:3]))
     return pl.pallas_call(
         functools.partial(place_kernel, e, first),
-        grid_spec=pltpu.PrefetchScalarGridSpec(
-            num_scalar_prefetch=1,
-            grid=(1,),
-            in_specs=[anywhere] * len(operands),
-            out_specs=[anywhere] * 3,
-            scratch_shapes=[
-                pltpu.VMEM((2, 3, rows, CHUNK), BF16),
-                pltpu.VMEM((2, 3, rows, CHUNK), F32),
-                pltpu.SemaphoreType.DMA((2,)),
-                pltpu.SemaphoreType.DMA((2, 2 + rows // CHUNK)),
-            ],
-        ),
-        out_shape=[jax.ShapeDtypeStruct(s, F32) for s in shapes],
-        input_output_aliases={} if first else {17: 0, 18: 1, 19: 2},
+        in_specs=[anywhere] * len(operands),
+        out_specs=[anywhere] * 3 + [pl.BlockSpec((8, 128), lambda: (0, 0))],
+        scratch_shapes=[
+            pltpu.VMEM((2, 3, rows, CHUNK), BF16),
+            pltpu.VMEM((2, 3, rows, CHUNK), F32),
+            pltpu.SemaphoreType.DMA((2,)),
+            pltpu.SemaphoreType.DMA((2, 2 + rows // CHUNK)),
+        ],
+        out_shape=[jax.ShapeDtypeStruct(s, F32) for s in (*shapes, (8, 128))],
+        input_output_aliases={} if first else {2: 0, 3: 1, 4: 2},
         compiler_params=pltpu.CompilerParams(vmem_limit_bytes=16 * MIB),
         cost_estimate=pl.CostEstimate(
             flops=0, bytes_accessed=16 * 9 * rows * CHUNK * 2, transcendentals=0
         ),
         name="place",
-    )(bits, *operands)
+    )(*operands)
 
 
 def body(
@@ -530,7 +683,6 @@
     length = tokens * context
     per = HEADS // context
     local = per * HDIM
-    score_scale = HDIM ** (-0.5)
     core, side = my_context % 2, my_context // 2
     bits = jnp.stack([core, my_dp * 2 + side, side * 2 + my_dp]).astype(jnp.int32)
     ring = [(my_group - s) % groups for s in range(groups)]
@@ -545,26 +697,37 @@
     pieces = [lax.dynamic_index_in_dim(columns, m, 0, keepdims=False) for m in members]
     pieces = [pieces[0]] + [swap(pieces[s], "context", s) for s in range(1, context)]
     half_w = take(jnp.stack(pieces), members).reshape(context * rows, 3 * local // 2)
-    hidden_all = lax.optimization_barrier((hidden_in[0], half_w))[0]
-    hidden_all = jnp.concatenate(context_gather(hidden_all), axis=0)
     small = jnp.concatenate(
         [attn_gain[None], q_gain[None], k_gain[None], ffn_gain[None], w_router.T], axis=0
     )
-    small = take(jnp.stack(context_gather(small)), members)
+    small = [small] + [swap(small, "context", s) for s in range(1, context)]
+    small = take(jnp.stack(small), members)
+    hidden_all = lax.optimization_barrier((hidden_in[0], half_w, small))[0]
+    hidden_all = jnp.concatenate(context_gather(hidden_all), axis=0)
     small = take(jnp.stack(ring_gather(small)), ring)
     small_all = small.transpose(2, 0, 1, 3).reshape(4 + experts_all, width)
-    routes_ring = ring_gather(routes[0])
-    halves = ring_gather(half_w)
-    others = [swap(h, "dp", 1) for h in halves]
+    halves, others = [half_w], [swap(half_w, "dp", 1)]
+    for s in range(1, groups):
+        before = lax.optimization_barrier((halves[-1], others[s - 2]))[0] if s > 1 else half_w
+        halves.append(shift(before, 1))
+        others.append(swap(halves[-1], "dp", 1))
+    routes_ring = ring_gather(lax.optimization_barrier((routes[0], halves[-1]))[0])
+    some = local // 2
     qkv_w = jnp.concatenate(
-        [jnp.concatenate(halves, axis=0), jnp.concatenate(others, axis=0)], axis=1
+        [
+            jnp.concatenate(
+                [w[:, i * some : (i + 1) * some] for i in range(3) for w in pair], axis=1
+            )
+            for pair in zip(halves, others)
+        ],
+        axis=0,
     )
     heads = [my_dp * 2, my_dp * 2 + 1, (1 - my_dp) * 2, (1 - my_dp) * 2 + 1]
     whole_heads = rows == HDIM
     if whole_heads:
         held = lax.optimization_barrier((w_out, halves[-1]))[0]
-        held = lax.all_gather(held, "expert", axis=0)
-        out_w = take(held, heads).reshape(local, width)
+        held = jnp.stack(ring_gather(held))
+        out_w = take(held, [(my_group - h) % groups for h in heads]).reshape(local, width)
     else:
         out_w = lax.all_gather(w_out, ("expert", "context"), axis=0, tiled=True)
         out_w = out_w.reshape(per, context, HDIM, width)
@@ -595,40 +758,27 @@
     normed = to_ring((source_all * factor_all * gain_attn).astype(BF16))
     source = hidden_in[0].astype(F32)
     factor_one = rms_factor(source)
-    qkv = dot(normed, qkv_w, (1, 0)).reshape(length, 2, 3, local // 2)
-    query_raw = qkv[:, :, 0].reshape(length, per, HDIM)
-    key_raw = qkv[:, :, 1].reshape(length, per, HDIM)
-    value_low = qkv[:, :, 2].astype(BF16).reshape(length, per, HDIM)
+    qkv = dot(normed, qkv_w, (1, 0))
 
     def slots(query, key):
-        return jnp.stack([jnp.sum(v, axis=(1, 2)).reshape(context, tokens) for v in (query, key)])
+        return jnp.stack([v.reshape(context, tokens) for v in (query, key)])
 
     def per_row(values):
-        return values.reshape(length)[:, None, None]
-
-    squares = context_total(slots(query_raw * query_raw, key_raw * key_raw))
+        return values.reshape(length)[:, None]
+
+    squares = jnp.sum(jnp.square(qkv[:, : 2 * local]).reshape(length, 2, local), axis=-1)
+    squares = context_total(slots(squares[:, 0], squares[:, 1]))
     factors = lax.rsqrt(squares / width + epsilon)
     factor_query, factor_key = per_row(factors[0]), per_row(factors[1])
     starts = jnp.stack([m * tokens for m in members])
     positions = (starts[:, None] + jnp.arange(tokens, dtype=jnp.int32)).reshape(length).astype(F32)
     frequency = rope_base ** (-jnp.arange(HDIM // 2, dtype=F32) * 2.0 / HDIM)
     angles = positions[:, None] * frequency[None, :]
-    cosine = jnp.cos(angles)[:, None, :]
-    sine_part = jnp.sin(angles)[:, None, :]
-    query_low = rotate(query_raw * factor_query * gain_query, cosine, sine_part).astype(BF16)
-    key_low = rotate(key_raw * factor_key * gain_key, cosine, sine_part).astype(BF16)
-    scores = (
-        jnp.einsum("qhd,khd->hqk", query_low, key_low, preferred_element_type=F32) * score_scale
-    )
-    score_max = jnp.max(scores, axis=-1, keepdims=True)
-    denominator = jnp.sum(jnp.exp(scores - score_max), axis=-1, keepdims=True)
-    logsum = score_max + jnp.log(denominator)
-    probs = jnp.exp(scores - logsum)
-    mixed_low = (
-        jnp.einsum("hqk,khd->qhd", probs.astype(BF16), value_low, preferred_element_type=F32)
-        .reshape(length, local)
-        .astype(BF16)
-    )
+    cosine = jnp.tile(jnp.cos(angles), (1, 2))
+    sine_part = jnp.sin(angles)
+    sine_part = jnp.concatenate([-sine_part, sine_part], axis=1)
+    turn = (factor_query, factor_key, gain_query[:, None], gain_key[:, None], cosine, sine_part)
+    query_low, key_low, value_low, mixed_low, logsum = attend(qkv, *turn)
     mixed_out = dot(mixed_low, out_w, (1, 0)).astype(BF16).reshape(context, tokens, width)
     residual = source + context_sum([mixed_out[s] for s in range(context)])
     factor_two = rms_factor(residual)
@@ -640,7 +790,7 @@
     order = Order()
 
     def upstream_of(slot):
-        return lax.dynamic_index_in_dim(upstream_all, ring[slot], 0, keepdims=False)
+        return lax.dynamic_index_in_dim(order.tie(upstream_all), ring[slot], 0, keepdims=False)
 
     def rows_of(first, count, x, u, mask):
         result = run_rows(order.tie(at), first, count, x, u, mask, router_wide, w_gate, w_up, w_down)
@@ -652,8 +802,10 @@
         near = [[(0, 2), (2, 2)]] * 2
     blocks = [normed_two, shift(normed_two, 1)]
     segments = [([0], []), ([1], [])]
-    ups = [out_grad[0], upstream_of(1)]
+    ups = [out_grad[0]]
     for slot in range(2):
+        if slot == 1:
+            ups.append(upstream_of(1))
         for i, (first, count) in enumerate(near[slot]):
             result = rows_of(first, count, blocks[slot], ups[slot], masks[slot])
             segments[slot][1].append((first, count, result))
@@ -694,12 +846,27 @@
     during = {
         1: ([(0, "halves")], []),
         2: ([(0, "quarters"), (1, "halves")], [(0, "finals")]),
-        3: ([(2, "halves")], [(1, "quarters")]),
+        3: ([(1, "quarters"), (2, "halves")], []),
     }
+
+    def total_of(slot, index):
+        for pair, calls in segments:
+            if slot in pair:
+                at_row = pair.index(slot) * tokens
+                parts = [result[index][at_row : at_row + tokens] for _, _, result in calls]
+                return total_low(parts)
+
+    def hop(index, total, slot):
+        term = total_of(slot % groups, index)
+        return order.run(add_low, term, shift(total, 1))
+
+    row_total = total_of(1, 1)
     for e in range(local_experts):
         for i, (x, u, mask) in enumerate(far):
             segments[2 + i][1].append((e, 1, rows_of(e, 1, x, u, mask)))
         advance(during.get(e, ([], []))[0])
+        if e == local_experts - 1:
+            row_total = hop(1, row_total, 2)
         bunches = [[0, 1, 2]] + [[s, s + 1] for s in range(3, len(segments), 2)]
         results = []
         for bunch in bunches:
@@ -713,17 +880,6 @@
         summed.append(Summed(order, send, keep))
         advance(during.get(e, ([], []))[1])
 
-    def total_of(slot, index):
-        for pair, calls in segments:
-            if slot in pair:
-                at_row = pair.index(slot) * tokens
-                parts = [result[index][at_row : at_row + tokens] for _, _, result in calls]
-                return total_low(parts)
-
-    def hop(index, total, slot):
-        term = total_of(slot % groups, index)
-        return order.run(add_low, term, shift(total, 1))
-
     gate_grad = [
         functools.reduce(
             lambda a, b: a + b,
@@ -737,15 +893,12 @@
     gate_grad = take(gate_grad, [(g - my_group) % groups for g in range(groups)])
     gate_grad = gate_grad.reshape(experts_all, tokens).T
 
-    row_total = total_of(1, 1)
     events = [
-        [(3, "halves")],
-        [(2, "quarters")],
-        [(1, "finals")],
+        [],
     ]
-    for slot in range(2, groups + 1):
+    for slot in range(3, groups + 1):
         row_total = hop(1, row_total, slot)
-        advance(events[slot - 2] if slot - 2 < len(events) else [])
+        advance(events[slot - 3] if slot - 3 < len(events) else [])
     row_back = row_total.astype(F32)
 
     upstream = out_grad[0].astype(F32)
@@ -760,57 +913,53 @@
     attn_grad = order.tie(residual_grad.astype(BF16))
     order.did(attn_grad)
     attn_grad = context_gather(attn_grad)
-    advance([(3, "quarters"), (0, "spread")])
+    advance([(1, "finals"), (3, "halves"), (2, "quarters")])
     out_total = hop(0, total_of(1, 0), 2)
-    advance([(2, "finals")])
     attn_grad = order.tie(jnp.concatenate(attn_grad, axis=0))
     order.did(attn_grad)
     out_w_grad = dot(mixed_low, attn_grad, (0, 0)).astype(BF16).reshape(per, HDIM, width)
-    mixed_grad = dot(attn_grad, out_w, (1, 1)).astype(BF16).reshape(length, per, HDIM)
+    mixed_grad = dot(attn_grad, out_w, (1, 1)).astype(BF16)
     order.did(mixed_grad)
-    for slot in range(3, groups + 1):
+    advance([(2, "finals"), (3, "quarters")])
+    out_total = hop(0, out_total, 3) if groups > 2 else out_total
+    mixed_grad = order.tie(mixed_grad)
+    query_back, key_back, value_grad, query_sum, key_sum, q_gain_grad, k_gain_grad = attend_back(
+        query_low, key_low, value_low, mixed_grad, logsum, qkv, *turn
+    )
+    order.did(value_grad)
+    value_w_grad = dot(normed, value_grad, (0, 0)).astype(BF16)
+    value_w_grad = ring_sum(list(value_w_grad.reshape(groups, context * rows, local)), add_low)
+    sums = context_total(slots(jnp.sum(query_sum, axis=1), jnp.sum(key_sum, axis=1))) / width
+    advance([(3, "finals")])
+    for slot in range(4, groups + 1):
         out_total = hop(0, out_total, slot)
     hidden_out = (residual + out_total.astype(F32)).astype(BF16)[None]
-    scores = (
-        jnp.einsum("qhd,khd->hqk", query_low, key_low, preferred_element_type=F32) * score_scale
-    )
-    probs = jnp.exp(scores - logsum)
-    prob_grad = jnp.einsum("qhd,khd->hqk", mixed_grad, value_low, preferred_element_type=F32)
-    row_shift = jnp.sum(probs * prob_grad, axis=-1, keepdims=True)
-    score_grad = (probs * (prob_grad - row_shift)).astype(BF16)
-    query_rot = (
-        jnp.einsum("hqk,khd->qhd", score_grad, key_low, preferred_element_type=F32) * score_scale
-    )
-    key_rot = (
-        jnp.einsum("hqk,qhd->khd", score_grad, query_low, preferred_element_type=F32) * score_scale
-    )
-    value_grad = jnp.einsum(
-        "hqk,qhd->khd", probs.astype(BF16), mixed_grad, preferred_element_type=F32
-    )
-    order.did(value_grad)
-    advance([(3, "finals"), (0, "cross"), (1, "spread")])
-    query_rot = order.tie(query_rot)
-    query_back = rotate(query_rot, cosine, -sine_part)
-    key_back = rotate(key_rot, cosine, -sine_part)
-    sums = context_total(slots(query_back * gain_query * query_raw, key_back * gain_key * key_raw))
-    sums = sums / width
-    query_grad = (
-        factor_query * query_back * gain_query - query_raw * factor_query**3 * per_row(sums[0])
-    )
-    key_grad = factor_key * key_back * gain_key - key_raw * factor_key**3 * per_row(sums[1])
-    q_gain_grad = jnp.sum(query_back * query_raw * factor_query, axis=0)
-    k_gain_grad = jnp.sum(key_back * key_raw * factor_key, axis=0)
-    qkv_grad = jnp.stack(
-        [
-            g.astype(BF16).reshape(length, 2, local // 2)
-            for g in (query_grad, key_grad, value_grad)
-        ],
-        axis=2,
-    ).reshape(length, 3 * local)
+    shapes = (w_gate.shape, w_up.shape, w_down.shape)
+    expert_grads = None
+
+    def place(experts):
+        outs = expert_grads
+        for e in experts:
+            if e < local_experts:
+                summed[e].reach("finals")
+                outs = place_grads(e, summed[e].all, order.last, outs, shapes)
+                order.did(outs[3])
+        return outs
+
+    def low_grad(back, raw, factor, gain, total):
+        return (
+            factor * back * gain.reshape(1, local) - raw * factor**3 * per_row(total)
+        ).astype(BF16)
+
+    query_grad = low_grad(query_back, qkv[:, :local], factor_query, gain_query, sums[0])
+    key_grad = low_grad(key_back, qkv[:, local : 2 * local], factor_key, gain_key, sums[1])
+    qkv_grad = order.tie(jnp.concatenate([query_grad, key_grad, value_grad], axis=1))
     normed_grad = dot(qkv_grad, qkv_w, (1, 1)).astype(BF16).reshape(context, tokens, width)
-    order.did(normed_grad)
-    advance([(2, "spread"), (1, "cross"), (3, "spread")])
     normed_grad = context_sum([normed_grad[s] for s in range(context)])
+    qk_w_grad = dot(normed, qkv_grad[:, : 2 * local], (0, 0)).astype(BF16)
+    order.did(qk_w_grad)
+    qk_w_grad = ring_sum(list(qk_w_grad.reshape(groups, context * rows, 2 * local)), add_low)
+    expert_grads = place([0, 1, 2])
     parts = [
         lax.dynamic_slice_in_dim(normed_grad, (my_group - m) % groups * block, block, axis=1)
         for m in range(groups)
@@ -819,18 +968,16 @@
     source_part, attn_gain_grad = norm_back(normed_grad, source, factor_one, gain_attn)
     input_grad = (residual_grad + source_part).astype(BF16)[None]
 
-    qkv_w_grad = dot(normed, qkv_grad, (0, 0)).astype(BF16)
-    mine_w = ring_sum(list(qkv_w_grad.reshape(groups, context * rows, 3 * local)), add_low)
-    flipped = mine_w.reshape(context, rows, 2, 3 * local // 2)
-    got = swap(flipped, "dp", 1)
+    mine_w = jnp.concatenate([qk_w_grad, value_w_grad], axis=1).reshape(context, rows, 3, 2, some)
+    got = swap(mine_w, "dp", 1)
     mine_w = jnp.stack(
-        [add_low(flipped[:, :, 0], got[:, :, 1]), add_low(flipped[:, :, 1], got[:, :, 0])], axis=1
+        [add_low(mine_w[:, :, :, i], got[:, :, :, 1 - i]) for i in range(2)], axis=3
     )
     pieces = [lax.dynamic_index_in_dim(mine_w, m, 0, keepdims=False) for m in members]
     pieces = [pieces[0]] + [swap(pieces[s], "context", s) for s in range(1, context)]
     dense = take(jnp.stack(pieces), members)
-    dense = jnp.where(my_dp == 0, dense, dense[:, ::-1]).astype(F32)
-    dense = dense.reshape(context, 2, rows, 3, per // 2, HDIM).transpose(3, 2, 1, 4, 0, 5)
+    dense = jnp.where(my_dp == 0, dense, dense[:, :, :, ::-1]).astype(F32)
+    dense = dense.reshape(context, rows, 3, per, HDIM).transpose(2, 1, 3, 0, 4)
     dense = dense.reshape(3, rows, width)
     if whole_heads:
         ordered = take(out_w_grad, [(m // 2 ^ my_dp) * 2 + m % 2 for m in ring])
@@ -848,7 +995,7 @@
         out_w_grad = lax.psum(spread, "dp").astype(F32)
     gains = jnp.zeros((2, per, context, HDIM), F32)
     for h in range(per):
-        pair = jnp.stack([q_gain_grad[h], k_gain_grad[h]])[:, None, None]
+        pair = jnp.stack([q_gain_grad[h], k_gain_grad[h]])[:, None]
         gains = lax.dynamic_update_slice(gains, pair, (0, heads[h], my_context, 0))
     small_grad = jnp.concatenate(
         [attn_gain_grad[None], ffn_gain_grad[None], gains.reshape(2, width), router_grad], axis=0
@@ -859,12 +1006,7 @@
     got = swap(jnp.stack([small_grad[1], small_grad[3]]), "context", 1)
     small_grad = small_grad[0] + got[0] + swap(small_grad[2] + got[1], "context", 2)
     small_grad = small_grad + swap(small_grad, "dp", 1)
-    advance([(2, "cross"), (3, "cross")])
-    expert_grads = None
-    shapes = (w_gate.shape, w_up.shape, w_down.shape)
-    for e in range(local_experts):
-        summed[e].reach("cross")
-        expert_grads = summed[e].place(bits, e, expert_grads, shapes)
+    expert_grads = place([3])
     return (
         hidden_out,
         input_grad,

time: 1410 us -> 1270 us (0.901)
  other arithmetic: 183 us -> 90.3 us
  matrix products: 95.7 us -> 38.6 us
  Pallas kernels: 335 us -> 391 us
  waiting for transfers between devices: 588 us -> 537 us
    ppermute x108 -> x52, waiting for transfers between devices: 356 us -> 278 us  [swap(): lax.ppermute(values, axis, [(i, i ^ bit) for i in range(lax.axis_size(axi...]
    pallas_call x4 -> x18, Pallas kernels: 56.6 us -> 114 us  [the longest x4 44 us: place_grads(): pl.pallas_call(functools.partial(place_kernel, e, first), in_specs=[anywh...]
    convert_element_type x53 -> x16, other arithmetic: 74.1 us -> 17.3 us  [add_low(): return (left.astype(F32) + right.astype(F32)).astype(BF16)]
    unnamed x381 -> x350, local copies, waits for them, and re-layouts: 22 us -> 70.1 us
    dot_general x6 -> x0, matrix products: 44.1 us -> none  [the longest x1 11.5 us: body(): jnp.einsum('qhd,khd->hqk', mixed_grad, value_low, preferred_element_type=...]
    ppermute x108 -> x52, starting transfers between devices: 72.7 us -> 42.3 us  [swap(): lax.ppermute(values, axis, [(i, i ^ bit) for i in range(lax.axis_size(axi...]
    ppermute x30 -> x36, waiting for transfers between devices: 229 us -> 259 us  [shift(): return lax.ppermute(values, 'expert', [(i, (i + by) % n) for i in range(n)])]
    ppermute x30 -> x36, starting transfers between devices: 14.2 us -> 40 us  [shift(): return lax.ppermute(values, 'expert', [(i, (i + by) % n) for i in range(n)])]
  transfers between devices with their start and end apart: 140 -> 93, of which waited for: 54 -> 46; matrix products, arithmetic and copies ran while one was open for 22% -> 13% of each run, Pallas kernels for 17% -> 24%
where the time goes in v2:
time: 1270 us
  waiting for transfers between devices  537 us (42%)
  Pallas kernels  391 us (31%)
  local copies, waits for them, and re-layouts  108 us (9%)
  other arithmetic  90.3 us (7%)
  starting transfers between devices  82.5 us (6%)
  matrix products  38.6 us (3%)
  between operations  17.8 us (1%)
    ppermute x52, waiting for transfers between devices, swap(): lax.ppermute(values, axis, [(i, i ^ bit) for i in range(lax.axis_size(axi...  278 us
    ppermute x36, waiting for transfers between devices, shift(): return lax.ppermute(values, 'expert', [(i, (i + by) % n) for i in range(n)])  259 us
    pallas_call x8, Pallas kernels, run_rows(): pl.pallas_call(functools.partial(rows_kernel, first), grid_spec=pltpu.Pre...  183 us
    pallas_call x4, Pallas kernels, run_grads(): pl.pallas_call(functools.partial(grads_kernel, sizes), grid_spec=pltpu.Pr...  94.1 us
    unnamed x350, local copies, waits for them, and re-layouts  70.1 us
    pallas_call x4, Pallas kernels, place_grads(): pl.pallas_call(functools.partial(place_kernel, e, first), in_specs=[anywh...  44 us
    ppermute x52, starting transfers between devices, swap(): lax.ppermute(values, axis, [(i, i ^ bit) for i in range(lax.axis_size(axi...  42.3 us
    ppermute x36, starting transfers between devices, shift(): return lax.ppermute(values, 'expert', [(i, (i + by) % n) for i in range(n)])  40 us
  transfers between devices with their start and end apart: 93, of which 46 were waited for; matrix products, arithmetic and copies ran while one was open for 13% of the time, Pallas kernels for 24%

profile of v2, /device:TPU:0, one launch (start us, length us, event | category | flops | bytes accessed | tf_op | source)
XLA Modules:
  0.0 1265.7 jit_solution(5312752443694318540)
XLA Ops:
  31.0 4.7 collective-permute-done.11
  42.2 14.5 %collective-permute-done.13 = bf16[512,768]{1,0:T(8,128)(2,1)S(1)} collective-permute-done((bf16[512,768]{1,0:T(8,128)(2,1)S(1)}, bf16[512,768]{1,0:T(8,128)(2,1)S(1)}, u32[]{:S(2)}, u32[]{:S(2)}) %collective-permute-start.13) | collective-permute-done | bytes 786464 | tf_op jit(solution)/shard_map/ppermute | solution.py:224
  62.5 11.6 collective-permute-done.15
  77.3 7.3 fusion.2
  85.2 6.9 collective-permute-done.17
  93.8 12.4 collective-permute-done.18
  107.4 9.5 fusion.23.q_ref.k_ref.v_ref
  122.2 6.6 reshape.445
  137.8 11.4 collective-permute-done.22
  149.2 11.3 collective-permute-start.23
  164.7 15.4 %attend.1 = (bf16[1024,512]{1,0:T(8,128)(2,1)S(1)}, bf16[1024,512]{1,0:T(8,128)(2,1)S(1)}, bf16[1024,512]{1,0:T(8,128)(2,1)S(1)}, bf16[1024,512]{1,0:T(8,128)(2,1)S(1)}, f32[4,1,1024]{2,1,0:T(1,128)S(1)}) custom-call(f32[1024,1536]{1,0:T(8,128)S(1)} %copy-done.1, f32[1024,1536]{1,0:T(8,128)S(1)} %copy-done.1, f32[1024,1536]{1,0:T(8,128)S(1)} %copy-done.1, ...), custom_call_target="tpu_custom_call" | custom-call | flops 5368709120 | bytes 10485760 | tf_op jit(solution)/shard_map/attend/pallas_call | solution.py:164
  207.8 5.3 collective-permute-done.30
  213.7 5.1 collective-permute-done.31
  228.8 22.5 %rows.8 = (bf16[256,2048]{1,0:T(8,128)(2,1)}, bf16[256,2048]{1,0:T(8,128)(2,1)}, f32[256,128]{1,0:T(8,128)}, f32[256,128]{1,0:T(8,128)}, bf16[2048,256]{1,0:T(8,...) custom-call(s32[1]{0:T(128)} %bitcast.54.at_ref, bf16[256,2048]{1,0:T(8,128)(2,1)} %copy-done.68, ...), custom_call_target="tpu_custom_call" | custom-call | flops 12884901888 | bytes 25165824 | tf_op jit(solution)/shard_map/rows/pallas_call | solution.py:353
  251.3 26.4 %collective-permute-done.26.x_ref = bf16[256,2048]{1,0:T(8,128)(2,1)S(1)} collective-permute-done((bf16[256,2048]{1,0:T(8,128)(2,1)S(1)}, bf16[256,2048]{1,0:T(8,128)(2,1)S(1)}, u32[]{:S(2)}, u32[]{:S(2)}) %collective-permute-start.26) | collective-permute-done | bytes 1048608 | tf_op jit(solution)/shard_map/ppermute | solution.py:224
  277.7 14.8 %collective-permute-start.27 = (bf16[256,2048]{1,0:T(8,128)(2,1)S(1)}, bf16[256,2048]{1,0:T(8,128)(2,1)S(1)}, u32[]{:S(2)}, u32[]{:S(2)}) collective-permute-start(bf16[256,2048]{1,0:T(8,128)(2,1)S(1)} %collective-permute-done.26.x_ref), channel_id=1, source_target_pairs={{0,8},{8,16},{16,24},{24,0},{1,9},{9,17},{17,25},{25,1},{2,10},{10... | collective-permute-start | bytes 3145736 | tf_op jit(solution)/shard_map/ppermute | solution.py:224
  292.5 22.4 %rows.9 = (bf16[256,2048]{1,0:T(8,128)(2,1)}, bf16[256,2048]{1,0:T(8,128)(2,1)}, f32[256,128]{1,0:T(8,128)}, f32[256,128]{1,0:T(8,128)}, bf16[2048,256]{1,0:T(8,...) custom-call(s32[1]{0:T(128)} %bitcast.54.at_ref, bf16[256,2048]{1,0:T(8,128)(2,1)} %copy-done.68, ...), custom_call_target="tpu_custom_call" | custom-call | flops 12884901888 | bytes 25165824 | tf_op jit(solution)/shard_map/rows/pallas_call | solution.py:353
  321.4 22.3 %rows.10 = (bf16[256,2048]{1,0:T(8,128)(2,1)}, bf16[256,2048]{1,0:T(8,128)(2,1)}, f32[256,128]{1,0:T(8,128)}, f32[256,128]{1,0:T(8,128)}, bf16[2048,256]{1,0:T(8...) custom-call(s32[1]{0:T(128)} %bitcast.54.at_ref, bf16[256,2048]{1,0:T(8,128)(2,1)} %copy-done.81, ...), custom_call_target="tpu_custom_call" | custom-call | flops 12884901888 | bytes 25165824 | tf_op jit(solution)/shard_map/rows/pallas_call | solution.py:353
  343.7 22.4 %rows.11 = (bf16[256,2048]{1,0:T(8,128)(2,1)}, bf16[256,2048]{1,0:T(8,128)(2,1)}, f32[256,128]{1,0:T(8,128)}, f32[256,128]{1,0:T(8,128)}, bf16[2048,256]{1,0:T(8...) custom-call(s32[1]{0:T(128)} %bitcast.54.at_ref, bf16[256,2048]{1,0:T(8,128)(2,1)} %copy-done.81, ...), custom_call_target="tpu_custom_call" | custom-call | flops 12884901888 | bytes 25165824 | tf_op jit(solution)/shard_map/rows/pallas_call | solution.py:353
  371.1 23.4 %rows.12 = (bf16[512,2048]{1,0:T(8,128)(2,1)}, bf16[512,2048]{1,0:T(8,128)(2,1)}, f32[512,128]{1,0:T(8,128)}, f32[512,128]{1,0:T(8,128)}, bf16[2048,512]{1,0:T(8...) custom-call(s32[1]{0:T(128)} %bitcast.54.at_ref, bf16[512,2048]{1,0:T(8,128)(2,1)} %copy-done.63, ...), custom_call_target="tpu_custom_call" | custom-call | flops 12884901888 | bytes 12582912 | tf_op jit(solution)/shard_map/rows/pallas_call | solution.py:353
  394.5 23.3 %grads.4 = (bf16[2,4,3,512,256]{4,3,2,1,0:T(8,128)(2,1)}, bf16[2,4,3,512,256]{4,3,2,1,0:T(8,128)(2,1)}) custom-call(s32[3]{0:T(128)} %pad_add_fusion.1.bits_ref, bf16[2048,256]{1,0:T(8,128)(2,1)} %get-tuple-element.183.refs_0_, bf16[2048,256]{1,0:T(8,128)(2,1)} %get-tuple-element.184.refs_1_, bf16[2048,512]{1,0:T(8,128)(2,1)} %get-tuple-element.185.refs_2_, ...), custom_call_target="tpu_custom_call" | custom-call | flops 12884901888 | bytes 29360128 | tf_op jit(solution)/shard_map/grads/pallas_call | solution.py:470
  417.9 23.5 %rows.13 = (bf16[512,2048]{1,0:T(8,128)(2,1)}, bf16[512,2048]{1,0:T(8,128)(2,1)}, f32[512,128]{1,0:T(8,128)}, f32[512,128]{1,0:T(8,128)}, bf16[2048,512]{1,0:T(8...) custom-call(s32[1]{0:T(128)} %bitcast.54.at_ref, bf16[512,2048]{1,0:T(8,128)(2,1)} %copy-done.63, ...), custom_call_target="tpu_custom_call" | custom-call | flops 12884901888 | bytes 12582912 | tf_op jit(solution)/shard_map/rows/pallas_call | solution.py:353
  443.0 4.7 add_pieces.12
  451.2 23.4 %grads.5 = (bf16[2,4,3,512,256]{4,3,2,1,0:T(8,128)(2,1)}, bf16[2,4,3,512,256]{4,3,2,1,0:T(8,128)(2,1)}) custom-call(s32[3]{0:T(128)} %pad_add_fusion.1.bits_ref, bf16[2048,256]{1,0:T(8,128)(2,1)} %get-tuple-element.183.refs_0_, bf16[2048,256]{1,0:T(8,128)(2,1)} %get-tuple-element.184.refs_1_, bf16[2048,512]{1,0:T(8,128)(2,1)} %get-tuple-element.199.refs_2_, ...), custom_call_target="tpu_custom_call" | custom-call | flops 12884901888 | bytes 29360128 | tf_op jit(solution)/shard_map/grads/pallas_call | solution.py:470
  478.5 23.4 %rows.14 = (bf16[512,2048]{1,0:T(8,128)(2,1)}, bf16[512,2048]{1,0:T(8,128)(2,1)}, f32[512,128]{1,0:T(8,128)}, f32[512,128]{1,0:T(8,128)}, bf16[2048,512]{1,0:T(8...) custom-call(s32[1]{0:T(128)} %bitcast.54.at_ref, bf16[512,2048]{1,0:T(8,128)(2,1)} %copy-done.63, ...), custom_call_target="tpu_custom_call" | custom-call | flops 12884901888 | bytes 12582912 | tf_op jit(solution)/shard_map/rows/pallas_call | solution.py:353
  501.9 10.3 collective-permute-done.33.refs_2_
  530.1 23.7 %grads.6 = (bf16[2,4,3,512,256]{4,3,2,1,0:T(8,128)(2,1)}, bf16[2,4,3,512,256]{4,3,2,1,0:T(8,128)(2,1)}) custom-call(s32[3]{0:T(128)} %pad_add_fusion.1.bits_ref, bf16[2048,256]{1,0:T(8,128)(2,1)} %get-tuple-element.216.refs_0_, bf16[2048,256]{1,0:T(8,128)(2,1)} %get-tuple-element.217.refs_1_, bf16[2048,512]{1,0:T(8,128)(2,1)} %get-tuple-element.218.refs_2_, ...), custom_call_target="tpu_custom_call" | custom-call | flops 12884901888 | bytes 29360128 | tf_op jit(solution)/shard_map/grads/pallas_call | solution.py:470
  574.3 23.5 %rows.15 = (bf16[512,2048]{1,0:T(8,128)(2,1)}, bf16[512,2048]{1,0:T(8,128)(2,1)}, f32[512,128]{1,0:T(8,128)}, f32[512,128]{1,0:T(8,128)}, bf16[2048,512]{1,0:T(8...) custom-call(s32[1]{0:T(128)} %bitcast.54.at_ref, bf16[512,2048]{1,0:T(8,128)(2,1)} %copy-done.63, ...), custom_call_target="tpu_custom_call" | custom-call | flops 12884901888 | bytes 12582912 | tf_op jit(solution)/shard_map/rows/pallas_call | solution.py:353
  601.3 6.5 add_convert_fusion.12
  607.8 24.6 %collective-permute-done.39.refs_2_ = bf16[2,3,512,256]{3,2,1,0:T(8,128)(2,1)S(1)} collective-permute-done((bf16[2,3,512,256]{3,2,1,0:T(8,128)(2,1)S(1)}, bf16[2,3,512,256]{3,2,1,0:T(8,128)(2,1)S(1)}, u32[]{:S(2)}, u32[]{:S(2)}) %collective-permute-start.39) | collective-permute-done | bytes 1572896 | tf_op jit(solution)/shard_map/ppermute | solution.py:219
  639.7 5.0 add_pieces.17
  652.1 23.7 %grads.7 = (bf16[2,4,3,512,256]{4,3,2,1,0:T(8,128)(2,1)}, bf16[2,4,3,512,256]{4,3,2,1,0:T(8,128)(2,1)}) custom-call(s32[3]{0:T(128)} %pad_add_fusion.1.bits_ref, bf16[2048,256]{1,0:T(8,128)(2,1)} %get-tuple-element.216.refs_0_, bf16[2048,256]{1,0:T(8,128)(2,1)} %get-tuple-element.217.refs_1_, bf16[2048,512]{1,0:T(8,128)(2,1)} %get-tuple-element.239.refs_2_, ...), custom_call_target="tpu_custom_call" | custom-call | flops 12884901888 | bytes 29360128 | tf_op jit(solution)/shard_map/grads/pallas_call | solution.py:470
  682.6 19.0 %collective-permute-done.49 = bf16[256,2048]{1,0:T(8,128)(2,1)} collective-permute-done((bf16[256,2048]{1,0:T(8,128)(2,1)}, bf16[256,2048]{1,0:T(8,128)(2,1)}, u32[]{:S(2)}, u32[]{:S(2)}) %collective-permute-start.49) | collective-permute-done | bytes 1048608 | tf_op jit(solution)/shard_map/ppermute | solution.py:224
  712.1 38.6 %collective-permute-done.57 = bf16[256,2048]{1,0:T(8,128)(2,1)S(1)} collective-permute-done((bf16[256,2048]{1,0:T(8,128)(2,1)S(1)}, bf16[256,2048]{1,0:T(8,128)(2,1)S(1)}, u32[]{:S(2)}, u32[]{:S(2)}) %collective-permute-start.57) | collective-permute-done | bytes 1048608 | tf_op jit(solution)/shard_map/ppermute | solution.py:219
  752.9 5.1 add_convert_fusion.6
  767.4 42.5 %collective-permute-done.53.refs_3_ = bf16[2,3,512,256]{3,2,1,0:T(8,128)(2,1)S(1)} collective-permute-done((bf16[2,3,512,256]{3,2,1,0:T(8,128)(2,1)}, bf16[2,3,512,256]{3,2,1,0:T(8,128)(2,1)S(1)}, u32[]{:S(2)}, u32[]{:S(2)}) %collective-permute-start.53) | collective-permute-done | bytes 1572896 | tf_op jit(solution)/shard_map/ppermute | solution.py:219
  818.8 16.0 %collective-permute-done.54.refs_2_ = bf16[3,512,256]{2,1,0:T(8,128)(2,1)S(1)} collective-permute-done((bf16[3,512,256]{2,1,0:T(8,128)(2,1)S(1)}, bf16[3,512,256]{2,1,0:T(8,128)(2,1)S(1)}, u32[]{:S(2)}, u32[]{:S(2)}) %collective-permute-start.54) | collective-permute-done | bytes 786464 | tf_op jit(solution)/shard_map/ppermute | solution.py:219
  840.2 54.6 %collective-permute-done.50.refs_2_ = bf16[2,3,512,256]{3,2,1,0:T(8,128)(2,1)S(1)} collective-permute-done((bf16[2,3,512,256]{3,2,1,0:T(8,128)(2,1)}, bf16[2,3,512,256]{3,2,1,0:T(8,128)(2,1)S(1)}, u32[]{:S(2)}, u32[]{:S(2)}) %collective-permute-start.50) | collective-permute-done | bytes 1572896 | tf_op jit(solution)/shard_map/ppermute | solution.py:219
  901.5 18.9 %attend_back.1 = (f32[1024,512]{1,0:T(8,128)}, f32[1024,512]{1,0:T(8,128)}, bf16[1024,512]{1,0:T(8,128)(2,1)S(1)}, f32[1024,128]{1,0:T(8,128)S(1)}, f32[1024,128...) custom-call(bf16[1024,512]{1,0:T(8,128)(2,1)S(1)} %copy-done.57, bf16[1024,512]{1,0:T(8,128)(2,1)} %copy-done.58, ...), custom_call_target="tpu_custom_call" | custom-call | flops 10737418240 | bytes 15728640 | tf_op jit(solution)/shard_map/attend_back/pallas_call | solution.py:191
  920.4 13.9 %collective-permute-done.60.refs_2_ = bf16[3,512,256]{2,1,0:T(8,128)(2,1)S(1)} collective-permute-done((bf16[3,512,256]{2,1,0:T(8,128)(2,1)S(1)}, bf16[3,512,256]{2,1,0:T(8,128)(2,1)S(1)}, u32[]{:S(2)}, u32[]{:S(2)}) %collective-permute-start.60) | collective-permute-done | bytes 786464 | tf_op jit(solution)/shard_map/ppermute | solution.py:219
  942.3 13.3 %collective-permute-done.84 = bf16[128,2048]{1,0:T(8,128)(2,1)S(1)} collective-permute-done((bf16[128,2048]{1,0:T(8,128)(2,1)S(1)}, bf16[128,2048]{1,0:T(8,128)(2,1)S(1)}, u32[]{:S(2)}, u32[]{:S(2)}) %collective-permute-start.84) | collective-permute-done | bytes 524320 | tf_op jit(solution)/shard_map/ppermute | solution.py:224
  958.0 12.0 collective-permute-done.85
  972.7 4.7 convolution_convert_fusion.4
  980.8 8.3 collective-permute-done.86
  992.9 14.2 %collective-permute-done.63 = bf16[256,2048]{1,0:T(8,128)(2,1)} collective-permute-done((bf16[256,2048]{1,0:T(8,128)(2,1)}, bf16[256,2048]{1,0:T(8,128)(2,1)}, u32[]{:S(2)}, u32[]{:S(2)}) %collective-permute-start.63) | collective-permute-done | bytes 1048608 | tf_op jit(solution)/shard_map/ppermute | solution.py:224
  1009.8 9.1 convolution_convert_fusion
  1022.0 5.4 convolution_convert_fusion.2.last_ref
  1031.8 23.7 %collective-permute-done.74 = bf16[512,1024]{1,0:T(8,128)(2,1)S(1)} collective-permute-done((bf16[512,1024]{1,0:T(8,128)(2,1)S(1)}, bf16[512,1024]{1,0:T(8,128)(2,1)S(1)}, u32[]{:S(2)}, u32[]{:S(2)}) %collective-permute-start.74) | collective-permute-done | bytes 1048608 | tf_op jit(solution)/shard_map/ppermute | solution.py:224
  1057.9 8.8 collective-permute-done.78
  1066.9 22.3 %collective-permute-done.75 = bf16[512,1024]{1,0:T(8,128)(2,1)S(1)} collective-permute-done((bf16[512,1024]{1,0:T(8,128)(2,1)S(1)}, bf16[512,1024]{1,0:T(8,128)(2,1)S(1)}, u32[]{:S(2)}, u32[]{:S(2)}) %collective-permute-start.75) | collective-permute-done | bytes 1048608 | tf_op jit(solution)/shard_map/ppermute | solution.py:224
  1092.5 7.9 collective-permute-done.79
  1100.6 20.3 %collective-permute-done.68 = f32[4,20,128]{2,1,0:T(8,128)S(1)} collective-permute-done((f32[4,20,128]{2,1,0:T(8,128)S(1)}, f32[4,20,128]{2,1,0:T(8,128)S(1)}, u32[]{:S(2)}, u32[]{:S(2)}) %collective-permute-start.68) | collective-permute-done | bytes 40992 | tf_op jit(solution)/shard_map/ppermute | solution.py:224
  1121.4 5.4 collective-permute-done.69
  1140.7 22.1 %collective-permute-done.73 = f32[20,128]{1,0:T(8,128)S(1)} collective-permute-done((f32[20,128]{1,0:T(8,128)S(1)}, f32[20,128]{1,0:T(8,128)S(1)}, u32[]{:S(2)}, u32[]{:S(2)}) %collective-permute-start.73) | collective-permute-done | bytes 10272 | tf_op jit(solution)/shard_map/ppermute | solution.py:219
  1166.5 8.4 collective-permute-done.83
  1175.0 8.4 collective-permute-done.82
  1196.2 4.6 copy-done.4
  1200.8 10.9 place.4
  1211.7 4.6 copy-done.5
  1216.3 10.9 place.5
  1227.2 4.6 copy-done.6
  1231.8 10.9 place.6
  1242.7 4.6 copy-done.7
  1247.2 11.5 place.7
  (707 shorter events, 291.0 us)
Async XLA Ops:
  7.2 311.9 %all-gather.11.cloned.1.call-start = ((), (), s32[]{:S(2)}) async-start(), calls=%async_computation | async-start | bytes 5242880 | tf_op jit(solution)/shard_map/all_gather | solution.py:737
  16.3 19.4 %collective-permute-start.2 = (bf16[128,768]{0,1:T(8,128)(2,1)S(1)}, bf16[128,768]{0,1:T(8,128)(2,1)S(1)}, u32[]{:S(2)}, u32[]{:S(2)}) collective-permute-start(bf16[128,768]{0,1:T(8,128)(2,1)S(1)} %get-tuple-element.378), channel_id=1, source_target_pairs={{0,6},{2,4},{4,2},{6,0},{1,7},{3,5},{5,3},{7,1},{8,14},{10,12},{12... | collective-permute-start | bytes 589832 | tf_op jit(solution)/shard_map/ppermute | solution.py:219
  17.8 17.9 %collective-permute-start.1 = (bf16[128,768]{0,1:T(8,128)(2,1)S(1)}, bf16[128,768]{0,1:T(8,128)(2,1)S(1)}, u32[]{:S(2)}, u32[]{:S(2)}) collective-permute-start(bf16[128,768]{0,1:T(8,128)(2,1)S(1)} %get-tuple-element.379), channel_id=1, source_target_pairs={{0,4},{2,6},{4,0},{6,2},{1,5},{3,7},{5,1},{7,3},{8,12},{10,14},{12... | collective-permute-start | bytes 589832 | tf_op jit(solution)/shard_map/ppermute | solution.py:219
  38.3 18.4 %collective-permute-start.13 = (bf16[512,768]{1,0:T(8,128)(2,1)S(1)}, bf16[512,768]{1,0:T(8,128)(2,1)S(1)}, u32[]{:S(2)}, u32[]{:S(2)}) collective-permute-start(bf16[512,768]{1,0:T(8,128)(2,1)S(1)} %bitcast.312), channel_id=1, source_target_pairs={{0,8},{8,16},{16,24},{24,0},{1,9},{9,17},{17,25},{25,1},{2,10},{10... | collective-permute-start | bytes 2359304 | tf_op jit(solution)/shard_map/ppermute | solution.py:224
  38.4 18.3 %collective-permute-start.12 = (bf16[512,768]{1,0:T(8,128)(2,1)S(1)}, bf16[512,768]{1,0:T(8,128)(2,1)S(1)}, u32[]{:S(2)}, u32[]{:S(2)}) collective-permute-start(bf16[512,768]{1,0:T(8,128)(2,1)S(1)} %bitcast.313), channel_id=1, source_target_pairs={{0,1},{1,0},{2,3},{3,2},{4,5},{5,4},{6,7},{7,6},{8,9},{9,8},{10,11... | collective-permute-start | bytes 2359304 | tf_op jit(solution)/shard_map/ppermute | solution.py:219
  40.7 21.9 %collective-permute-start.7 = (bf16[256,2048]{1,0:T(8,128)(2,1)S(1)}, bf16[256,2048]{1,0:T(8,128)(2,1)S(1)}, u32[]{:S(2)}, u32[]{:S(2)}) collective-permute-start(bf16[256,2048]{1,0:T(8,128)(2,1)S(1)} %bitcast.295), channel_id=1, source_target_pairs={{0,4},{2,6},{4,0},{6,2},{1,5},{3,7},{5,1},{7,3},{8,12},{10,14},{12... | collective-permute-start | bytes 3145736 | tf_op jit(solution)/shard_map/ppermute | solution.py:219
  42.2 34.0 %collective-permute-start.6 = (bf16[256,2048]{1,0:T(8,128)(2,1)S(1)}, bf16[256,2048]{1,0:T(8,128)(2,1)S(1)}, u32[]{:S(2)}, u32[]{:S(2)}) collective-permute-start(bf16[256,2048]{1,0:T(8,128)(2,1)S(1)} %bitcast.296), channel_id=1, source_target_pairs={{0,2},{2,0},{4,6},{6,4},{1,3},{3,1},{5,7},{7,5},{8,10},{10,8},{12,... | collective-permute-start | bytes 3145736 | tf_op jit(solution)/shard_map/ppermute | solution.py:219
  74.2 17.9 %collective-permute-start.17 = (bf16[512,768]{1,0:T(8,128)(2,1)S(1)}, bf16[512,768]{1,0:T(8,128)(2,1)S(1)}, u32[]{:S(2)}, u32[]{:S(2)}) collective-permute-start(bf16[512,768]{1,0:T(8,128)(2,1)S(1)} %collective-permute-done.15), channel_id=1, source_target_pairs={{0,8},{8,16},{16,24},{24,0},{1,9},{9,17},{17,25},{25,1},{2,10},{10... | collective-permute-start | bytes 2359304 | tf_op jit(solution)/shard_map/ppermute | solution.py:224
  74.4 19.2 %collective-permute-start.16 = (bf16[512,768]{1,0:T(8,128)(2,1)S(1)}, bf16[512,768]{1,0:T(8,128)(2,1)S(1)}, u32[]{:S(2)}, u32[]{:S(2)}) collective-permute-start(bf16[512,768]{1,0:T(8,128)(2,1)S(1)} %collective-permute-done.15), channel_id=1, source_target_pairs={{0,1},{1,0},{2,3},{3,2},{4,5},{5,4},{6,7},{7,6},{8,9},{9,8},{10,11... | collective-permute-start | bytes 2359304 | tf_op jit(solution)/shard_map/ppermute | solution.py:219
  92.1 40.8 %collective-permute-start.21 = (bf16[128,2048]{1,0:T(8,128)(2,1)S(1)}, bf16[128,2048]{1,0:T(8,128)(2,1)S(1)}, u32[]{:S(2)}, u32[]{:S(2)}) collective-permute-start(bf16[128,2048]{1,0:T(8,128)(2,1)S(1)} %copy-done.113), channel_id=1, source_target_pairs={{0,8},{8,16},{16,24},{24,0},{1,9},{9,17},{17,25},{25,1},{2,10},{10... | collective-permute-start | bytes 1572872 | tf_op jit(solution)/shard_map/ppermute | solution.py:224
  149.2 31.0 %collective-permute-start.23 = (bf16[128,2048]{1,0:T(8,128)(2,1)}, bf16[128,2048]{1,0:T(8,128)(2,1)}, u32[]{:S(2)}, u32[]{:S(2)}) collective-permute-start(bf16[128,2048]{1,0:T(8,128)(2,1)} %collective-permute-done.22), channel_id=1, source_target_pairs={{0,8},{8,16},{16,24},{24,0},{1,9},{9,17},{17,25},{25,1},{2,10},{10... | collective-permute-start | bytes 1572872 | tf_op jit(solution)/shard_map/ppermute | solution.py:224
  190.2 1003.8 %all-gather.13.cloned.1.call-start = ((), (), s32[]{:S(2)}) async-start(), calls=%async_computation.1 | async-start | bytes 14155776 | tf_op jit(solution)/shard_map/all_gather | solution.py:570
  197.5 25.4 %collective-permute-start.25 = (bf16[256,2048]{1,0:T(8,128)(2,1)S(1)}, bf16[256,2048]{1,0:T(8,128)(2,1)}, u32[]{:S(2)}, u32[]{:S(2)}) collective-permute-start(bf16[256,2048]{1,0:T(8,128)(2,1)S(1)} %fusion.19), channel_id=1, source_target_pairs={{0,4},{2,6},{4,0},{6,2},{1,5},{3,7},{5,1},{7,3},{8,12},{10,14},{12... | collective-permute-start | bytes 3145736 | tf_op jit(solution)/shard_map/ppermute | solution.py:219
  227.8 49.9 %collective-permute-start.26 = (bf16[256,2048]{1,0:T(8,128)(2,1)S(1)}, bf16[256,2048]{1,0:T(8,128)(2,1)S(1)}, u32[]{:S(2)}, u32[]{:S(2)}) collective-permute-start(bf16[256,2048]{1,0:T(8,128)(2,1)S(1)} %multiply_convert_fusion.x_ref), channel_id=1, source_target_pairs={{0,8},{8,16},{16,24},{24,0},{1,9},{9,17},{17,25},{25,1},{2,10},{10... | collective-permute-start | bytes 3145736 | tf_op jit(solution)/shard_map/ppermute | solution.py:224
  277.7 41.0 %collective-permute-start.27 = (bf16[256,2048]{1,0:T(8,128)(2,1)S(1)}, bf16[256,2048]{1,0:T(8,128)(2,1)S(1)}, u32[]{:S(2)}, u32[]{:S(2)}) collective-permute-start(bf16[256,2048]{1,0:T(8,128)(2,1)S(1)} %collective-permute-done.26.x_ref), channel_id=1, source_target_pairs={{0,8},{8,16},{16,24},{24,0},{1,9},{9,17},{17,25},{25,1},{2,10},{10... | collective-permute-start | bytes 3145736 | tf_op jit(solution)/shard_map/ppermute | solution.py:224
  318.7 51.0 %collective-permute-start.29 = (bf16[256,2048]{1,0:T(8,128)(2,1)S(1)}, bf16[256,2048]{1,0:T(8,128)(2,1)S(1)}, u32[]{:S(2)}, u32[]{:S(2)}) collective-permute-start(bf16[256,2048]{1,0:T(8,128)(2,1)S(1)} %collective-permute-done.27), channel_id=1, source_target_pairs={{0,8},{8,16},{16,24},{24,0},{1,9},{9,17},{17,25},{25,1},{2,10},{10... | collective-permute-start | bytes 3145736 | tf_op jit(solution)/shard_map/ppermute | solution.py:224
  417.8 23.6 %collective-permute-start.32 = (bf16[2,4,3,512,256]{4,3,2,1,0:T(8,128)(2,1)}, bf16[2,4,3,512,256]{4,3,2,1,0:T(8,128)(2,1)}, u32[]{:S(2)}, u32[]{:S(2)}) collective-permute-start(bf16[2,4,3,512,256]{4,3,2,1,0:T(8,128)(2,1)} %get-tuple-element.192), channel_id=1, source_target_pairs={{0,2},{2,0},{4,6},{6,4},{1,3},{3,1},{5,7},{7,5},{8,10},{10,8},{12,... | collective-permute-start | bytes 18874376 | tf_op jit(solution)/shard_map/ppermute | solution.py:219
  474.5 49.3 %collective-permute-start.37 = (bf16[2,4,3,512,256]{4,3,2,1,0:T(8,128)(2,1)}, bf16[2,4,3,512,256]{4,3,2,1,0:T(8,128)(2,1)S(1)}, u32[]{:S(2)}, u32[]{:S(2)}) collective-permute-start(bf16[2,4,3,512,256]{4,3,2,1,0:T(8,128)(2,1)} %get-tuple-element.202), channel_id=1, source_target_pairs={{0,2},{2,0},{4,6},{6,4},{1,3},{3,1},{5,7},{7,5},{8,10},{10,8},{12,... | collective-permute-start | bytes 18874376 | tf_op jit(solution)/shard_map/ppermute | solution.py:219
  475.5 36.7 %collective-permute-start.33 = (bf16[2,3,512,256]{3,2,1,0:T(8,128)(2,1)}, bf16[2,3,512,256]{3,2,1,0:T(8,128)(2,1)}, u32[]{:S(2)}, u32[]{:S(2)}) collective-permute-start(bf16[2,3,512,256]{3,2,1,0:T(8,128)(2,1)} %copy-done.53), channel_id=1, source_target_pairs={{0,1},{1,0},{2,3},{3,2},{4,5},{5,4},{6,7},{7,6},{8,9},{9,8},{10,11... | collective-permute-start | bytes 4718600 | tf_op jit(solution)/shard_map/ppermute | solution.py:219
  477.0 36.4 %collective-permute-start.34 = (bf16[2,3,512,256]{3,2,1,0:T(8,128)(2,1)}, bf16[2,3,512,256]{3,2,1,0:T(8,128)(2,1)}, u32[]{:S(2)}, u32[]{:S(2)}) collective-permute-start(bf16[2,3,512,256]{3,2,1,0:T(8,128)(2,1)} %copy-done.52), channel_id=1, source_target_pairs={{0,4},{2,6},{4,0},{6,2},{1,5},{3,7},{5,1},{7,3},{8,12},{10,14},{12... | collective-permute-start | bytes 4718600 | tf_op jit(solution)/shard_map/ppermute | solution.py:219
  521.8 32.0 %collective-permute-start.35 = (bf16[3,512,256]{2,1,0:T(8,128)(2,1)}, bf16[3,512,256]{2,1,0:T(8,128)(2,1)}, u32[]{:S(2)}, u32[]{:S(2)}) collective-permute-start(bf16[3,512,256]{2,1,0:T(8,128)(2,1)} %get-tuple-element.211.refs_2_), channel_id=1, source_target_pairs={{0,4},{2,6},{4,0},{6,2},{1,5},{3,7},{5,1},{7,3},{8,12},{10,14},{12... | collective-permute-start | bytes 2359304 | tf_op jit(solution)/shard_map/ppermute | solution.py:219
  523.3 30.5 %collective-permute-start.36 = (bf16[3,512,256]{2,1,0:T(8,128)(2,1)}, bf16[3,512,256]{2,1,0:T(8,128)(2,1)}, u32[]{:S(2)}, u32[]{:S(2)}) collective-permute-start(bf16[3,512,256]{2,1,0:T(8,128)(2,1)} %get-tuple-element.212), channel_id=1, source_target_pairs={{0,1},{1,0},{2,3},{3,2},{4,5},{5,4},{6,7},{7,6},{8,9},{9,8},{10,11... | collective-permute-start | bytes 2359304 | tf_op jit(solution)/shard_map/ppermute | solution.py:219
  560.5 651.2 %all-gather.15.cloned.1.call-start = ((), (), s32[]{:S(2)}) async-start(), calls=%async_computation.2 | async-start | bytes 14155776 | tf_op jit(solution)/shard_map/all_gather | solution.py:570
  560.5 79.1 %collective-permute-start.38 = (bf16[2,4,3,512,256]{4,3,2,1,0:T(8,128)(2,1)}, bf16[2,4,3,512,256]{4,3,2,1,0:T(8,128)(2,1)}, u32[]{:S(2)}, u32[]{:S(2)}) collective-permute-start(bf16[2,4,3,512,256]{4,3,2,1,0:T(8,128)(2,1)} %get-tuple-element.225.refs_4_), channel_id=1, source_target_pairs={{0,2},{2,0},{4,6},{6,4},{1,3},{3,1},{5,7},{7,5},{8,10},{10,8},{12,... | collective-permute-start | bytes 18874376 | tf_op jit(solution)/shard_map/ppermute | solution.py:219
  565.8 83.6 %collective-permute-start.41 = (bf16[256,2048]{1,0:T(8,128)(2,1)}, bf16[256,2048]{1,0:T(8,128)(2,1)}, u32[]{:S(2)}, u32[]{:S(2)}) collective-permute-start(bf16[256,2048]{1,0:T(8,128)(2,1)} %add_convert_fusion.15), channel_id=1, source_target_pairs={{0,8},{8,16},{16,24},{24,0},{1,9},{9,17},{17,25},{25,1},{2,10},{10... | collective-permute-start | bytes 3145736 | tf_op jit(solution)/shard_map/ppermute | solution.py:224
  567.2 110.3 %collective-permute-start.45 = (f32[4,256]{0,1:T(8,128)}, f32[4,256]{0,1:T(8,128)}, u32[]{:S(2)}, u32[]{:S(2)}) collective-permute-start(f32[4,256]{0,1:T(8,128)} %fusion.43), channel_id=1, source_target_pairs={{0,24},{8,0},{16,8},{24,16},{1,25},{9,1},{17,9},{25,17},{2,26},{10... | collective-permute-start | bytes 12296 | tf_op jit(solution)/shard_map/ppermute | solution.py:224
  572.3 60.1 %collective-permute-start.39 = (bf16[2,3,512,256]{3,2,1,0:T(8,128)(2,1)S(1)}, bf16[2,3,512,256]{3,2,1,0:T(8,128)(2,1)S(1)}, u32[]{:S(2)}, u32[]{:S(2)}) collective-permute-start(bf16[2,3,512,256]{3,2,1,0:T(8,128)(2,1)S(1)} %copy-done.48), channel_id=1, source_target_pairs={{0,1},{1,0},{2,3},{3,2},{4,5},{5,4},{6,7},{7,6},{8,9},{9,8},{10,11... | collective-permute-start | bytes 4718600 | tf_op jit(solution)/shard_map/ppermute | solution.py:219
  573.7 59.8 %collective-permute-start.40 = (bf16[2,3,512,256]{3,2,1,0:T(8,128)(2,1)S(1)}, bf16[2,3,512,256]{3,2,1,0:T(8,128)(2,1)S(1)}, u32[]{:S(2)}, u32[]{:S(2)}) collective-permute-start(bf16[2,3,512,256]{3,2,1,0:T(8,128)(2,1)S(1)} %copy-done.46), channel_id=1, source_target_pairs={{0,4},{2,6},{4,0},{6,2},{1,5},{3,7},{5,1},{7,3},{8,12},{10,14},{12... | collective-permute-start | bytes 4718600 | tf_op jit(solution)/shard_map/ppermute | solution.py:219
  632.4 46.3 %collective-permute-start.47 = (f32[4,256]{0,1:T(8,128)}, f32[4,256]{0,1:T(8,128)S(1)}, u32[]{:S(2)}, u32[]{:S(2)}) collective-permute-start(f32[4,256]{0,1:T(8,128)} %fusion.41), channel_id=1, source_target_pairs={{0,8},{8,16},{16,24},{24,0},{1,9},{9,17},{17,25},{25,1},{2,10},{10... | collective-permute-start | bytes 12296 | tf_op jit(solution)/shard_map/ppermute | solution.py:224
  633.5 45.2 %collective-permute-start.46 = (f32[4,256]{0,1:T(8,128)}, f32[4,256]{0,1:T(8,128)}, u32[]{:S(2)}, u32[]{:S(2)}) collective-permute-start(f32[4,256]{0,1:T(8,128)} %fusion.42), channel_id=1, source_target_pairs={{0,16},{8,24},{16,0},{24,8},{1,17},{9,25},{17,1},{25,9},{2,18},{10... | collective-permute-start | bytes 12296 | tf_op jit(solution)/shard_map/ppermute | solution.py:224
  651.0 24.9 %collective-permute-start.48 = (bf16[256,2048]{1,0:T(8,128)(2,1)S(1)}, bf16[256,2048]{1,0:T(8,128)(2,1)S(1)}, u32[]{:S(2)}, u32[]{:S(2)}) collective-permute-start(bf16[256,2048]{1,0:T(8,128)(2,1)S(1)} %add_convert_fusion.14), channel_id=1, source_target_pairs={{0,8},{8,16},{16,24},{24,0},{1,9},{9,17},{17,25},{25,1},{2,10},{10... | collective-permute-start | bytes 3145736 | tf_op jit(solution)/shard_map/ppermute | solution.py:224
  677.3 24.3 %collective-permute-start.49 = (bf16[256,2048]{1,0:T(8,128)(2,1)}, bf16[256,2048]{1,0:T(8,128)(2,1)}, u32[]{:S(2)}, u32[]{:S(2)}) collective-permute-start(bf16[256,2048]{1,0:T(8,128)(2,1)} %add_convert_fusion.11), channel_id=1, source_target_pairs={{0,8},{8,16},{16,24},{24,0},{1,9},{9,17},{17,25},{25,1},{2,10},{10... | collective-permute-start | bytes 3145736 | tf_op jit(solution)/shard_map/ppermute | solution.py:224
  680.6 25.4 %collective-permute-start.43 = (bf16[3,512,256]{2,1,0:T(8,128)(2,1)}, bf16[3,512,256]{2,1,0:T(8,128)(2,1)S(1)}, u32[]{:S(2)}, u32[]{:S(2)}) collective-permute-start(bf16[3,512,256]{2,1,0:T(8,128)(2,1)} %get-tuple-element.233.refs_2_), channel_id=1, source_target_pairs={{0,4},{2,6},{4,0},{6,2},{1,5},{3,7},{5,1},{7,3},{8,12},{10,14},{12... | collective-permute-start | bytes 2359304 | tf_op jit(solution)/shard_map/ppermute | solution.py:219
  681.5 24.4 %collective-permute-start.44 = (bf16[3,512,256]{2,1,0:T(8,128)(2,1)}, bf16[3,512,256]{2,1,0:T(8,128)(2,1)S(1)}, u32[]{:S(2)}, u32[]{:S(2)}) collective-permute-start(bf16[3,512,256]{2,1,0:T(8,128)(2,1)} %get-tuple-element.246), channel_id=1, source_target_pairs={{0,1},{1,0},{2,3},{3,2},{4,5},{5,4},{6,7},{7,6},{8,9},{9,8},{10,11... | collective-permute-start | bytes 2359304 | tf_op jit(solution)/shard_map/ppermute | solution.py:219
  708.0 519.2 %all-gather.17.cloned.1.call-start = ((), (), s32[]{:S(2)}) async-start(), calls=%async_computation.3 | async-start | bytes 14155776 | tf_op jit(solution)/shard_map/all_gather | solution.py:570
  708.1 52.2 %collective-permute-start.42 = (bf16[2,4,3,512,256]{4,3,2,1,0:T(8,128)(2,1)}, bf16[2,4,3,512,256]{4,3,2,1,0:T(8,128)(2,1)S(1)}, u32[]{:S(2)}, u32[]{:S(2)}) collective-permute-start(bf16[2,4,3,512,256]{4,3,2,1,0:T(8,128)(2,1)} %get-tuple-element.243), channel_id=1, source_target_pairs={{0,2},{2,0},{4,6},{6,4},{1,3},{3,1},{5,7},{7,5},{8,10},{10,8},{12,... | collective-permute-start | bytes 18874376 | tf_op jit(solution)/shard_map/ppermute | solution.py:219
  708.2 42.5 %collective-permute-start.57 = (bf16[256,2048]{1,0:T(8,128)(2,1)S(1)}, bf16[256,2048]{1,0:T(8,128)(2,1)S(1)}, u32[]{:S(2)}, u32[]{:S(2)}) collective-permute-start(bf16[256,2048]{1,0:T(8,128)(2,1)S(1)} %get-tuple-element.260.refs_4_), channel_id=1, source_target_pairs={{0,4},{2,6},{4,0},{6,2},{1,5},{3,7},{5,1},{7,3},{8,12},{10,14},{12... | collective-permute-start | bytes 3145736 | tf_op jit(solution)/shard_map/ppermute | solution.py:219
  709.1 43.6 %collective-permute-start.56 = (bf16[256,2048]{1,0:T(8,128)(2,1)S(1)}, bf16[256,2048]{1,0:T(8,128)(2,1)S(1)}, u32[]{:S(2)}, u32[]{:S(2)}) collective-permute-start(bf16[256,2048]{1,0:T(8,128)(2,1)S(1)} %get-tuple-element.260.refs_4_), channel_id=1, source_target_pairs={{0,2},{2,0},{4,6},{6,4},{1,3},{3,1},{5,7},{7,5},{8,10},{10,8},{12,... | collective-permute-start | bytes 3145736 | tf_op jit(solution)/shard_map/ppermute | solution.py:219
  709.3 58.1 %collective-permute-start.52 = (bf16[2,3,512,256]{3,2,1,0:T(8,128)(2,1)}, bf16[2,3,512,256]{3,2,1,0:T(8,128)(2,1)S(1)}, u32[]{:S(2)}, u32[]{:S(2)}) collective-permute-start(bf16[2,3,512,256]{3,2,1,0:T(8,128)(2,1)} %copy-done.50), channel_id=1, source_target_pairs={{0,1},{1,0},{2,3},{3,2},{4,5},{5,4},{6,7},{7,6},{8,9},{9,8},{10,11... | collective-permute-start | bytes 4718600 | tf_op jit(solution)/shard_map/ppermute | solution.py:219
  710.6 99.2 %collective-permute-start.53 = (bf16[2,3,512,256]{3,2,1,0:T(8,128)(2,1)}, bf16[2,3,512,256]{3,2,1,0:T(8,128)(2,1)S(1)}, u32[]{:S(2)}, u32[]{:S(2)}) collective-permute-start(bf16[2,3,512,256]{3,2,1,0:T(8,128)(2,1)} %copy-done.49), channel_id=1, source_target_pairs={{0,4},{2,6},{4,0},{6,2},{1,5},{3,7},{5,1},{7,3},{8,12},{10,14},{12... | collective-permute-start | bytes 4718600 | tf_op jit(solution)/shard_map/ppermute | solution.py:219
  752.8 61.1 %collective-permute-start.59 = (bf16[256,2048]{1,0:T(8,128)(2,1)S(1)}, bf16[256,2048]{1,0:T(8,128)(2,1)}, u32[]{:S(2)}, u32[]{:S(2)}) collective-permute-start(bf16[256,2048]{1,0:T(8,128)(2,1)S(1)} %add_convert_fusion.8), channel_id=1, source_target_pairs={{0,8},{8,16},{16,24},{24,0},{1,9},{9,17},{17,25},{25,1},{2,10},{10... | collective-permute-start | bytes 3145736 | tf_op jit(solution)/shard_map/ppermute | solution.py:224
  811.3 23.5 %collective-permute-start.54 = (bf16[3,512,256]{2,1,0:T(8,128)(2,1)S(1)}, bf16[3,512,256]{2,1,0:T(8,128)(2,1)S(1)}, u32[]{:S(2)}, u32[]{:S(2)}) collective-permute-start(bf16[3,512,256]{2,1,0:T(8,128)(2,1)S(1)} %get-tuple-element.270), channel_id=1, source_target_pairs={{0,4},{2,6},{4,0},{6,2},{1,5},{3,7},{5,1},{7,3},{8,12},{10,14},{12... | collective-permute-start | bytes 2359304 | tf_op jit(solution)/shard_map/ppermute | solution.py:219
  812.9 22.0 %collective-permute-start.55 = (bf16[3,512,256]{2,1,0:T(8,128)(2,1)S(1)}, bf16[3,512,256]{2,1,0:T(8,128)(2,1)S(1)}, u32[]{:S(2)}, u32[]{:S(2)}) collective-permute-start(bf16[3,512,256]{2,1,0:T(8,128)(2,1)S(1)} %get-tuple-element.271), channel_id=1, source_target_pairs={{0,1},{1,0},{2,3},{3,2},{4,5},{5,4},{6,7},{7,6},{8,9},{9,8},{10,11... | collective-permute-start | bytes 2359304 | tf_op jit(solution)/shard_map/ppermute | solution.py:219
  837.9 404.8 %all-gather.19.cloned.1.call-start = ((), (), s32[]{:S(2)}) async-start(), calls=%async_computation.4 | async-start | bytes 14155776 | tf_op jit(solution)/shard_map/all_gather | solution.py:570
  837.9 56.9 %collective-permute-start.50 = (bf16[2,3,512,256]{3,2,1,0:T(8,128)(2,1)}, bf16[2,3,512,256]{3,2,1,0:T(8,128)(2,1)S(1)}, u32[]{:S(2)}, u32[]{:S(2)}) collective-permute-start(bf16[2,3,512,256]{3,2,1,0:T(8,128)(2,1)} %copy-done.31), channel_id=1, source_target_pairs={{0,1},{1,0},{2,3},{3,2},{4,5},{5,4},{6,7},{7,6},{8,9},{9,8},{10,11... | collective-permute-start | bytes 4718600 | tf_op jit(solution)/shard_map/ppermute | solution.py:219
  839.7 57.9 %collective-permute-start.51 = (bf16[2,3,512,256]{3,2,1,0:T(8,128)(2,1)}, bf16[2,3,512,256]{3,2,1,0:T(8,128)(2,1)S(1)}, u32[]{:S(2)}, u32[]{:S(2)}) collective-permute-start(bf16[2,3,512,256]{3,2,1,0:T(8,128)(2,1)} %copy-done.51), channel_id=1, source_target_pairs={{0,4},{2,6},{4,0},{6,2},{1,5},{3,7},{5,1},{7,3},{8,12},{10,14},{12... | collective-permute-start | bytes 4718600 | tf_op jit(solution)/shard_map/ppermute | solution.py:219
  840.2 59.9 %collective-permute-start.62 = (bf16[256,2048]{1,0:T(8,128)(2,1)}, bf16[256,2048]{1,0:T(8,128)(2,1)S(1)}, u32[]{:S(2)}, u32[]{:S(2)}) collective-permute-start(bf16[256,2048]{1,0:T(8,128)(2,1)} %add_convert_fusion.7), channel_id=1, source_target_pairs={{0,8},{8,16},{16,24},{24,0},{1,9},{9,17},{17,25},{25,1},{2,10},{10... | collective-permute-start | bytes 3145736 | tf_op jit(solution)/shard_map/ppermute | solution.py:224
  899.2 35.1 %collective-permute-start.60 = (bf16[3,512,256]{2,1,0:T(8,128)(2,1)S(1)}, bf16[3,512,256]{2,1,0:T(8,128)(2,1)S(1)}, u32[]{:S(2)}, u32[]{:S(2)}) collective-permute-start(bf16[3,512,256]{2,1,0:T(8,128)(2,1)S(1)} %get-tuple-element.276), channel_id=1, source_target_pairs={{0,4},{2,6},{4,0},{6,2},{1,5},{3,7},{5,1},{7,3},{8,12},{10,14},{12... | collective-permute-start | bytes 2359304 | tf_op jit(solution)/shard_map/ppermute | solution.py:219
  900.1 34.8 %collective-permute-start.61 = (bf16[3,512,256]{2,1,0:T(8,128)(2,1)S(1)}, bf16[3,512,256]{2,1,0:T(8,128)(2,1)S(1)}, u32[]{:S(2)}, u32[]{:S(2)}) collective-permute-start(bf16[3,512,256]{2,1,0:T(8,128)(2,1)S(1)} %get-tuple-element.277), channel_id=1, source_target_pairs={{0,1},{1,0},{2,3},{3,2},{4,5},{5,4},{6,7},{7,6},{8,9},{9,8},{10,11... | collective-permute-start | bytes 2359304 | tf_op jit(solution)/shard_map/ppermute | solution.py:219
  972.1 35.0 %collective-permute-start.63 = (bf16[256,2048]{1,0:T(8,128)(2,1)}, bf16[256,2048]{1,0:T(8,128)(2,1)}, u32[]{:S(2)}, u32[]{:S(2)}) collective-permute-start(bf16[256,2048]{1,0:T(8,128)(2,1)} %add_convert_fusion.5), channel_id=1, source_target_pairs={{0,8},{8,16},{16,24},{24,0},{1,9},{9,17},{17,25},{25,1},{2,10},{10... | collective-permute-start | bytes 3145736 | tf_op jit(solution)/shard_map/ppermute | solution.py:224
  978.2 49.5 %collective-permute-start.77 = (bf16[512,512]{1,0:T(8,128)(2,1)}, bf16[512,512]{1,0:T(8,128)(2,1)}, u32[]{:S(2)}, u32[]{:S(2)}) collective-permute-start(bf16[512,512]{1,0:T(8,128)(2,1)} %unstack.47), channel_id=1, source_target_pairs={{0,8},{8,16},{16,24},{24,0},{1,9},{9,17},{17,25},{25,1},{2,10},{10... | collective-permute-start | bytes 1572872 | tf_op jit(solution)/shard_map/ppermute | solution.py:224
  991.2 141.7 %collective-permute-start.87 = (bf16[128,2048]{1,0:T(8,128)(2,1)}, bf16[128,2048]{1,0:T(8,128)(2,1)}, u32[]{:S(2)}, u32[]{:S(2)}) collective-permute-start(bf16[128,2048]{1,0:T(8,128)(2,1)} %fusion.28), channel_id=1, source_target_pairs={{0,1},{1,0},{2,3},{3,2},{4,5},{5,4},{6,7},{7,6},{8,9},{9,8},{10,11... | collective-permute-start | bytes 1572872 | tf_op jit(solution)/shard_map/ppermute | solution.py:219
  1019.4 36.6 %collective-permute-start.66 = (bf16[2,256,2048]{2,1,0:T(8,128)(2,1)S(1)}, bf16[2,256,2048]{2,1,0:T(8,128)(2,1)S(1)}, u32[]{:S(2)}, u32[]{:S(2)}) collective-permute-start(bf16[2,256,2048]{2,1,0:T(8,128)(2,1)S(1)} %pad_maximum_fusion.9), channel_id=1, source_target_pairs={{0,2},{2,0},{4,6},{6,4},{1,3},{3,1},{5,7},{7,5},{8,10},{10,8},{12,... | collective-permute-start | bytes 6291464 | tf_op jit(solution)/shard_map/ppermute | solution.py:219
  1027.5 27.9 %collective-permute-start.74 = (bf16[512,1024]{1,0:T(8,128)(2,1)S(1)}, bf16[512,1024]{1,0:T(8,128)(2,1)S(1)}, u32[]{:S(2)}, u32[]{:S(2)}) collective-permute-start(bf16[512,1024]{1,0:T(8,128)(2,1)S(1)} %unstack.43), channel_id=1, source_target_pairs={{0,8},{8,16},{16,24},{24,0},{1,9},{9,17},{17,25},{25,1},{2,10},{10... | collective-permute-start | bytes 3145736 | tf_op jit(solution)/shard_map/ppermute | solution.py:224
  1031.7 35.0 %collective-permute-start.78 = (bf16[512,512]{1,0:T(8,128)(2,1)S(1)}, bf16[512,512]{1,0:T(8,128)(2,1)S(1)}, u32[]{:S(2)}, u32[]{:S(2)}) collective-permute-start(bf16[512,512]{1,0:T(8,128)(2,1)S(1)} %add_convert_fusion.22), channel_id=1, source_target_pairs={{0,8},{8,16},{16,24},{24,0},{1,9},{9,17},{17,25},{25,1},{2,10},{10... | collective-permute-start | bytes 1572872 | tf_op jit(solution)/shard_map/ppermute | solution.py:224
  1055.9 33.3 %collective-permute-start.75 = (bf16[512,1024]{1,0:T(8,128)(2,1)S(1)}, bf16[512,1024]{1,0:T(8,128)(2,1)S(1)}, u32[]{:S(2)}, u32[]{:S(2)}) collective-permute-start(bf16[512,1024]{1,0:T(8,128)(2,1)S(1)} %add_convert_fusion.2), channel_id=1, source_target_pairs={{0,8},{8,16},{16,24},{24,0},{1,9},{9,17},{17,25},{25,1},{2,10},{10... | collective-permute-start | bytes 3145736 | tf_op jit(solution)/shard_map/ppermute | solution.py:224
  1056.4 33.3 %collective-permute-start.67 = (bf16[256,2048]{1,0:T(8,128)(2,1)S(1)}, bf16[256,2048]{1,0:T(8,128)(2,1)S(1)}, u32[]{:S(2)}, u32[]{:S(2)}) collective-permute-start(bf16[256,2048]{1,0:T(8,128)(2,1)S(1)} %fusion.17), channel_id=1, source_target_pairs={{0,4},{2,6},{4,0},{6,2},{1,5},{3,7},{5,1},{7,3},{8,12},{10,14},{12... | collective-permute-start | bytes 3145736 | tf_op jit(solution)/shard_map/ppermute | solution.py:219
  1066.9 33.6 %collective-permute-start.79 = (bf16[512,512]{1,0:T(8,128)(2,1)S(1)}, bf16[512,512]{1,0:T(8,128)(2,1)S(1)}, u32[]{:S(2)}, u32[]{:S(2)}) collective-permute-start(bf16[512,512]{1,0:T(8,128)(2,1)S(1)} %add_convert_fusion.21), channel_id=1, source_target_pairs={{0,8},{8,16},{16,24},{24,0},{1,9},{9,17},{17,25},{25,1},{2,10},{10... | collective-permute-start | bytes 1572872 | tf_op jit(solution)/shard_map/ppermute | solution.py:224
  1089.6 31.4 %collective-permute-start.76 = (bf16[512,1024]{1,0:T(8,128)(2,1)S(1)}, bf16[512,1024]{1,0:T(8,128)(2,1)S(1)}, u32[]{:S(2)}, u32[]{:S(2)}) collective-permute-start(bf16[512,1024]{1,0:T(8,128)(2,1)S(1)} %add_convert_fusion.1), channel_id=1, source_target_pairs={{0,8},{8,16},{16,24},{24,0},{1,9},{9,17},{17,25},{25,1},{2,10},{10... | collective-permute-start | bytes 3145736 | tf_op jit(solution)/shard_map/ppermute | solution.py:224
  1092.2 28.7 %collective-permute-start.68 = (f32[4,20,128]{2,1,0:T(8,128)S(1)}, f32[4,20,128]{2,1,0:T(8,128)S(1)}, u32[]{:S(2)}, u32[]{:S(2)}) collective-permute-start(f32[4,20,128]{2,1,0:T(8,128)S(1)} %dynamic-slice_bitcast_fusion.7), channel_id=1, source_target_pairs={{0,8},{8,16},{16,24},{24,0},{1,9},{9,17},{17,25},{25,1},{2,10},{10... | collective-permute-start | bytes 122888 | tf_op jit(solution)/shard_map/ppermute | solution.py:224
  1130.2 32.5 %collective-permute-start.80 = (bf16[4,128,3,2,256]{4,1,3,2,0:T(8,128)(2,1)S(1)}, bf16[4,128,3,2,256]{4,1,3,2,0:T(8,128)(2,1)S(1)}, u32[]{:S(2)}, u32[]{:S(2)}) collective-permute-start(bf16[4,128,3,2,256]{4,1,3,2,0:T(8,128)(2,1)S(1)} %copy.247), channel_id=1, source_target_pairs={{0,1},{1,0},{2,3},{3,2},{4,5},{5,4},{6,7},{7,6},{8,9},{9,8},{10,11... | collective-permute-start | bytes 4718600 | tf_op jit(solution)/shard_map/ppermute | solution.py:219
  1139.0 23.7 %collective-permute-start.73 = (f32[20,128]{1,0:T(8,128)S(1)}, f32[20,128]{1,0:T(8,128)S(1)}, u32[]{:S(2)}, u32[]{:S(2)}) collective-permute-start(f32[20,128]{1,0:T(8,128)S(1)} %fusion.50), channel_id=1, source_target_pairs={{0,1},{1,0},{2,3},{3,2},{4,5},{5,4},{6,7},{7,6},{8,9},{9,8},{10,11... | collective-permute-start | bytes 30728 | tf_op jit(solution)/shard_map/ppermute | solution.py:219
  1163.6 19.8 %collective-permute-start.82 = (bf16[128,3,2,256]{3,0,2,1:T(8,128)(2,1)S(1)}, bf16[128,3,2,256]{3,0,2,1:T(8,128)(2,1)S(1)}, u32[]{:S(2)}, u32[]{:S(2)}) collective-permute-start(bf16[128,3,2,256]{3,0,2,1:T(8,128)(2,1)S(1)} %get-tuple-element.370), channel_id=1, source_target_pairs={{0,4},{2,6},{4,0},{6,2},{1,5},{3,7},{5,1},{7,3},{8,12},{10,14},{12... | collective-permute-start | bytes 1179656 | tf_op jit(solution)/shard_map/ppermute | solution.py:219
  1165.0 18.3 %collective-permute-start.81 = (bf16[128,3,2,256]{3,0,2,1:T(8,128)(2,1)S(1)}, bf16[128,3,2,256]{3,0,2,1:T(8,128)(2,1)S(1)}, u32[]{:S(2)}, u32[]{:S(2)}) collective-permute-start(bf16[128,3,2,256]{3,0,2,1:T(8,128)(2,1)S(1)} %get-tuple-element.369), channel_id=1, source_target_pairs={{0,2},{2,0},{4,6},{6,4},{1,3},{3,1},{5,7},{7,5},{8,10},{10,8},{12,... | collective-permute-start | bytes 1179656 | tf_op jit(solution)/shard_map/ppermute | solution.py:219
  (184 other events, 2490.7 us)
Sparse Core Ops, SparseCore 0:
  190.3 104.8 all-gather.10
  560.6 98.3 all-gather.12
  708.1 116.5 all-gather.14
  838.0 106.9 all-gather.16
  946.7 79.5 all-gather.18

commit v3 on v2

--- a/solution.py
+++ b/solution.py
@@ -12,7 +12,6 @@
 HDIM = 128
 CHUNK = 256
 ROWS = 1024
-PIECES = 4
 
 epsilon = 1e-06
 rope_base = 10000.0
@@ -37,24 +36,34 @@
 
 FIRST = (("dp", 1), ("context", 2))
 SECOND = (("context", 2), ("dp", 1))
+PIECES = 4
+
+
+def nothing_of(values, dtype):
+    return (values[(0,) * values.ndim].astype(F32) * 0.0).astype(dtype)
+
+
+def after(values, *others):
+    for other in others:
+        values = values + nothing_of(other, values.dtype)
+    return values
+
+
+ANYWHERE = pl.BlockSpec(memory_space=pl.ANY)
+TOKEN = jax.ShapeDtypeStruct((8, 128), F32)
+
+
+def token_spec():
+    return pl.BlockSpec((8, 128), lambda *_: (0, 0))
 
 
 class Order:
     def __init__(self):
-        self.last = None
-
-    def tie(self, values):
-        if self.last is None:
-            return values
-        return lax.optimization_barrier((values, self.last))[0]
-
-    def did(self, result):
-        self.last = result
-
-    def run(self, step, first, *rest):
-        result = step(self.tie(first), *rest)
-        self.did(result)
-        return result
+        self.token = jnp.zeros((8, 128), F32)
+
+    def run(self, call, *args):
+        *results, self.token = call(self.token, *args)
+        return results
 
 
 def rms_factor(values):
@@ -75,9 +84,9 @@
 
 
 def attend_kernel(
-    q_ref, k_ref, v_ref, fq_ref, fk_ref, gq_ref, gk_ref, cos_ref, sin_ref,
-    ql_ref, kl_ref, vl_ref, mixed_ref, logsum_ref,
+    q_ref, k_ref, v_ref, fq_ref, fk_ref, gq_ref, gk_ref, cos_ref, sin_ref, *refs
 ):
+    ql_ref, kl_ref, vl_ref, mixed_ref, logsum_ref = refs[-5:]
     length = q_ref.shape[0]
     block = min(256, length)
     cosine, sine = cos_ref[...], sin_ref[...]
@@ -101,8 +110,10 @@
 
 def attend_back_kernel(
     ql_ref, kl_ref, vl_ref, grad_ref, logsum_ref, q_ref, k_ref, fq_ref, fk_ref, gq_ref, gk_ref,
-    cos_ref, sin_ref, qb_ref, kb_ref, vg_ref, qs_ref, ks_ref, qg_ref, kg_ref, k_acc, v_acc, q_acc,
+    cos_ref, sin_ref, _, qb_ref, kb_ref, vg_ref, qs_ref, ks_ref, qg_ref, kg_ref, token_ref,
+    k_acc, v_acc, q_acc,
 ):
+    token_ref[...] = jnp.zeros_like(token_ref)
     length = ql_ref.shape[0]
     block = min(256, length)
     scale = HDIM ** (-0.5)
@@ -153,7 +164,7 @@
     }
 
 
-def attend(qkv, fq, fk, gq, gk, cosine, sine):
+def attend(qkv, fq, fk, gq, gk, cosine, sine, before):
     length, heads = qkv.shape[0], gq.shape[0]
     spec = head_specs(length)
 
@@ -165,20 +176,21 @@
         attend_kernel,
         grid=(heads,),
         in_specs=[part(0), part(1), part(2)]
-        + [spec[n] for n in ("column", "column", "gain", "gain", "whole", "whole")],
+        + [spec[n] for n in ("column", "column", "gain", "gain", "whole", "whole")]
+        + [ANYWHERE] * len(before),
         out_specs=[spec["head"]] * 4 + [spec["row"]],
         out_shape=[low] * 4 + [jax.ShapeDtypeStruct((heads, 1, length), F32)],
-        compiler_params=pltpu.CompilerParams(vmem_limit_bytes=40 * MIB),
+        compiler_params=pltpu.CompilerParams(vmem_limit_bytes=60 * MIB),
         cost_estimate=pl.CostEstimate(
             flops=10 * heads * length * length * HDIM,
             bytes_accessed=20 * length * heads * HDIM,
             transcendentals=heads * length * length,
         ),
         name="attend",
-    )(qkv, qkv, qkv, fq, fk, gq, gk, cosine, sine)
-
-
-def attend_back(ql, kl, vl, grad, logsum, qkv, fq, fk, gq, gk, cosine, sine):
+    )(qkv, qkv, qkv, fq, fk, gq, gk, cosine, sine, *before)
+
+
+def attend_back(token, ql, kl, vl, grad, logsum, qkv, fq, fk, gq, gk, cosine, sine):
     length, heads = qkv.shape[0], gq.shape[0]
     spec = head_specs(length)
 
@@ -193,8 +205,9 @@
         grid=(heads,),
         in_specs=[spec["head"]] * 4
         + [spec["row"], part(0), part(1)]
-        + [spec[n] for n in ("column", "column", "gain", "gain", "whole", "whole")],
-        out_specs=[spec["head"]] * 3 + [spec["whole"]] * 2 + [spec["gain"]] * 2,
+        + [spec[n] for n in ("column", "column", "gain", "gain", "whole", "whole")]
+        + [ANYWHERE],
+        out_specs=[spec["head"]] * 3 + [spec["whole"]] * 2 + [spec["gain"]] * 2 + [token_spec()],
         out_shape=[
             shape(F32, length, heads * HDIM),
             shape(F32, length, heads * HDIM),
@@ -203,16 +216,17 @@
             shape(F32, length, HDIM),
             shape(F32, heads, 1, HDIM),
             shape(F32, heads, 1, HDIM),
+            TOKEN,
         ],
         scratch_shapes=[pltpu.VMEM((length, HDIM), F32)] * 3,
-        compiler_params=pltpu.CompilerParams(vmem_limit_bytes=48 * MIB),
+        compiler_params=pltpu.CompilerParams(vmem_limit_bytes=60 * MIB),
         cost_estimate=pl.CostEstimate(
             flops=20 * heads * length * length * HDIM,
             bytes_accessed=30 * length * heads * HDIM,
             transcendentals=heads * length * length,
         ),
         name="attend_back",
-    )(ql, kl, vl, grad, logsum, qkv, qkv, fq, fk, gq, gk, cosine, sine)
+    )(ql, kl, vl, grad, logsum, qkv, qkv, fq, fk, gq, gk, cosine, sine, token)
 
 
 def swap(values, axis, bit):
@@ -250,12 +264,8 @@
     return held
 
 
-def ring_sum(blocks, combine):
-    n = len(blocks)
-    total = blocks[1 % n]
-    for s in range(2, n + 1):
-        total = combine(blocks[s % n], shift(total, 1))
-    return total
+def ring_direct(own):
+    return [own] + [shift(own, s) for s in range(1, lax.axis_size("expert"))]
 
 
 def take(blocks, index):
@@ -272,23 +282,28 @@
     wg_ref,
     wu_ref,
     wd_ref,
-    out_ref,
-    row_ref,
-    gate_ref,
-    weights_ref,
-    turned_ref,
-    both_ref,
-    hidden_ref,
-    out_acc,
-    row_acc,
-    lanes,
-    both_w,
+    *refs,
 ):
+    (
+        out_ref,
+        row_ref,
+        gate_ref,
+        weights_ref,
+        turned_ref,
+        both_ref,
+        hidden_ref,
+        token_ref,
+        out_acc,
+        row_acc,
+        lanes,
+        both_w,
+    ) = refs[-12:]
     e, step = pl.program_id(0), pl.program_id(1)
     start = jnp.logical_and(e == 0, step == 0)
     rows, width = x_ref.shape
     chunk = wg_ref.shape[1]
     lane = lax.broadcasted_iota(jnp.int32, (rows, 128), 1)
+    token_ref[...] = jnp.zeros_like(token_ref)
 
     @pl.when(start)
     def _():
@@ -340,7 +355,7 @@
         row_ref[...] = row_acc[...].astype(BF16)
 
 
-def run_rows(at, first, count, x, u, mask, router, w_gate, w_up, w_down):
+def run_rows(token, at, first, count, x, u, mask, router, w_gate, w_up, w_down, *ready):
     rows, width = x.shape
     ff = w_gate.shape[2]
     steps = ff // CHUNK
@@ -363,7 +378,8 @@
                 pl.BlockSpec((None, width, CHUNK), lambda e, s, a: (first + e, 0, s)),
                 pl.BlockSpec((None, width, CHUNK), lambda e, s, a: (first + e, 0, s)),
                 pl.BlockSpec((None, CHUNK, width), lambda e, s, a: (first + e, s, 0)),
-            ],
+            ]
+            + [ANYWHERE] * (1 + len(ready)),
             out_specs=[
                 whole((rows, width)),
                 whole((rows, width)),
@@ -372,6 +388,7 @@
                 whole((width, rows)),
                 pl.BlockSpec((None, None, rows, 2 * CHUNK), lambda e, s, a: (e, s, 0, 0)),
                 pl.BlockSpec((None, None, rows, CHUNK), lambda e, s, a: (e, s, 0, 0)),
+                token_spec(),
             ],
             scratch_shapes=[
                 pltpu.VMEM((rows, width), F32),
@@ -388,6 +405,7 @@
             jax.ShapeDtypeStruct((width, rows), BF16),
             jax.ShapeDtypeStruct((count, steps, rows, 2 * CHUNK), BF16),
             jax.ShapeDtypeStruct((count, steps, rows, CHUNK), BF16),
+            TOKEN,
         ],
         compiler_params=pltpu.CompilerParams(vmem_limit_bytes=56 * MIB),
         cost_estimate=pl.CostEstimate(
@@ -396,14 +414,130 @@
             transcendentals=rows * ff * count,
         ),
         name="rows",
-    )(at, x, u, mask, router, w_gate, w_up, w_down)
-
-
-def grads_kernel(sizes, bits_ref, *refs):
+    )(at, x, u, mask, router, w_gate, w_up, w_down, token, *ready)
+
+
+def grads_kernel(sizes, *refs):
     n = len(sizes)
     turned, ups, boths, hiddens = (refs[i * n : (i + 1) * n] for i in range(4))
-    send_ref, keep_ref, x_all, u_all, both, hidden = refs[4 * n :]
-    step, steps = pl.program_id(0), pl.num_programs(0)
+    gate_ref, up_ref, down_ref, token_ref, x_all, u_all, both, hidden = refs[-8:]
+    token_ref[...] = jnp.zeros_like(token_ref)
+    width, chunk = x_all.shape[0], hidden.shape[1]
+
+    spans, at = [], 0
+    for size in sizes:
+        spans.append(slice(at, at + size))
+        at += size
+
+    @pl.when(pl.program_id(0) == 0)
+    def _():
+        for span, t, u in zip(spans, turned, ups):
+            x_all[:, span] = t[...]
+            u_all[span, :] = u[...]
+
+    for span, b, h in zip(spans, boths, hiddens):
+        both[span, :] = b[...]
+        hidden[span, :] = h[...]
+    hidden_turned = hidden[...].T
+    piece = width // 4
+    for p in range(4):
+        r = slice(p * piece, (p + 1) * piece)
+        got = dot(x_all[r, :], both[...], (1, 0)).astype(BF16)
+        gate_ref[r, :] = got[:, :chunk]
+        up_ref[r, :] = got[:, chunk:]
+        down_ref[:, r] = dot(hidden_turned, u_all[:, r], (1, 0)).astype(BF16)
+
+
+def run_grads(token, segments):
+    turned, ups, boths, hiddens, places = zip(*segments)
+    width = turned[0].shape[0]
+    sizes = tuple(u.shape[0] for u in ups)
+    total = sum(sizes)
+    steps = boths[0].shape[1]
+
+    def whole(shape):
+        return pl.BlockSpec(shape, lambda s: (0, 0), pipeline_mode=pl.Buffered(1))
+
+    def chunked(size, columns, place):
+        return pl.BlockSpec((None, None, size, columns), lambda s: (place, s, 0, 0))
+
+    return pl.pallas_call(
+        functools.partial(grads_kernel, sizes),
+        grid=(steps,),
+        in_specs=[whole((width, size)) for size in sizes]
+        + [whole((size, width)) for size in sizes]
+        + [chunked(size, 2 * CHUNK, p) for size, p in zip(sizes, places)]
+        + [chunked(size, CHUNK, p) for size, p in zip(sizes, places)]
+        + [ANYWHERE],
+        out_specs=[
+            pl.BlockSpec((width, CHUNK), lambda s: (0, s)),
+            pl.BlockSpec((width, CHUNK), lambda s: (0, s)),
+            pl.BlockSpec((CHUNK, width), lambda s: (s, 0)),
+            token_spec(),
+        ],
+        out_shape=[
+            jax.ShapeDtypeStruct((width, steps * CHUNK), BF16),
+            jax.ShapeDtypeStruct((width, steps * CHUNK), BF16),
+            jax.ShapeDtypeStruct((steps * CHUNK, width), BF16),
+            TOKEN,
+        ],
+        scratch_shapes=[
+            pltpu.VMEM((width, total), BF16),
+            pltpu.VMEM((total, width), BF16),
+            pltpu.VMEM((total, 2 * CHUNK), BF16),
+            pltpu.VMEM((total, CHUNK), BF16),
+        ],
+        compiler_params=pltpu.CompilerParams(vmem_limit_bytes=56 * MIB),
+        cost_estimate=pl.CostEstimate(
+            flops=6 * total * width * steps * CHUNK,
+            bytes_accessed=6 * width * steps * CHUNK + 8 * total * width,
+            transcendentals=0,
+        ),
+        name="grads",
+    )(*turned, *ups, *boths, *hiddens, token)
+
+
+def place_kernel(*refs):
+    outs, token_ref = refs[-4:-1], refs[-1]
+    token_ref[...] = jnp.zeros_like(token_ref)
+    for low, out in zip(refs[:3], outs):
+        out[...] = low[...].astype(F32)
+
+
+def place_grads(token, e, summed, outs, shapes):
+    steps = 8
+
+    def cut(shape):
+        return pl.BlockSpec((shape[0] // steps, shape[1]), lambda i: (i, 0))
+
+    def cut_out(shape):
+        return pl.BlockSpec((None, shape[1] // steps, shape[2]), lambda i: (e, i, 0))
+
+    held = [] if outs is None else list(outs[:3])
+    return pl.pallas_call(
+        place_kernel,
+        grid=(steps,),
+        in_specs=[cut(v.shape) for v in summed] + [ANYWHERE] * (1 + len(held)),
+        out_specs=[cut_out(s) for s in shapes] + [token_spec()],
+        out_shape=[jax.ShapeDtypeStruct(s, F32) for s in shapes] + [TOKEN],
+        input_output_aliases={4 + i: i for i in range(len(held))},
+        compiler_params=pltpu.CompilerParams(vmem_limit_bytes=60 * MIB),
+        cost_estimate=pl.CostEstimate(
+            flops=0,
+            bytes_accessed=6 * sum(math.prod(v.shape) for v in summed),
+            transcendentals=0,
+        ),
+        name="place",
+    )(*summed, token, *held)
+
+
+def split_kernel(sizes, bits_ref, *refs):
+    n = len(sizes)
+    turned, ups, boths, hiddens = (refs[i * n : (i + 1) * n] for i in range(4))
+    sends = refs[4 * n + 1 : 4 * n + 5]
+    keep_ref, token_ref, x_all, u_all, both, hidden = refs[4 * n + 5 :]
+    token_ref[...] = jnp.zeros_like(token_ref)
+    step = pl.program_id(0)
     width = x_all.shape[0]
     chunk = hidden.shape[1]
 
@@ -424,28 +558,31 @@
     hidden_turned = hidden[...].T
     piece_rows = width // PIECES
 
-    def store(ref):
-        mask = jnp.where(step % 2 == 0, bits_ref[1], bits_ref[2])
-        for p in range(PIECES):
-            place = p ^ mask
-            r = slice(p * piece_rows, (p + 1) * piece_rows)
+    def store(mask, place_of):
+        for place in range(PIECES):
+            ref = place_of(place)
+            p = place ^ mask
+            r = pl.ds(pl.multiple_of(p * piece_rows, piece_rows), piece_rows)
             got = dot(x_all[r, :], both[...], (1, 0)).astype(BF16)
-            ref[place, 0] = got[:, :chunk]
-            ref[place, 1] = got[:, chunk:]
+            ref[0] = got[:, :chunk]
+            ref[1] = got[:, chunk:]
             down = dot(hidden_turned, u_all[:, r], (1, 0)).astype(BF16)
             for j in range(piece_rows // chunk):
-                ref[place, 2, j * chunk : (j + 1) * chunk, :] = down[:, j * chunk : (j + 1) * chunk]
-
-    @pl.when(step < steps // 2)
+                ref[2, j * chunk : (j + 1) * chunk, :] = down[:, j * chunk : (j + 1) * chunk]
+
+    def sent(path):
+        store(bits_ref[1 + path], lambda place: sends[path * 2 + place // 2].at[place % 2])
+
+    pl.when(step == 0)(functools.partial(sent, 0))
+    pl.when(step == 1)(functools.partial(sent, 1))
+
+    @pl.when(step >= 2)
     def _():
-        store(send_ref.at[0])
-
-    @pl.when(step >= steps // 2)
-    def _():
-        store(keep_ref.at[0])
-
-
-def run_grads(bits, segments):
+        mask = jnp.where(step % 2 == 0, bits_ref[1], bits_ref[2])
+        store(mask, lambda place: keep_ref.at[0, place])
+
+
+def run_split(token, segments, bits):
     turned, ups, boths, hiddens, places = zip(*segments)
     width = turned[0].shape[0]
     sizes = tuple(u.shape[0] for u in ups)
@@ -466,19 +603,25 @@
         )
 
     grads = (1, PIECES, 3, piece_rows, CHUNK)
+    away = (PIECES // 2,) + grads[2:]
     grads_out = jax.ShapeDtypeStruct((half,) + grads[1:], BF16)
     return pl.pallas_call(
-        functools.partial(grads_kernel, sizes),
+        functools.partial(split_kernel, sizes),
         grid_spec=pltpu.PrefetchScalarGridSpec(
             num_scalar_prefetch=1,
             grid=(steps,),
             in_specs=[whole((width, size)) for size in sizes]
             + [whole((size, width)) for size in sizes]
             + [chunked(size, 2 * CHUNK, p) for size, p in zip(sizes, places)]
-            + [chunked(size, CHUNK, p) for size, p in zip(sizes, places)],
+            + [chunked(size, CHUNK, p) for size, p in zip(sizes, places)]
+            + [ANYWHERE],
             out_specs=[
-                pl.BlockSpec(grads, lambda s, b: (jnp.minimum(s, half - 1), 0, 0, 0, 0)),
+                pl.BlockSpec(away, lambda s, b: (0, 0, 0, 0), pipeline_mode=pl.Buffered(1))
+                for _ in range(4)
+            ]
+            + [
                 pl.BlockSpec(grads, lambda s, b: (jnp.maximum(s - half, 0), 0, 0, 0, 0)),
+                token_spec(),
             ],
             scratch_shapes=[
                 pltpu.VMEM((width, total), BF16),
@@ -487,18 +630,20 @@
                 pltpu.VMEM((total, CHUNK), BF16),
             ],
         ),
-        out_shape=[grads_out, grads_out],
+        out_shape=[jax.ShapeDtypeStruct(away, BF16)] * 4 + [grads_out, TOKEN],
         compiler_params=pltpu.CompilerParams(vmem_limit_bytes=56 * MIB),
         cost_estimate=pl.CostEstimate(
             flops=6 * total * width * steps * CHUNK,
             bytes_accessed=6 * width * steps * CHUNK + 8 * total * width,
             transcendentals=0,
         ),
-        name="grads",
-    )(bits, *turned, *ups, *boths, *hiddens)
+        name="split",
+    )(bits, *turned, *ups, *boths, *hiddens, token)
 
 
 def add_kernel(picks, joined, *refs):
+    *refs, token_ref = refs
+    token_ref[...] = jnp.zeros_like(token_ref)
     outs = [refs[-1].at[i] for i in range(len(picks))] if joined else refs[-len(picks) :]
 
     def at(ref, index):
@@ -509,7 +654,7 @@
         out[...] = (left.astype(F32) + right.astype(F32)).astype(BF16)
 
 
-def add_pieces(picks, shapes, ins, last, joined=False):
+def add_pieces(token, picks, shapes, ins, joined=False):
 
     parts = 4
 
@@ -521,38 +666,36 @@
     return pl.pallas_call(
         functools.partial(add_kernel, picks, joined),
         grid=(parts,),
-        in_specs=[cut(i.shape) for i in ins] + [pl.BlockSpec(memory_space=pl.ANY)],
-        out_specs=[cut(s) for s in shapes],
-        out_shape=[jax.ShapeDtypeStruct(s, BF16) for s in shapes],
-        compiler_params=pltpu.CompilerParams(vmem_limit_bytes=32 * MIB),
+        in_specs=[cut(i.shape) for i in ins] + [ANYWHERE],
+        out_specs=[cut(s) for s in shapes] + [token_spec()],
+        out_shape=[jax.ShapeDtypeStruct(s, BF16) for s in shapes] + [TOKEN],
+        compiler_params=pltpu.CompilerParams(vmem_limit_bytes=60 * MIB),
         cost_estimate=pl.CostEstimate(flops=moved, bytes_accessed=2 * moved, transcendentals=0),
         name="add_pieces",
-    )(*ins, last)
+    )(*ins, token)
 
 
 class Summed:
-    def __init__(self, order, send, keep):
+    def __init__(self, order, sends, keep):
         self.order, self.keep = order, keep
         self.ahead = ["halves", "quarters", "finals"]
-        self.got = swap(send, "context", 1)
+        self.got = [swap(sends[i], "context", 1) for i in (1, 3, 0, 2)]
 
     def reach(self, name):
         while name in self.ahead:
             getattr(self, self.ahead.pop(0))()
 
     def add(self, picks, shapes, ins, joined=False):
-        outs = add_pieces(picks, shapes, ins, self.order.last, joined)
-        self.order.did(outs[0])
-        return outs
+        return self.order.run(add_pieces, picks, shapes, ins, joined)
 
     def halves(self):
         shape = (2,) + self.keep.shape[2:]
         picks = [
-            [(0, (path, slice(at, at + 2))), (1, (path, slice(at, at + 2)))]
-            for at in (2, 0)
+            [(0, (path, slice(at, at + 2))), (1 + i * 2 + path, None)]
+            for i, at in enumerate((2, 0))
             for path in range(2)
         ]
-        outs = self.add(picks, [shape] * 4, [self.keep, self.got])
+        outs = self.add(picks, [shape] * 4, [self.keep, *self.got])
         self.coming = [swap(outs[path], *FIRST[path]) for path in range(2)]
         self.kept = outs[2:]
 
@@ -570,9 +713,9 @@
         self.all = lax.all_gather(own, ("context", "dp"), axis=0)
 
 
-def place_kernel(e, first, last_ref, *refs):
+def place_pieces_kernel(e, first, *refs):
     source = refs[0]
-    outs = refs[1:4] if first else refs[4:7]
+    outs = refs[2:5] if first else refs[5:8]
     token_ref, low, wide, in_sem, out_sem = refs[-5:]
     rows = low.shape[2]
     count = 2 * source.shape[0]
@@ -628,29 +771,58 @@
             copy.wait()
 
 
-def place_grads(e, gathered, last, outs, shapes):
+def place_pieces(token, e, gathered, outs, shapes):
     first = outs is None
     rows = gathered.shape[3]
-    anywhere = pl.BlockSpec(memory_space=pl.ANY)
-    operands = [last, gathered] + ([] if first else list(outs[:3]))
+    operands = [gathered, token] + ([] if first else list(outs[:3]))
     return pl.pallas_call(
-        functools.partial(place_kernel, e, first),
-        in_specs=[anywhere] * len(operands),
-        out_specs=[anywhere] * 3 + [pl.BlockSpec((8, 128), lambda: (0, 0))],
+        functools.partial(place_pieces_kernel, e, first),
+        in_specs=[ANYWHERE] * len(operands),
+        out_specs=[ANYWHERE] * 3 + [token_spec()],
         scratch_shapes=[
             pltpu.VMEM((2, 3, rows, CHUNK), BF16),
             pltpu.VMEM((2, 3, rows, CHUNK), F32),
             pltpu.SemaphoreType.DMA((2,)),
             pltpu.SemaphoreType.DMA((2, 2 + rows // CHUNK)),
         ],
-        out_shape=[jax.ShapeDtypeStruct(s, F32) for s in (*shapes, (8, 128))],
+        out_shape=[jax.ShapeDtypeStruct(s, F32) for s in shapes] + [TOKEN],
         input_output_aliases={} if first else {2: 0, 3: 1, 4: 2},
-        compiler_params=pltpu.CompilerParams(vmem_limit_bytes=16 * MIB),
+        compiler_params=pltpu.CompilerParams(vmem_limit_bytes=60 * MIB),
         cost_estimate=pl.CostEstimate(
             flops=0, bytes_accessed=16 * 9 * rows * CHUNK * 2, transcendentals=0
         ),
-        name="place",
+        name="place_pieces",
     )(*operands)
+
+
+def hop_kernel(*refs):
+    *parts, got, _, out_ref, token_ref = refs
+    token_ref[...] = jnp.zeros_like(token_ref)
+    total = parts[0][...].astype(F32)
+    for part in parts[1:]:
+        total = total + part[...].astype(F32)
+    out_ref[...] = (total + got[...].astype(F32)).astype(BF16)
+
+
+def hop_add(token, parts, got):
+    rows, width = got.shape
+    half = rows // 2
+
+    def at(place):
+        return pl.BlockSpec((half, width), lambda i: (2 * place + i, 0))
+
+    return pl.pallas_call(
+        hop_kernel,
+        grid=(2,),
+        in_specs=[at(p) for _, p in parts] + [at(0), ANYWHERE],
+        out_specs=[at(0), token_spec()],
+        out_shape=[jax.ShapeDtypeStruct((rows, width), BF16), TOKEN],
+        compiler_params=pltpu.CompilerParams(vmem_limit_bytes=60 * MIB),
+        cost_estimate=pl.CostEstimate(
+            flops=rows * width * 5, bytes_accessed=14 * rows * width, transcendentals=0
+        ),
+        name="hop",
+    )(*(a for a, _ in parts), got, token)
 
 
 def body(
@@ -702,16 +874,14 @@
     )
     small = [small] + [swap(small, "context", s) for s in range(1, context)]
     small = take(jnp.stack(small), members)
-    hidden_all = lax.optimization_barrier((hidden_in[0], half_w, small))[0]
+    hidden_all = after(hidden_in[0], half_w)
     hidden_all = jnp.concatenate(context_gather(hidden_all), axis=0)
-    small = take(jnp.stack(ring_gather(small)), ring)
+    small = take(jnp.stack(ring_direct(small)), ring)
     small_all = small.transpose(2, 0, 1, 3).reshape(4 + experts_all, width)
     halves, others = [half_w], [swap(half_w, "dp", 1)]
     for s in range(1, groups):
-        before = lax.optimization_barrier((halves[-1], others[s - 2]))[0] if s > 1 else half_w
-        halves.append(shift(before, 1))
+        halves.append(shift(halves[-1], 1))
         others.append(swap(halves[-1], "dp", 1))
-    routes_ring = ring_gather(lax.optimization_barrier((routes[0], halves[-1]))[0])
     some = local // 2
     qkv_w = jnp.concatenate(
         [
@@ -724,17 +894,10 @@
     )
     heads = [my_dp * 2, my_dp * 2 + 1, (1 - my_dp) * 2, (1 - my_dp) * 2 + 1]
     whole_heads = rows == HDIM
+    routes_ring = ring_direct(after(routes[0], halves[1 % groups]))
     if whole_heads:
-        held = lax.optimization_barrier((w_out, halves[-1]))[0]
-        held = jnp.stack(ring_gather(held))
-        out_w = take(held, [(my_group - h) % groups for h in heads]).reshape(local, width)
-    else:
-        out_w = lax.all_gather(w_out, ("expert", "context"), axis=0, tiled=True)
-        out_w = out_w.reshape(per, context, HDIM, width)
-        out_w = lax.dynamic_index_in_dim(out_w, my_context, 1, keepdims=False)
-        out_w = take(out_w, heads).reshape(local, width)
-    upstream_all = lax.optimization_barrier((out_grad[0], halves[-1]))[0]
-    upstream_all = lax.all_gather(upstream_all, "expert", axis=0)
+        out_all = lax.all_gather(after(w_out, halves[-1]), "expert", axis=0)
+    upstream_all = lax.all_gather(after(out_grad[0], halves[-1]), "expert", axis=0)
 
     gain_attn = small_all[0].astype(F32)
     gain_ffn = small_all[3].astype(F32)
@@ -758,7 +921,7 @@
     normed = to_ring((source_all * factor_all * gain_attn).astype(BF16))
     source = hidden_in[0].astype(F32)
     factor_one = rms_factor(source)
-    qkv = dot(normed, qkv_w, (1, 0))
+    qkv = dot(normed, after(qkv_w, *routes_ring[1:]), (1, 0))
 
     def slots(query, key):
         return jnp.stack([v.reshape(context, tokens) for v in (query, key)])
@@ -766,8 +929,8 @@
     def per_row(values):
         return values.reshape(length)[:, None]
 
-    squares = jnp.sum(jnp.square(qkv[:, : 2 * local]).reshape(length, 2, local), axis=-1)
-    squares = context_total(slots(squares[:, 0], squares[:, 1]))
+    squares = [jnp.sum(jnp.square(qkv[:, i * local : (i + 1) * local]), axis=-1) for i in range(2)]
+    squares = context_total(slots(*squares))
     factors = lax.rsqrt(squares / width + epsilon)
     factor_query, factor_key = per_row(factors[0]), per_row(factors[1])
     starts = jnp.stack([m * tokens for m in members])
@@ -778,44 +941,53 @@
     sine_part = jnp.sin(angles)
     sine_part = jnp.concatenate([-sine_part, sine_part], axis=1)
     turn = (factor_query, factor_key, gain_query[:, None], gain_key[:, None], cosine, sine_part)
-    query_low, key_low, value_low, mixed_low, logsum = attend(qkv, *turn)
+    query_low, key_low, value_low, mixed_low, logsum = attend(qkv, *turn, [])
+    if whole_heads:
+        out_w = take(out_all, heads).reshape(local, width)
+    else:
+        out_w = lax.all_gather(w_out, ("expert", "context"), axis=0, tiled=True)
+        out_w = out_w.reshape(per, context, HDIM, width)
+        out_w = lax.dynamic_index_in_dim(out_w, my_context, 1, keepdims=False)
+        out_w = take(out_w, heads).reshape(local, width)
+    ids = jnp.arange(128, dtype=jnp.int32)
+    masks = [jnp.any(r[:, :, None] == ids, axis=1).astype(F32) for r in routes_ring]
     mixed_out = dot(mixed_low, out_w, (1, 0)).astype(BF16).reshape(context, tokens, width)
     residual = source + context_sum([mixed_out[s] for s in range(context)])
     factor_two = rms_factor(residual)
     normed_two = (residual * factor_two * gain_ffn).astype(BF16)
 
-    ids = jnp.arange(128, dtype=jnp.int32)
-    masks = [jnp.any(r[:, :, None] == ids, axis=1).astype(F32) for r in routes_ring]
     at = jnp.reshape(my_group * local_experts, (1,)).astype(jnp.int32)
     order = Order()
 
-    def upstream_of(slot):
-        return lax.dynamic_index_in_dim(order.tie(upstream_all), ring[slot], 0, keepdims=False)
-
-    def rows_of(first, count, x, u, mask):
-        result = run_rows(order.tie(at), first, count, x, u, mask, router_wide, w_gate, w_up, w_down)
-        order.did(result[0])
-        return result
+    def rows_of(first, count, x, u, mask, *ready):
+        return order.run(
+            run_rows, at, first, count, x, u, mask, router_wide, w_gate, w_up, w_down, *ready
+        )
 
     near = [[(0, local_experts)], [(0, local_experts)]]
     if local_experts == 4:
         near = [[(0, 2), (2, 2)]] * 2
-    blocks = [normed_two, shift(normed_two, 1)]
+    blocks = ring_gather(normed_two)
     segments = [([0], []), ([1], [])]
+
     ups = [out_grad[0]]
+
+    def upstream_of(slot):
+        m = ring[slot] + order.token[0, 0].astype(jnp.int32)
+        return lax.dynamic_index_in_dim(upstream_all, m, 0, keepdims=False)
+
+    def near_rows(slot, i):
+        first, count = near[slot][i]
+        ready = [upstream_all] if (slot, i) == (0, 1) else []
+        result = rows_of(first, count, blocks[slot], ups[slot], masks[slot], *ready)
+        segments[slot][1].append((first, count, result))
+
     for slot in range(2):
         if slot == 1:
             ups.append(upstream_of(1))
-        for i, (first, count) in enumerate(near[slot]):
-            result = rows_of(first, count, blocks[slot], ups[slot], masks[slot])
-            segments[slot][1].append((first, count, result))
-            if slot == 0 or i == 0:
-                if len(blocks) < groups:
-                    held = order.tie(blocks[-1])
-                    order.did(held)
-                    blocks.append(shift(held, 1))
-    while len(blocks) < groups:
-        blocks.append(shift(blocks[-1], 1))
+        for i in range(len(near[slot])):
+            if (slot, i) != (1, 1):
+                near_rows(slot, i)
     far = []
     for slot in range(2, groups, 2):
         pair = [slot, slot + 1]
@@ -838,47 +1010,52 @@
 
     summed = []
 
-    def advance(events):
+    def sum_grads():
+        e = len(summed)
+        if e == local_experts:
+            return
+        call = functools.partial(run_split, bits=bits) if e else run_grads
+        bunches = [[0, 1, 2]] + [[s, s + 1] for s in range(3, len(segments), 2)]
+        results = []
+        for bunch in bunches:
+            bunch = [segment_of(s, e) for s in bunch if s < len(segments)]
+            results.append(order.run(call, bunch))
+        grads = [
+            total_low(list(terms)) if len(terms) > 1 else terms[0] for terms in zip(*results)
+        ]
+        if e:
+            summed.append(Summed(order, grads[:4], grads[4]))
+        else:
+            summed.append(lax.psum(grads, ("context", "dp")))
+
+    def advance(*events):
         for e, name in events:
-            if e < len(summed):
+            if e < local_experts:
                 summed[e].reach(name)
 
-    during = {
-        1: ([(0, "halves")], []),
-        2: ([(0, "quarters"), (1, "halves")], [(0, "finals")]),
-        3: ([(1, "quarters"), (2, "halves")], []),
-    }
-
-    def total_of(slot, index):
+    def parts_of(slot, index):
         for pair, calls in segments:
             if slot in pair:
-                at_row = pair.index(slot) * tokens
-                parts = [result[index][at_row : at_row + tokens] for _, _, result in calls]
-                return total_low(parts)
+                return [(result[index], pair.index(slot)) for _, _, result in calls]
 
     def hop(index, total, slot):
-        term = total_of(slot % groups, index)
-        return order.run(add_low, term, shift(total, 1))
-
-    row_total = total_of(1, 1)
+        return order.run(hop_add, parts_of(slot % groups, index), shift(total, 1))[0]
+
+    def first_hop(index):
+        return total_low([r[p * tokens : (p + 1) * tokens] for r, p in parts_of(1, index)])
+
     for e in range(local_experts):
         for i, (x, u, mask) in enumerate(far):
             segments[2 + i][1].append((e, 1, rows_of(e, 1, x, u, mask)))
-        advance(during.get(e, ([], []))[0])
-        if e == local_experts - 1:
-            row_total = hop(1, row_total, 2)
-        bunches = [[0, 1, 2]] + [[s, s + 1] for s in range(3, len(segments), 2)]
-        results = []
-        for bunch in bunches:
-            got = run_grads(order.tie(bits), [segment_of(s, e) for s in bunch if s < len(segments)])
-            order.did(got[0])
-            results.append(got)
-        send, keep = (
-            total_low([r[i] for r in results]) if len(results) > 1 else results[0][i]
-            for i in range(2)
-        )
-        summed.append(Summed(order, send, keep))
-        advance(during.get(e, ([], []))[1])
+        if e < 2:
+            sum_grads()
+        if e == 0 and len(near[1]) > 1:
+            near_rows(1, 1)
+        if e == 2:
+            advance((1, "halves"))
+    row_total = hop(1, first_hop(1), 2)
+    sum_grads()
+    advance((1, "quarters"))
 
     gate_grad = [
         functools.reduce(
@@ -893,13 +1070,26 @@
     gate_grad = take(gate_grad, [(g - my_group) % groups for g in range(groups)])
     gate_grad = gate_grad.reshape(experts_all, tokens).T
 
-    events = [
-        [],
-    ]
     for slot in range(3, groups + 1):
         row_total = hop(1, row_total, slot)
-        advance(events[slot - 3] if slot - 3 < len(events) else [])
+        if slot == 3:
+            sum_grads()
+            advance((1, "finals"), (2, "halves"))
     row_back = row_total.astype(F32)
+    shapes = (w_gate.shape, w_up.shape, w_down.shape)
+    expert_grads = None
+
+    def place(experts):
+        outs = expert_grads
+        for e in experts:
+            if e < local_experts:
+                if e:
+                    summed[e].reach("finals")
+                    outs = order.run(place_pieces, e, summed[e].all, outs, shapes)
+                else:
+                    outs = order.run(place_grads, e, summed[e], outs, shapes)
+        return outs
+
 
     upstream = out_grad[0].astype(F32)
     weights_own = segments[0][1][0][2][3][:, :experts_all]
@@ -910,42 +1100,22 @@
     residual_part, ffn_gain_grad = norm_back(normed_two_grad, residual, factor_two, gain_ffn)
     residual_grad = upstream + residual_part
 
-    attn_grad = order.tie(residual_grad.astype(BF16))
-    order.did(attn_grad)
-    attn_grad = context_gather(attn_grad)
-    advance([(1, "finals"), (3, "halves"), (2, "quarters")])
-    out_total = hop(0, total_of(1, 0), 2)
-    attn_grad = order.tie(jnp.concatenate(attn_grad, axis=0))
-    order.did(attn_grad)
-    out_w_grad = dot(mixed_low, attn_grad, (0, 0)).astype(BF16).reshape(per, HDIM, width)
+    attn_grad = context_gather(residual_grad.astype(BF16))
+    out_total = hop(0, first_hop(0), 2)
+    attn_grad = jnp.concatenate(attn_grad, axis=0)
     mixed_grad = dot(attn_grad, out_w, (1, 1)).astype(BF16)
-    order.did(mixed_grad)
-    advance([(2, "finals"), (3, "quarters")])
-    out_total = hop(0, out_total, 3) if groups > 2 else out_total
-    mixed_grad = order.tie(mixed_grad)
-    query_back, key_back, value_grad, query_sum, key_sum, q_gain_grad, k_gain_grad = attend_back(
-        query_low, key_low, value_low, mixed_grad, logsum, qkv, *turn
+    query_back, key_back, value_grad, query_sum, key_sum, q_gain_grad, k_gain_grad = order.run(
+        attend_back, query_low, key_low, value_low, mixed_grad, logsum, qkv, *turn
     )
-    order.did(value_grad)
-    value_w_grad = dot(normed, value_grad, (0, 0)).astype(BF16)
-    value_w_grad = ring_sum(list(value_w_grad.reshape(groups, context * rows, local)), add_low)
+    out_w_grad = dot(mixed_low, after(attn_grad, order.token), (0, 0)).astype(BF16)
+    for slot in range(3, groups):
+        out_total = hop(0, out_total, slot)
     sums = context_total(slots(jnp.sum(query_sum, axis=1), jnp.sum(key_sum, axis=1))) / width
-    advance([(3, "finals")])
-    for slot in range(4, groups + 1):
-        out_total = hop(0, out_total, slot)
+    order.token = after(order.token, sums)
+    advance((2, "quarters"), (3, "halves"))
+    if groups > 2:
+        out_total = hop(0, out_total, groups)
     hidden_out = (residual + out_total.astype(F32)).astype(BF16)[None]
-    shapes = (w_gate.shape, w_up.shape, w_down.shape)
-    expert_grads = None
-
-    def place(experts):
-        outs = expert_grads
-        for e in experts:
-            if e < local_experts:
-                summed[e].reach("finals")
-                outs = place_grads(e, summed[e].all, order.last, outs, shapes)
-                order.did(outs[3])
-        return outs
-
     def low_grad(back, raw, factor, gain, total):
         return (
             factor * back * gain.reshape(1, local) - raw * factor**3 * per_row(total)
@@ -953,13 +1123,49 @@
 
     query_grad = low_grad(query_back, qkv[:, :local], factor_query, gain_query, sums[0])
     key_grad = low_grad(key_back, qkv[:, local : 2 * local], factor_key, gain_key, sums[1])
-    qkv_grad = order.tie(jnp.concatenate([query_grad, key_grad, value_grad], axis=1))
-    normed_grad = dot(qkv_grad, qkv_w, (1, 1)).astype(BF16).reshape(context, tokens, width)
+    qkv_grad = jnp.concatenate([query_grad, key_grad, value_grad], axis=1)
+    qkv_w_grad = dot(normed, qkv_grad, (0, 0)).astype(BF16)
+    normed_grad = dot(qkv_grad, qkv_w, (1, 1)).astype(BF16)
+    order.token = after(order.token, qkv_w_grad, normed_grad)
+    normed_grad = normed_grad.reshape(context, tokens, width)
     normed_grad = context_sum([normed_grad[s] for s in range(context)])
-    qk_w_grad = dot(normed, qkv_grad[:, : 2 * local], (0, 0)).astype(BF16)
-    order.did(qk_w_grad)
-    qk_w_grad = ring_sum(list(qk_w_grad.reshape(groups, context * rows, 2 * local)), add_low)
-    expert_grads = place([0, 1, 2])
+
+    class Ring:
+        def __init__(self, terms):
+            self.terms, self.size, self.slot = terms, terms.shape[0] // groups, 1
+            at = 1 % groups * self.size
+            self.total = terms[at : at + self.size]
+            self.coming = shift(self.total, 1)
+
+        def hop(self):
+            if self.slot < groups:
+                self.slot += 1
+                self.total = order.run(hop_add, [(self.terms, self.slot % groups)], self.coming)[0]
+                self.coming = shift(self.total, 1)
+
+        def whole(self):
+            while self.slot < groups:
+                self.hop()
+            return self.total
+
+    qkv_ring = Ring(qkv_w_grad)
+    advance((2, "finals"), (3, "quarters"))
+    if whole_heads:
+        ordered = take(
+            out_w_grad.reshape(per, HDIM, width), [(m // 2 ^ my_dp) * 2 + m % 2 for m in ring]
+        )
+        out_ring = Ring(ordered.reshape(local, width))
+        out_ring.hop()
+        out_ring.hop()
+    qkv_ring.hop()
+    advance((3, "finals"))
+    if whole_heads:
+        mine_out = out_ring.whole()
+        out_w_grad = mine_out.astype(F32) + swap(mine_out, "dp", 1).astype(F32)
+    expert_grads = place([0])
+    qkv_ring.hop()
+    expert_grads = place([1, 2])
+    qkv_w_grad = qkv_ring.whole()
     parts = [
         lax.dynamic_slice_in_dim(normed_grad, (my_group - m) % groups * block, block, axis=1)
         for m in range(groups)
@@ -968,7 +1174,7 @@
     source_part, attn_gain_grad = norm_back(normed_grad, source, factor_one, gain_attn)
     input_grad = (residual_grad + source_part).astype(BF16)[None]
 
-    mine_w = jnp.concatenate([qk_w_grad, value_w_grad], axis=1).reshape(context, rows, 3, 2, some)
+    mine_w = qkv_w_grad.reshape(context, rows, 3, 2, some)
     got = swap(mine_w, "dp", 1)
     mine_w = jnp.stack(
         [add_low(mine_w[:, :, :, i], got[:, :, :, 1 - i]) for i in range(2)], axis=3
@@ -979,16 +1185,11 @@
     dense = jnp.where(my_dp == 0, dense, dense[:, :, :, ::-1]).astype(F32)
     dense = dense.reshape(context, rows, 3, per, HDIM).transpose(2, 1, 3, 0, 4)
     dense = dense.reshape(3, rows, width)
-    if whole_heads:
-        ordered = take(out_w_grad, [(m // 2 ^ my_dp) * 2 + m % 2 for m in ring])
-        mine_out = ring_sum(list(ordered), add_low)
-        out_w_grad = mine_out.astype(F32) + swap(mine_out, "dp", 1).astype(F32)
-    else:
+    if not whole_heads:
         spread = jnp.zeros((per, context, HDIM, width), BF16)
         for h in range(per):
-            spread = lax.dynamic_update_slice(
-                spread, out_w_grad[h][None, None], (heads[h], my_context, 0, 0)
-            )
+            term = out_w_grad.reshape(per, HDIM, width)[h][None, None]
+            spread = lax.dynamic_update_slice(spread, term, (heads[h], my_context, 0, 0))
         spread = lax.psum_scatter(
             spread.reshape(width, width), ("expert", "context"), scatter_dimension=0, tiled=True
         )
@@ -1001,7 +1202,11 @@
         [attn_gain_grad[None], ffn_gain_grad[None], gains.reshape(2, width), router_grad], axis=0
     )
     small_grad = small_grad.reshape(4 + experts_all, groups, context, rows).transpose(1, 2, 0, 3)
-    small_grad = ring_sum(list(take(small_grad, ring)), lambda a, b: a + b)
+    small_grad = take(small_grad, ring)
+    small_grad = functools.reduce(
+        lambda a, b: a + b,
+        [small_grad[0]] + [shift(small_grad[s], -s) for s in range(1, groups)],
+    )
     small_grad = take(small_grad, members)
     got = swap(jnp.stack([small_grad[1], small_grad[3]]), "context", 1)
     small_grad = small_grad[0] + got[0] + swap(small_grad[2] + got[1], "context", 2)

time: 1270 us -> 1160 us (0.913)
  waiting for transfers between devices: 537 us -> 384 us
  Pallas kernels: 391 us -> 469 us
  other arithmetic: 90.3 us -> 60.4 us
  local copies, waits for them, and re-layouts: 108 us -> 84 us
    ppermute x36 -> x30, waiting for transfers between devices: 259 us -> 179 us  [shift(): return lax.ppermute(values, 'expert', [(i, (i + by) % n) for i in range(n)])]
    ppermute x52 -> x56, waiting for transfers between devices: 278 us -> 205 us  [swap(): lax.ppermute(values, axis, [(i, i ^ bit) for i in range(lax.axis_size(axi...]
    pallas_call x8 -> x20, Pallas kernels: 138 us -> 195 us  [the longest x3 73.6 us: run_split(): pl.pallas_call(functools.partial(split_kernel, sizes), grid_spec=pltpu.Pr...]
    unnamed x350 -> x241, local copies, waits for them, and re-layouts: 70.1 us -> 38.3 us
    pallas_call x12 -> x9, Pallas kernels: 35.2 us -> 52.2 us  [add_pieces(): pl.pallas_call(functools.partial(add_kernel, picks, joined), grid=(parts,...]
    convert_element_type x6 -> x2, other arithmetic: 18.1 us -> 1.74 us  [total_low(): functools.reduce(lambda a, b: a + b, [t.astype(F32) for t in terms])]
    convert_element_type x16 -> x3, other arithmetic: 17.3 us -> 3.85 us  [add_low(): return (left.astype(F32) + right.astype(F32)).astype(BF16)]
    dot_general x9 -> x8, matrix products: 38.6 us -> 44.9 us  [dot(): lax.dot_general(left, right, (((contract[0],), (contract[1],)), ((), ()))...]
  transfers between devices with their start and end apart: 93 -> 92, of which waited for: 46 -> 32; matrix products, arithmetic and copies ran while one was open for 13% -> 14% of each run, Pallas kernels for 24% -> 33%
where the time goes in v3:
time: 1160 us; the launch traced here: 1150 us
  Pallas kernels  469 us (40%)
  waiting for transfers between devices  384 us (33%)
  local copies, waits for them, and re-layouts  84 us (7%)
  starting transfers between devices  82.3 us (7%)
  other arithmetic  60.4 us (5%)
  matrix products  44.9 us (4%)
  between operations  24.7 us (2%)
    ppermute x56, waiting for transfers between devices, swap(): lax.ppermute(values, axis, [(i, i ^ bit) for i in range(lax.axis_size(axi...  205 us
    pallas_call x8, Pallas kernels, run_rows(): pl.pallas_call(functools.partial(rows_kernel, first), grid_spec=pltpu.Pre...  185 us
    ppermute x30, waiting for transfers between devices, shift(): return lax.ppermute(values, 'expert', [(i, (i + by) % n) for i in range(n)])  179 us
    pallas_call x3, Pallas kernels, run_split(): pl.pallas_call(functools.partial(split_kernel, sizes), grid_spec=pltpu.Pr...  73.6 us
    pallas_call x9, Pallas kernels, add_pieces(): pl.pallas_call(functools.partial(add_kernel, picks, joined), grid=(parts,...  52.2 us
    pallas_call x3, Pallas kernels, place_pieces(): pl.pallas_call(functools.partial(place_pieces_kernel, e, first), in_specs...  51.8 us
    dot_general x8, matrix products, dot(): lax.dot_general(left, right, (((contract[0],), (contract[1],)), ((), ()))...  44.9 us
    ppermute x56, starting transfers between devices, swap(): lax.ppermute(values, axis, [(i, i ^ bit) for i in range(lax.axis_size(axi...  44.1 us
  transfers between devices with their start and end apart: 92, of which 32 were waited for; matrix products, arithmetic and copies ran while one was open for 14% of the time, Pallas kernels for 33%

profile of v3, /device:TPU:0, one launch (start us, length us, event | category | flops | bytes accessed | tf_op | source)
XLA Modules:
  0.0 1150.2 jit_solution(17393532882965624678)
XLA Ops:
  28.4 5.6 collective-permute-done.2
  39.9 15.3 %collective-permute-done.13 = bf16[512,768]{1,0:T(8,128)(2,1)S(1)} collective-permute-done((bf16[512,768]{1,0:T(8,128)(2,1)S(1)}, bf16[512,768]{1,0:T(8,128)(2,1)S(1)}, u32[]{:S(2)}, u32[]{:S(2)}) %collective-permute-start.13) | collective-permute-done | bytes 786464 | tf_op jit(solution)/shard_map/ppermute | solution.py:238
  58.1 4.3 collective-permute-start.15
  66.1 18.6 %collective-permute-done.20 = s32[256,8]{1,0:T(8,128)S(1)} collective-permute-done((s32[256,8]{1,0:T(8,128)S(1)}, s32[256,8]{1,0:T(8,128)S(1)}, u32[]{:S(2)}, u32[]{:S(2)}) %collective-permute-start.20) | collective-permute-done | bytes 8224 | tf_op jit(solution)/shard_map/ppermute | solution.py:238
  94.2 7.3 fusion.2
  103.4 7.2 collective-permute-done.17
  124.2 8.3 collective-permute-done.18
  133.9 9.5 fusion.3.q_ref.k_ref.v_ref
  155.1 16.9 %attend.1 = (bf16[1024,512]{1,0:T(8,128)(2,1)}, bf16[1024,512]{1,0:T(8,128)(2,1)}, bf16[1024,512]{1,0:T(8,128)(2,1)}, bf16[1024,512]{1,0:T(8,128)(2,1)}, f32[4,1,1024]{2,1,0:T(1,128)}) custom-call(f32[1024,1536]{1,0:T(8,128)} %copy-done, f32[1024,1536]{1,0:T(8,128)} %copy-done, f32[1024,1536]{1,0:T(8,128)} %copy-done, f32[1024,1]{1,0:T(8,128)} %bitcast.308, ...), custom_call_target="tpu_custom_call" | custom-call | flops 5368709120 | bytes 10485760 | tf_op jit(solution)/shard_map/attend/pallas_call | solution.py:175
  177.8 4.1 collective-permute-done.24
  191.1 17.8 %collective-permute-done.25 = bf16[256,2048]{1,0:T(8,128)(2,1)} collective-permute-done((bf16[256,2048]{1,0:T(8,128)(2,1)S(1)}, bf16[256,2048]{1,0:T(8,128)(2,1)}, u32[]{:S(2)}, u32[]{:S(2)}) %collective-permute-start.25) | collective-permute-done | bytes 1048608 | tf_op jit(solution)/shard_map/ppermute | solution.py:233
  214.6 22.4 %rows.8 = (bf16[256,2048]{1,0:T(8,128)(2,1)}, bf16[256,2048]{1,0:T(8,128)(2,1)}, f32[256,128]{1,0:T(8,128)}, f32[256,128]{1,0:T(8,128)}, bf16[2048,256]{1,0:T(8,...) custom-call(s32[1]{0:T(128)} %bitcast.65.at_ref, ...), custom_call_target="tpu_custom_call" | custom-call | flops 12884901888 | bytes 25165824 | tf_op jit(solution)/shard_map/rows/pallas_call | solution.py:368
  236.9 24.7 %collective-permute-done.26.x_ref = bf16[256,2048]{1,0:T(8,128)(2,1)S(1)} collective-permute-done((bf16[256,2048]{1,0:T(8,128)(2,1)S(1)}, bf16[256,2048]{1,0:T(8,128)(2,1)S(1)}, u32[]{:S(2)}, u32[]{:S(2)}) %collective-permute-start.26) | collective-permute-done | bytes 1048608 | tf_op jit(solution)/shard_map/ppermute | solution.py:238
  261.6 22.8 %rows.9 = (bf16[256,2048]{1,0:T(8,128)(2,1)}, bf16[256,2048]{1,0:T(8,128)(2,1)}, f32[256,128]{1,0:T(8,128)}, f32[256,128]{1,0:T(8,128)}, bf16[2048,256]{1,0:T(8,...) custom-call(s32[1]{0:T(128)} %bitcast.65.at_ref, ...), custom_call_target="tpu_custom_call" | custom-call | flops 12884901888 | bytes 25165824 | tf_op jit(solution)/shard_map/rows/pallas_call | solution.py:368
  288.8 22.4 %rows.10 = (bf16[256,2048]{1,0:T(8,128)(2,1)}, bf16[256,2048]{1,0:T(8,128)(2,1)}, f32[256,128]{1,0:T(8,128)}, f32[256,128]{1,0:T(8,128)}, bf16[2048,256]{1,0:T(8...) custom-call(s32[1]{0:T(128)} %bitcast.65.at_ref, ...), custom_call_target="tpu_custom_call" | custom-call | flops 12884901888 | bytes 25165824 | tf_op jit(solution)/shard_map/rows/pallas_call | solution.py:368
  317.9 23.4 %rows.11 = (bf16[512,2048]{1,0:T(8,128)(2,1)}, bf16[512,2048]{1,0:T(8,128)(2,1)}, f32[512,128]{1,0:T(8,128)}, f32[512,128]{1,0:T(8,128)}, bf16[2048,512]{1,0:T(8...) custom-call(s32[1]{0:T(128)} %bitcast.65.at_ref, ...), custom_call_target="tpu_custom_call" | custom-call | flops 12884901888 | bytes 12582912 | tf_op jit(solution)/shard_map/rows/pallas_call | solution.py:368
  341.3 20.2 %grads.1 = (bf16[2048,1024]{1,0:T(8,128)(2,1)}, bf16[2048,1024]{1,0:T(8,128)(2,1)}, bf16[1024,2048]{1,0:T(8,128)(2,1)}, f32[8,128]{1,0:T(8,128)}) custom-call(bf16[2048,256]{1,0:T(8,128)(2,1)} %get-tuple-element.188.refs_0_, bf16[2048,256]{1,0:T(8,128)(2,1)} %get-tuple-element.189.refs_1_, bf16[2048,512]{1,0:T(8,128)(2,1)} %get-tuple-element.190.refs_2_, ...), custom_call_target="tpu_custom_call" | custom-call | flops 12884901888 | bytes 29360128 | tf_op jit(solution)/shard_map/grads/pallas_call | solution.py:464
  361.5 22.6 %rows.12 = (bf16[256,2048]{1,0:T(8,128)(2,1)}, bf16[256,2048]{1,0:T(8,128)(2,1)}, f32[256,128]{1,0:T(8,128)}, f32[256,128]{1,0:T(8,128)}, bf16[2048,256]{1,0:T(8...) custom-call(s32[1]{0:T(128)} %bitcast.65.at_ref, ...), custom_call_target="tpu_custom_call" | custom-call | flops 12884901888 | bytes 25165824 | tf_op jit(solution)/shard_map/rows/pallas_call | solution.py:368
  384.1 23.3 %rows.13 = (bf16[512,2048]{1,0:T(8,128)(2,1)}, bf16[512,2048]{1,0:T(8,128)(2,1)}, f32[512,128]{1,0:T(8,128)}, f32[512,128]{1,0:T(8,128)}, bf16[2048,512]{1,0:T(8...) custom-call(s32[1]{0:T(128)} %bitcast.65.at_ref, ...), custom_call_target="tpu_custom_call" | custom-call | flops 12884901888 | bytes 12582912 | tf_op jit(solution)/shard_map/rows/pallas_call | solution.py:368
  407.5 24.8 %split.3 = (bf16[2,3,512,256]{3,2,1,0:T(8,128)(2,1)}, bf16[2,3,512,256]{3,2,1,0:T(8,128)(2,1)}, bf16[2,3,512,256]{3,2,1,0:T(8,128)(2,1)}, bf16[2,3,512,256]{3,2,...) custom-call(s32[3]{0:T(128)} %pad_add_fusion.1.bits_ref, ...), custom_call_target="tpu_custom_call" | custom-call | flops 12884901888 | bytes 29360128 | tf_op jit(solution)/shard_map/split/pallas_call | solution.py:608
  435.6 24.0 %rows.14 = (bf16[512,2048]{1,0:T(8,128)(2,1)}, bf16[512,2048]{1,0:T(8,128)(2,1)}, f32[512,128]{1,0:T(8,128)}, f32[512,128]{1,0:T(8,128)}, bf16[2048,512]{1,0:T(8...) custom-call(s32[1]{0:T(128)} %bitcast.65.at_ref, ...), custom_call_target="tpu_custom_call" | custom-call | flops 12884901888 | bytes 12582912 | tf_op jit(solution)/shard_map/rows/pallas_call | solution.py:368
  461.3 7.9 add_pieces.9
  472.4 24.4 %rows.15 = (bf16[512,2048]{1,0:T(8,128)(2,1)}, bf16[512,2048]{1,0:T(8,128)(2,1)}, f32[512,128]{1,0:T(8,128)}, f32[512,128]{1,0:T(8,128)}, bf16[2048,512]{1,0:T(8...) custom-call(s32[1]{0:T(128)} %bitcast.65.at_ref, ...), custom_call_target="tpu_custom_call" | custom-call | flops 12884901888 | bytes 12582912 | tf_op jit(solution)/shard_map/rows/pallas_call | solution.py:368
  496.8 3.6 hop.12
  503.5 24.4 %split.4 = (bf16[2,3,512,256]{3,2,1,0:T(8,128)(2,1)}, bf16[2,3,512,256]{3,2,1,0:T(8,128)(2,1)}, bf16[2,3,512,256]{3,2,1,0:T(8,128)(2,1)}, bf16[2,3,512,256]{3,2,...) custom-call(s32[3]{0:T(128)} %pad_add_fusion.1.bits_ref, ...), custom_call_target="tpu_custom_call" | custom-call | flops 12884901888 | bytes 29360128 | tf_op jit(solution)/shard_map/split/pallas_call | solution.py:608
  529.6 5.1 add_pieces.10
  536.8 3.6 hop.13
  540.4 24.5 %split.5 = (bf16[2,3,512,256]{3,2,1,0:T(8,128)(2,1)}, bf16[2,3,512,256]{3,2,1,0:T(8,128)(2,1)}, bf16[2,3,512,256]{3,2,1,0:T(8,128)(2,1)}, bf16[2,3,512,256]{3,2,...) custom-call(s32[3]{0:T(128)} %pad_add_fusion.1.bits_ref, ...), custom_call_target="tpu_custom_call" | custom-call | flops 12884901888 | bytes 29360128 | tf_op jit(solution)/shard_map/split/pallas_call | solution.py:608
  566.0 4.2 add_pieces.11
  579.5 4.9 collective-permute-done.47
  586.4 4.8 collective-permute-done.48
  598.2 8.2 add_pieces.12
  606.5 9.8 collective-permute-done.38.refs_2_
  624.6 37.5 %collective-permute-done.50 = bf16[256,2048]{1,0:T(8,128)(2,1)} collective-permute-done((bf16[256,2048]{1,0:T(8,128)(2,1)S(1)}, bf16[256,2048]{1,0:T(8,128)(2,1)}, u32[]{:S(2)}, u32[]{:S(2)}) %collective-permute-start.50) | collective-permute-done | bytes 1048608 | tf_op jit(solution)/shard_map/ppermute | solution.py:233
  662.3 3.7 hop.15
  666.6 6.0 convolution_convert_fusion.3.grad_ref
  672.6 20.3 %attend_back.1 = (f32[1024,512]{1,0:T(8,128)}, f32[1024,512]{1,0:T(8,128)}, bf16[1024,512]{1,0:T(8,128)(2,1)}, f32[1024,128]{1,0:T(8,128)}, f32[1024,128]{1,0:T(...) custom-call(bf16[1024,512]{1,0:T(8,128)(2,1)} %get-tuple-element.262.ql_ref, ...), custom_call_target="tpu_custom_call" | custom-call | flops 10737418240 | bytes 15728640 | tf_op jit(solution)/shard_map/attend_back/pallas_call | solution.py:203
  698.9 3.6 hop.16
  703.1 4.2 subtract_convert_fusion.1
  707.3 25.4 %collective-permute-done.57.refs_2_ = bf16[2,3,512,256]{3,2,1,0:T(8,128)(2,1)} collective-permute-done((bf16[2,3,512,256]{3,2,1,0:T(8,128)(2,1)}, bf16[2,3,512,256]{3,2,1,0:T(8,128)(2,1)}, u32[]{:S(2)}, u32[]{:S(2)}) %collective-permute-start.57) | collective-permute-done | bytes 1572896 | tf_op jit(solution)/shard_map/ppermute | solution.py:233
  733.9 9.3 convolution_convert_fusion.refs_0_
  745.0 23.6 %collective-permute-done.58.refs_3_ = bf16[2,3,512,256]{3,2,1,0:T(8,128)(2,1)} collective-permute-done((bf16[2,3,512,256]{3,2,1,0:T(8,128)(2,1)S(1)}, bf16[2,3,512,256]{3,2,1,0:T(8,128)(2,1)}, u32[]{:S(2)}, u32[]{:S(2)}) %collective-permute-start.58) | collective-permute-done | bytes 1572896 | tf_op jit(solution)/shard_map/ppermute | solution.py:233
  768.7 5.3 add_pieces.13
  776.7 10.4 convolution_convert_fusion.1
  790.6 7.7 add_pieces.14
  802.4 4.2 add_pieces.15
  813.7 4.8 fusion.12
  822.6 35.8 %collective-permute-done.71.refs_2_ = bf16[2,3,512,256]{3,2,1,0:T(8,128)(2,1)} collective-permute-done((bf16[2,3,512,256]{3,2,1,0:T(8,128)(2,1)}, bf16[2,3,512,256]{3,2,1,0:T(8,128)(2,1)}, u32[]{:S(2)}, u32[]{:S(2)}) %collective-permute-start.71) | collective-permute-done | bytes 1572896 | tf_op jit(solution)/shard_map/ppermute | solution.py:233
  858.7 5.5 add_pieces.16
  871.6 12.0 %collective-permute-done.75.refs_1_ = bf16[128,2048]{1,0:T(8,128)(2,1)S(1)} collective-permute-done((bf16[128,2048]{1,0:T(8,128)(2,1)}, bf16[128,2048]{1,0:T(8,128)(2,1)S(1)}, u32[]{:S(2)}, u32[]{:S(2)}) %collective-permute-start.75) | collective-permute-done | bytes 524320 | tf_op jit(solution)/shard_map/ppermute | solution.py:238
  889.3 11.3 collective-permute-done.78.refs_2_
  901.3 4.1 add_pieces.17
  909.2 4.0 collective-permute-done.61
  918.8 3.8 collective-permute-start.77
  922.6 44.4 %collective-permute-done.77.refs_1_ = bf16[128,2048]{1,0:T(8,128)(2,1)S(1)} collective-permute-done((bf16[128,2048]{1,0:T(8,128)(2,1)S(1)}, bf16[128,2048]{1,0:T(8,128)(2,1)S(1)}, u32[]{:S(2)}, u32[]{:S(2)}) %collective-permute-start.77) | collective-permute-done | bytes 524320 | tf_op jit(solution)/shard_map/ppermute | solution.py:238
  970.0 14.0 %place.1 = (f32[4,2048,1024]{2,1,0:T(8,128)}, f32[4,2048,1024]{2,1,0:T(8,128)}, f32[4,1024,2048]{2,1,0:T(8,128)}, f32[8,128]{1,0:T(8,128)}) custom-call(bf16[2048,1024]{1,0:T(8,128)(2,1)} %get-tuple-element.368.refs_0_, bf16[2048,1024]{1,0:T(8,128)(2,1)} %get-tuple-element.369.refs_1_, bf16[1024,2048]{1,0:T(8,128)(2,1)} %get-tuple-element.370.refs_2_, ...), custom_call_target="tpu_custom_call" | custom-call | bytes 37748736 | tf_op jit(solution)/shard_map/place/pallas_call | solution.py:517
  984.0 3.4 fusion.24
  1000.9 27.8 %collective-permute-done.63 = f32[4,20,128]{2,1,0:T(8,128)S(1)} collective-permute-done((f32[4,20,128]{2,1,0:T(8,128)S(1)}, f32[4,20,128]{2,1,0:T(8,128)S(1)}, u32[]{:S(2)}, u32[]{:S(2)}) %collective-permute-start.63) | collective-permute-done | bytes 40992 | tf_op jit(solution)/shard_map/ppermute | solution.py:238
  1028.7 3.7 collective-permute-done.64
  1032.5 17.3 %place_pieces.3 = (f32[4,2048,1024]{2,1,0:T(8,128)}, f32[4,2048,1024]{2,1,0:T(8,128)}, f32[4,1024,2048]{2,1,0:T(8,128)}, f32[8,128]{1,0:T(8,128)}) custom-call(bf16[8,2,3,512,256]{4,3,2,1,0:T(8,128)(2,1)} %bitcast.294, f32[8,128]{1,0:T(8,128)} %get-tuple-element.329.refs_1_, ...), custom_call_target="tpu_custom_call", output_to_operand_aliasing={{0}: (2, {}), {1}: (3, {}), {2}: (4, {})} | custom-call | bytes 37748736 | tf_op jit(solution)/shard_map/place_pieces/pallas_call | solution.py:778
  1049.8 17.3 %place_pieces.4 = (f32[4,2048,1024]{2,1,0:T(8,128)}, f32[4,2048,1024]{2,1,0:T(8,128)}, f32[4,1024,2048]{2,1,0:T(8,128)}, f32[8,128]{1,0:T(8,128)}) custom-call(bf16[8,2,3,512,256]{4,3,2,1,0:T(8,128)(2,1)} %bitcast.295, f32[8,128]{1,0:T(8,128)} %get-tuple-element.333.refs_1_, ...), custom_call_target="tpu_custom_call", output_to_operand_aliasing={{0}: (2, {}), {1}: (3, {}), {2}: (4, {})} | custom-call | bytes 37748736 | tf_op jit(solution)/shard_map/place_pieces/pallas_call | solution.py:778
  1070.0 3.6 reshape.474
  1082.2 28.9 %collective-permute-done.68 = f32[20,128]{1,0:T(8,128)S(1)} collective-permute-done((f32[20,128]{1,0:T(8,128)S(1)}, f32[20,128]{1,0:T(8,128)S(1)}, u32[]{:S(2)}, u32[]{:S(2)}) %collective-permute-start.68) | collective-permute-done | bytes 10272 | tf_op jit(solution)/shard_map/ppermute | solution.py:233
  1114.8 17.3 %place_pieces.5 = (f32[4,2048,1024]{2,1,0:T(8,128)}, f32[4,2048,1024]{2,1,0:T(8,128)}, f32[4,1024,2048]{2,1,0:T(8,128)}, f32[8,128]{1,0:T(8,128)}) custom-call(bf16[8,2,3,512,256]{4,3,2,1,0:T(8,128)(2,1)} %bitcast.296, f32[8,128]{1,0:T(8,128)} %get-tuple-element.341.refs_1_, ...), custom_call_target="tpu_custom_call", output_to_operand_aliasing={{0}: (2, {}), {1}: (3, {}), {2}: (4, {})} | custom-call | bytes 37748736 | tf_op jit(solution)/shard_map/place_pieces/pallas_call | solution.py:778
  (589 shorter events, 234.7 us)
Async XLA Ops:
  7.2 164.8 %all-gather.12.cloned.1.call-start = ((), (), s32[]{:S(2)}) async-start(), calls=%async_computation.1 | async-start | bytes 2621440 | tf_op jit(solution)/shard_map/all_gather | solution.py:899
  34.5 20.7 %collective-permute-start.13 = (bf16[512,768]{1,0:T(8,128)(2,1)S(1)}, bf16[512,768]{1,0:T(8,128)(2,1)S(1)}, u32[]{:S(2)}, u32[]{:S(2)}) collective-permute-start(bf16[512,768]{1,0:T(8,128)(2,1)S(1)} %bitcast.302), channel_id=1, source_target_pairs={{0,8},{8,16},{16,24},{24,0},{1,9},{9,17},{17,25},{25,1},{2,10},{10... | collective-permute-start | bytes 2359304 | tf_op jit(solution)/shard_map/ppermute | solution.py:238
  38.6 48.5 %collective-permute-start.4 = (bf16[256,2048]{1,0:T(8,128)(2,1)S(1)}, bf16[256,2048]{1,0:T(8,128)(2,1)S(1)}, u32[]{:S(2)}, u32[]{:S(2)}) collective-permute-start(bf16[256,2048]{1,0:T(8,128)(2,1)S(1)} %add_bitcast_fusion), channel_id=1, source_target_pairs={{0,4},{2,6},{4,0},{6,2},{1,5},{3,7},{5,1},{7,3},{8,12},{10,14},{12... | collective-permute-start | bytes 3145736 | tf_op jit(solution)/shard_map/ppermute | solution.py:233
  56.4 28.3 %collective-permute-start.20 = (s32[256,8]{1,0:T(8,128)S(1)}, s32[256,8]{1,0:T(8,128)S(1)}, u32[]{:S(2)}, u32[]{:S(2)}) collective-permute-start(s32[256,8]{1,0:T(8,128)S(1)} %add_bitcast_fusion.1), channel_id=1, source_target_pairs={{0,16},{8,24},{16,0},{24,8},{1,17},{9,25},{17,1},{25,9},{2,18},{10... | collective-permute-start | bytes 24584 | tf_op jit(solution)/shard_map/ppermute | solution.py:238
  56.6 35.3 %collective-permute-start.14 = (bf16[512,768]{1,0:T(8,128)(2,1)S(1)}, bf16[512,768]{1,0:T(8,128)(2,1)S(1)}, u32[]{:S(2)}, u32[]{:S(2)}) collective-permute-start(bf16[512,768]{1,0:T(8,128)(2,1)S(1)} %collective-permute-done.13), channel_id=1, source_target_pairs={{0,1},{1,0},{2,3},{3,2},{4,5},{5,4},{6,7},{7,6},{8,9},{9,8},{10,11... | collective-permute-start | bytes 2359304 | tf_op jit(solution)/shard_map/ppermute | solution.py:233
  58.1 29.6 %collective-permute-start.15 = (bf16[512,768]{1,0:T(8,128)(2,1)S(1)}, bf16[512,768]{1,0:T(8,128)(2,1)}, u32[]{:S(2)}, u32[]{:S(2)}) collective-permute-start(bf16[512,768]{1,0:T(8,128)(2,1)S(1)} %collective-permute-done.13), channel_id=1, source_target_pairs={{0,8},{8,16},{16,24},{24,0},{1,9},{9,17},{17,25},{25,1},{2,10},{10... | collective-permute-start | bytes 2359304 | tf_op jit(solution)/shard_map/ppermute | solution.py:238
  64.8 21.1 %collective-permute-start.21 = (s32[256,8]{1,0:T(8,128)S(1)}, s32[256,8]{1,0:T(8,128)S(1)}, u32[]{:S(2)}, u32[]{:S(2)}) collective-permute-start(s32[256,8]{1,0:T(8,128)S(1)} %add_bitcast_fusion.1), channel_id=1, source_target_pairs={{0,24},{8,0},{16,8},{24,16},{1,25},{9,1},{17,9},{25,17},{2,26},{10... | collective-permute-start | bytes 24584 | tf_op jit(solution)/shard_map/ppermute | solution.py:238
  87.7 27.8 %collective-permute-start.16 = (bf16[512,768]{1,0:T(8,128)(2,1)}, bf16[512,768]{1,0:T(8,128)(2,1)}, u32[]{:S(2)}, u32[]{:S(2)}) collective-permute-start(bf16[512,768]{1,0:T(8,128)(2,1)} %collective-permute-done.15), channel_id=1, source_target_pairs={{0,1},{1,0},{2,3},{3,2},{4,5},{5,4},{6,7},{7,6},{8,9},{9,8},{10,11... | collective-permute-start | bytes 2359304 | tf_op jit(solution)/shard_map/ppermute | solution.py:233
  89.2 21.4 %collective-permute-start.17 = (bf16[512,768]{1,0:T(8,128)(2,1)}, bf16[512,768]{1,0:T(8,128)(2,1)S(1)}, u32[]{:S(2)}, u32[]{:S(2)}) collective-permute-start(bf16[512,768]{1,0:T(8,128)(2,1)} %collective-permute-done.15), channel_id=1, source_target_pairs={{0,8},{8,16},{16,24},{24,0},{1,9},{9,17},{17,25},{25,1},{2,10},{10... | collective-permute-start | bytes 2359304 | tf_op jit(solution)/shard_map/ppermute | solution.py:238
  113.6 148.1 %all-gather.10.cloned.1.call-start = ((), (), s32[]{:S(2)}) async-start(), calls=%async_computation | async-start | bytes 5242880 | tf_op jit(solution)/shard_map/all_gather | solution.py:900
  151.7 818.3 %all-reduce.4.cloned.1.call-start = ((), (), s32[]{:S(2)}) async-start(), calls=%async_computation.5 | async-start | bytes 25165824 | tf_op jit(solution)/shard_map/psum | solution.py:1029
  183.2 25.6 %collective-permute-start.25 = (bf16[256,2048]{1,0:T(8,128)(2,1)S(1)}, bf16[256,2048]{1,0:T(8,128)(2,1)}, u32[]{:S(2)}, u32[]{:S(2)}) collective-permute-start(bf16[256,2048]{1,0:T(8,128)(2,1)S(1)} %fusion.25), channel_id=1, source_target_pairs={{0,4},{2,6},{4,0},{6,2},{1,5},{3,7},{5,1},{7,3},{8,12},{10,14},{12... | collective-permute-start | bytes 3145736 | tf_op jit(solution)/shard_map/ppermute | solution.py:233
  213.4 48.3 %collective-permute-start.26 = (bf16[256,2048]{1,0:T(8,128)(2,1)S(1)}, bf16[256,2048]{1,0:T(8,128)(2,1)S(1)}, u32[]{:S(2)}, u32[]{:S(2)}) collective-permute-start(bf16[256,2048]{1,0:T(8,128)(2,1)S(1)} %multiply_convert_fusion.x_ref), channel_id=1, source_target_pairs={{0,8},{8,16},{16,24},{24,0},{1,9},{9,17},{17,25},{25,1},{2,10},{10... | collective-permute-start | bytes 3145736 | tf_op jit(solution)/shard_map/ppermute | solution.py:238
  261.6 27.0 %collective-permute-start.27 = (bf16[256,2048]{1,0:T(8,128)(2,1)S(1)}, bf16[256,2048]{1,0:T(8,128)(2,1)S(1)}, u32[]{:S(2)}, u32[]{:S(2)}) collective-permute-start(bf16[256,2048]{1,0:T(8,128)(2,1)S(1)} %collective-permute-done.26.x_ref), channel_id=1, source_target_pairs={{0,8},{8,16},{16,24},{24,0},{1,9},{9,17},{17,25},{25,1},{2,10},{10... | collective-permute-start | bytes 3145736 | tf_op jit(solution)/shard_map/ppermute | solution.py:238
  288.6 27.9 %collective-permute-start.28 = (bf16[256,2048]{1,0:T(8,128)(2,1)S(1)}, bf16[256,2048]{1,0:T(8,128)(2,1)S(1)}, u32[]{:S(2)}, u32[]{:S(2)}) collective-permute-start(bf16[256,2048]{1,0:T(8,128)(2,1)S(1)} %collective-permute-done.27), channel_id=1, source_target_pairs={{0,8},{8,16},{16,24},{24,0},{1,9},{9,17},{17,25},{25,1},{2,10},{10... | collective-permute-start | bytes 3145736 | tf_op jit(solution)/shard_map/ppermute | solution.py:238
  407.5 625.1 %all-gather.16.cloned.1.call-start = ((), (), s32[]{:S(2)}) async-start(), calls=%async_computation.3 | async-start | bytes 14155776 | tf_op jit(solution)/shard_map/all_gather | solution.py:713
  432.3 27.3 %collective-permute-start.29 = (bf16[2,3,512,256]{3,2,1,0:T(8,128)(2,1)}, bf16[2,3,512,256]{3,2,1,0:T(8,128)(2,1)S(1)}, u32[]{:S(2)}, u32[]{:S(2)}) collective-permute-start(bf16[2,3,512,256]{3,2,1,0:T(8,128)(2,1)} %get-tuple-element.208), channel_id=1, source_target_pairs={{0,2},{2,0},{4,6},{6,4},{1,3},{3,1},{5,7},{7,5},{8,10},{10,8},{12,... | collective-permute-start | bytes 4718600 | tf_op jit(solution)/shard_map/ppermute | solution.py:233
  432.4 27.2 %collective-permute-start.30 = (bf16[2,3,512,256]{3,2,1,0:T(8,128)(2,1)}, bf16[2,3,512,256]{3,2,1,0:T(8,128)(2,1)S(1)}, u32[]{:S(2)}, u32[]{:S(2)}) collective-permute-start(bf16[2,3,512,256]{3,2,1,0:T(8,128)(2,1)} %get-tuple-element.209), channel_id=1, source_target_pairs={{0,2},{2,0},{4,6},{6,4},{1,3},{3,1},{5,7},{7,5},{8,10},{10,8},{12,... | collective-permute-start | bytes 4718600 | tf_op jit(solution)/shard_map/ppermute | solution.py:233
  432.9 26.8 %collective-permute-start.31 = (bf16[2,3,512,256]{3,2,1,0:T(8,128)(2,1)}, bf16[2,3,512,256]{3,2,1,0:T(8,128)(2,1)}, u32[]{:S(2)}, u32[]{:S(2)}) collective-permute-start(bf16[2,3,512,256]{3,2,1,0:T(8,128)(2,1)} %get-tuple-element.210), channel_id=1, source_target_pairs={{0,2},{2,0},{4,6},{6,4},{1,3},{3,1},{5,7},{7,5},{8,10},{10,8},{12,... | collective-permute-start | bytes 4718600 | tf_op jit(solution)/shard_map/ppermute | solution.py:233
  432.9 26.7 %collective-permute-start.32 = (bf16[2,3,512,256]{3,2,1,0:T(8,128)(2,1)}, bf16[2,3,512,256]{3,2,1,0:T(8,128)(2,1)}, u32[]{:S(2)}, u32[]{:S(2)}) collective-permute-start(bf16[2,3,512,256]{3,2,1,0:T(8,128)(2,1)} %get-tuple-element.211), channel_id=1, source_target_pairs={{0,2},{2,0},{4,6},{6,4},{1,3},{3,1},{5,7},{7,5},{8,10},{10,8},{12,... | collective-permute-start | bytes 4718600 | tf_op jit(solution)/shard_map/ppermute | solution.py:233
  434.7 62.0 %collective-permute-start.34 = (bf16[256,2048]{1,0:T(8,128)(2,1)}, bf16[256,2048]{1,0:T(8,128)(2,1)}, u32[]{:S(2)}, u32[]{:S(2)}) collective-permute-start(bf16[256,2048]{1,0:T(8,128)(2,1)} %add_convert_fusion.1), channel_id=1, source_target_pairs={{0,8},{8,16},{16,24},{24,0},{1,9},{9,17},{17,25},{25,1},{2,10},{10... | collective-permute-start | bytes 3145736 | tf_op jit(solution)/shard_map/ppermute | solution.py:238
  469.2 58.7 %collective-permute-start.36 = (bf16[2,3,512,256]{3,2,1,0:T(8,128)(2,1)}, bf16[2,3,512,256]{3,2,1,0:T(8,128)(2,1)S(1)}, u32[]{:S(2)}, u32[]{:S(2)}) collective-permute-start(bf16[2,3,512,256]{3,2,1,0:T(8,128)(2,1)} %get-tuple-element.229), channel_id=1, source_target_pairs={{0,1},{1,0},{2,3},{3,2},{4,5},{5,4},{6,7},{7,6},{8,9},{9,8},{10,11... | collective-permute-start | bytes 4718600 | tf_op jit(solution)/shard_map/ppermute | solution.py:233
  470.8 57.3 %collective-permute-start.37 = (bf16[2,3,512,256]{3,2,1,0:T(8,128)(2,1)}, bf16[2,3,512,256]{3,2,1,0:T(8,128)(2,1)S(1)}, u32[]{:S(2)}, u32[]{:S(2)}) collective-permute-start(bf16[2,3,512,256]{3,2,1,0:T(8,128)(2,1)} %get-tuple-element.230), channel_id=1, source_target_pairs={{0,4},{2,6},{4,0},{6,2},{1,5},{3,7},{5,1},{7,3},{8,12},{10,14},{12... | collective-permute-start | bytes 4718600 | tf_op jit(solution)/shard_map/ppermute | solution.py:233
  500.4 36.4 %collective-permute-start.35 = (bf16[256,2048]{1,0:T(8,128)(2,1)}, bf16[256,2048]{1,0:T(8,128)(2,1)}, u32[]{:S(2)}, u32[]{:S(2)}) collective-permute-start(bf16[256,2048]{1,0:T(8,128)(2,1)} %get-tuple-element.226), channel_id=1, source_target_pairs={{0,8},{8,16},{16,24},{24,0},{1,9},{9,17},{17,25},{25,1},{2,10},{10... | collective-permute-start | bytes 3145736 | tf_op jit(solution)/shard_map/ppermute | solution.py:238
  534.7 30.2 %collective-permute-start.43 = (bf16[3,512,256]{2,1,0:T(8,128)(2,1)}, bf16[3,512,256]{2,1,0:T(8,128)(2,1)S(1)}, u32[]{:S(2)}, u32[]{:S(2)}) collective-permute-start(bf16[3,512,256]{2,1,0:T(8,128)(2,1)} %get-tuple-element.251), channel_id=1, source_target_pairs={{0,4},{2,6},{4,0},{6,2},{1,5},{3,7},{5,1},{7,3},{8,12},{10,14},{12... | collective-permute-start | bytes 2359304 | tf_op jit(solution)/shard_map/ppermute | solution.py:233
  536.8 28.1 %collective-permute-start.44 = (bf16[3,512,256]{2,1,0:T(8,128)(2,1)}, bf16[3,512,256]{2,1,0:T(8,128)(2,1)S(1)}, u32[]{:S(2)}, u32[]{:S(2)}) collective-permute-start(bf16[3,512,256]{2,1,0:T(8,128)(2,1)} %get-tuple-element.252), channel_id=1, source_target_pairs={{0,1},{1,0},{2,3},{3,2},{4,5},{5,4},{6,7},{7,6},{8,9},{9,8},{10,11... | collective-permute-start | bytes 2359304 | tf_op jit(solution)/shard_map/ppermute | solution.py:233
  570.2 479.6 %all-gather.14.cloned.1.call-start = ((), (), s32[]{:S(2)}) async-start(), calls=%async_computation.2 | async-start | bytes 14155776 | tf_op jit(solution)/shard_map/all_gather | solution.py:713
  573.2 23.3 %collective-permute-start.39 = (bf16[2,3,512,256]{3,2,1,0:T(8,128)(2,1)}, bf16[2,3,512,256]{3,2,1,0:T(8,128)(2,1)S(1)}, u32[]{:S(2)}, u32[]{:S(2)}) collective-permute-start(bf16[2,3,512,256]{3,2,1,0:T(8,128)(2,1)} %get-tuple-element.245), channel_id=1, source_target_pairs={{0,2},{2,0},{4,6},{6,4},{1,3},{3,1},{5,7},{7,5},{8,10},{10,8},{12,... | collective-permute-start | bytes 4718600 | tf_op jit(solution)/shard_map/ppermute | solution.py:233
  573.3 23.2 %collective-permute-start.40 = (bf16[2,3,512,256]{3,2,1,0:T(8,128)(2,1)}, bf16[2,3,512,256]{3,2,1,0:T(8,128)(2,1)S(1)}, u32[]{:S(2)}, u32[]{:S(2)}) collective-permute-start(bf16[2,3,512,256]{3,2,1,0:T(8,128)(2,1)} %get-tuple-element.246), channel_id=1, source_target_pairs={{0,2},{2,0},{4,6},{6,4},{1,3},{3,1},{5,7},{7,5},{8,10},{10,8},{12,... | collective-permute-start | bytes 4718600 | tf_op jit(solution)/shard_map/ppermute | solution.py:233
  573.8 22.7 %collective-permute-start.41 = (bf16[2,3,512,256]{3,2,1,0:T(8,128)(2,1)}, bf16[2,3,512,256]{3,2,1,0:T(8,128)(2,1)}, u32[]{:S(2)}, u32[]{:S(2)}) collective-permute-start(bf16[2,3,512,256]{3,2,1,0:T(8,128)(2,1)} %get-tuple-element.247), channel_id=1, source_target_pairs={{0,2},{2,0},{4,6},{6,4},{1,3},{3,1},{5,7},{7,5},{8,10},{10,8},{12,... | collective-permute-start | bytes 4718600 | tf_op jit(solution)/shard_map/ppermute | solution.py:233
  573.8 22.6 %collective-permute-start.42 = (bf16[2,3,512,256]{3,2,1,0:T(8,128)(2,1)}, bf16[2,3,512,256]{3,2,1,0:T(8,128)(2,1)}, u32[]{:S(2)}, u32[]{:S(2)}) collective-permute-start(bf16[2,3,512,256]{3,2,1,0:T(8,128)(2,1)} %get-tuple-element.248), channel_id=1, source_target_pairs={{0,2},{2,0},{4,6},{6,4},{1,3},{3,1},{5,7},{7,5},{8,10},{10,8},{12,... | collective-permute-start | bytes 4718600 | tf_op jit(solution)/shard_map/ppermute | solution.py:233
  591.8 24.5 %collective-permute-start.38 = (bf16[256,2048]{1,0:T(8,128)(2,1)}, bf16[256,2048]{1,0:T(8,128)(2,1)}, u32[]{:S(2)}, u32[]{:S(2)}) collective-permute-start(bf16[256,2048]{1,0:T(8,128)(2,1)} %get-tuple-element.243), channel_id=1, source_target_pairs={{0,8},{8,16},{16,24},{24,0},{1,9},{9,17},{17,25},{25,1},{2,10},{10... | collective-permute-start | bytes 3145736 | tf_op jit(solution)/shard_map/ppermute | solution.py:238
  623.9 38.2 %collective-permute-start.50 = (bf16[256,2048]{1,0:T(8,128)(2,1)S(1)}, bf16[256,2048]{1,0:T(8,128)(2,1)}, u32[]{:S(2)}, u32[]{:S(2)}) collective-permute-start(bf16[256,2048]{1,0:T(8,128)(2,1)S(1)} %get-tuple-element.371), channel_id=1, source_target_pairs={{0,4},{2,6},{4,0},{6,2},{1,5},{3,7},{5,1},{7,3},{8,12},{10,14},{12... | collective-permute-start | bytes 3145736 | tf_op jit(solution)/shard_map/ppermute | solution.py:233
  624.5 37.8 %collective-permute-start.33 = (bf16[256,2048]{1,0:T(8,128)(2,1)S(1)}, bf16[256,2048]{1,0:T(8,128)(2,1)}, u32[]{:S(2)}, u32[]{:S(2)}) collective-permute-start(bf16[256,2048]{1,0:T(8,128)(2,1)S(1)} %add_convert_fusion.2), channel_id=1, source_target_pairs={{0,8},{8,16},{16,24},{24,0},{1,9},{9,17},{17,25},{25,1},{2,10},{10... | collective-permute-start | bytes 3145736 | tf_op jit(solution)/shard_map/ppermute | solution.py:238
  624.5 41.4 %collective-permute-start.49 = (bf16[256,2048]{1,0:T(8,128)(2,1)S(1)}, bf16[256,2048]{1,0:T(8,128)(2,1)}, u32[]{:S(2)}, u32[]{:S(2)}) collective-permute-start(bf16[256,2048]{1,0:T(8,128)(2,1)S(1)} %get-tuple-element.371), channel_id=1, source_target_pairs={{0,2},{2,0},{4,6},{6,4},{1,3},{3,1},{5,7},{7,5},{8,10},{10,8},{12,... | collective-permute-start | bytes 3145736 | tf_op jit(solution)/shard_map/ppermute | solution.py:233
  665.9 32.9 %collective-permute-start.45 = (bf16[256,2048]{1,0:T(8,128)(2,1)}, bf16[256,2048]{1,0:T(8,128)(2,1)}, u32[]{:S(2)}, u32[]{:S(2)}) collective-permute-start(bf16[256,2048]{1,0:T(8,128)(2,1)} %get-tuple-element.261), channel_id=1, source_target_pairs={{0,8},{8,16},{16,24},{24,0},{1,9},{9,17},{17,25},{25,1},{2,10},{10... | collective-permute-start | bytes 3145736 | tf_op jit(solution)/shard_map/ppermute | solution.py:238
  695.6 37.1 %collective-permute-start.57 = (bf16[2,3,512,256]{3,2,1,0:T(8,128)(2,1)}, bf16[2,3,512,256]{3,2,1,0:T(8,128)(2,1)}, u32[]{:S(2)}, u32[]{:S(2)}) collective-permute-start(bf16[2,3,512,256]{3,2,1,0:T(8,128)(2,1)} %get-tuple-element.286), channel_id=1, source_target_pairs={{0,1},{1,0},{2,3},{3,2},{4,5},{5,4},{6,7},{7,6},{8,9},{9,8},{10,11... | collective-permute-start | bytes 4718600 | tf_op jit(solution)/shard_map/ppermute | solution.py:233
  698.3 75.6 %collective-permute-start.53 = (bf16[2,3,512,256]{3,2,1,0:T(8,128)(2,1)}, bf16[2,3,512,256]{3,2,1,0:T(8,128)(2,1)}, u32[]{:S(2)}, u32[]{:S(2)}) collective-permute-start(bf16[2,3,512,256]{3,2,1,0:T(8,128)(2,1)} %get-tuple-element.280), channel_id=1, source_target_pairs={{0,2},{2,0},{4,6},{6,4},{1,3},{3,1},{5,7},{7,5},{8,10},{10,8},{12,... | collective-permute-start | bytes 4718600 | tf_op jit(solution)/shard_map/ppermute | solution.py:233
  698.3 77.0 %collective-permute-start.54 = (bf16[2,3,512,256]{3,2,1,0:T(8,128)(2,1)}, bf16[2,3,512,256]{3,2,1,0:T(8,128)(2,1)}, u32[]{:S(2)}, u32[]{:S(2)}) collective-permute-start(bf16[2,3,512,256]{3,2,1,0:T(8,128)(2,1)} %get-tuple-element.281), channel_id=1, source_target_pairs={{0,2},{2,0},{4,6},{6,4},{1,3},{3,1},{5,7},{7,5},{8,10},{10,8},{12,... | collective-permute-start | bytes 4718600 | tf_op jit(solution)/shard_map/ppermute | solution.py:233
  698.9 91.7 %collective-permute-start.55 = (bf16[2,3,512,256]{3,2,1,0:T(8,128)(2,1)}, bf16[2,3,512,256]{3,2,1,0:T(8,128)(2,1)}, u32[]{:S(2)}, u32[]{:S(2)}) collective-permute-start(bf16[2,3,512,256]{3,2,1,0:T(8,128)(2,1)} %get-tuple-element.282), channel_id=1, source_target_pairs={{0,2},{2,0},{4,6},{6,4},{1,3},{3,1},{5,7},{7,5},{8,10},{10,8},{12,... | collective-permute-start | bytes 4718600 | tf_op jit(solution)/shard_map/ppermute | solution.py:233
  702.5 88.1 %collective-permute-start.56 = (bf16[2,3,512,256]{3,2,1,0:T(8,128)(2,1)}, bf16[2,3,512,256]{3,2,1,0:T(8,128)(2,1)}, u32[]{:S(2)}, u32[]{:S(2)}) collective-permute-start(bf16[2,3,512,256]{3,2,1,0:T(8,128)(2,1)} %get-tuple-element.283), channel_id=1, source_target_pairs={{0,2},{2,0},{4,6},{6,4},{1,3},{3,1},{5,7},{7,5},{8,10},{10,8},{12,... | collective-permute-start | bytes 4718600 | tf_op jit(solution)/shard_map/ppermute | solution.py:233
  732.7 36.0 %collective-permute-start.58 = (bf16[2,3,512,256]{3,2,1,0:T(8,128)(2,1)S(1)}, bf16[2,3,512,256]{3,2,1,0:T(8,128)(2,1)}, u32[]{:S(2)}, u32[]{:S(2)}) collective-permute-start(bf16[2,3,512,256]{3,2,1,0:T(8,128)(2,1)S(1)} %copy-done.95), channel_id=1, source_target_pairs={{0,4},{2,6},{4,0},{6,2},{1,5},{3,7},{5,1},{7,3},{8,12},{10,14},{12... | collective-permute-start | bytes 4718600 | tf_op jit(solution)/shard_map/ppermute | solution.py:233
  768.7 29.6 %collective-permute-start.52 = (bf16[256,2048]{1,0:T(8,128)(2,1)}, bf16[256,2048]{1,0:T(8,128)(2,1)}, u32[]{:S(2)}, u32[]{:S(2)}) collective-permute-start(bf16[256,2048]{1,0:T(8,128)(2,1)} %get-tuple-element.278), channel_id=1, source_target_pairs={{0,8},{8,16},{16,24},{24,0},{1,9},{9,17},{17,25},{25,1},{2,10},{10... | collective-permute-start | bytes 3145736 | tf_op jit(solution)/shard_map/ppermute | solution.py:238
  774.0 28.4 %collective-permute-start.73 = (bf16[3,512,256]{2,1,0:T(8,128)(2,1)}, bf16[3,512,256]{2,1,0:T(8,128)(2,1)}, u32[]{:S(2)}, u32[]{:S(2)}) collective-permute-start(bf16[3,512,256]{2,1,0:T(8,128)(2,1)} %get-tuple-element.305), channel_id=1, source_target_pairs={{0,4},{2,6},{4,0},{6,2},{1,5},{3,7},{5,1},{7,3},{8,12},{10,14},{12... | collective-permute-start | bytes 2359304 | tf_op jit(solution)/shard_map/ppermute | solution.py:233
  775.3 27.1 %collective-permute-start.74 = (bf16[3,512,256]{2,1,0:T(8,128)(2,1)}, bf16[3,512,256]{2,1,0:T(8,128)(2,1)}, u32[]{:S(2)}, u32[]{:S(2)}) collective-permute-start(bf16[3,512,256]{2,1,0:T(8,128)(2,1)} %get-tuple-element.306), channel_id=1, source_target_pairs={{0,1},{1,0},{2,3},{3,2},{4,5},{5,4},{6,7},{7,6},{8,9},{9,8},{10,11... | collective-permute-start | bytes 2359304 | tf_op jit(solution)/shard_map/ppermute | solution.py:233
  806.6 308.3 %all-gather.18.cloned.1.call-start = ((), (), s32[]{:S(2)}) async-start(), calls=%async_computation.4 | async-start | bytes 14155776 | tf_op jit(solution)/shard_map/all_gather | solution.py:713
  806.6 51.7 %collective-permute-start.71 = (bf16[2,3,512,256]{3,2,1,0:T(8,128)(2,1)}, bf16[2,3,512,256]{3,2,1,0:T(8,128)(2,1)}, u32[]{:S(2)}, u32[]{:S(2)}) collective-permute-start(bf16[2,3,512,256]{3,2,1,0:T(8,128)(2,1)} %get-tuple-element.301), channel_id=1, source_target_pairs={{0,1},{1,0},{2,3},{3,2},{4,5},{5,4},{6,7},{7,6},{8,9},{9,8},{10,11... | collective-permute-start | bytes 4718600 | tf_op jit(solution)/shard_map/ppermute | solution.py:233
  807.3 51.4 %collective-permute-start.72 = (bf16[2,3,512,256]{3,2,1,0:T(8,128)(2,1)}, bf16[2,3,512,256]{3,2,1,0:T(8,128)(2,1)}, u32[]{:S(2)}, u32[]{:S(2)}) collective-permute-start(bf16[2,3,512,256]{3,2,1,0:T(8,128)(2,1)} %get-tuple-element.302), channel_id=1, source_target_pairs={{0,4},{2,6},{4,0},{6,2},{1,5},{3,7},{5,1},{7,3},{8,12},{10,14},{12... | collective-permute-start | bytes 4718600 | tf_op jit(solution)/shard_map/ppermute | solution.py:233
  812.6 73.8 %collective-permute-start.69 = (bf16[512,1536]{1,0:T(8,128)(2,1)}, bf16[512,1536]{1,0:T(8,128)(2,1)}, u32[]{:S(2)}, u32[]{:S(2)}) collective-permute-start(bf16[512,1536]{1,0:T(8,128)(2,1)} %slice.557), channel_id=1, source_target_pairs={{0,8},{8,16},{16,24},{24,0},{1,9},{9,17},{17,25},{25,1},{2,10},{10... | collective-permute-start | bytes 4718600 | tf_op jit(solution)/shard_map/ppermute | solution.py:238
  819.4 49.9 %collective-permute-start.70 = (bf16[128,2048]{1,0:T(8,128)(2,1)}, bf16[128,2048]{1,0:T(8,128)(2,1)}, u32[]{:S(2)}, u32[]{:S(2)}) collective-permute-start(bf16[128,2048]{1,0:T(8,128)(2,1)} %bitcast.125), channel_id=1, source_target_pairs={{0,8},{8,16},{16,24},{24,0},{1,9},{9,17},{17,25},{25,1},{2,10},{10... | collective-permute-start | bytes 1572872 | tf_op jit(solution)/shard_map/ppermute | solution.py:238
  864.2 36.4 %collective-permute-start.78 = (bf16[3,512,256]{2,1,0:T(8,128)(2,1)}, bf16[3,512,256]{2,1,0:T(8,128)(2,1)}, u32[]{:S(2)}, u32[]{:S(2)}) collective-permute-start(bf16[3,512,256]{2,1,0:T(8,128)(2,1)} %get-tuple-element.320), channel_id=1, source_target_pairs={{0,4},{2,6},{4,0},{6,2},{1,5},{3,7},{5,1},{7,3},{8,12},{10,14},{12... | collective-permute-start | bytes 2359304 | tf_op jit(solution)/shard_map/ppermute | solution.py:233
  865.3 36.1 %collective-permute-start.79 = (bf16[3,512,256]{2,1,0:T(8,128)(2,1)}, bf16[3,512,256]{2,1,0:T(8,128)(2,1)}, u32[]{:S(2)}, u32[]{:S(2)}) collective-permute-start(bf16[3,512,256]{2,1,0:T(8,128)(2,1)} %get-tuple-element.321), channel_id=1, source_target_pairs={{0,1},{1,0},{2,3},{3,2},{4,5},{5,4},{6,7},{7,6},{8,9},{9,8},{10,11... | collective-permute-start | bytes 2359304 | tf_op jit(solution)/shard_map/ppermute | solution.py:233
  916.1 68.0 %collective-permute-start.62 = (bf16[256,2048]{1,0:T(8,128)(2,1)}, bf16[256,2048]{1,0:T(8,128)(2,1)S(1)}, u32[]{:S(2)}, u32[]{:S(2)}) collective-permute-start(bf16[256,2048]{1,0:T(8,128)(2,1)} %fusion.23), channel_id=1, source_target_pairs={{0,4},{2,6},{4,0},{6,2},{1,5},{3,7},{5,1},{7,3},{8,12},{10,14},{12... | collective-permute-start | bytes 3145736 | tf_op jit(solution)/shard_map/ppermute | solution.py:233
  917.4 70.0 %collective-permute-start.76 = (bf16[512,1536]{1,0:T(8,128)(2,1)}, bf16[512,1536]{1,0:T(8,128)(2,1)}, u32[]{:S(2)}, u32[]{:S(2)}) collective-permute-start(bf16[512,1536]{1,0:T(8,128)(2,1)} %get-tuple-element.313), channel_id=1, source_target_pairs={{0,8},{8,16},{16,24},{24,0},{1,9},{9,17},{17,25},{25,1},{2,10},{10... | collective-permute-start | bytes 4718600 | tf_op jit(solution)/shard_map/ppermute | solution.py:238
  918.8 48.3 %collective-permute-start.77 = (bf16[128,2048]{1,0:T(8,128)(2,1)S(1)}, bf16[128,2048]{1,0:T(8,128)(2,1)S(1)}, u32[]{:S(2)}, u32[]{:S(2)}) collective-permute-start(bf16[128,2048]{1,0:T(8,128)(2,1)S(1)} %copy-done.98), channel_id=1, source_target_pairs={{0,8},{8,16},{16,24},{24,0},{1,9},{9,17},{17,25},{25,1},{2,10},{10... | collective-permute-start | bytes 1572872 | tf_op jit(solution)/shard_map/ppermute | solution.py:238
  990.3 76.8 %collective-permute-start.80 = (bf16[512,1536]{1,0:T(8,128)(2,1)}, bf16[512,1536]{1,0:T(8,128)(2,1)}, u32[]{:S(2)}, u32[]{:S(2)}) collective-permute-start(bf16[512,1536]{1,0:T(8,128)(2,1)} %get-tuple-element.326), channel_id=1, source_target_pairs={{0,8},{8,16},{16,24},{24,0},{1,9},{9,17},{17,25},{25,1},{2,10},{10... | collective-permute-start | bytes 4718600 | tf_op jit(solution)/shard_map/ppermute | solution.py:238
  993.9 34.8 %collective-permute-start.63 = (f32[4,20,128]{2,1,0:T(8,128)S(1)}, f32[4,20,128]{2,1,0:T(8,128)S(1)}, u32[]{:S(2)}, u32[]{:S(2)}) collective-permute-start(f32[4,20,128]{2,1,0:T(8,128)S(1)} %get-tuple-element.429), channel_id=1, source_target_pairs={{0,24},{8,0},{16,8},{24,16},{1,25},{9,1},{17,9},{25,17},{2,26},{10... | collective-permute-start | bytes 122888 | tf_op jit(solution)/shard_map/ppermute | solution.py:238
  996.7 35.7 %collective-permute-start.64 = (f32[4,20,128]{2,1,0:T(8,128)S(1)}, f32[4,20,128]{2,1,0:T(8,128)S(1)}, u32[]{:S(2)}, u32[]{:S(2)}) collective-permute-start(f32[4,20,128]{2,1,0:T(8,128)S(1)} %get-tuple-element.431), channel_id=1, source_target_pairs={{0,16},{8,24},{16,0},{24,8},{1,17},{9,25},{17,1},{25,9},{2,18},{10... | collective-permute-start | bytes 122888 | tf_op jit(solution)/shard_map/ppermute | solution.py:238
  997.6 34.8 %collective-permute-start.65 = (f32[4,20,128]{2,1,0:T(8,128)S(1)}, f32[4,20,128]{2,1,0:T(8,128)S(1)}, u32[]{:S(2)}, u32[]{:S(2)}) collective-permute-start(f32[4,20,128]{2,1,0:T(8,128)S(1)} %get-tuple-element.430), channel_id=1, source_target_pairs={{0,8},{8,16},{16,24},{24,0},{1,9},{9,17},{17,25},{25,1},{2,10},{10... | collective-permute-start | bytes 122888 | tf_op jit(solution)/shard_map/ppermute | solution.py:238
  999.5 80.4 %collective-permute-start.85 = (bf16[128,2048]{1,0:T(8,128)(2,1)}, bf16[128,2048]{1,0:T(8,128)(2,1)}, u32[]{:S(2)}, u32[]{:S(2)}) collective-permute-start(bf16[128,2048]{1,0:T(8,128)(2,1)} %get-tuple-element.339), channel_id=1, source_target_pairs={{0,1},{1,0},{2,3},{3,2},{4,5},{5,4},{6,7},{7,6},{8,9},{9,8},{10,11... | collective-permute-start | bytes 1572872 | tf_op jit(solution)/shard_map/ppermute | solution.py:233
  1032.4 43.1 %collective-permute-start.66 = (f32[2,20,128]{2,1,0:T(8,128)S(1)}, f32[2,20,128]{2,1,0:T(8,128)S(1)}, u32[]{:S(2)}, u32[]{:S(2)}) collective-permute-start(f32[2,20,128]{2,1,0:T(8,128)S(1)} %pad_maximum_fusion.29), channel_id=1, source_target_pairs={{0,2},{2,0},{4,6},{6,4},{1,3},{3,1},{5,7},{7,5},{8,10},{10,8},{12,... | collective-permute-start | bytes 61448 | tf_op jit(solution)/shard_map/ppermute | solution.py:233
  1074.0 37.1 %collective-permute-start.81 = (bf16[4,128,3,2,256]{4,1,3,2,0:T(8,128)(2,1)S(1)}, bf16[4,128,3,2,256]{4,1,3,2,0:T(8,128)(2,1)S(1)}, u32[]{:S(2)}, u32[]{:S(2)}) collective-permute-start(bf16[4,128,3,2,256]{4,1,3,2,0:T(8,128)(2,1)S(1)} %copy.215), channel_id=1, source_target_pairs={{0,1},{1,0},{2,3},{3,2},{4,5},{5,4},{6,7},{7,6},{8,9},{9,8},{10,11... | collective-permute-start | bytes 4718600 | tf_op jit(solution)/shard_map/ppermute | solution.py:233
  1079.3 31.8 %collective-permute-start.68 = (f32[20,128]{1,0:T(8,128)S(1)}, f32[20,128]{1,0:T(8,128)S(1)}, u32[]{:S(2)}, u32[]{:S(2)}) collective-permute-start(f32[20,128]{1,0:T(8,128)S(1)} %fusion.54), channel_id=1, source_target_pairs={{0,1},{1,0},{2,3},{3,2},{4,5},{5,4},{6,7},{7,6},{8,9},{9,8},{10,11... | collective-permute-start | bytes 30728 | tf_op jit(solution)/shard_map/ppermute | solution.py:233
  1111.8 20.3 %collective-permute-start.82 = (bf16[128,3,2,256]{3,0,2,1:T(8,128)(2,1)S(1)}, bf16[128,3,2,256]{3,0,2,1:T(8,128)(2,1)S(1)}, u32[]{:S(2)}, u32[]{:S(2)}) collective-permute-start(bf16[128,3,2,256]{3,0,2,1:T(8,128)(2,1)S(1)} %get-tuple-element.409), channel_id=1, source_target_pairs={{0,2},{2,0},{4,6},{6,4},{1,3},{3,1},{5,7},{7,5},{8,10},{10,8},{12,... | collective-permute-start | bytes 1179656 | tf_op jit(solution)/shard_map/ppermute | solution.py:233
  (128 other events, 1701.6 us)
Sparse Core Ops, SparseCore 0:
  113.7 44.4 all-gather.11
  159.7 99.7 all-gather.9
  407.6 201.5 all-reduce.3
  611.1 87.8 all-gather.15
  806.7 107.0 all-gather.13
  915.7 88.2 all-gather.17

commit v4 on v3

--- a/solution.py
+++ b/solution.py
@@ -244,10 +244,14 @@
     return [own, near, far, swap(far, "context", 1)]
 
 
+def context_terms(blocks):
+    got = swap(jnp.stack([blocks[1], blocks[3]]), "context", 1)
+    return blocks[0], got[0], swap(add_low(blocks[2], got[1]), "context", 2)
+
+
 def context_sum(blocks):
-    got = swap(jnp.stack([blocks[1], blocks[3]]), "context", 1)
-    far = swap(add_low(blocks[2], got[1]), "context", 2)
-    return blocks[0].astype(F32) + got[0].astype(F32) + far.astype(F32)
+    own, near, far = context_terms(blocks)
+    return own.astype(F32) + near.astype(F32) + far.astype(F32)
 
 
 def context_total(terms):
@@ -534,8 +538,7 @@
 def split_kernel(sizes, bits_ref, *refs):
     n = len(sizes)
     turned, ups, boths, hiddens = (refs[i * n : (i + 1) * n] for i in range(4))
-    sends = refs[4 * n + 1 : 4 * n + 5]
-    keep_ref, token_ref, x_all, u_all, both, hidden = refs[4 * n + 5 :]
+    *sends, keep_ref, token_ref, x_all, u_all, both, hidden = refs[-10:]
     token_ref[...] = jnp.zeros_like(token_ref)
     step = pl.program_id(0)
     width = x_all.shape[0]
@@ -582,7 +585,7 @@
         store(mask, lambda place: keep_ref.at[0, place])
 
 
-def run_split(token, segments, bits):
+def run_split(token, segments, bits, ready=()):
     turned, ups, boths, hiddens, places = zip(*segments)
     width = turned[0].shape[0]
     sizes = tuple(u.shape[0] for u in ups)
@@ -614,7 +617,7 @@
             + [whole((size, width)) for size in sizes]
             + [chunked(size, 2 * CHUNK, p) for size, p in zip(sizes, places)]
             + [chunked(size, CHUNK, p) for size, p in zip(sizes, places)]
-            + [ANYWHERE],
+            + [ANYWHERE] * (1 + len(ready)),
             out_specs=[
                 pl.BlockSpec(away, lambda s, b: (0, 0, 0, 0), pipeline_mode=pl.Buffered(1))
                 for _ in range(4)
@@ -638,7 +641,7 @@
             transcendentals=0,
         ),
         name="split",
-    )(bits, *turned, *ups, *boths, *hiddens, token)
+    )(bits, *turned, *ups, *boths, *hiddens, token, *ready)
 
 
 def add_kernel(picks, joined, *refs):
@@ -654,7 +657,7 @@
         out[...] = (left.astype(F32) + right.astype(F32)).astype(BF16)
 
 
-def add_pieces(token, picks, shapes, ins, joined=False):
+def add_pieces(token, picks, shapes, ins, ready=(), joined=False):
 
     parts = 4
 
@@ -666,13 +669,13 @@
     return pl.pallas_call(
         functools.partial(add_kernel, picks, joined),
         grid=(parts,),
-        in_specs=[cut(i.shape) for i in ins] + [ANYWHERE],
+        in_specs=[cut(i.shape) for i in ins] + [ANYWHERE] * (1 + len(ready)),
         out_specs=[cut(s) for s in shapes] + [token_spec()],
         out_shape=[jax.ShapeDtypeStruct(s, BF16) for s in shapes] + [TOKEN],
         compiler_params=pltpu.CompilerParams(vmem_limit_bytes=60 * MIB),
         cost_estimate=pl.CostEstimate(flops=moved, bytes_accessed=2 * moved, transcendentals=0),
         name="add_pieces",
-    )(*ins, token)
+    )(*ins, token, *ready)
 
 
 class Summed:
@@ -685,8 +688,11 @@
         while name in self.ahead:
             getattr(self, self.ahead.pop(0))()
 
+    ready = ()
+
     def add(self, picks, shapes, ins, joined=False):
-        return self.order.run(add_pieces, picks, shapes, ins, joined)
+        ready, self.ready = self.ready, ()
+        return self.order.run(add_pieces, picks, shapes, ins, ready, joined)
 
     def halves(self):
         shape = (2,) + self.keep.shape[2:]
@@ -713,6 +719,9 @@
         self.all = lax.all_gather(own, ("context", "dp"), axis=0)
 
 
+DEEP = 4
+
+
 def place_pieces_kernel(e, first, *refs):
     source = refs[0]
     outs = refs[2:5] if first else refs[5:8]
@@ -722,7 +731,7 @@
     token_ref[...] = jnp.zeros_like(token_ref)
 
     def fetch(i):
-        return pltpu.make_async_copy(source.at[i // 2, i % 2], low.at[i % 2], in_sem.at[i % 2])
+        return pltpu.make_async_copy(source.at[i // 2, i % 2], low.at[i % DEEP], in_sem.at[i % DEEP])
 
     def drain(i):
         path, member = i % 2, i // 2
@@ -734,39 +743,40 @@
         for k in range(2):
             copies.append(
                 pltpu.make_async_copy(
-                    wide.at[i % 2, k],
+                    wide.at[i % DEEP, k],
                     outs[k].at[e, pl.ds(piece * rows, rows), columns],
-                    out_sem.at[i % 2, k],
+                    out_sem.at[i % DEEP, k],
                 )
             )
         for j in range(rows // CHUNK):
             copies.append(
                 pltpu.make_async_copy(
-                    wide.at[i % 2, 2, pl.ds(j * CHUNK, CHUNK)],
+                    wide.at[i % DEEP, 2, pl.ds(j * CHUNK, CHUNK)],
                     outs[2].at[e, columns, pl.ds(piece * rows + j * CHUNK, CHUNK)],
-                    out_sem.at[i % 2, 2 + j],
+                    out_sem.at[i % DEEP, 2 + j],
                 )
             )
         return copies
 
-    fetch(0).start()
+    for i in range(DEEP - 1):
+        fetch(i).start()
     for i in range(count):
-        if i + 1 < count:
-            fetch(i + 1).start()
+        if i + DEEP - 1 < count:
+            fetch(i + DEEP - 1).start()
         fetch(i).wait()
-        if i >= 2:
-            for copy in drain(i - 2):
+        if i >= DEEP:
+            for copy in drain(i - DEEP):
                 copy.wait()
         for k in range(3):
 
             @pl.loop(0, rows // 64)
             def _(t):
                 r = pl.ds(pl.multiple_of(t * 64, 64), 64)
-                wide[i % 2, k, r, :] = low[i % 2, k, r, :].astype(F32)
+                wide[i % DEEP, k, r, :] = low[i % DEEP, k, r, :].astype(F32)
 
         for copy in drain(i):
             copy.start()
-    for i in (count - 2, count - 1):
+    for i in range(count - DEEP, count):
         for copy in drain(i):
             copy.wait()
 
@@ -780,10 +790,10 @@
         in_specs=[ANYWHERE] * len(operands),
         out_specs=[ANYWHERE] * 3 + [token_spec()],
         scratch_shapes=[
-            pltpu.VMEM((2, 3, rows, CHUNK), BF16),
-            pltpu.VMEM((2, 3, rows, CHUNK), F32),
-            pltpu.SemaphoreType.DMA((2,)),
-            pltpu.SemaphoreType.DMA((2, 2 + rows // CHUNK)),
+            pltpu.VMEM((DEEP, 3, rows, CHUNK), BF16),
+            pltpu.VMEM((DEEP, 3, rows, CHUNK), F32),
+            pltpu.SemaphoreType.DMA((DEEP,)),
+            pltpu.SemaphoreType.DMA((DEEP, 2 + rows // CHUNK)),
         ],
         out_shape=[jax.ShapeDtypeStruct(s, F32) for s in shapes] + [TOKEN],
         input_output_aliases={} if first else {2: 0, 3: 1, 4: 2},
@@ -894,7 +904,7 @@
     )
     heads = [my_dp * 2, my_dp * 2 + 1, (1 - my_dp) * 2, (1 - my_dp) * 2 + 1]
     whole_heads = rows == HDIM
-    routes_ring = ring_direct(after(routes[0], halves[1 % groups]))
+    routes_ring = ring_direct(after(routes[0], halves[-1]))
     if whole_heads:
         out_all = lax.all_gather(after(w_out, halves[-1]), "expert", axis=0)
     upstream_all = lax.all_gather(after(out_grad[0], halves[-1]), "expert", axis=0)
@@ -921,7 +931,7 @@
     normed = to_ring((source_all * factor_all * gain_attn).astype(BF16))
     source = hidden_in[0].astype(F32)
     factor_one = rms_factor(source)
-    qkv = dot(normed, after(qkv_w, *routes_ring[1:]), (1, 0))
+    qkv = dot(normed, qkv_w, (1, 0))
 
     def slots(query, key):
         return jnp.stack([v.reshape(context, tokens) for v in (query, key)])
@@ -952,7 +962,7 @@
     ids = jnp.arange(128, dtype=jnp.int32)
     masks = [jnp.any(r[:, :, None] == ids, axis=1).astype(F32) for r in routes_ring]
     mixed_out = dot(mixed_low, out_w, (1, 0)).astype(BF16).reshape(context, tokens, width)
-    residual = source + context_sum([mixed_out[s] for s in range(context)])
+    residual = after(source, *routes_ring[1:]) + context_sum([mixed_out[s] for s in range(context)])
     factor_two = rms_factor(residual)
     normed_two = (residual * factor_two * gain_ffn).astype(BF16)
 
@@ -1008,13 +1018,16 @@
             if first <= e < first + count:
                 return (result[4], ups[segment], result[5], result[6], e - first)
 
+    whole_sums = min(1, local_experts)
     summed = []
 
     def sum_grads():
         e = len(summed)
         if e == local_experts:
             return
-        call = functools.partial(run_split, bits=bits) if e else run_grads
+        call = run_grads
+        if e >= whole_sums:
+            call = functools.partial(run_split, bits=bits)
         bunches = [[0, 1, 2]] + [[s, s + 1] for s in range(3, len(segments), 2)]
         results = []
         for bunch in bunches:
@@ -1023,14 +1036,14 @@
         grads = [
             total_low(list(terms)) if len(terms) > 1 else terms[0] for terms in zip(*results)
         ]
-        if e:
+        if e < whole_sums:
+            summed.append(lax.psum(grads, ("context", "dp")))
+        else:
             summed.append(Summed(order, grads[:4], grads[4]))
-        else:
-            summed.append(lax.psum(grads, ("context", "dp")))
 
     def advance(*events):
         for e, name in events:
-            if e < local_experts:
+            if whole_sums <= e < local_experts:
                 summed[e].reach(name)
 
     def parts_of(slot, index):
@@ -1083,7 +1096,7 @@
         outs = expert_grads
         for e in experts:
             if e < local_experts:
-                if e:
+                if e >= whole_sums:
                     summed[e].reach("finals")
                     outs = order.run(place_pieces, e, summed[e].all, outs, shapes)
                 else:
@@ -1108,14 +1121,41 @@
         attend_back, query_low, key_low, value_low, mixed_grad, logsum, qkv, *turn
     )
     out_w_grad = dot(mixed_low, after(attn_grad, order.token), (0, 0)).astype(BF16)
+    advance((2, "quarters"))
+
+    class Ring:
+        def __init__(self, terms):
+            self.terms, self.size, self.slot = terms, terms.shape[0] // groups, 1
+            at = 1 % groups * self.size
+            self.total = terms[at : at + self.size]
+            self.coming = shift(self.total, 1)
+
+        def hop(self):
+            if self.slot < groups:
+                self.slot += 1
+                self.total = order.run(hop_add, [(self.terms, self.slot % groups)], self.coming)[0]
+                self.coming = shift(self.total, 1)
+
+        def whole(self):
+            while self.slot < groups:
+                self.hop()
+            return self.total
+
+    if whole_heads:
+        ordered = take(
+            out_w_grad.reshape(per, HDIM, width), [(m // 2 ^ my_dp) * 2 + m % 2 for m in ring]
+        )
+        out_ring = Ring(ordered.reshape(local, width))
     for slot in range(3, groups):
         out_total = hop(0, out_total, slot)
     sums = context_total(slots(jnp.sum(query_sum, axis=1), jnp.sum(key_sum, axis=1))) / width
     order.token = after(order.token, sums)
-    advance((2, "quarters"), (3, "halves"))
+    advance((3, "halves"))
     if groups > 2:
         out_total = hop(0, out_total, groups)
     hidden_out = (residual + out_total.astype(F32)).astype(BF16)[None]
+    if whole_heads:
+        out_ring.hop()
     def low_grad(back, raw, factor, gain, total):
         return (
             factor * back * gain.reshape(1, local) - raw * factor**3 * per_row(total)
@@ -1128,44 +1168,24 @@
     normed_grad = dot(qkv_grad, qkv_w, (1, 1)).astype(BF16)
     order.token = after(order.token, qkv_w_grad, normed_grad)
     normed_grad = normed_grad.reshape(context, tokens, width)
-    normed_grad = context_sum([normed_grad[s] for s in range(context)])
-
-    class Ring:
-        def __init__(self, terms):
-            self.terms, self.size, self.slot = terms, terms.shape[0] // groups, 1
-            at = 1 % groups * self.size
-            self.total = terms[at : at + self.size]
-            self.coming = shift(self.total, 1)
-
-        def hop(self):
-            if self.slot < groups:
-                self.slot += 1
-                self.total = order.run(hop_add, [(self.terms, self.slot % groups)], self.coming)[0]
-                self.coming = shift(self.total, 1)
-
-        def whole(self):
-            while self.slot < groups:
-                self.hop()
-            return self.total
+    normed_own, normed_near, normed_far = context_terms([normed_grad[s] for s in range(context)])
 
     qkv_ring = Ring(qkv_w_grad)
-    advance((2, "finals"), (3, "quarters"))
+    advance((2, "finals"))
     if whole_heads:
-        ordered = take(
-            out_w_grad.reshape(per, HDIM, width), [(m // 2 ^ my_dp) * 2 + m % 2 for m in ring]
-        )
-        out_ring = Ring(ordered.reshape(local, width))
         out_ring.hop()
-        out_ring.hop()
+    advance((3, "quarters"))
     qkv_ring.hop()
-    advance((3, "finals"))
+    expert_grads = place([0])
     if whole_heads:
         mine_out = out_ring.whole()
         out_w_grad = mine_out.astype(F32) + swap(mine_out, "dp", 1).astype(F32)
-    expert_grads = place([0])
     qkv_ring.hop()
-    expert_grads = place([1, 2])
+    advance((3, "finals"))
+    expert_grads = place([1])
     qkv_w_grad = qkv_ring.whole()
+    normed_own = after(normed_own, order.token)
+    normed_grad = normed_own.astype(F32) + normed_near.astype(F32) + normed_far.astype(F32)
     parts = [
         lax.dynamic_slice_in_dim(normed_grad, (my_group - m) % groups * block, block, axis=1)
         for m in range(groups)
@@ -1176,11 +1196,15 @@
 
     mine_w = qkv_w_grad.reshape(context, rows, 3, 2, some)
     got = swap(mine_w, "dp", 1)
+    expert_grads = place([2])
+    mine_w = after(mine_w, order.token)
     mine_w = jnp.stack(
         [add_low(mine_w[:, :, :, i], got[:, :, :, 1 - i]) for i in range(2)], axis=3
     )
     pieces = [lax.dynamic_index_in_dim(mine_w, m, 0, keepdims=False) for m in members]
     pieces = [pieces[0]] + [swap(pieces[s], "context", s) for s in range(1, context)]
+    expert_grads = place([3])
+    pieces[0] = after(pieces[0], order.token)
     dense = take(jnp.stack(pieces), members)
     dense = jnp.where(my_dp == 0, dense, dense[:, :, :, ::-1]).astype(F32)
     dense = dense.reshape(context, rows, 3, per, HDIM).transpose(2, 1, 3, 0, 4)
@@ -1202,7 +1226,7 @@
         [attn_gain_grad[None], ffn_gain_grad[None], gains.reshape(2, width), router_grad], axis=0
     )
     small_grad = small_grad.reshape(4 + experts_all, groups, context, rows).transpose(1, 2, 0, 3)
-    small_grad = take(small_grad, ring)
+    small_grad = after(take(small_grad, ring), qkv_w_grad)
     small_grad = functools.reduce(
         lambda a, b: a + b,
         [small_grad[0]] + [shift(small_grad[s], -s) for s in range(1, groups)],
@@ -1211,7 +1235,6 @@
     got = swap(jnp.stack([small_grad[1], small_grad[3]]), "context", 1)
     small_grad = small_grad[0] + got[0] + swap(small_grad[2] + got[1], "context", 2)
     small_grad = small_grad + swap(small_grad, "dp", 1)
-    expert_grads = place([3])
     return (
         hidden_out,
         input_grad,

time: 1160 us -> 1110 us (0.957)
  waiting for transfers between devices: 384 us -> 328 us
    ppermute x56, waiting for transfers between devices: 205 us -> 153 us  [swap(): lax.ppermute(values, axis, [(i, i ^ bit) for i in range(lax.axis_size(axi...]
    unnamed x241 -> x229, local copies, waits for them, and re-layouts: 38.3 us -> 40.2 us
  transfers between devices with their start and end apart: 92 -> 92, of which waited for: 32 -> 32; matrix products, arithmetic and copies ran while one was open for 14% -> 15% of each run, Pallas kernels for 33% -> 32%
where the time goes in v4:
time: 1110 us; the launch traced here: 1100 us
  Pallas kernels  458 us (41%)
  waiting for transfers between devices  328 us (30%)
  starting transfers between devices  87.3 us (8%)
  local copies, waits for them, and re-layouts  87.1 us (8%)
  other arithmetic  64.8 us (6%)
  matrix products  45.6 us (4%)
  between operations  26.7 us (2%)
    pallas_call x8, Pallas kernels, run_rows(): pl.pallas_call(functools.partial(rows_kernel, first), grid_spec=pltpu.Pre...  185 us
    ppermute x30, waiting for transfers between devices, shift(): return lax.ppermute(values, 'expert', [(i, (i + by) % n) for i in range(n)])  172 us
    ppermute x56, waiting for transfers between devices, swap(): lax.ppermute(values, axis, [(i, i ^ bit) for i in range(lax.axis_size(axi...  153 us
    pallas_call x3, Pallas kernels, run_split(): pl.pallas_call(functools.partial(split_kernel, sizes), grid_spec=pltpu.Pr...  73.8 us
    pallas_call x9, Pallas kernels, add_pieces(): pl.pallas_call(functools.partial(add_kernel, picks, joined), grid=(parts,...  51.4 us
    dot_general x8, matrix products, dot(): lax.dot_general(left, right, (((contract[0],), (contract[1],)), ((), ()))...  45.6 us
    ppermute x30, starting transfers between devices, shift(): return lax.ppermute(values, 'expert', [(i, (i + by) % n) for i in range(n)])  43.5 us
    ppermute x56, starting transfers between devices, swap(): lax.ppermute(values, axis, [(i, i ^ bit) for i in range(lax.axis_size(axi...  43.1 us
  transfers between devices with their start and end apart: 92, of which 32 were waited for; matrix products, arithmetic and copies ran while one was open for 15% of the time, Pallas kernels for 32%

profile of v4, /device:TPU:0, one launch (start us, length us, event | category | flops | bytes accessed | tf_op | source)
XLA Modules:
  0.0 1097.8 jit_solution(3413952348781413895)
XLA Ops:
  28.4 5.5 collective-permute-done.2
  39.7 13.5 %collective-permute-done.18 = bf16[512,768]{1,0:T(8,128)(2,1)S(1)} collective-permute-done((bf16[512,768]{1,0:T(8,128)(2,1)S(1)}, bf16[512,768]{1,0:T(8,128)(2,1)S(1)}, u32[]{:S(2)}, u32[]{:S(2)}) %collective-permute-start.18) | collective-permute-done | bytes 786464 | tf_op jit(solution)/shard_map/ppermute | solution.py:233
  53.3 4.0 collective-permute-done.3
  58.0 4.6 collective-permute-done.10
  62.6 14.5 %collective-permute-done.4 = bf16[512,768]{1,0:T(8,128)(2,1)} collective-permute-done((bf16[512,768]{1,0:T(8,128)(2,1)S(1)}, bf16[512,768]{1,0:T(8,128)(2,1)}, u32[]{:S(2)}, u32[]{:S(2)}) %collective-permute-start.4) | collective-permute-done | bytes 786464 | tf_op jit(solution)/shard_map/ppermute | solution.py:238
  81.8 7.3 fusion.2
  90.9 5.8 collective-permute-done.5
  110.3 5.1 collective-permute-done.21
  116.8 9.5 fusion.25.q_ref.k_ref.v_ref
  130.7 4.4 collective-permute-start.23
  139.5 16.9 %attend.1 = (bf16[1024,512]{1,0:T(8,128)(2,1)}, bf16[1024,512]{1,0:T(8,128)(2,1)}, bf16[1024,512]{1,0:T(8,128)(2,1)}, bf16[1024,512]{1,0:T(8,128)(2,1)}, f32[4,1,1024]{2,1,0:T(1,128)}) custom-call(f32[1024,1536]{1,0:T(8,128)} %copy-done, f32[1024,1536]{1,0:T(8,128)} %copy-done, f32[1024,1536]{1,0:T(8,128)} %copy-done, f32[1024,1]{1,0:T(8,128)} %bitcast.314, ...), custom_call_target="tpu_custom_call" | custom-call | flops 5368709120 | bytes 10485760 | tf_op jit(solution)/shard_map/attend/pallas_call | solution.py:175
  165.3 4.4 collective-permute-done.24
  182.5 5.6 collective-permute-done.6
  189.3 8.5 collective-permute-done.7
  207.5 7.9 collective-permute-start.26
  216.0 22.4 %rows.8 = (bf16[256,2048]{1,0:T(8,128)(2,1)}, bf16[256,2048]{1,0:T(8,128)(2,1)}, f32[256,128]{1,0:T(8,128)}, f32[256,128]{1,0:T(8,128)}, bf16[2048,256]{1,0:T(8,...) custom-call(s32[1]{0:T(128)} %bitcast.65.at_ref, ...), custom_call_target="tpu_custom_call" | custom-call | flops 12884901888 | bytes 25165824 | tf_op jit(solution)/shard_map/rows/pallas_call | solution.py:372
  238.4 18.5 %collective-permute-done.26.x_ref = bf16[256,2048]{1,0:T(8,128)(2,1)S(1)} collective-permute-done((bf16[256,2048]{1,0:T(8,128)(2,1)S(1)}, bf16[256,2048]{1,0:T(8,128)(2,1)S(1)}, u32[]{:S(2)}, u32[]{:S(2)}) %collective-permute-start.26) | collective-permute-done | bytes 1048608 | tf_op jit(solution)/shard_map/ppermute | solution.py:238
  259.6 22.4 %rows.9 = (bf16[256,2048]{1,0:T(8,128)(2,1)}, bf16[256,2048]{1,0:T(8,128)(2,1)}, f32[256,128]{1,0:T(8,128)}, f32[256,128]{1,0:T(8,128)}, bf16[2048,256]{1,0:T(8,...) custom-call(s32[1]{0:T(128)} %bitcast.65.at_ref, ...), custom_call_target="tpu_custom_call" | custom-call | flops 12884901888 | bytes 25165824 | tf_op jit(solution)/shard_map/rows/pallas_call | solution.py:372
  286.4 22.4 %rows.10 = (bf16[256,2048]{1,0:T(8,128)(2,1)}, bf16[256,2048]{1,0:T(8,128)(2,1)}, f32[256,128]{1,0:T(8,128)}, f32[256,128]{1,0:T(8,128)}, bf16[2048,256]{1,0:T(8...) custom-call(s32[1]{0:T(128)} %bitcast.65.at_ref, ...), custom_call_target="tpu_custom_call" | custom-call | flops 12884901888 | bytes 25165824 | tf_op jit(solution)/shard_map/rows/pallas_call | solution.py:372
  315.6 23.4 %rows.11 = (bf16[512,2048]{1,0:T(8,128)(2,1)}, bf16[512,2048]{1,0:T(8,128)(2,1)}, f32[512,128]{1,0:T(8,128)}, f32[512,128]{1,0:T(8,128)}, bf16[2048,512]{1,0:T(8...) custom-call(s32[1]{0:T(128)} %bitcast.65.at_ref, ...), custom_call_target="tpu_custom_call" | custom-call | flops 12884901888 | bytes 12582912 | tf_op jit(solution)/shard_map/rows/pallas_call | solution.py:372
  339.0 20.2 %grads.1 = (bf16[2048,1024]{1,0:T(8,128)(2,1)}, bf16[2048,1024]{1,0:T(8,128)(2,1)}, bf16[1024,2048]{1,0:T(8,128)(2,1)}, f32[8,128]{1,0:T(8,128)}) custom-call(bf16[2048,256]{1,0:T(8,128)(2,1)} %get-tuple-element.189.refs_0_, bf16[2048,256]{1,0:T(8,128)(2,1)} %get-tuple-element.190.refs_1_, bf16[2048,512]{1,0:T(8,128)(2,1)} %get-tuple-element.191.refs_2_, ...), custom_call_target="tpu_custom_call" | custom-call | flops 12884901888 | bytes 29360128 | tf_op jit(solution)/shard_map/grads/pallas_call | solution.py:468
  359.2 22.6 %rows.12 = (bf16[256,2048]{1,0:T(8,128)(2,1)}, bf16[256,2048]{1,0:T(8,128)(2,1)}, f32[256,128]{1,0:T(8,128)}, f32[256,128]{1,0:T(8,128)}, bf16[2048,256]{1,0:T(8...) custom-call(s32[1]{0:T(128)} %bitcast.65.at_ref, ...), custom_call_target="tpu_custom_call" | custom-call | flops 12884901888 | bytes 25165824 | tf_op jit(solution)/shard_map/rows/pallas_call | solution.py:372
  381.8 23.3 %rows.13 = (bf16[512,2048]{1,0:T(8,128)(2,1)}, bf16[512,2048]{1,0:T(8,128)(2,1)}, f32[512,128]{1,0:T(8,128)}, f32[512,128]{1,0:T(8,128)}, bf16[2048,512]{1,0:T(8...) custom-call(s32[1]{0:T(128)} %bitcast.65.at_ref, ...), custom_call_target="tpu_custom_call" | custom-call | flops 12884901888 | bytes 12582912 | tf_op jit(solution)/shard_map/rows/pallas_call | solution.py:372
  405.2 24.8 %split.3 = (bf16[2,3,512,256]{3,2,1,0:T(8,128)(2,1)}, bf16[2,3,512,256]{3,2,1,0:T(8,128)(2,1)}, bf16[2,3,512,256]{3,2,1,0:T(8,128)(2,1)}, bf16[2,3,512,256]{3,2,...) custom-call(s32[3]{0:T(128)} %pad_add_fusion.1.bits_ref, ...), custom_call_target="tpu_custom_call" | custom-call | flops 12884901888 | bytes 29360128 | tf_op jit(solution)/shard_map/split/pallas_call | solution.py:611
  432.8 23.9 %rows.14 = (bf16[512,2048]{1,0:T(8,128)(2,1)}, bf16[512,2048]{1,0:T(8,128)(2,1)}, f32[512,128]{1,0:T(8,128)}, f32[512,128]{1,0:T(8,128)}, bf16[2048,512]{1,0:T(8...) custom-call(s32[1]{0:T(128)} %bitcast.65.at_ref, ...), custom_call_target="tpu_custom_call" | custom-call | flops 12884901888 | bytes 12582912 | tf_op jit(solution)/shard_map/rows/pallas_call | solution.py:372
  458.3 7.8 add_pieces.9
  469.8 24.3 %rows.15 = (bf16[512,2048]{1,0:T(8,128)(2,1)}, bf16[512,2048]{1,0:T(8,128)(2,1)}, f32[512,128]{1,0:T(8,128)}, f32[512,128]{1,0:T(8,128)}, bf16[2048,512]{1,0:T(8...) custom-call(s32[1]{0:T(128)} %bitcast.65.at_ref, ...), custom_call_target="tpu_custom_call" | custom-call | flops 12884901888 | bytes 12582912 | tf_op jit(solution)/shard_map/rows/pallas_call | solution.py:372
  494.1 3.6 hop.12
  499.3 24.5 %split.4 = (bf16[2,3,512,256]{3,2,1,0:T(8,128)(2,1)}, bf16[2,3,512,256]{3,2,1,0:T(8,128)(2,1)}, bf16[2,3,512,256]{3,2,1,0:T(8,128)(2,1)}, bf16[2,3,512,256]{3,2,...) custom-call(s32[3]{0:T(128)} %pad_add_fusion.1.bits_ref, ...), custom_call_target="tpu_custom_call" | custom-call | flops 12884901888 | bytes 29360128 | tf_op jit(solution)/shard_map/split/pallas_call | solution.py:611
  526.5 5.1 add_pieces.10
  534.1 3.6 hop.13
  537.7 24.5 %split.5 = (bf16[2,3,512,256]{3,2,1,0:T(8,128)(2,1)}, bf16[2,3,512,256]{3,2,1,0:T(8,128)(2,1)}, bf16[2,3,512,256]{3,2,1,0:T(8,128)(2,1)}, bf16[2,3,512,256]{3,2,...) custom-call(s32[3]{0:T(128)} %pad_add_fusion.1.bits_ref, ...), custom_call_target="tpu_custom_call" | custom-call | flops 12884901888 | bytes 29360128 | tf_op jit(solution)/shard_map/split/pallas_call | solution.py:611
  563.3 4.2 add_pieces.11
  573.5 3.7 collective-permute-start.49
  577.3 5.2 collective-permute-done.49
  582.6 6.7 collective-permute-done.50
  596.2 8.2 add_pieces.12
  604.5 11.1 %collective-permute-done.38.refs_2_ = bf16[256,2048]{1,0:T(8,128)(2,1)} collective-permute-done((bf16[256,2048]{1,0:T(8,128)(2,1)}, bf16[256,2048]{1,0:T(8,128)(2,1)}, u32[]{:S(2)}, u32[]{:S(2)}) %collective-permute-start.38) | collective-permute-done | bytes 1048608 | tf_op jit(solution)/shard_map/ppermute | solution.py:238
  625.3 34.7 %collective-permute-done.52 = bf16[256,2048]{1,0:T(8,128)(2,1)} collective-permute-done((bf16[256,2048]{1,0:T(8,128)(2,1)S(1)}, bf16[256,2048]{1,0:T(8,128)(2,1)}, u32[]{:S(2)}, u32[]{:S(2)}) %collective-permute-start.52) | collective-permute-done | bytes 1048608 | tf_op jit(solution)/shard_map/ppermute | solution.py:233
  662.8 3.6 hop.15
  667.7 5.9 convolution_convert_fusion.3.grad_ref
  673.6 20.4 %attend_back.1 = (f32[1024,512]{1,0:T(8,128)}, f32[1024,512]{1,0:T(8,128)}, bf16[1024,512]{1,0:T(8,128)(2,1)}, f32[1024,128]{1,0:T(8,128)}, f32[1024,128]{1,0:T(...) custom-call(bf16[1024,512]{1,0:T(8,128)(2,1)} %get-tuple-element.267.ql_ref, ...), custom_call_target="tpu_custom_call" | custom-call | flops 10737418240 | bytes 15728640 | tf_op jit(solution)/shard_map/attend_back/pallas_call | solution.py:203
  698.5 4.6 fusion.5
  706.6 22.1 %collective-permute-done.46.refs_2_ = bf16[2,3,512,256]{3,2,1,0:T(8,128)(2,1)} collective-permute-done((bf16[2,3,512,256]{3,2,1,0:T(8,128)(2,1)}, bf16[2,3,512,256]{3,2,1,0:T(8,128)(2,1)}, u32[]{:S(2)}, u32[]{:S(2)}) %collective-permute-start.46) | collective-permute-done | bytes 1572896 | tf_op jit(solution)/shard_map/ppermute | solution.py:233
  729.2 5.1 add_pieces.13
  739.6 5.3 subtract_convert_fusion.1
  745.0 8.9 convolution_convert_fusion.refs_0_
  757.3 11.8 %convolution_convert_fusion.1 = bf16[1024,2048]{1,0:T(8,128)(2,1)} fusion(bf16[1024,512]{1,0:T(8,128)(2,1)} %get-tuple-element.297, bf16[1024,512]{1,0:T(8,128)(2,1)} %get-tuple-element.378, bf16[1024,512]{1,0:T(8,128)(2,1)} %get-tuple-element.377, bf16[512,1536]{1,0:T(8,128)(2,1)} %copy-done.71, bf16[512,1536]{1,0:T(8,128)(2,1)} %slice_dynamic-update-slice_fusion.6, ...), kind=kOutput, calls=%fused_computation.17 | convolution fusion | flops 6479151104 | bytes 13631488 | tf_op jit(solution)/shard_map/dot_general | solution.py:24
  773.8 7.7 add_pieces.14
  788.5 4.1 add_pieces.15
  799.9 46.0 %collective-permute-done.65.refs_1_ = bf16[128,2048]{1,0:T(8,128)(2,1)S(1)} collective-permute-done((bf16[128,2048]{1,0:T(8,128)(2,1)S(1)}, bf16[128,2048]{1,0:T(8,128)(2,1)S(1)}, u32[]{:S(2)}, u32[]{:S(2)}) %collective-permute-start.65) | collective-permute-done | bytes 524320 | tf_op jit(solution)/shard_map/ppermute | solution.py:238
  848.7 5.1 add_pieces.16
  856.8 3.9 collective-permute-start.68
  862.4 14.0 %place.1 = (f32[4,2048,1024]{2,1,0:T(8,128)}, f32[4,2048,1024]{2,1,0:T(8,128)}, f32[4,1024,2048]{2,1,0:T(8,128)}, f32[8,128]{1,0:T(8,128)}) custom-call(bf16[2048,1024]{1,0:T(8,128)(2,1)} %get-tuple-element.370.refs_0_, bf16[2048,1024]{1,0:T(8,128)(2,1)} %get-tuple-element.371.refs_1_, bf16[1024,2048]{1,0:T(8,128)(2,1)} %get-tuple-element.372.refs_2_, ...), custom_call_target="tpu_custom_call" | custom-call | bytes 37748736 | tf_op jit(solution)/shard_map/place/pallas_call | solution.py:521
  876.3 27.9 %collective-permute-done.69.refs_1_ = bf16[128,2048]{1,0:T(8,128)(2,1)} collective-permute-done((bf16[128,2048]{1,0:T(8,128)(2,1)}, bf16[128,2048]{1,0:T(8,128)(2,1)}, u32[]{:S(2)}, u32[]{:S(2)}) %collective-permute-start.69) | collective-permute-done | bytes 524320 | tf_op jit(solution)/shard_map/ppermute | solution.py:238
  910.1 4.1 add_pieces.17
  918.0 4.0 collective-permute-done.73
  925.2 13.8 %place_pieces.3 = (f32[4,2048,1024]{2,1,0:T(8,128)}, f32[4,2048,1024]{2,1,0:T(8,128)}, f32[4,1024,2048]{2,1,0:T(8,128)}, f32[8,128]{1,0:T(8,128)}) custom-call(bf16[8,2,3,512,256]{4,3,2,1,0:T(8,128)(2,1)} %bitcast.300, f32[8,128]{1,0:T(8,128)} %get-tuple-element.327.refs_1_, ...), custom_call_target="tpu_custom_call", output_to_operand_aliasing={{0}: (2, {}), {1}: (3, {}), {2}: (4, {})} | custom-call | bytes 37748736 | tf_op jit(solution)/shard_map/place_pieces/pallas_call | solution.py:788
  939.1 17.9 %collective-permute-done.70.refs_1_ = bf16[512,1536]{1,0:T(8,128)(2,1)} collective-permute-done((bf16[512,1536]{1,0:T(8,128)(2,1)}, bf16[512,1536]{1,0:T(8,128)(2,1)}, u32[]{:S(2)}, u32[]{:S(2)}) %collective-permute-start.70) | collective-permute-done | bytes 1572896 | tf_op jit(solution)/shard_map/ppermute | solution.py:238
  981.0 13.9 %place_pieces.4 = (f32[4,2048,1024]{2,1,0:T(8,128)}, f32[4,2048,1024]{2,1,0:T(8,128)}, f32[4,1024,2048]{2,1,0:T(8,128)}, f32[8,128]{1,0:T(8,128)}) custom-call(bf16[8,2,3,512,256]{4,3,2,1,0:T(8,128)(2,1)} %bitcast.301, f32[8,128]{1,0:T(8,128)} %get-tuple-element.332.refs_1_, ...), custom_call_target="tpu_custom_call", output_to_operand_aliasing={{0}: (2, {}), {1}: (3, {}), {2}: (4, {})} | custom-call | bytes 37748736 | tf_op jit(solution)/shard_map/place_pieces/pallas_call | solution.py:788
  1010.2 33.4 %collective-permute-done.80 = f32[20,128]{1,0:T(8,128)S(1)} collective-permute-done((f32[20,128]{1,0:T(8,128)S(1)}, f32[20,128]{1,0:T(8,128)S(1)}, u32[]{:S(2)}, u32[]{:S(2)}) %collective-permute-start.80) | collective-permute-done | bytes 10272 | tf_op jit(solution)/shard_map/ppermute | solution.py:233
  1044.2 13.8 %place_pieces.5 = (f32[4,2048,1024]{2,1,0:T(8,128)}, f32[4,2048,1024]{2,1,0:T(8,128)}, f32[4,1024,2048]{2,1,0:T(8,128)}, f32[8,128]{1,0:T(8,128)}) custom-call(bf16[8,2,3,512,256]{4,3,2,1,0:T(8,128)(2,1)} %bitcast.302, f32[8,128]{1,0:T(8,128)} %get-tuple-element.340.refs_1_, ...), custom_call_target="tpu_custom_call", output_to_operand_aliasing={{0}: (2, {}), {1}: (3, {}), {2}: (4, {})} | custom-call | bytes 37748736 | tf_op jit(solution)/shard_map/place_pieces/pallas_call | solution.py:788
  1063.2 9.0 collective-permute-done.83
  1072.2 7.5 collective-permute-done.84
  (582 shorter events, 248.5 us)
Async XLA Ops:
  7.2 149.3 %all-gather.12.cloned.1.call-start = ((), (), s32[]{:S(2)}) async-start(), calls=%async_computation.1 | async-start | bytes 2621440 | tf_op jit(solution)/shard_map/all_gather | solution.py:909
  34.4 18.9 %collective-permute-start.18 = (bf16[512,768]{1,0:T(8,128)(2,1)S(1)}, bf16[512,768]{1,0:T(8,128)(2,1)S(1)}, u32[]{:S(2)}, u32[]{:S(2)}) collective-permute-start(bf16[512,768]{1,0:T(8,128)(2,1)S(1)} %bitcast.308), channel_id=1, source_target_pairs={{0,1},{1,0},{2,3},{3,2},{4,5},{5,4},{6,7},{7,6},{8,9},{9,8},{10,11... | collective-permute-start | bytes 2359304 | tf_op jit(solution)/shard_map/ppermute | solution.py:233
  37.0 20.3 %collective-permute-start.3 = (bf16[512,768]{1,0:T(8,128)(2,1)S(1)}, bf16[512,768]{1,0:T(8,128)(2,1)S(1)}, u32[]{:S(2)}, u32[]{:S(2)}) collective-permute-start(bf16[512,768]{1,0:T(8,128)(2,1)S(1)} %bitcast.310), channel_id=1, source_target_pairs={{0,8},{8,16},{16,24},{24,0},{1,9},{9,17},{17,25},{25,1},{2,10},{10... | collective-permute-start | bytes 2359304 | tf_op jit(solution)/shard_map/ppermute | solution.py:238
  38.5 24.1 %collective-permute-start.10 = (bf16[256,2048]{1,0:T(8,128)(2,1)S(1)}, bf16[256,2048]{1,0:T(8,128)(2,1)S(1)}, u32[]{:S(2)}, u32[]{:S(2)}) collective-permute-start(bf16[256,2048]{1,0:T(8,128)(2,1)S(1)} %add_bitcast_fusion), channel_id=1, source_target_pairs={{0,4},{2,6},{4,0},{6,2},{1,5},{3,7},{5,1},{7,3},{8,12},{10,14},{12... | collective-permute-start | bytes 3145736 | tf_op jit(solution)/shard_map/ppermute | solution.py:233
  39.7 40.8 %collective-permute-start.9 = (bf16[256,2048]{1,0:T(8,128)(2,1)S(1)}, bf16[256,2048]{1,0:T(8,128)(2,1)S(1)}, u32[]{:S(2)}, u32[]{:S(2)}) collective-permute-start(bf16[256,2048]{1,0:T(8,128)(2,1)S(1)} %add_bitcast_fusion), channel_id=1, source_target_pairs={{0,2},{2,0},{4,6},{6,4},{1,3},{3,1},{5,7},{7,5},{8,10},{10,8},{12,... | collective-permute-start | bytes 3145736 | tf_op jit(solution)/shard_map/ppermute | solution.py:233
  57.4 23.0 %collective-permute-start.19 = (bf16[512,768]{1,0:T(8,128)(2,1)S(1)}, bf16[512,768]{1,0:T(8,128)(2,1)S(1)}, u32[]{:S(2)}, u32[]{:S(2)}) collective-permute-start(bf16[512,768]{1,0:T(8,128)(2,1)S(1)} %collective-permute-done.3), channel_id=1, source_target_pairs={{0,1},{1,0},{2,3},{3,2},{4,5},{5,4},{6,7},{7,6},{8,9},{9,8},{10,11... | collective-permute-start | bytes 2359304 | tf_op jit(solution)/shard_map/ppermute | solution.py:233
  57.9 19.2 %collective-permute-start.4 = (bf16[512,768]{1,0:T(8,128)(2,1)S(1)}, bf16[512,768]{1,0:T(8,128)(2,1)}, u32[]{:S(2)}, u32[]{:S(2)}) collective-permute-start(bf16[512,768]{1,0:T(8,128)(2,1)S(1)} %collective-permute-done.3), channel_id=1, source_target_pairs={{0,8},{8,16},{16,24},{24,0},{1,9},{9,17},{17,25},{25,1},{2,10},{10... | collective-permute-start | bytes 2359304 | tf_op jit(solution)/shard_map/ppermute | solution.py:238
  77.1 24.4 %collective-permute-start.20 = (bf16[512,768]{1,0:T(8,128)(2,1)}, bf16[512,768]{1,0:T(8,128)(2,1)}, u32[]{:S(2)}, u32[]{:S(2)}) collective-permute-start(bf16[512,768]{1,0:T(8,128)(2,1)} %collective-permute-done.4), channel_id=1, source_target_pairs={{0,1},{1,0},{2,3},{3,2},{4,5},{5,4},{6,7},{7,6},{8,9},{9,8},{10,11... | collective-permute-start | bytes 2359304 | tf_op jit(solution)/shard_map/ppermute | solution.py:233
  78.6 18.1 %collective-permute-start.5 = (bf16[512,768]{1,0:T(8,128)(2,1)}, bf16[512,768]{1,0:T(8,128)(2,1)S(1)}, u32[]{:S(2)}, u32[]{:S(2)}) collective-permute-start(bf16[512,768]{1,0:T(8,128)(2,1)} %collective-permute-done.4), channel_id=1, source_target_pairs={{0,8},{8,16},{16,24},{24,0},{1,9},{9,17},{17,25},{25,1},{2,10},{10... | collective-permute-start | bytes 2359304 | tf_op jit(solution)/shard_map/ppermute | solution.py:238
  99.7 160.0 %all-gather.10.cloned.1.call-start = ((), (), s32[]{:S(2)}) async-start(), calls=%async_computation | async-start | bytes 5242880 | tf_op jit(solution)/shard_map/all_gather | solution.py:910
  136.2 726.2 %all-reduce.4.cloned.1.call-start = ((), (), s32[]{:S(2)}) async-start(), calls=%async_computation.5 | async-start | bytes 25165824 | tf_op jit(solution)/shard_map/psum | solution.py:1040
  173.0 29.9 %collective-permute-start.25 = (bf16[256,2048]{1,0:T(8,128)(2,1)}, bf16[256,2048]{1,0:T(8,128)(2,1)}, u32[]{:S(2)}, u32[]{:S(2)}) collective-permute-start(bf16[256,2048]{1,0:T(8,128)(2,1)} %fusion.21), channel_id=1, source_target_pairs={{0,4},{2,6},{4,0},{6,2},{1,5},{3,7},{5,1},{7,3},{8,12},{10,14},{12... | collective-permute-start | bytes 3145736 | tf_op jit(solution)/shard_map/ppermute | solution.py:233
  177.2 20.6 %collective-permute-start.7 = (s32[256,8]{1,0:T(8,128)S(1)}, s32[256,8]{1,0:T(8,128)S(1)}, u32[]{:S(2)}, u32[]{:S(2)}) collective-permute-start(s32[256,8]{1,0:T(8,128)S(1)} %add_bitcast_fusion.1), channel_id=1, source_target_pairs={{0,16},{8,24},{16,0},{24,8},{1,17},{9,25},{17,1},{25,9},{2,18},{10... | collective-permute-start | bytes 24584 | tf_op jit(solution)/shard_map/ppermute | solution.py:238
  177.8 21.1 %collective-permute-start.8 = (s32[256,8]{1,0:T(8,128)S(1)}, s32[256,8]{1,0:T(8,128)S(1)}, u32[]{:S(2)}, u32[]{:S(2)}) collective-permute-start(s32[256,8]{1,0:T(8,128)S(1)} %add_bitcast_fusion.1), channel_id=1, source_target_pairs={{0,24},{8,0},{16,8},{24,16},{1,25},{9,1},{17,9},{25,17},{2,26},{10... | collective-permute-start | bytes 24584 | tf_op jit(solution)/shard_map/ppermute | solution.py:238
  207.5 49.4 %collective-permute-start.26 = (bf16[256,2048]{1,0:T(8,128)(2,1)S(1)}, bf16[256,2048]{1,0:T(8,128)(2,1)S(1)}, u32[]{:S(2)}, u32[]{:S(2)}) collective-permute-start(bf16[256,2048]{1,0:T(8,128)(2,1)S(1)} %multiply_convert_fusion.x_ref), channel_id=1, source_target_pairs={{0,8},{8,16},{16,24},{24,0},{1,9},{9,17},{17,25},{25,1},{2,10},{10... | collective-permute-start | bytes 3145736 | tf_op jit(solution)/shard_map/ppermute | solution.py:238
  256.9 29.3 %collective-permute-start.27 = (bf16[256,2048]{1,0:T(8,128)(2,1)S(1)}, bf16[256,2048]{1,0:T(8,128)(2,1)S(1)}, u32[]{:S(2)}, u32[]{:S(2)}) collective-permute-start(bf16[256,2048]{1,0:T(8,128)(2,1)S(1)} %collective-permute-done.26.x_ref), channel_id=1, source_target_pairs={{0,8},{8,16},{16,24},{24,0},{1,9},{9,17},{17,25},{25,1},{2,10},{10... | collective-permute-start | bytes 3145736 | tf_op jit(solution)/shard_map/ppermute | solution.py:238
  286.2 27.9 %collective-permute-start.28 = (bf16[256,2048]{1,0:T(8,128)(2,1)S(1)}, bf16[256,2048]{1,0:T(8,128)(2,1)S(1)}, u32[]{:S(2)}, u32[]{:S(2)}) collective-permute-start(bf16[256,2048]{1,0:T(8,128)(2,1)S(1)} %collective-permute-done.27), channel_id=1, source_target_pairs={{0,8},{8,16},{16,24},{24,0},{1,9},{9,17},{17,25},{25,1},{2,10},{10... | collective-permute-start | bytes 3145736 | tf_op jit(solution)/shard_map/ppermute | solution.py:238
  405.1 520.1 %all-gather.14.cloned.1.call-start = ((), (), s32[]{:S(2)}) async-start(), calls=%async_computation.2 | async-start | bytes 14155776 | tf_op jit(solution)/shard_map/all_gather | solution.py:719
  430.0 26.7 %collective-permute-start.29 = (bf16[2,3,512,256]{3,2,1,0:T(8,128)(2,1)}, bf16[2,3,512,256]{3,2,1,0:T(8,128)(2,1)S(1)}, u32[]{:S(2)}, u32[]{:S(2)}) collective-permute-start(bf16[2,3,512,256]{3,2,1,0:T(8,128)(2,1)} %get-tuple-element.209), channel_id=1, source_target_pairs={{0,2},{2,0},{4,6},{6,4},{1,3},{3,1},{5,7},{7,5},{8,10},{10,8},{12,... | collective-permute-start | bytes 4718600 | tf_op jit(solution)/shard_map/ppermute | solution.py:233
  430.1 26.6 %collective-permute-start.30 = (bf16[2,3,512,256]{3,2,1,0:T(8,128)(2,1)}, bf16[2,3,512,256]{3,2,1,0:T(8,128)(2,1)S(1)}, u32[]{:S(2)}, u32[]{:S(2)}) collective-permute-start(bf16[2,3,512,256]{3,2,1,0:T(8,128)(2,1)} %get-tuple-element.210), channel_id=1, source_target_pairs={{0,2},{2,0},{4,6},{6,4},{1,3},{3,1},{5,7},{7,5},{8,10},{10,8},{12,... | collective-permute-start | bytes 4718600 | tf_op jit(solution)/shard_map/ppermute | solution.py:233
  430.6 26.1 %collective-permute-start.31 = (bf16[2,3,512,256]{3,2,1,0:T(8,128)(2,1)}, bf16[2,3,512,256]{3,2,1,0:T(8,128)(2,1)}, u32[]{:S(2)}, u32[]{:S(2)}) collective-permute-start(bf16[2,3,512,256]{3,2,1,0:T(8,128)(2,1)} %get-tuple-element.211), channel_id=1, source_target_pairs={{0,2},{2,0},{4,6},{6,4},{1,3},{3,1},{5,7},{7,5},{8,10},{10,8},{12,... | collective-permute-start | bytes 4718600 | tf_op jit(solution)/shard_map/ppermute | solution.py:233
  430.6 26.1 %collective-permute-start.32 = (bf16[2,3,512,256]{3,2,1,0:T(8,128)(2,1)}, bf16[2,3,512,256]{3,2,1,0:T(8,128)(2,1)}, u32[]{:S(2)}, u32[]{:S(2)}) collective-permute-start(bf16[2,3,512,256]{3,2,1,0:T(8,128)(2,1)} %get-tuple-element.212), channel_id=1, source_target_pairs={{0,2},{2,0},{4,6},{6,4},{1,3},{3,1},{5,7},{7,5},{8,10},{10,8},{12,... | collective-permute-start | bytes 4718600 | tf_op jit(solution)/shard_map/ppermute | solution.py:233
  432.5 61.6 %collective-permute-start.34 = (bf16[256,2048]{1,0:T(8,128)(2,1)}, bf16[256,2048]{1,0:T(8,128)(2,1)}, u32[]{:S(2)}, u32[]{:S(2)}) collective-permute-start(bf16[256,2048]{1,0:T(8,128)(2,1)} %add_convert_fusion.1), channel_id=1, source_target_pairs={{0,8},{8,16},{16,24},{24,0},{1,9},{9,17},{17,25},{25,1},{2,10},{10... | collective-permute-start | bytes 3145736 | tf_op jit(solution)/shard_map/ppermute | solution.py:238
  466.1 57.7 %collective-permute-start.36 = (bf16[2,3,512,256]{3,2,1,0:T(8,128)(2,1)}, bf16[2,3,512,256]{3,2,1,0:T(8,128)(2,1)S(1)}, u32[]{:S(2)}, u32[]{:S(2)}) collective-permute-start(bf16[2,3,512,256]{3,2,1,0:T(8,128)(2,1)} %get-tuple-element.230), channel_id=1, source_target_pairs={{0,1},{1,0},{2,3},{3,2},{4,5},{5,4},{6,7},{7,6},{8,9},{9,8},{10,11... | collective-permute-start | bytes 4718600 | tf_op jit(solution)/shard_map/ppermute | solution.py:233
  468.0 57.4 %collective-permute-start.37 = (bf16[2,3,512,256]{3,2,1,0:T(8,128)(2,1)}, bf16[2,3,512,256]{3,2,1,0:T(8,128)(2,1)S(1)}, u32[]{:S(2)}, u32[]{:S(2)}) collective-permute-start(bf16[2,3,512,256]{3,2,1,0:T(8,128)(2,1)} %get-tuple-element.231), channel_id=1, source_target_pairs={{0,4},{2,6},{4,0},{6,2},{1,5},{3,7},{5,1},{7,3},{8,12},{10,14},{12... | collective-permute-start | bytes 4718600 | tf_op jit(solution)/shard_map/ppermute | solution.py:233
  497.7 36.3 %collective-permute-start.35 = (bf16[256,2048]{1,0:T(8,128)(2,1)}, bf16[256,2048]{1,0:T(8,128)(2,1)}, u32[]{:S(2)}, u32[]{:S(2)}) collective-permute-start(bf16[256,2048]{1,0:T(8,128)(2,1)} %get-tuple-element.227), channel_id=1, source_target_pairs={{0,8},{8,16},{16,24},{24,0},{1,9},{9,17},{17,25},{25,1},{2,10},{10... | collective-permute-start | bytes 3145736 | tf_op jit(solution)/shard_map/ppermute | solution.py:238
  531.6 30.5 %collective-permute-start.43 = (bf16[3,512,256]{2,1,0:T(8,128)(2,1)}, bf16[3,512,256]{2,1,0:T(8,128)(2,1)S(1)}, u32[]{:S(2)}, u32[]{:S(2)}) collective-permute-start(bf16[3,512,256]{2,1,0:T(8,128)(2,1)} %get-tuple-element.252), channel_id=1, source_target_pairs={{0,4},{2,6},{4,0},{6,2},{1,5},{3,7},{5,1},{7,3},{8,12},{10,14},{12... | collective-permute-start | bytes 2359304 | tf_op jit(solution)/shard_map/ppermute | solution.py:233
  534.1 28.1 %collective-permute-start.44 = (bf16[3,512,256]{2,1,0:T(8,128)(2,1)}, bf16[3,512,256]{2,1,0:T(8,128)(2,1)S(1)}, u32[]{:S(2)}, u32[]{:S(2)}) collective-permute-start(bf16[3,512,256]{2,1,0:T(8,128)(2,1)} %get-tuple-element.253), channel_id=1, source_target_pairs={{0,1},{1,0},{2,3},{3,2},{4,5},{5,4},{6,7},{7,6},{8,9},{9,8},{10,11... | collective-permute-start | bytes 2359304 | tf_op jit(solution)/shard_map/ppermute | solution.py:233
  567.6 413.5 %all-gather.16.cloned.1.call-start = ((), (), s32[]{:S(2)}) async-start(), calls=%async_computation.3 | async-start | bytes 14155776 | tf_op jit(solution)/shard_map/all_gather | solution.py:719
  571.1 23.3 %collective-permute-start.39 = (bf16[2,3,512,256]{3,2,1,0:T(8,128)(2,1)}, bf16[2,3,512,256]{3,2,1,0:T(8,128)(2,1)S(1)}, u32[]{:S(2)}, u32[]{:S(2)}) collective-permute-start(bf16[2,3,512,256]{3,2,1,0:T(8,128)(2,1)} %get-tuple-element.246), channel_id=1, source_target_pairs={{0,2},{2,0},{4,6},{6,4},{1,3},{3,1},{5,7},{7,5},{8,10},{10,8},{12,... | collective-permute-start | bytes 4718600 | tf_op jit(solution)/shard_map/ppermute | solution.py:233
  571.2 23.2 %collective-permute-start.40 = (bf16[2,3,512,256]{3,2,1,0:T(8,128)(2,1)}, bf16[2,3,512,256]{3,2,1,0:T(8,128)(2,1)S(1)}, u32[]{:S(2)}, u32[]{:S(2)}) collective-permute-start(bf16[2,3,512,256]{3,2,1,0:T(8,128)(2,1)} %get-tuple-element.247), channel_id=1, source_target_pairs={{0,2},{2,0},{4,6},{6,4},{1,3},{3,1},{5,7},{7,5},{8,10},{10,8},{12,... | collective-permute-start | bytes 4718600 | tf_op jit(solution)/shard_map/ppermute | solution.py:233
  571.7 22.8 %collective-permute-start.41 = (bf16[2,3,512,256]{3,2,1,0:T(8,128)(2,1)}, bf16[2,3,512,256]{3,2,1,0:T(8,128)(2,1)}, u32[]{:S(2)}, u32[]{:S(2)}) collective-permute-start(bf16[2,3,512,256]{3,2,1,0:T(8,128)(2,1)} %get-tuple-element.248), channel_id=1, source_target_pairs={{0,2},{2,0},{4,6},{6,4},{1,3},{3,1},{5,7},{7,5},{8,10},{10,8},{12,... | collective-permute-start | bytes 4718600 | tf_op jit(solution)/shard_map/ppermute | solution.py:233
  571.8 22.7 %collective-permute-start.42 = (bf16[2,3,512,256]{3,2,1,0:T(8,128)(2,1)}, bf16[2,3,512,256]{3,2,1,0:T(8,128)(2,1)}, u32[]{:S(2)}, u32[]{:S(2)}) collective-permute-start(bf16[2,3,512,256]{3,2,1,0:T(8,128)(2,1)} %get-tuple-element.249), channel_id=1, source_target_pairs={{0,2},{2,0},{4,6},{6,4},{1,3},{3,1},{5,7},{7,5},{8,10},{10,8},{12,... | collective-permute-start | bytes 4718600 | tf_op jit(solution)/shard_map/ppermute | solution.py:233
  590.0 25.6 %collective-permute-start.38 = (bf16[256,2048]{1,0:T(8,128)(2,1)}, bf16[256,2048]{1,0:T(8,128)(2,1)}, u32[]{:S(2)}, u32[]{:S(2)}) collective-permute-start(bf16[256,2048]{1,0:T(8,128)(2,1)} %get-tuple-element.244), channel_id=1, source_target_pairs={{0,8},{8,16},{16,24},{24,0},{1,9},{9,17},{17,25},{25,1},{2,10},{10... | collective-permute-start | bytes 3145736 | tf_op jit(solution)/shard_map/ppermute | solution.py:238
  623.5 36.5 %collective-permute-start.52 = (bf16[256,2048]{1,0:T(8,128)(2,1)S(1)}, bf16[256,2048]{1,0:T(8,128)(2,1)}, u32[]{:S(2)}, u32[]{:S(2)}) collective-permute-start(bf16[256,2048]{1,0:T(8,128)(2,1)S(1)} %get-tuple-element.373), channel_id=1, source_target_pairs={{0,4},{2,6},{4,0},{6,2},{1,5},{3,7},{5,1},{7,3},{8,12},{10,14},{12... | collective-permute-start | bytes 3145736 | tf_op jit(solution)/shard_map/ppermute | solution.py:233
  625.3 36.9 %collective-permute-start.33 = (bf16[256,2048]{1,0:T(8,128)(2,1)}, bf16[256,2048]{1,0:T(8,128)(2,1)}, u32[]{:S(2)}, u32[]{:S(2)}) collective-permute-start(bf16[256,2048]{1,0:T(8,128)(2,1)} %add_convert_fusion.2), channel_id=1, source_target_pairs={{0,8},{8,16},{16,24},{24,0},{1,9},{9,17},{17,25},{25,1},{2,10},{10... | collective-permute-start | bytes 3145736 | tf_op jit(solution)/shard_map/ppermute | solution.py:238
  625.3 41.1 %collective-permute-start.51 = (bf16[256,2048]{1,0:T(8,128)(2,1)S(1)}, bf16[256,2048]{1,0:T(8,128)(2,1)}, u32[]{:S(2)}, u32[]{:S(2)}) collective-permute-start(bf16[256,2048]{1,0:T(8,128)(2,1)S(1)} %get-tuple-element.373), channel_id=1, source_target_pairs={{0,2},{2,0},{4,6},{6,4},{1,3},{3,1},{5,7},{7,5},{8,10},{10,8},{12,... | collective-permute-start | bytes 3145736 | tf_op jit(solution)/shard_map/ppermute | solution.py:233
  660.2 93.7 %collective-permute-start.55 = (bf16[2,3,512,256]{3,2,1,0:T(8,128)(2,1)}, bf16[2,3,512,256]{3,2,1,0:T(8,128)(2,1)}, u32[]{:S(2)}, u32[]{:S(2)}) collective-permute-start(bf16[2,3,512,256]{3,2,1,0:T(8,128)(2,1)} %get-tuple-element.286), channel_id=1, source_target_pairs={{0,2},{2,0},{4,6},{6,4},{1,3},{3,1},{5,7},{7,5},{8,10},{10,8},{12,... | collective-permute-start | bytes 4718600 | tf_op jit(solution)/shard_map/ppermute | solution.py:233
  660.7 68.0 %collective-permute-start.46 = (bf16[2,3,512,256]{3,2,1,0:T(8,128)(2,1)}, bf16[2,3,512,256]{3,2,1,0:T(8,128)(2,1)}, u32[]{:S(2)}, u32[]{:S(2)}) collective-permute-start(bf16[2,3,512,256]{3,2,1,0:T(8,128)(2,1)} %get-tuple-element.265), channel_id=1, source_target_pairs={{0,1},{1,0},{2,3},{3,2},{4,5},{5,4},{6,7},{7,6},{8,9},{9,8},{10,11... | collective-permute-start | bytes 4718600 | tf_op jit(solution)/shard_map/ppermute | solution.py:233
  662.2 66.6 %collective-permute-start.47 = (bf16[2,3,512,256]{3,2,1,0:T(8,128)(2,1)}, bf16[2,3,512,256]{3,2,1,0:T(8,128)(2,1)}, u32[]{:S(2)}, u32[]{:S(2)}) collective-permute-start(bf16[2,3,512,256]{3,2,1,0:T(8,128)(2,1)} %get-tuple-element.266), channel_id=1, source_target_pairs={{0,4},{2,6},{4,0},{6,2},{1,5},{3,7},{5,1},{7,3},{8,12},{10,14},{12... | collective-permute-start | bytes 4718600 | tf_op jit(solution)/shard_map/ppermute | solution.py:233
  666.4 67.9 %collective-permute-start.45 = (bf16[256,2048]{1,0:T(8,128)(2,1)}, bf16[256,2048]{1,0:T(8,128)(2,1)}, u32[]{:S(2)}, u32[]{:S(2)}) collective-permute-start(bf16[256,2048]{1,0:T(8,128)(2,1)} %get-tuple-element.262), channel_id=1, source_target_pairs={{0,8},{8,16},{16,24},{24,0},{1,9},{9,17},{17,25},{25,1},{2,10},{10... | collective-permute-start | bytes 3145736 | tf_op jit(solution)/shard_map/ppermute | solution.py:238
  703.4 34.6 %collective-permute-start.60 = (f32[2,4,256]{2,1,0:T(4,128)S(1)}, f32[2,4,256]{2,1,0:T(4,128)S(1)}, u32[]{:S(2)}, u32[]{:S(2)}) collective-permute-start(f32[2,4,256]{2,1,0:T(4,128)S(1)} %maximum_add_fusion.3), channel_id=1, source_target_pairs={{0,4},{2,6},{4,0},{6,2},{1,5},{3,7},{5,1},{7,3},{8,12},{10,14},{12... | collective-permute-start | bytes 24584 | tf_op jit(solution)/shard_map/ppermute | solution.py:233
  728.7 26.7 %collective-permute-start.56 = (bf16[2,3,512,256]{3,2,1,0:T(8,128)(2,1)}, bf16[2,3,512,256]{3,2,1,0:T(8,128)(2,1)}, u32[]{:S(2)}, u32[]{:S(2)}) collective-permute-start(bf16[2,3,512,256]{3,2,1,0:T(8,128)(2,1)} %get-tuple-element.287), channel_id=1, source_target_pairs={{0,2},{2,0},{4,6},{6,4},{1,3},{3,1},{5,7},{7,5},{8,10},{10,8},{12,... | collective-permute-start | bytes 4718600 | tf_op jit(solution)/shard_map/ppermute | solution.py:233
  728.8 27.2 %collective-permute-start.57 = (bf16[2,3,512,256]{3,2,1,0:T(8,128)(2,1)}, bf16[2,3,512,256]{3,2,1,0:T(8,128)(2,1)}, u32[]{:S(2)}, u32[]{:S(2)}) collective-permute-start(bf16[2,3,512,256]{3,2,1,0:T(8,128)(2,1)} %get-tuple-element.288), channel_id=1, source_target_pairs={{0,2},{2,0},{4,6},{6,4},{1,3},{3,1},{5,7},{7,5},{8,10},{10,8},{12,... | collective-permute-start | bytes 4718600 | tf_op jit(solution)/shard_map/ppermute | solution.py:233
  734.3 39.5 %collective-permute-start.58 = (bf16[2,3,512,256]{3,2,1,0:T(8,128)(2,1)}, bf16[2,3,512,256]{3,2,1,0:T(8,128)(2,1)}, u32[]{:S(2)}, u32[]{:S(2)}) collective-permute-start(bf16[2,3,512,256]{3,2,1,0:T(8,128)(2,1)} %get-tuple-element.289), channel_id=1, source_target_pairs={{0,2},{2,0},{4,6},{6,4},{1,3},{3,1},{5,7},{7,5},{8,10},{10,8},{12,... | collective-permute-start | bytes 4718600 | tf_op jit(solution)/shard_map/ppermute | solution.py:233
  738.0 47.2 %collective-permute-start.64 = (bf16[128,2048]{1,0:T(8,128)(2,1)S(1)}, bf16[128,2048]{1,0:T(8,128)(2,1)}, u32[]{:S(2)}, u32[]{:S(2)}) collective-permute-start(bf16[128,2048]{1,0:T(8,128)(2,1)S(1)} %bitcast.323), channel_id=1, source_target_pairs={{0,8},{8,16},{16,24},{24,0},{1,9},{9,17},{17,25},{25,1},{2,10},{10... | collective-permute-start | bytes 1572872 | tf_op jit(solution)/shard_map/ppermute | solution.py:238
  753.9 27.6 %collective-permute-start.54 = (bf16[256,2048]{1,0:T(8,128)(2,1)}, bf16[256,2048]{1,0:T(8,128)(2,1)S(1)}, u32[]{:S(2)}, u32[]{:S(2)}) collective-permute-start(bf16[256,2048]{1,0:T(8,128)(2,1)} %get-tuple-element.284), channel_id=1, source_target_pairs={{0,8},{8,16},{16,24},{24,0},{1,9},{9,17},{17,25},{25,1},{2,10},{10... | collective-permute-start | bytes 3145736 | tf_op jit(solution)/shard_map/ppermute | solution.py:238
  755.4 33.1 %collective-permute-start.66 = (bf16[3,512,256]{2,1,0:T(8,128)(2,1)}, bf16[3,512,256]{2,1,0:T(8,128)(2,1)}, u32[]{:S(2)}, u32[]{:S(2)}) collective-permute-start(bf16[3,512,256]{2,1,0:T(8,128)(2,1)} %get-tuple-element.306), channel_id=1, source_target_pairs={{0,4},{2,6},{4,0},{6,2},{1,5},{3,7},{5,1},{7,3},{8,12},{10,14},{12... | collective-permute-start | bytes 2359304 | tf_op jit(solution)/shard_map/ppermute | solution.py:233
  756.0 32.5 %collective-permute-start.67 = (bf16[3,512,256]{2,1,0:T(8,128)(2,1)}, bf16[3,512,256]{2,1,0:T(8,128)(2,1)}, u32[]{:S(2)}, u32[]{:S(2)}) collective-permute-start(bf16[3,512,256]{2,1,0:T(8,128)(2,1)} %get-tuple-element.307), channel_id=1, source_target_pairs={{0,1},{1,0},{2,3},{3,2},{4,5},{5,4},{6,7},{7,6},{8,9},{9,8},{10,11... | collective-permute-start | bytes 2359304 | tf_op jit(solution)/shard_map/ppermute | solution.py:233
  792.7 251.6 %all-gather.18.cloned.1.call-start = ((), (), s32[]{:S(2)}) async-start(), calls=%async_computation.4 | async-start | bytes 14155776 | tf_op jit(solution)/shard_map/all_gather | solution.py:719
  793.0 55.7 %collective-permute-start.62 = (bf16[2,3,512,256]{3,2,1,0:T(8,128)(2,1)}, bf16[2,3,512,256]{3,2,1,0:T(8,128)(2,1)}, u32[]{:S(2)}, u32[]{:S(2)}) collective-permute-start(bf16[2,3,512,256]{3,2,1,0:T(8,128)(2,1)} %get-tuple-element.300), channel_id=1, source_target_pairs={{0,1},{1,0},{2,3},{3,2},{4,5},{5,4},{6,7},{7,6},{8,9},{9,8},{10,11... | collective-permute-start | bytes 4718600 | tf_op jit(solution)/shard_map/ppermute | solution.py:233
  793.8 54.9 %collective-permute-start.63 = (bf16[2,3,512,256]{3,2,1,0:T(8,128)(2,1)}, bf16[2,3,512,256]{3,2,1,0:T(8,128)(2,1)}, u32[]{:S(2)}, u32[]{:S(2)}) collective-permute-start(bf16[2,3,512,256]{3,2,1,0:T(8,128)(2,1)} %get-tuple-element.301), channel_id=1, source_target_pairs={{0,4},{2,6},{4,0},{6,2},{1,5},{3,7},{5,1},{7,3},{8,12},{10,14},{12... | collective-permute-start | bytes 4718600 | tf_op jit(solution)/shard_map/ppermute | solution.py:233
  797.9 55.9 %collective-permute-start.61 = (bf16[512,1536]{1,0:T(8,128)(2,1)}, bf16[512,1536]{1,0:T(8,128)(2,1)}, u32[]{:S(2)}, u32[]{:S(2)}) collective-permute-start(bf16[512,1536]{1,0:T(8,128)(2,1)} %slice.577), channel_id=1, source_target_pairs={{0,8},{8,16},{16,24},{24,0},{1,9},{9,17},{17,25},{25,1},{2,10},{10... | collective-permute-start | bytes 4718600 | tf_op jit(solution)/shard_map/ppermute | solution.py:238
  799.4 46.5 %collective-permute-start.65 = (bf16[128,2048]{1,0:T(8,128)(2,1)S(1)}, bf16[128,2048]{1,0:T(8,128)(2,1)S(1)}, u32[]{:S(2)}, u32[]{:S(2)}) collective-permute-start(bf16[128,2048]{1,0:T(8,128)(2,1)S(1)} %copy-done.93), channel_id=1, source_target_pairs={{0,8},{8,16},{16,24},{24,0},{1,9},{9,17},{17,25},{25,1},{2,10},{10... | collective-permute-start | bytes 1572872 | tf_op jit(solution)/shard_map/ppermute | solution.py:238
  856.8 49.5 %collective-permute-start.68 = (bf16[512,1536]{1,0:T(8,128)(2,1)}, bf16[512,1536]{1,0:T(8,128)(2,1)}, u32[]{:S(2)}, u32[]{:S(2)}) collective-permute-start(bf16[512,1536]{1,0:T(8,128)(2,1)} %get-tuple-element.312), channel_id=1, source_target_pairs={{0,8},{8,16},{16,24},{24,0},{1,9},{9,17},{17,25},{25,1},{2,10},{10... | collective-permute-start | bytes 4718600 | tf_op jit(solution)/shard_map/ppermute | solution.py:238
  860.6 48.6 %collective-permute-start.71 = (bf16[3,512,256]{2,1,0:T(8,128)(2,1)}, bf16[3,512,256]{2,1,0:T(8,128)(2,1)S(1)}, u32[]{:S(2)}, u32[]{:S(2)}) collective-permute-start(bf16[3,512,256]{2,1,0:T(8,128)(2,1)} %get-tuple-element.324), channel_id=1, source_target_pairs={{0,4},{2,6},{4,0},{6,2},{1,5},{3,7},{5,1},{7,3},{8,12},{10,14},{12... | collective-permute-start | bytes 2359304 | tf_op jit(solution)/shard_map/ppermute | solution.py:233
  861.2 48.0 %collective-permute-start.72 = (bf16[3,512,256]{2,1,0:T(8,128)(2,1)}, bf16[3,512,256]{2,1,0:T(8,128)(2,1)}, u32[]{:S(2)}, u32[]{:S(2)}) collective-permute-start(bf16[3,512,256]{2,1,0:T(8,128)(2,1)} %get-tuple-element.325), channel_id=1, source_target_pairs={{0,1},{1,0},{2,3},{3,2},{4,5},{5,4},{6,7},{7,6},{8,9},{9,8},{10,11... | collective-permute-start | bytes 2359304 | tf_op jit(solution)/shard_map/ppermute | solution.py:233
  861.6 42.7 %collective-permute-start.69 = (bf16[128,2048]{1,0:T(8,128)(2,1)}, bf16[128,2048]{1,0:T(8,128)(2,1)}, u32[]{:S(2)}, u32[]{:S(2)}) collective-permute-start(bf16[128,2048]{1,0:T(8,128)(2,1)} %get-tuple-element.313), channel_id=1, source_target_pairs={{0,8},{8,16},{16,24},{24,0},{1,9},{9,17},{17,25},{25,1},{2,10},{10... | collective-permute-start | bytes 1572872 | tf_op jit(solution)/shard_map/ppermute | solution.py:238
  918.0 39.0 %collective-permute-start.70 = (bf16[512,1536]{1,0:T(8,128)(2,1)}, bf16[512,1536]{1,0:T(8,128)(2,1)}, u32[]{:S(2)}, u32[]{:S(2)}) collective-permute-start(bf16[512,1536]{1,0:T(8,128)(2,1)} %get-tuple-element.320), channel_id=1, source_target_pairs={{0,8},{8,16},{16,24},{24,0},{1,9},{9,17},{17,25},{25,1},{2,10},{10... | collective-permute-start | bytes 4718600 | tf_op jit(solution)/shard_map/ppermute | solution.py:238
  924.0 39.5 %collective-permute-start.74 = (bf16[256,2048]{1,0:T(8,128)(2,1)S(1)}, bf16[256,2048]{1,0:T(8,128)(2,1)}, u32[]{:S(2)}, u32[]{:S(2)}) collective-permute-start(bf16[256,2048]{1,0:T(8,128)(2,1)S(1)} %fusion.19), channel_id=1, source_target_pairs={{0,4},{2,6},{4,0},{6,2},{1,5},{3,7},{5,1},{7,3},{8,12},{10,14},{12... | collective-permute-start | bytes 3145736 | tf_op jit(solution)/shard_map/ppermute | solution.py:233
  974.9 25.8 %collective-permute-start.85 = (bf16[128,2048]{1,0:T(8,128)(2,1)}, bf16[128,2048]{1,0:T(8,128)(2,1)}, u32[]{:S(2)}, u32[]{:S(2)}) collective-permute-start(bf16[128,2048]{1,0:T(8,128)(2,1)} %get-tuple-element.346), channel_id=1, source_target_pairs={{0,1},{1,0},{2,3},{3,2},{4,5},{5,4},{6,7},{7,6},{8,9},{9,8},{10,11... | collective-permute-start | bytes 1572872 | tf_op jit(solution)/shard_map/ppermute | solution.py:233
  980.9 22.1 %collective-permute-start.78 = (f32[2,20,128]{2,1,0:T(8,128)S(1)}, f32[2,20,128]{2,1,0:T(8,128)S(1)}, u32[]{:S(2)}, u32[]{:S(2)}) collective-permute-start(f32[2,20,128]{2,1,0:T(8,128)S(1)} %pad_maximum_fusion.29), channel_id=1, source_target_pairs={{0,2},{2,0},{4,6},{6,4},{1,3},{3,1},{5,7},{7,5},{8,10},{10,8},{12,... | collective-permute-start | bytes 61448 | tf_op jit(solution)/shard_map/ppermute | solution.py:233
  997.1 46.6 %collective-permute-start.81 = (bf16[4,128,3,2,256]{4,1,3,2,0:T(8,128)(2,1)S(1)}, bf16[4,128,3,2,256]{4,1,3,2,0:T(8,128)(2,1)S(1)}, u32[]{:S(2)}, u32[]{:S(2)}) collective-permute-start(bf16[4,128,3,2,256]{4,1,3,2,0:T(8,128)(2,1)S(1)} %get-tuple-element.415), channel_id=1, source_target_pairs={{0,1},{1,0},{2,3},{3,2},{4,5},{5,4},{6,7},{7,6},{8,9},{9,8},{10,11... | collective-permute-start | bytes 4718600 | tf_op jit(solution)/shard_map/ppermute | solution.py:233
  1006.8 36.9 %collective-permute-start.80 = (f32[20,128]{1,0:T(8,128)S(1)}, f32[20,128]{1,0:T(8,128)S(1)}, u32[]{:S(2)}, u32[]{:S(2)}) collective-permute-start(f32[20,128]{1,0:T(8,128)S(1)} %fusion.53), channel_id=1, source_target_pairs={{0,1},{1,0},{2,3},{3,2},{4,5},{5,4},{6,7},{7,6},{8,9},{9,8},{10,11... | collective-permute-start | bytes 30728 | tf_op jit(solution)/shard_map/ppermute | solution.py:233
  (122 other events, 1458.1 us)
Sparse Core Ops, SparseCore 0:
  99.8 45.2 all-gather.11
  146.6 112.9 all-gather.9
  405.3 200.9 all-reduce.3
  608.2 119.6 all-gather.13
  792.8 106.0 all-gather.15
  914.3 106.5 all-gather.17

commit v5 on v4

--- a/solution.py
+++ b/solution.py
@@ -1182,7 +1182,7 @@
         out_w_grad = mine_out.astype(F32) + swap(mine_out, "dp", 1).astype(F32)
     qkv_ring.hop()
     advance((3, "finals"))
-    expert_grads = place([1])
+    expert_grads = place([1, 2])
     qkv_w_grad = qkv_ring.whole()
     normed_own = after(normed_own, order.token)
     normed_grad = normed_own.astype(F32) + normed_near.astype(F32) + normed_far.astype(F32)
@@ -1196,15 +1196,13 @@
 
     mine_w = qkv_w_grad.reshape(context, rows, 3, 2, some)
     got = swap(mine_w, "dp", 1)
-    expert_grads = place([2])
+    expert_grads = place([3])
     mine_w = after(mine_w, order.token)
     mine_w = jnp.stack(
         [add_low(mine_w[:, :, :, i], got[:, :, :, 1 - i]) for i in range(2)], axis=3
     )
     pieces = [lax.dynamic_index_in_dim(mine_w, m, 0, keepdims=False) for m in members]
     pieces = [pieces[0]] + [swap(pieces[s], "context", s) for s in range(1, context)]
-    expert_grads = place([3])
-    pieces[0] = after(pieces[0], order.token)
     dense = take(jnp.stack(pieces), members)
     dense = jnp.where(my_dp == 0, dense, dense[:, :, :, ::-1]).astype(F32)
     dense = dense.reshape(context, rows, 3, per, HDIM).transpose(2, 1, 3, 0, 4)

time: 1110 us -> 1110 us (level)
  waiting for transfers between devices: 328 us -> 340 us
    all_gather x3, waiting for transfers between devices: 0.06 us -> 32.1 us  [finals(): self.all = lax.all_gather(own, ('context', 'dp'), axis=0)]
    ppermute x30, waiting for transfers between devices: 172 us -> 159 us  [shift(): return lax.ppermute(values, 'expert', [(i, (i + by) % n) for i in range(n)])]
    unnamed x229 -> x243, local copies, waits for them, and re-layouts: 40.2 us -> 42.9 us
  transfers between devices with their start and end apart: 92 -> 92, of which waited for: 32 -> 35; matrix products, arithmetic and copies ran while one was open for 15% -> 14% of each run, Pallas kernels for 32% -> 33%
where the time goes in v5:
time: 1110 us; the launch traced here: 1100 us
  Pallas kernels  458 us (41%)
  waiting for transfers between devices  340 us (31%)
  local copies, waits for them, and re-layouts  87 us (8%)
  starting transfers between devices  84.4 us (8%)
  other arithmetic  64.2 us (6%)
  matrix products  43.9 us (4%)
  between operations  26.1 us (2%)
    pallas_call x8, Pallas kernels, run_rows(): pl.pallas_call(functools.partial(rows_kernel, first), grid_spec=pltpu.Pre...  185 us
    ppermute x30, waiting for transfers between devices, shift(): return lax.ppermute(values, 'expert', [(i, (i + by) % n) for i in range(n)])  159 us
    ppermute x56, waiting for transfers between devices, swap(): lax.ppermute(values, axis, [(i, i ^ bit) for i in range(lax.axis_size(axi...  146 us
    pallas_call x3, Pallas kernels, run_split(): pl.pallas_call(functools.partial(split_kernel, sizes), grid_spec=pltpu.Pr...  73.8 us
    pallas_call x9, Pallas kernels, add_pieces(): pl.pallas_call(functools.partial(add_kernel, picks, joined), grid=(parts,...  51.2 us
    ppermute x56, starting transfers between devices, swap(): lax.ppermute(values, axis, [(i, i ^ bit) for i in range(lax.axis_size(axi...  45.8 us
    dot_general x8, matrix products, dot(): lax.dot_general(left, right, (((contract[0],), (contract[1],)), ((), ()))...  43.9 us
    unnamed x243, local copies, waits for them, and re-layouts  42.9 us
  transfers between devices with their start and end apart: 92, of which 35 were waited for; matrix products, arithmetic and copies ran while one was open for 14% of the time, Pallas kernels for 33%

profile of v5, /device:TPU:0, one launch (start us, length us, event | category | flops | bytes accessed | tf_op | source)
XLA Modules:
  0.0 1103.6 jit_solution(13720695716656436135)
XLA Ops:
  28.4 5.4 collective-permute-done.2
  39.8 13.5 %collective-permute-done.18 = bf16[512,768]{1,0:T(8,128)(2,1)S(1)} collective-permute-done((bf16[512,768]{1,0:T(8,128)(2,1)S(1)}, bf16[512,768]{1,0:T(8,128)(2,1)S(1)}, u32[]{:S(2)}, u32[]{:S(2)}) %collective-permute-start.18) | collective-permute-done | bytes 786464 | tf_op jit(solution)/shard_map/ppermute | solution.py:233
  53.3 4.1 collective-permute-done.3
  58.0 4.6 collective-permute-done.10
  62.6 14.5 %collective-permute-done.4 = bf16[512,768]{1,0:T(8,128)(2,1)} collective-permute-done((bf16[512,768]{1,0:T(8,128)(2,1)S(1)}, bf16[512,768]{1,0:T(8,128)(2,1)}, u32[]{:S(2)}, u32[]{:S(2)}) %collective-permute-start.4) | collective-permute-done | bytes 786464 | tf_op jit(solution)/shard_map/ppermute | solution.py:238
  81.7 7.3 fusion.2
  90.9 5.9 collective-permute-done.5
  110.3 5.2 collective-permute-done.21
  116.8 9.5 fusion.25.q_ref.k_ref.v_ref
  130.7 4.4 collective-permute-start.23
  139.4 16.9 %attend.1 = (bf16[1024,512]{1,0:T(8,128)(2,1)}, bf16[1024,512]{1,0:T(8,128)(2,1)}, bf16[1024,512]{1,0:T(8,128)(2,1)}, bf16[1024,512]{1,0:T(8,128)(2,1)}, f32[4,1,1024]{2,1,0:T(1,128)}) custom-call(f32[1024,1536]{1,0:T(8,128)} %copy-done, f32[1024,1536]{1,0:T(8,128)} %copy-done, f32[1024,1536]{1,0:T(8,128)} %copy-done, f32[1024,1]{1,0:T(8,128)} %bitcast.313, ...), custom_call_target="tpu_custom_call" | custom-call | flops 5368709120 | bytes 10485760 | tf_op jit(solution)/shard_map/attend/pallas_call | solution.py:175
  165.2 4.4 collective-permute-done.24
  182.4 5.6 collective-permute-done.6
  189.2 8.6 collective-permute-done.7
  207.7 7.8 collective-permute-start.26
  216.0 22.4 %rows.8 = (bf16[256,2048]{1,0:T(8,128)(2,1)}, bf16[256,2048]{1,0:T(8,128)(2,1)}, f32[256,128]{1,0:T(8,128)}, f32[256,128]{1,0:T(8,128)}, bf16[2048,256]{1,0:T(8,...) custom-call(s32[1]{0:T(128)} %bitcast.65.at_ref, ...), custom_call_target="tpu_custom_call" | custom-call | flops 12884901888 | bytes 25165824 | tf_op jit(solution)/shard_map/rows/pallas_call | solution.py:372
  238.4 18.5 %collective-permute-done.26.x_ref = bf16[256,2048]{1,0:T(8,128)(2,1)S(1)} collective-permute-done((bf16[256,2048]{1,0:T(8,128)(2,1)S(1)}, bf16[256,2048]{1,0:T(8,128)(2,1)S(1)}, u32[]{:S(2)}, u32[]{:S(2)}) %collective-permute-start.26) | collective-permute-done | bytes 1048608 | tf_op jit(solution)/shard_map/ppermute | solution.py:238
  259.7 22.4 %rows.9 = (bf16[256,2048]{1,0:T(8,128)(2,1)}, bf16[256,2048]{1,0:T(8,128)(2,1)}, f32[256,128]{1,0:T(8,128)}, f32[256,128]{1,0:T(8,128)}, bf16[2048,256]{1,0:T(8,...) custom-call(s32[1]{0:T(128)} %bitcast.65.at_ref, ...), custom_call_target="tpu_custom_call" | custom-call | flops 12884901888 | bytes 25165824 | tf_op jit(solution)/shard_map/rows/pallas_call | solution.py:372
  286.4 22.4 %rows.10 = (bf16[256,2048]{1,0:T(8,128)(2,1)}, bf16[256,2048]{1,0:T(8,128)(2,1)}, f32[256,128]{1,0:T(8,128)}, f32[256,128]{1,0:T(8,128)}, bf16[2048,256]{1,0:T(8...) custom-call(s32[1]{0:T(128)} %bitcast.65.at_ref, ...), custom_call_target="tpu_custom_call" | custom-call | flops 12884901888 | bytes 25165824 | tf_op jit(solution)/shard_map/rows/pallas_call | solution.py:372
  315.6 23.4 %rows.11 = (bf16[512,2048]{1,0:T(8,128)(2,1)}, bf16[512,2048]{1,0:T(8,128)(2,1)}, f32[512,128]{1,0:T(8,128)}, f32[512,128]{1,0:T(8,128)}, bf16[2048,512]{1,0:T(8...) custom-call(s32[1]{0:T(128)} %bitcast.65.at_ref, ...), custom_call_target="tpu_custom_call" | custom-call | flops 12884901888 | bytes 12582912 | tf_op jit(solution)/shard_map/rows/pallas_call | solution.py:372
  339.0 20.2 %grads.1 = (bf16[2048,1024]{1,0:T(8,128)(2,1)}, bf16[2048,1024]{1,0:T(8,128)(2,1)}, bf16[1024,2048]{1,0:T(8,128)(2,1)}, f32[8,128]{1,0:T(8,128)}) custom-call(bf16[2048,256]{1,0:T(8,128)(2,1)} %get-tuple-element.189.refs_0_, bf16[2048,256]{1,0:T(8,128)(2,1)} %get-tuple-element.190.refs_1_, bf16[2048,512]{1,0:T(8,128)(2,1)} %get-tuple-element.191.refs_2_, ...), custom_call_target="tpu_custom_call" | custom-call | flops 12884901888 | bytes 29360128 | tf_op jit(solution)/shard_map/grads/pallas_call | solution.py:468
  359.1 22.6 %rows.12 = (bf16[256,2048]{1,0:T(8,128)(2,1)}, bf16[256,2048]{1,0:T(8,128)(2,1)}, f32[256,128]{1,0:T(8,128)}, f32[256,128]{1,0:T(8,128)}, bf16[2048,256]{1,0:T(8...) custom-call(s32[1]{0:T(128)} %bitcast.65.at_ref, ...), custom_call_target="tpu_custom_call" | custom-call | flops 12884901888 | bytes 25165824 | tf_op jit(solution)/shard_map/rows/pallas_call | solution.py:372
  381.7 23.3 %rows.13 = (bf16[512,2048]{1,0:T(8,128)(2,1)}, bf16[512,2048]{1,0:T(8,128)(2,1)}, f32[512,128]{1,0:T(8,128)}, f32[512,128]{1,0:T(8,128)}, bf16[2048,512]{1,0:T(8...) custom-call(s32[1]{0:T(128)} %bitcast.65.at_ref, ...), custom_call_target="tpu_custom_call" | custom-call | flops 12884901888 | bytes 12582912 | tf_op jit(solution)/shard_map/rows/pallas_call | solution.py:372
  405.1 24.8 %split.3 = (bf16[2,3,512,256]{3,2,1,0:T(8,128)(2,1)}, bf16[2,3,512,256]{3,2,1,0:T(8,128)(2,1)}, bf16[2,3,512,256]{3,2,1,0:T(8,128)(2,1)}, bf16[2,3,512,256]{3,2,...) custom-call(s32[3]{0:T(128)} %pad_add_fusion.1.bits_ref, ...), custom_call_target="tpu_custom_call" | custom-call | flops 12884901888 | bytes 29360128 | tf_op jit(solution)/shard_map/split/pallas_call | solution.py:611
  432.6 23.9 %rows.14 = (bf16[512,2048]{1,0:T(8,128)(2,1)}, bf16[512,2048]{1,0:T(8,128)(2,1)}, f32[512,128]{1,0:T(8,128)}, f32[512,128]{1,0:T(8,128)}, bf16[2048,512]{1,0:T(8...) custom-call(s32[1]{0:T(128)} %bitcast.65.at_ref, ...), custom_call_target="tpu_custom_call" | custom-call | flops 12884901888 | bytes 12582912 | tf_op jit(solution)/shard_map/rows/pallas_call | solution.py:372
  458.1 7.7 add_pieces.9
  469.6 24.3 %rows.15 = (bf16[512,2048]{1,0:T(8,128)(2,1)}, bf16[512,2048]{1,0:T(8,128)(2,1)}, f32[512,128]{1,0:T(8,128)}, f32[512,128]{1,0:T(8,128)}, bf16[2048,512]{1,0:T(8...) custom-call(s32[1]{0:T(128)} %bitcast.65.at_ref, ...), custom_call_target="tpu_custom_call" | custom-call | flops 12884901888 | bytes 12582912 | tf_op jit(solution)/shard_map/rows/pallas_call | solution.py:372
  499.2 24.5 %split.4 = (bf16[2,3,512,256]{3,2,1,0:T(8,128)(2,1)}, bf16[2,3,512,256]{3,2,1,0:T(8,128)(2,1)}, bf16[2,3,512,256]{3,2,1,0:T(8,128)(2,1)}, bf16[2,3,512,256]{3,2,...) custom-call(s32[3]{0:T(128)} %pad_add_fusion.1.bits_ref, ...), custom_call_target="tpu_custom_call" | custom-call | flops 12884901888 | bytes 29360128 | tf_op jit(solution)/shard_map/split/pallas_call | solution.py:611
  526.3 5.1 add_pieces.10
  533.9 3.6 hop.13
  537.5 24.5 %split.5 = (bf16[2,3,512,256]{3,2,1,0:T(8,128)(2,1)}, bf16[2,3,512,256]{3,2,1,0:T(8,128)(2,1)}, bf16[2,3,512,256]{3,2,1,0:T(8,128)(2,1)}, bf16[2,3,512,256]{3,2,...) custom-call(s32[3]{0:T(128)} %pad_add_fusion.1.bits_ref, ...), custom_call_target="tpu_custom_call" | custom-call | flops 12884901888 | bytes 29360128 | tf_op jit(solution)/shard_map/split/pallas_call | solution.py:611
  563.1 4.2 add_pieces.11
  573.3 3.8 collective-permute-start.49
  577.2 5.1 collective-permute-done.49
  582.7 6.4 collective-permute-done.50
  595.8 8.2 add_pieces.12
  604.1 11.1 %collective-permute-done.38.refs_2_ = bf16[256,2048]{1,0:T(8,128)(2,1)} collective-permute-done((bf16[256,2048]{1,0:T(8,128)(2,1)}, bf16[256,2048]{1,0:T(8,128)(2,1)}, u32[]{:S(2)}, u32[]{:S(2)}) %collective-permute-start.38) | collective-permute-done | bytes 1048608 | tf_op jit(solution)/shard_map/ppermute | solution.py:238
  625.3 34.6 %collective-permute-done.52 = bf16[256,2048]{1,0:T(8,128)(2,1)} collective-permute-done((bf16[256,2048]{1,0:T(8,128)(2,1)S(1)}, bf16[256,2048]{1,0:T(8,128)(2,1)}, u32[]{:S(2)}, u32[]{:S(2)}) %collective-permute-start.52) | collective-permute-done | bytes 1048608 | tf_op jit(solution)/shard_map/ppermute | solution.py:233
  663.1 3.8 hop.15
  668.4 5.2 convolution_convert_fusion.3.grad_ref
  673.6 20.5 %attend_back.1 = (f32[1024,512]{1,0:T(8,128)}, f32[1024,512]{1,0:T(8,128)}, bf16[1024,512]{1,0:T(8,128)(2,1)}, f32[1024,128]{1,0:T(8,128)}, f32[1024,128]{1,0:T(...) custom-call(bf16[1024,512]{1,0:T(8,128)(2,1)} %get-tuple-element.267.ql_ref, ...), custom_call_target="tpu_custom_call" | custom-call | flops 10737418240 | bytes 15728640 | tf_op jit(solution)/shard_map/attend_back/pallas_call | solution.py:203
  698.6 4.3 fusion.5
  705.7 22.8 %collective-permute-done.46.refs_2_ = bf16[2,3,512,256]{3,2,1,0:T(8,128)(2,1)} collective-permute-done((bf16[2,3,512,256]{3,2,1,0:T(8,128)(2,1)}, bf16[2,3,512,256]{3,2,1,0:T(8,128)(2,1)}, u32[]{:S(2)}, u32[]{:S(2)}) %collective-permute-start.46) | collective-permute-done | bytes 1572896 | tf_op jit(solution)/shard_map/ppermute | solution.py:233
  729.0 5.1 add_pieces.13
  734.3 3.7 hop.16
  739.6 4.7 subtract_convert_fusion.1
  744.3 8.9 convolution_convert_fusion.refs_0_
  756.8 10.4 convolution_convert_fusion.1
  771.7 7.6 add_pieces.14
  787.6 4.1 add_pieces.15
  796.9 46.9 %collective-permute-done.65.refs_1_ = bf16[128,2048]{1,0:T(8,128)(2,1)S(1)} collective-permute-done((bf16[128,2048]{1,0:T(8,128)(2,1)}, bf16[128,2048]{1,0:T(8,128)(2,1)S(1)}, u32[]{:S(2)}, u32[]{:S(2)}) %collective-permute-start.65) | collective-permute-done | bytes 524320 | tf_op jit(solution)/shard_map/ppermute | solution.py:238
  849.5 5.1 add_pieces.16
  862.2 14.0 %place.1 = (f32[4,2048,1024]{2,1,0:T(8,128)}, f32[4,2048,1024]{2,1,0:T(8,128)}, f32[4,1024,2048]{2,1,0:T(8,128)}, f32[8,128]{1,0:T(8,128)}) custom-call(bf16[2048,1024]{1,0:T(8,128)(2,1)} %get-tuple-element.370.refs_0_, bf16[2048,1024]{1,0:T(8,128)(2,1)} %get-tuple-element.371.refs_1_, bf16[1024,2048]{1,0:T(8,128)(2,1)} %get-tuple-element.372.refs_2_, ...), custom_call_target="tpu_custom_call" | custom-call | bytes 37748736 | tf_op jit(solution)/shard_map/place/pallas_call | solution.py:521
  876.2 27.1 %collective-permute-done.69.refs_1_ = bf16[128,2048]{1,0:T(8,128)(2,1)} collective-permute-done((bf16[128,2048]{1,0:T(8,128)(2,1)}, bf16[128,2048]{1,0:T(8,128)(2,1)}, u32[]{:S(2)}, u32[]{:S(2)}) %collective-permute-start.69) | collective-permute-done | bytes 524320 | tf_op jit(solution)/shard_map/ppermute | solution.py:238
  910.5 4.0 add_pieces.17
  918.4 3.8 collective-permute-done.73
  925.7 13.8 %place_pieces.3 = (f32[4,2048,1024]{2,1,0:T(8,128)}, f32[4,2048,1024]{2,1,0:T(8,128)}, f32[4,1024,2048]{2,1,0:T(8,128)}, f32[8,128]{1,0:T(8,128)}) custom-call(bf16[8,2,3,512,256]{4,3,2,1,0:T(8,128)(2,1)} %bitcast.299, f32[8,128]{1,0:T(8,128)} %get-tuple-element.328.refs_1_, ...), custom_call_target="tpu_custom_call", output_to_operand_aliasing={{0}: (2, {}), {1}: (3, {}), {2}: (4, {})} | custom-call | bytes 37748736 | tf_op jit(solution)/shard_map/place_pieces/pallas_call | solution.py:788
  939.6 13.8 %place_pieces.4 = (f32[4,2048,1024]{2,1,0:T(8,128)}, f32[4,2048,1024]{2,1,0:T(8,128)}, f32[4,1024,2048]{2,1,0:T(8,128)}, f32[8,128]{1,0:T(8,128)}) custom-call(bf16[8,2,3,512,256]{4,3,2,1,0:T(8,128)(2,1)} %bitcast.300, f32[8,128]{1,0:T(8,128)} %get-tuple-element.332.refs_1_, ...), custom_call_target="tpu_custom_call", output_to_operand_aliasing={{0}: (2, {}), {1}: (3, {}), {2}: (4, {})} | custom-call | bytes 37748736 | tf_op jit(solution)/shard_map/place_pieces/pallas_call | solution.py:788
  953.4 3.8 collective-permute-done.70.refs_1_
  980.3 32.1 %all-gather.18.cloned.1.call-done = bf16[16,3,512,256]{3,2,1,0:T(8,128)(2,1)} async-done(((bf16[2,3,512,256]{3,2,1,0:T(8,128)(2,1)}), bf16[16,3,512,256]{3,2,1,0:T(8,128)(2,1)}) %all-gather.18.cloned.1.call-update) | async-done | bytes 12582928 | tf_op jit(solution)/shard_map/all_gather | solution.py:719
  1012.4 13.8 %place_pieces.5 = (f32[4,2048,1024]{2,1,0:T(8,128)}, f32[4,2048,1024]{2,1,0:T(8,128)}, f32[4,1024,2048]{2,1,0:T(8,128)}, f32[8,128]{1,0:T(8,128)}) custom-call(bf16[8,2,3,512,256]{4,3,2,1,0:T(8,128)(2,1)} %bitcast.301, f32[8,128]{1,0:T(8,128)} %get-tuple-element.337.refs_1_, ...), custom_call_target="tpu_custom_call", output_to_operand_aliasing={{0}: (2, {}), {1}: (3, {}), {2}: (4, {})} | custom-call | bytes 37748736 | tf_op jit(solution)/shard_map/place_pieces/pallas_call | solution.py:788
  1038.2 27.1 %collective-permute-done.80 = f32[20,128]{1,0:T(8,128)S(1)} collective-permute-done((f32[20,128]{1,0:T(8,128)S(1)}, f32[20,128]{1,0:T(8,128)S(1)}, u32[]{:S(2)}, u32[]{:S(2)}) %collective-permute-start.80) | collective-permute-done | bytes 10272 | tf_op jit(solution)/shard_map/ppermute | solution.py:233
  1069.0 9.0 collective-permute-done.83
  1078.0 7.5 collective-permute-done.84
  (595 shorter events, 249.8 us)
Async XLA Ops:
  7.2 149.2 %all-gather.12.cloned.1.call-start = ((), (), s32[]{:S(2)}) async-start(), calls=%async_computation.1 | async-start | bytes 2621440 | tf_op jit(solution)/shard_map/all_gather | solution.py:909
  34.4 18.9 %collective-permute-start.18 = (bf16[512,768]{1,0:T(8,128)(2,1)S(1)}, bf16[512,768]{1,0:T(8,128)(2,1)S(1)}, u32[]{:S(2)}, u32[]{:S(2)}) collective-permute-start(bf16[512,768]{1,0:T(8,128)(2,1)S(1)} %bitcast.307), channel_id=1, source_target_pairs={{0,1},{1,0},{2,3},{3,2},{4,5},{5,4},{6,7},{7,6},{8,9},{9,8},{10,11... | collective-permute-start | bytes 2359304 | tf_op jit(solution)/shard_map/ppermute | solution.py:233
  37.1 20.3 %collective-permute-start.3 = (bf16[512,768]{1,0:T(8,128)(2,1)S(1)}, bf16[512,768]{1,0:T(8,128)(2,1)S(1)}, u32[]{:S(2)}, u32[]{:S(2)}) collective-permute-start(bf16[512,768]{1,0:T(8,128)(2,1)S(1)} %bitcast.309), channel_id=1, source_target_pairs={{0,8},{8,16},{16,24},{24,0},{1,9},{9,17},{17,25},{25,1},{2,10},{10... | collective-permute-start | bytes 2359304 | tf_op jit(solution)/shard_map/ppermute | solution.py:238
  38.5 24.1 %collective-permute-start.10 = (bf16[256,2048]{1,0:T(8,128)(2,1)S(1)}, bf16[256,2048]{1,0:T(8,128)(2,1)S(1)}, u32[]{:S(2)}, u32[]{:S(2)}) collective-permute-start(bf16[256,2048]{1,0:T(8,128)(2,1)S(1)} %add_bitcast_fusion), channel_id=1, source_target_pairs={{0,4},{2,6},{4,0},{6,2},{1,5},{3,7},{5,1},{7,3},{8,12},{10,14},{12... | collective-permute-start | bytes 3145736 | tf_op jit(solution)/shard_map/ppermute | solution.py:233
  39.8 40.8 %collective-permute-start.9 = (bf16[256,2048]{1,0:T(8,128)(2,1)S(1)}, bf16[256,2048]{1,0:T(8,128)(2,1)S(1)}, u32[]{:S(2)}, u32[]{:S(2)}) collective-permute-start(bf16[256,2048]{1,0:T(8,128)(2,1)S(1)} %add_bitcast_fusion), channel_id=1, source_target_pairs={{0,2},{2,0},{4,6},{6,4},{1,3},{3,1},{5,7},{7,5},{8,10},{10,8},{12,... | collective-permute-start | bytes 3145736 | tf_op jit(solution)/shard_map/ppermute | solution.py:233
  57.4 23.1 %collective-permute-start.19 = (bf16[512,768]{1,0:T(8,128)(2,1)S(1)}, bf16[512,768]{1,0:T(8,128)(2,1)S(1)}, u32[]{:S(2)}, u32[]{:S(2)}) collective-permute-start(bf16[512,768]{1,0:T(8,128)(2,1)S(1)} %collective-permute-done.3), channel_id=1, source_target_pairs={{0,1},{1,0},{2,3},{3,2},{4,5},{5,4},{6,7},{7,6},{8,9},{9,8},{10,11... | collective-permute-start | bytes 2359304 | tf_op jit(solution)/shard_map/ppermute | solution.py:233
  57.9 19.2 %collective-permute-start.4 = (bf16[512,768]{1,0:T(8,128)(2,1)S(1)}, bf16[512,768]{1,0:T(8,128)(2,1)}, u32[]{:S(2)}, u32[]{:S(2)}) collective-permute-start(bf16[512,768]{1,0:T(8,128)(2,1)S(1)} %collective-permute-done.3), channel_id=1, source_target_pairs={{0,8},{8,16},{16,24},{24,0},{1,9},{9,17},{17,25},{25,1},{2,10},{10... | collective-permute-start | bytes 2359304 | tf_op jit(solution)/shard_map/ppermute | solution.py:238
  77.2 24.4 %collective-permute-start.20 = (bf16[512,768]{1,0:T(8,128)(2,1)}, bf16[512,768]{1,0:T(8,128)(2,1)}, u32[]{:S(2)}, u32[]{:S(2)}) collective-permute-start(bf16[512,768]{1,0:T(8,128)(2,1)} %collective-permute-done.4), channel_id=1, source_target_pairs={{0,1},{1,0},{2,3},{3,2},{4,5},{5,4},{6,7},{7,6},{8,9},{9,8},{10,11... | collective-permute-start | bytes 2359304 | tf_op jit(solution)/shard_map/ppermute | solution.py:233
  78.7 18.1 %collective-permute-start.5 = (bf16[512,768]{1,0:T(8,128)(2,1)}, bf16[512,768]{1,0:T(8,128)(2,1)S(1)}, u32[]{:S(2)}, u32[]{:S(2)}) collective-permute-start(bf16[512,768]{1,0:T(8,128)(2,1)} %collective-permute-done.4), channel_id=1, source_target_pairs={{0,8},{8,16},{16,24},{24,0},{1,9},{9,17},{17,25},{25,1},{2,10},{10... | collective-permute-start | bytes 2359304 | tf_op jit(solution)/shard_map/ppermute | solution.py:238
  99.7 160.0 %all-gather.10.cloned.1.call-start = ((), (), s32[]{:S(2)}) async-start(), calls=%async_computation | async-start | bytes 5242880 | tf_op jit(solution)/shard_map/all_gather | solution.py:910
  136.2 726.1 %all-reduce.4.cloned.1.call-start = ((), (), s32[]{:S(2)}) async-start(), calls=%async_computation.5 | async-start | bytes 25165824 | tf_op jit(solution)/shard_map/psum | solution.py:1040
  172.9 30.0 %collective-permute-start.25 = (bf16[256,2048]{1,0:T(8,128)(2,1)}, bf16[256,2048]{1,0:T(8,128)(2,1)}, u32[]{:S(2)}, u32[]{:S(2)}) collective-permute-start(bf16[256,2048]{1,0:T(8,128)(2,1)} %fusion.21), channel_id=1, source_target_pairs={{0,4},{2,6},{4,0},{6,2},{1,5},{3,7},{5,1},{7,3},{8,12},{10,14},{12... | collective-permute-start | bytes 3145736 | tf_op jit(solution)/shard_map/ppermute | solution.py:233
  177.1 20.7 %collective-permute-start.7 = (s32[256,8]{1,0:T(8,128)S(1)}, s32[256,8]{1,0:T(8,128)S(1)}, u32[]{:S(2)}, u32[]{:S(2)}) collective-permute-start(s32[256,8]{1,0:T(8,128)S(1)} %add_bitcast_fusion.1), channel_id=1, source_target_pairs={{0,16},{8,24},{16,0},{24,8},{1,17},{9,25},{17,1},{25,9},{2,18},{10... | collective-permute-start | bytes 24584 | tf_op jit(solution)/shard_map/ppermute | solution.py:238
  177.7 21.3 %collective-permute-start.8 = (s32[256,8]{1,0:T(8,128)S(1)}, s32[256,8]{1,0:T(8,128)S(1)}, u32[]{:S(2)}, u32[]{:S(2)}) collective-permute-start(s32[256,8]{1,0:T(8,128)S(1)} %add_bitcast_fusion.1), channel_id=1, source_target_pairs={{0,24},{8,0},{16,8},{24,16},{1,25},{9,1},{17,9},{25,17},{2,26},{10... | collective-permute-start | bytes 24584 | tf_op jit(solution)/shard_map/ppermute | solution.py:238
  207.7 49.3 %collective-permute-start.26 = (bf16[256,2048]{1,0:T(8,128)(2,1)S(1)}, bf16[256,2048]{1,0:T(8,128)(2,1)S(1)}, u32[]{:S(2)}, u32[]{:S(2)}) collective-permute-start(bf16[256,2048]{1,0:T(8,128)(2,1)S(1)} %multiply_convert_fusion.x_ref), channel_id=1, source_target_pairs={{0,8},{8,16},{16,24},{24,0},{1,9},{9,17},{17,25},{25,1},{2,10},{10... | collective-permute-start | bytes 3145736 | tf_op jit(solution)/shard_map/ppermute | solution.py:238
  256.9 29.3 %collective-permute-start.27 = (bf16[256,2048]{1,0:T(8,128)(2,1)S(1)}, bf16[256,2048]{1,0:T(8,128)(2,1)S(1)}, u32[]{:S(2)}, u32[]{:S(2)}) collective-permute-start(bf16[256,2048]{1,0:T(8,128)(2,1)S(1)} %collective-permute-done.26.x_ref), channel_id=1, source_target_pairs={{0,8},{8,16},{16,24},{24,0},{1,9},{9,17},{17,25},{25,1},{2,10},{10... | collective-permute-start | bytes 3145736 | tf_op jit(solution)/shard_map/ppermute | solution.py:238
  286.2 27.8 %collective-permute-start.28 = (bf16[256,2048]{1,0:T(8,128)(2,1)S(1)}, bf16[256,2048]{1,0:T(8,128)(2,1)S(1)}, u32[]{:S(2)}, u32[]{:S(2)}) collective-permute-start(bf16[256,2048]{1,0:T(8,128)(2,1)S(1)} %collective-permute-done.27), channel_id=1, source_target_pairs={{0,8},{8,16},{16,24},{24,0},{1,9},{9,17},{17,25},{25,1},{2,10},{10... | collective-permute-start | bytes 3145736 | tf_op jit(solution)/shard_map/ppermute | solution.py:238
  405.1 520.6 %all-gather.16.cloned.1.call-start = ((), (), s32[]{:S(2)}) async-start(), calls=%async_computation.3 | async-start | bytes 14155776 | tf_op jit(solution)/shard_map/all_gather | solution.py:719
  429.9 26.6 %collective-permute-start.29 = (bf16[2,3,512,256]{3,2,1,0:T(8,128)(2,1)}, bf16[2,3,512,256]{3,2,1,0:T(8,128)(2,1)S(1)}, u32[]{:S(2)}, u32[]{:S(2)}) collective-permute-start(bf16[2,3,512,256]{3,2,1,0:T(8,128)(2,1)} %get-tuple-element.209), channel_id=1, source_target_pairs={{0,2},{2,0},{4,6},{6,4},{1,3},{3,1},{5,7},{7,5},{8,10},{10,8},{12,... | collective-permute-start | bytes 4718600 | tf_op jit(solution)/shard_map/ppermute | solution.py:233
  430.0 26.5 %collective-permute-start.30 = (bf16[2,3,512,256]{3,2,1,0:T(8,128)(2,1)}, bf16[2,3,512,256]{3,2,1,0:T(8,128)(2,1)S(1)}, u32[]{:S(2)}, u32[]{:S(2)}) collective-permute-start(bf16[2,3,512,256]{3,2,1,0:T(8,128)(2,1)} %get-tuple-element.210), channel_id=1, source_target_pairs={{0,2},{2,0},{4,6},{6,4},{1,3},{3,1},{5,7},{7,5},{8,10},{10,8},{12,... | collective-permute-start | bytes 4718600 | tf_op jit(solution)/shard_map/ppermute | solution.py:233
  430.5 26.1 %collective-permute-start.31 = (bf16[2,3,512,256]{3,2,1,0:T(8,128)(2,1)}, bf16[2,3,512,256]{3,2,1,0:T(8,128)(2,1)}, u32[]{:S(2)}, u32[]{:S(2)}) collective-permute-start(bf16[2,3,512,256]{3,2,1,0:T(8,128)(2,1)} %get-tuple-element.211), channel_id=1, source_target_pairs={{0,2},{2,0},{4,6},{6,4},{1,3},{3,1},{5,7},{7,5},{8,10},{10,8},{12,... | collective-permute-start | bytes 4718600 | tf_op jit(solution)/shard_map/ppermute | solution.py:233
  430.6 26.0 %collective-permute-start.32 = (bf16[2,3,512,256]{3,2,1,0:T(8,128)(2,1)}, bf16[2,3,512,256]{3,2,1,0:T(8,128)(2,1)}, u32[]{:S(2)}, u32[]{:S(2)}) collective-permute-start(bf16[2,3,512,256]{3,2,1,0:T(8,128)(2,1)} %get-tuple-element.212), channel_id=1, source_target_pairs={{0,2},{2,0},{4,6},{6,4},{1,3},{3,1},{5,7},{7,5},{8,10},{10,8},{12,... | collective-permute-start | bytes 4718600 | tf_op jit(solution)/shard_map/ppermute | solution.py:233
  432.4 61.6 %collective-permute-start.34 = (bf16[256,2048]{1,0:T(8,128)(2,1)}, bf16[256,2048]{1,0:T(8,128)(2,1)}, u32[]{:S(2)}, u32[]{:S(2)}) collective-permute-start(bf16[256,2048]{1,0:T(8,128)(2,1)} %add_convert_fusion.1), channel_id=1, source_target_pairs={{0,8},{8,16},{16,24},{24,0},{1,9},{9,17},{17,25},{25,1},{2,10},{10... | collective-permute-start | bytes 3145736 | tf_op jit(solution)/shard_map/ppermute | solution.py:238
  465.9 57.9 %collective-permute-start.36 = (bf16[2,3,512,256]{3,2,1,0:T(8,128)(2,1)}, bf16[2,3,512,256]{3,2,1,0:T(8,128)(2,1)S(1)}, u32[]{:S(2)}, u32[]{:S(2)}) collective-permute-start(bf16[2,3,512,256]{3,2,1,0:T(8,128)(2,1)} %get-tuple-element.230), channel_id=1, source_target_pairs={{0,1},{1,0},{2,3},{3,2},{4,5},{5,4},{6,7},{7,6},{8,9},{9,8},{10,11... | collective-permute-start | bytes 4718600 | tf_op jit(solution)/shard_map/ppermute | solution.py:233
  467.9 57.3 %collective-permute-start.37 = (bf16[2,3,512,256]{3,2,1,0:T(8,128)(2,1)}, bf16[2,3,512,256]{3,2,1,0:T(8,128)(2,1)S(1)}, u32[]{:S(2)}, u32[]{:S(2)}) collective-permute-start(bf16[2,3,512,256]{3,2,1,0:T(8,128)(2,1)} %get-tuple-element.231), channel_id=1, source_target_pairs={{0,4},{2,6},{4,0},{6,2},{1,5},{3,7},{5,1},{7,3},{8,12},{10,14},{12... | collective-permute-start | bytes 4718600 | tf_op jit(solution)/shard_map/ppermute | solution.py:233
  497.6 36.3 %collective-permute-start.35 = (bf16[256,2048]{1,0:T(8,128)(2,1)}, bf16[256,2048]{1,0:T(8,128)(2,1)}, u32[]{:S(2)}, u32[]{:S(2)}) collective-permute-start(bf16[256,2048]{1,0:T(8,128)(2,1)} %get-tuple-element.227), channel_id=1, source_target_pairs={{0,8},{8,16},{16,24},{24,0},{1,9},{9,17},{17,25},{25,1},{2,10},{10... | collective-permute-start | bytes 3145736 | tf_op jit(solution)/shard_map/ppermute | solution.py:238
  531.4 30.5 %collective-permute-start.43 = (bf16[3,512,256]{2,1,0:T(8,128)(2,1)}, bf16[3,512,256]{2,1,0:T(8,128)(2,1)S(1)}, u32[]{:S(2)}, u32[]{:S(2)}) collective-permute-start(bf16[3,512,256]{2,1,0:T(8,128)(2,1)} %get-tuple-element.252), channel_id=1, source_target_pairs={{0,4},{2,6},{4,0},{6,2},{1,5},{3,7},{5,1},{7,3},{8,12},{10,14},{12... | collective-permute-start | bytes 2359304 | tf_op jit(solution)/shard_map/ppermute | solution.py:233
  533.9 28.1 %collective-permute-start.44 = (bf16[3,512,256]{2,1,0:T(8,128)(2,1)}, bf16[3,512,256]{2,1,0:T(8,128)(2,1)S(1)}, u32[]{:S(2)}, u32[]{:S(2)}) collective-permute-start(bf16[3,512,256]{2,1,0:T(8,128)(2,1)} %get-tuple-element.253), channel_id=1, source_target_pairs={{0,1},{1,0},{2,3},{3,2},{4,5},{5,4},{6,7},{7,6},{8,9},{9,8},{10,11... | collective-permute-start | bytes 2359304 | tf_op jit(solution)/shard_map/ppermute | solution.py:233
  567.3 372.2 %all-gather.14.cloned.1.call-start = ((), (), s32[]{:S(2)}) async-start(), calls=%async_computation.2 | async-start | bytes 14155776 | tf_op jit(solution)/shard_map/all_gather | solution.py:719
  570.9 23.3 %collective-permute-start.39 = (bf16[2,3,512,256]{3,2,1,0:T(8,128)(2,1)}, bf16[2,3,512,256]{3,2,1,0:T(8,128)(2,1)S(1)}, u32[]{:S(2)}, u32[]{:S(2)}) collective-permute-start(bf16[2,3,512,256]{3,2,1,0:T(8,128)(2,1)} %get-tuple-element.246), channel_id=1, source_target_pairs={{0,2},{2,0},{4,6},{6,4},{1,3},{3,1},{5,7},{7,5},{8,10},{10,8},{12,... | collective-permute-start | bytes 4718600 | tf_op jit(solution)/shard_map/ppermute | solution.py:233
  571.0 23.2 %collective-permute-start.40 = (bf16[2,3,512,256]{3,2,1,0:T(8,128)(2,1)}, bf16[2,3,512,256]{3,2,1,0:T(8,128)(2,1)S(1)}, u32[]{:S(2)}, u32[]{:S(2)}) collective-permute-start(bf16[2,3,512,256]{3,2,1,0:T(8,128)(2,1)} %get-tuple-element.247), channel_id=1, source_target_pairs={{0,2},{2,0},{4,6},{6,4},{1,3},{3,1},{5,7},{7,5},{8,10},{10,8},{12,... | collective-permute-start | bytes 4718600 | tf_op jit(solution)/shard_map/ppermute | solution.py:233
  571.5 22.7 %collective-permute-start.41 = (bf16[2,3,512,256]{3,2,1,0:T(8,128)(2,1)}, bf16[2,3,512,256]{3,2,1,0:T(8,128)(2,1)}, u32[]{:S(2)}, u32[]{:S(2)}) collective-permute-start(bf16[2,3,512,256]{3,2,1,0:T(8,128)(2,1)} %get-tuple-element.248), channel_id=1, source_target_pairs={{0,2},{2,0},{4,6},{6,4},{1,3},{3,1},{5,7},{7,5},{8,10},{10,8},{12,... | collective-permute-start | bytes 4718600 | tf_op jit(solution)/shard_map/ppermute | solution.py:233
  571.5 22.7 %collective-permute-start.42 = (bf16[2,3,512,256]{3,2,1,0:T(8,128)(2,1)}, bf16[2,3,512,256]{3,2,1,0:T(8,128)(2,1)}, u32[]{:S(2)}, u32[]{:S(2)}) collective-permute-start(bf16[2,3,512,256]{3,2,1,0:T(8,128)(2,1)} %get-tuple-element.249), channel_id=1, source_target_pairs={{0,2},{2,0},{4,6},{6,4},{1,3},{3,1},{5,7},{7,5},{8,10},{10,8},{12,... | collective-permute-start | bytes 4718600 | tf_op jit(solution)/shard_map/ppermute | solution.py:233
  589.7 25.5 %collective-permute-start.38 = (bf16[256,2048]{1,0:T(8,128)(2,1)}, bf16[256,2048]{1,0:T(8,128)(2,1)}, u32[]{:S(2)}, u32[]{:S(2)}) collective-permute-start(bf16[256,2048]{1,0:T(8,128)(2,1)} %get-tuple-element.244), channel_id=1, source_target_pairs={{0,8},{8,16},{16,24},{24,0},{1,9},{9,17},{17,25},{25,1},{2,10},{10... | collective-permute-start | bytes 3145736 | tf_op jit(solution)/shard_map/ppermute | solution.py:238
  623.9 36.1 %collective-permute-start.52 = (bf16[256,2048]{1,0:T(8,128)(2,1)S(1)}, bf16[256,2048]{1,0:T(8,128)(2,1)}, u32[]{:S(2)}, u32[]{:S(2)}) collective-permute-start(bf16[256,2048]{1,0:T(8,128)(2,1)S(1)} %get-tuple-element.373), channel_id=1, source_target_pairs={{0,4},{2,6},{4,0},{6,2},{1,5},{3,7},{5,1},{7,3},{8,12},{10,14},{12... | collective-permute-start | bytes 3145736 | tf_op jit(solution)/shard_map/ppermute | solution.py:233
  625.3 36.8 %collective-permute-start.33 = (bf16[256,2048]{1,0:T(8,128)(2,1)}, bf16[256,2048]{1,0:T(8,128)(2,1)S(1)}, u32[]{:S(2)}, u32[]{:S(2)}) collective-permute-start(bf16[256,2048]{1,0:T(8,128)(2,1)} %add_convert_fusion.2), channel_id=1, source_target_pairs={{0,8},{8,16},{16,24},{24,0},{1,9},{9,17},{17,25},{25,1},{2,10},{10... | collective-permute-start | bytes 3145736 | tf_op jit(solution)/shard_map/ppermute | solution.py:238
  625.3 41.5 %collective-permute-start.51 = (bf16[256,2048]{1,0:T(8,128)(2,1)S(1)}, bf16[256,2048]{1,0:T(8,128)(2,1)}, u32[]{:S(2)}, u32[]{:S(2)}) collective-permute-start(bf16[256,2048]{1,0:T(8,128)(2,1)S(1)} %get-tuple-element.373), channel_id=1, source_target_pairs={{0,2},{2,0},{4,6},{6,4},{1,3},{3,1},{5,7},{7,5},{8,10},{10,8},{12,... | collective-permute-start | bytes 3145736 | tf_op jit(solution)/shard_map/ppermute | solution.py:233
  660.1 93.2 %collective-permute-start.55 = (bf16[2,3,512,256]{3,2,1,0:T(8,128)(2,1)}, bf16[2,3,512,256]{3,2,1,0:T(8,128)(2,1)}, u32[]{:S(2)}, u32[]{:S(2)}) collective-permute-start(bf16[2,3,512,256]{3,2,1,0:T(8,128)(2,1)} %get-tuple-element.286), channel_id=1, source_target_pairs={{0,2},{2,0},{4,6},{6,4},{1,3},{3,1},{5,7},{7,5},{8,10},{10,8},{12,... | collective-permute-start | bytes 4718600 | tf_op jit(solution)/shard_map/ppermute | solution.py:233
  660.7 67.9 %collective-permute-start.46 = (bf16[2,3,512,256]{3,2,1,0:T(8,128)(2,1)}, bf16[2,3,512,256]{3,2,1,0:T(8,128)(2,1)}, u32[]{:S(2)}, u32[]{:S(2)}) collective-permute-start(bf16[2,3,512,256]{3,2,1,0:T(8,128)(2,1)} %get-tuple-element.265), channel_id=1, source_target_pairs={{0,1},{1,0},{2,3},{3,2},{4,5},{5,4},{6,7},{7,6},{8,9},{9,8},{10,11... | collective-permute-start | bytes 4718600 | tf_op jit(solution)/shard_map/ppermute | solution.py:233
  662.1 66.5 %collective-permute-start.47 = (bf16[2,3,512,256]{3,2,1,0:T(8,128)(2,1)}, bf16[2,3,512,256]{3,2,1,0:T(8,128)(2,1)}, u32[]{:S(2)}, u32[]{:S(2)}) collective-permute-start(bf16[2,3,512,256]{3,2,1,0:T(8,128)(2,1)} %get-tuple-element.266), channel_id=1, source_target_pairs={{0,4},{2,6},{4,0},{6,2},{1,5},{3,7},{5,1},{7,3},{8,12},{10,14},{12... | collective-permute-start | bytes 4718600 | tf_op jit(solution)/shard_map/ppermute | solution.py:233
  666.9 67.2 %collective-permute-start.45 = (bf16[256,2048]{1,0:T(8,128)(2,1)}, bf16[256,2048]{1,0:T(8,128)(2,1)}, u32[]{:S(2)}, u32[]{:S(2)}) collective-permute-start(bf16[256,2048]{1,0:T(8,128)(2,1)} %get-tuple-element.262), channel_id=1, source_target_pairs={{0,8},{8,16},{16,24},{24,0},{1,9},{9,17},{17,25},{25,1},{2,10},{10... | collective-permute-start | bytes 3145736 | tf_op jit(solution)/shard_map/ppermute | solution.py:238
  703.1 34.9 %collective-permute-start.60 = (f32[2,4,256]{2,1,0:T(4,128)S(1)}, f32[2,4,256]{2,1,0:T(4,128)S(1)}, u32[]{:S(2)}, u32[]{:S(2)}) collective-permute-start(f32[2,4,256]{2,1,0:T(4,128)S(1)} %maximum_add_fusion.3), channel_id=1, source_target_pairs={{0,4},{2,6},{4,0},{6,2},{1,5},{3,7},{5,1},{7,3},{8,12},{10,14},{12... | collective-permute-start | bytes 24584 | tf_op jit(solution)/shard_map/ppermute | solution.py:233
  728.5 26.3 %collective-permute-start.56 = (bf16[2,3,512,256]{3,2,1,0:T(8,128)(2,1)}, bf16[2,3,512,256]{3,2,1,0:T(8,128)(2,1)}, u32[]{:S(2)}, u32[]{:S(2)}) collective-permute-start(bf16[2,3,512,256]{3,2,1,0:T(8,128)(2,1)} %get-tuple-element.287), channel_id=1, source_target_pairs={{0,2},{2,0},{4,6},{6,4},{1,3},{3,1},{5,7},{7,5},{8,10},{10,8},{12,... | collective-permute-start | bytes 4718600 | tf_op jit(solution)/shard_map/ppermute | solution.py:233
  728.6 26.7 %collective-permute-start.57 = (bf16[2,3,512,256]{3,2,1,0:T(8,128)(2,1)}, bf16[2,3,512,256]{3,2,1,0:T(8,128)(2,1)}, u32[]{:S(2)}, u32[]{:S(2)}) collective-permute-start(bf16[2,3,512,256]{3,2,1,0:T(8,128)(2,1)} %get-tuple-element.288), channel_id=1, source_target_pairs={{0,2},{2,0},{4,6},{6,4},{1,3},{3,1},{5,7},{7,5},{8,10},{10,8},{12,... | collective-permute-start | bytes 4718600 | tf_op jit(solution)/shard_map/ppermute | solution.py:233
  734.1 37.6 %collective-permute-start.58 = (bf16[2,3,512,256]{3,2,1,0:T(8,128)(2,1)}, bf16[2,3,512,256]{3,2,1,0:T(8,128)(2,1)}, u32[]{:S(2)}, u32[]{:S(2)}) collective-permute-start(bf16[2,3,512,256]{3,2,1,0:T(8,128)(2,1)} %get-tuple-element.289), channel_id=1, source_target_pairs={{0,2},{2,0},{4,6},{6,4},{1,3},{3,1},{5,7},{7,5},{8,10},{10,8},{12,... | collective-permute-start | bytes 4718600 | tf_op jit(solution)/shard_map/ppermute | solution.py:233
  738.0 46.3 %collective-permute-start.64 = (bf16[128,2048]{1,0:T(8,128)(2,1)S(1)}, bf16[128,2048]{1,0:T(8,128)(2,1)}, u32[]{:S(2)}, u32[]{:S(2)}) collective-permute-start(bf16[128,2048]{1,0:T(8,128)(2,1)S(1)} %bitcast.322), channel_id=1, source_target_pairs={{0,8},{8,16},{16,24},{24,0},{1,9},{9,17},{17,25},{25,1},{2,10},{10... | collective-permute-start | bytes 1572872 | tf_op jit(solution)/shard_map/ppermute | solution.py:238
  753.3 27.3 %collective-permute-start.54 = (bf16[256,2048]{1,0:T(8,128)(2,1)}, bf16[256,2048]{1,0:T(8,128)(2,1)S(1)}, u32[]{:S(2)}, u32[]{:S(2)}) collective-permute-start(bf16[256,2048]{1,0:T(8,128)(2,1)} %get-tuple-element.284), channel_id=1, source_target_pairs={{0,8},{8,16},{16,24},{24,0},{1,9},{9,17},{17,25},{25,1},{2,10},{10... | collective-permute-start | bytes 3145736 | tf_op jit(solution)/shard_map/ppermute | solution.py:238
  754.8 32.8 %collective-permute-start.66 = (bf16[3,512,256]{2,1,0:T(8,128)(2,1)}, bf16[3,512,256]{2,1,0:T(8,128)(2,1)}, u32[]{:S(2)}, u32[]{:S(2)}) collective-permute-start(bf16[3,512,256]{2,1,0:T(8,128)(2,1)} %get-tuple-element.306), channel_id=1, source_target_pairs={{0,4},{2,6},{4,0},{6,2},{1,5},{3,7},{5,1},{7,3},{8,12},{10,14},{12... | collective-permute-start | bytes 2359304 | tf_op jit(solution)/shard_map/ppermute | solution.py:233
  755.4 32.2 %collective-permute-start.67 = (bf16[3,512,256]{2,1,0:T(8,128)(2,1)}, bf16[3,512,256]{2,1,0:T(8,128)(2,1)}, u32[]{:S(2)}, u32[]{:S(2)}) collective-permute-start(bf16[3,512,256]{2,1,0:T(8,128)(2,1)} %get-tuple-element.307), channel_id=1, source_target_pairs={{0,1},{1,0},{2,3},{3,2},{4,5},{5,4},{6,7},{7,6},{8,9},{9,8},{10,11... | collective-permute-start | bytes 2359304 | tf_op jit(solution)/shard_map/ppermute | solution.py:233
  791.7 220.7 %all-gather.18.cloned.1.call-start = ((), (), s32[]{:S(2)}) async-start(), calls=%async_computation.4 | async-start | bytes 14155776 | tf_op jit(solution)/shard_map/all_gather | solution.py:719
  792.0 56.3 %collective-permute-start.62 = (bf16[2,3,512,256]{3,2,1,0:T(8,128)(2,1)}, bf16[2,3,512,256]{3,2,1,0:T(8,128)(2,1)}, u32[]{:S(2)}, u32[]{:S(2)}) collective-permute-start(bf16[2,3,512,256]{3,2,1,0:T(8,128)(2,1)} %get-tuple-element.300), channel_id=1, source_target_pairs={{0,1},{1,0},{2,3},{3,2},{4,5},{5,4},{6,7},{7,6},{8,9},{9,8},{10,11... | collective-permute-start | bytes 4718600 | tf_op jit(solution)/shard_map/ppermute | solution.py:233
  793.1 56.4 %collective-permute-start.63 = (bf16[2,3,512,256]{3,2,1,0:T(8,128)(2,1)}, bf16[2,3,512,256]{3,2,1,0:T(8,128)(2,1)}, u32[]{:S(2)}, u32[]{:S(2)}) collective-permute-start(bf16[2,3,512,256]{3,2,1,0:T(8,128)(2,1)} %get-tuple-element.301), channel_id=1, source_target_pairs={{0,4},{2,6},{4,0},{6,2},{1,5},{3,7},{5,1},{7,3},{8,12},{10,14},{12... | collective-permute-start | bytes 4718600 | tf_op jit(solution)/shard_map/ppermute | solution.py:233
  795.6 59.1 %collective-permute-start.61 = (bf16[512,1536]{1,0:T(8,128)(2,1)S(1)}, bf16[512,1536]{1,0:T(8,128)(2,1)S(1)}, u32[]{:S(2)}, u32[]{:S(2)}) collective-permute-start(bf16[512,1536]{1,0:T(8,128)(2,1)S(1)} %slice.573), channel_id=1, source_target_pairs={{0,8},{8,16},{16,24},{24,0},{1,9},{9,17},{17,25},{25,1},{2,10},{10... | collective-permute-start | bytes 4718600 | tf_op jit(solution)/shard_map/ppermute | solution.py:238
  796.1 47.7 %collective-permute-start.65 = (bf16[128,2048]{1,0:T(8,128)(2,1)}, bf16[128,2048]{1,0:T(8,128)(2,1)S(1)}, u32[]{:S(2)}, u32[]{:S(2)}) collective-permute-start(bf16[128,2048]{1,0:T(8,128)(2,1)} %get-tuple-element.303), channel_id=1, source_target_pairs={{0,8},{8,16},{16,24},{24,0},{1,9},{9,17},{17,25},{25,1},{2,10},{10... | collective-permute-start | bytes 1572872 | tf_op jit(solution)/shard_map/ppermute | solution.py:238
  858.8 46.5 %collective-permute-start.68 = (bf16[512,1536]{1,0:T(8,128)(2,1)}, bf16[512,1536]{1,0:T(8,128)(2,1)S(1)}, u32[]{:S(2)}, u32[]{:S(2)}) collective-permute-start(bf16[512,1536]{1,0:T(8,128)(2,1)} %get-tuple-element.312), channel_id=1, source_target_pairs={{0,8},{8,16},{16,24},{24,0},{1,9},{9,17},{17,25},{25,1},{2,10},{10... | collective-permute-start | bytes 4718600 | tf_op jit(solution)/shard_map/ppermute | solution.py:238
  859.4 50.0 %collective-permute-start.71 = (bf16[3,512,256]{2,1,0:T(8,128)(2,1)}, bf16[3,512,256]{2,1,0:T(8,128)(2,1)S(1)}, u32[]{:S(2)}, u32[]{:S(2)}) collective-permute-start(bf16[3,512,256]{2,1,0:T(8,128)(2,1)} %get-tuple-element.325), channel_id=1, source_target_pairs={{0,4},{2,6},{4,0},{6,2},{1,5},{3,7},{5,1},{7,3},{8,12},{10,14},{12... | collective-permute-start | bytes 2359304 | tf_op jit(solution)/shard_map/ppermute | solution.py:233
  861.0 48.4 %collective-permute-start.72 = (bf16[3,512,256]{2,1,0:T(8,128)(2,1)}, bf16[3,512,256]{2,1,0:T(8,128)(2,1)S(1)}, u32[]{:S(2)}, u32[]{:S(2)}) collective-permute-start(bf16[3,512,256]{2,1,0:T(8,128)(2,1)} %get-tuple-element.326), channel_id=1, source_target_pairs={{0,1},{1,0},{2,3},{3,2},{4,5},{5,4},{6,7},{7,6},{8,9},{9,8},{10,11... | collective-permute-start | bytes 2359304 | tf_op jit(solution)/shard_map/ppermute | solution.py:233
  862.2 41.1 %collective-permute-start.69 = (bf16[128,2048]{1,0:T(8,128)(2,1)}, bf16[128,2048]{1,0:T(8,128)(2,1)}, u32[]{:S(2)}, u32[]{:S(2)}) collective-permute-start(bf16[128,2048]{1,0:T(8,128)(2,1)} %get-tuple-element.313), channel_id=1, source_target_pairs={{0,8},{8,16},{16,24},{24,0},{1,9},{9,17},{17,25},{25,1},{2,10},{10... | collective-permute-start | bytes 1572872 | tf_op jit(solution)/shard_map/ppermute | solution.py:238
  918.3 39.0 %collective-permute-start.70 = (bf16[512,1536]{1,0:T(8,128)(2,1)}, bf16[512,1536]{1,0:T(8,128)(2,1)}, u32[]{:S(2)}, u32[]{:S(2)}) collective-permute-start(bf16[512,1536]{1,0:T(8,128)(2,1)} %get-tuple-element.320), channel_id=1, source_target_pairs={{0,8},{8,16},{16,24},{24,0},{1,9},{9,17},{17,25},{25,1},{2,10},{10... | collective-permute-start | bytes 4718600 | tf_op jit(solution)/shard_map/ppermute | solution.py:238
  924.0 39.8 %collective-permute-start.74 = (bf16[256,2048]{1,0:T(8,128)(2,1)S(1)}, bf16[256,2048]{1,0:T(8,128)(2,1)}, u32[]{:S(2)}, u32[]{:S(2)}) collective-permute-start(bf16[256,2048]{1,0:T(8,128)(2,1)S(1)} %fusion.19), channel_id=1, source_target_pairs={{0,4},{2,6},{4,0},{6,2},{1,5},{3,7},{5,1},{7,3},{8,12},{10,14},{12... | collective-permute-start | bytes 3145736 | tf_op jit(solution)/shard_map/ppermute | solution.py:233
  974.0 54.8 %collective-permute-start.85 = (bf16[128,2048]{1,0:T(8,128)(2,1)}, bf16[128,2048]{1,0:T(8,128)(2,1)}, u32[]{:S(2)}, u32[]{:S(2)}) collective-permute-start(bf16[128,2048]{1,0:T(8,128)(2,1)} %get-tuple-element.346), channel_id=1, source_target_pairs={{0,1},{1,0},{2,3},{3,2},{4,5},{5,4},{6,7},{7,6},{8,9},{9,8},{10,11... | collective-permute-start | bytes 1572872 | tf_op jit(solution)/shard_map/ppermute | solution.py:233
  980.2 51.1 %collective-permute-start.78 = (f32[2,20,128]{2,1,0:T(8,128)S(1)}, f32[2,20,128]{2,1,0:T(8,128)S(1)}, u32[]{:S(2)}, u32[]{:S(2)}) collective-permute-start(f32[2,20,128]{2,1,0:T(8,128)S(1)} %pad_maximum_fusion.29), channel_id=1, source_target_pairs={{0,2},{2,0},{4,6},{6,4},{1,3},{3,1},{5,7},{7,5},{8,10},{10,8},{12,... | collective-permute-start | bytes 61448 | tf_op jit(solution)/shard_map/ppermute | solution.py:233
  1028.4 36.9 %collective-permute-start.81 = (bf16[4,128,3,2,256]{4,1,3,2,0:T(8,128)(2,1)S(1)}, bf16[4,128,3,2,256]{4,1,3,2,0:T(8,128)(2,1)S(1)}, u32[]{:S(2)}, u32[]{:S(2)}) collective-permute-start(bf16[4,128,3,2,256]{4,1,3,2,0:T(8,128)(2,1)S(1)} %get-tuple-element.415), channel_id=1, source_target_pairs={{0,1},{1,0},{2,3},{3,2},{4,5},{5,4},{6,7},{7,6},{8,9},{9,8},{10,11... | collective-permute-start | bytes 4718600 | tf_op jit(solution)/shard_map/ppermute | solution.py:233
  1035.1 30.2 %collective-permute-start.80 = (f32[20,128]{1,0:T(8,128)S(1)}, f32[20,128]{1,0:T(8,128)S(1)}, u32[]{:S(2)}, u32[]{:S(2)}) collective-permute-start(f32[20,128]{1,0:T(8,128)S(1)} %fusion.52), channel_id=1, source_target_pairs={{0,1},{1,0},{2,3},{3,2},{4,5},{5,4},{6,7},{7,6},{8,9},{9,8},{10,11... | collective-permute-start | bytes 30728 | tf_op jit(solution)/shard_map/ppermute | solution.py:233
  (129 other events, 1462.2 us)
Sparse Core Ops, SparseCore 0:
  99.8 45.2 all-gather.11
  146.7 112.9 all-gather.9
  405.2 200.9 all-reduce.3
  608.0 119.4 all-gather.15
  791.8 106.0 all-gather.13
  914.7 97.6 all-gather.17
